TPU v7x, 32 devices: a whole 2x2x4 slice. The times are simulated.
32 devices in a mesh: ctx: 16 (over z, x, core), tp: 2 (over y).
Axes of the slice: x: 2, y: 2, z: 4, core: 2. Of those that a mesh axis runs over, the one named last changes fastest.
Arguments:
- post_gate: bfloat16 [2048, 2048], P('ctx', 'tp'), may hold values from -6 to 6
- pre_gate: bfloat16 [2048, 2048], P('ctx', 'tp'), may hold values from -6 to 6
- features: bfloat16 [2048, 2048], P('ctx', 'tp'), may hold values from -6 to 6
- filters: float32 [2048, 2048], P('ctx', 'tp'), may hold values from -1.1 to 1.1
- token_ids: int32 [2048], P('ctx'), may hold values from 0 to 5
- out_weight: bfloat16 [2048, 2048], P('tp'), may hold values from -0.125 to 0.125
- out_grad: bfloat16 [2048, 2048], P('ctx', 'tp'), may hold values from -6 to 6
Outputs:
- output: bfloat16 [2048, 2048], P('ctx', 'tp')
- grad_post: bfloat16 [2048, 2048], P('ctx', 'tp')
- grad_pre: bfloat16 [2048, 2048], P('ctx', 'tp')
- grad_features: bfloat16 [2048, 2048], P('ctx', 'tp')
All inputs are finite; a program needn't handle non-finite values.
Results may differ from a plain program's by a relative error of at most 0.022.
Values may be sent and summed in bfloat16 or wider, within the bound.
No kernel may reach another device: no remote copies, remote signals or barrier semaphores. Data moves between devices by JAX's collectives and lax.ppermute only.
A program may use at most 128 MiB of HBM per device.

v0:
```python
import math

import jax
import jax.numpy as jnp
from jax import lax
from jax.sharding import PartitionSpec as P

BASES = 4


exact_mode = lax.Precision.HIGHEST


def angle_table(left_index, right_index, modulus):
    product = left_index[:, None] * right_index[None, :] % modulus
    return product.astype(jnp.float32) * (2.0 * math.pi / modulus)


def frequency_order(ctx_count):
    position = jnp.arange(2 * ctx_count, dtype=jnp.int32)
    pair_index = position // 2
    mirrored = jnp.where(pair_index == 0, ctx_count, 2 * ctx_count - pair_index)
    return jnp.where(position % 2 == 0, pair_index, mirrored)


def contract(einsum_form, matrix_tab, operand):
    return jnp.einsum(einsum_form, matrix_tab, operand, precision=exact_mode)


def regroup_tokens(signal):
    return lax.all_to_all(
        signal.astype(jnp.bfloat16), "ctx", split_axis=1, concat_axis=0, tiled=True
    ).astype(signal.dtype)


def regroup_spectra(real_part, imag_part):
    return (
        lax.all_to_all(
            real_part.astype(jnp.bfloat16), "ctx", split_axis=1, concat_axis=0, tiled=True
        ).astype(real_part.dtype),
        lax.all_to_all(
            imag_part.astype(jnp.bfloat16), "ctx", split_axis=1, concat_axis=0, tiled=True
        ).astype(imag_part.dtype),
    )


def frequency_response(signal):
    ctx_count = lax.axis_size("ctx")
    ctx_rank = lax.axis_index("ctx")
    tokens = signal.shape[0]
    block_len = tokens // ctx_count
    wide_len = 2 * ctx_count
    full_len = tokens * wide_len
    freq_order = frequency_order(ctx_count)
    sources = jnp.arange(ctx_count, dtype=jnp.int32)
    outer_angle = angle_table(freq_order, sources, wide_len)
    outer_cos = jnp.cos(outer_angle)
    outer_sin = jnp.sin(outer_angle)
    columns = regroup_tokens(signal[None])
    real_mid = contract("mb,bac->amc", outer_cos, columns)
    imag_mid = -contract("mb,bac->amc", outer_sin, columns)
    positions = ctx_rank * block_len + jnp.arange(block_len, dtype=jnp.int32)
    twist_angle = angle_table(positions, freq_order, full_len)[:, :, None]
    twist_cos = jnp.cos(twist_angle)
    twist_sin = jnp.sin(twist_angle)
    real_tw = real_mid * twist_cos + imag_mid * twist_sin
    imag_tw = imag_mid * twist_cos - real_mid * twist_sin
    real_all, imag_all = regroup_spectra(real_tw, imag_tw)
    steps_index = jnp.arange(tokens, dtype=jnp.int32)
    inner_angle = angle_table(steps_index, steps_index, tokens)
    inner_cos = jnp.cos(inner_angle)
    inner_sin = jnp.sin(inner_angle)
    real_out = contract("ka,asc->ksc", inner_cos, real_all) + contract(
        "ka,asc->ksc", inner_sin, imag_all
    )
    imag_out = contract("ka,asc->ksc", inner_cos, imag_all) - contract(
        "ka,asc->ksc", inner_sin, real_all
    )
    return (real_out, imag_out)


def to_signal(real_spec, imag_spec):
    ctx_count = lax.axis_size("ctx")
    ctx_rank = lax.axis_index("ctx")
    tokens = real_spec.shape[0]
    wide_len = 2 * ctx_count
    full_len = tokens * wide_len
    steps_index = jnp.arange(tokens, dtype=jnp.int32)
    inner_angle = angle_table(steps_index, steps_index, tokens)
    inner_cos = jnp.cos(inner_angle)
    inner_sin = jnp.sin(inner_angle)
    real_mid = contract("ak,ksc->sac", inner_cos, real_spec) - contract(
        "ak,ksc->sac", inner_sin, imag_spec
    )
    imag_mid = contract("ak,ksc->sac", inner_cos, imag_spec) + contract(
        "ak,ksc->sac", inner_sin, real_spec
    )
    freq_order = frequency_order(ctx_count)
    local_order = lax.dynamic_slice_in_dim(freq_order, 2 * ctx_rank, 2)
    twist_angle = angle_table(local_order, steps_index, full_len)[:, :, None]
    twist_cos = jnp.cos(twist_angle)
    twist_sin = jnp.sin(twist_angle)
    real_tw = real_mid * twist_cos - imag_mid * twist_sin
    imag_tw = imag_mid * twist_cos + real_mid * twist_sin
    real_all, imag_all = regroup_spectra(real_tw, imag_tw)
    targets = jnp.arange(ctx_count, dtype=jnp.int32)
    outer_angle = angle_table(targets, freq_order, wide_len)
    signal = contract("bm,mac->abc", jnp.cos(outer_angle), real_all) - contract(
        "bm,mac->abc", jnp.sin(outer_angle), imag_all
    )
    signal = signal * (1.0 / full_len)
    return regroup_tokens(signal).reshape(tokens, -1)


def on_device(post_gate, pre_gate, features, filters, token_ids, out_weight, out_grad):
    channels = post_gate.shape[1]
    keep_mask = (token_ids < BASES).astype(jnp.float32)[:, None]
    post_wide = post_gate.astype(jnp.float32)
    pre_wide = pre_gate.astype(jnp.float32)
    feat_wide = features.astype(jnp.float32)
    mixer_input = pre_wide * feat_wide * keep_mask
    stacked = jnp.concatenate([mixer_input, filters], axis=1)
    real_spec, imag_spec = frequency_response(stacked)
    input_real = real_spec[:, :, :channels]
    input_imag = imag_spec[:, :, :channels]
    filter_real = real_spec[:, :, channels:]
    filter_imag = imag_spec[:, :, channels:]
    mixed_signal = to_signal(
        input_real * filter_real - input_imag * filter_imag,
        input_real * filter_imag + input_imag * filter_real,
    )
    gated_out = (post_wide * mixed_signal).astype(jnp.bfloat16)
    incomplete_result = jnp.dot(gated_out, out_weight, preferred_element_type=jnp.float32)
    summed = lax.psum(incomplete_result.astype(jnp.bfloat16), "tp").astype(jnp.float32)
    column_share = out_grad.shape[1]
    output = lax.dynamic_slice_in_dim(
        summed, lax.axis_index("tp") * column_share, column_share, 1
    ).astype(jnp.bfloat16)
    grad_gated = lax.dot_general(
        lax.all_gather(out_grad, "tp", axis=1, tiled=True),
        out_weight,
        (((1,), (1,)), ((), ())),
        preferred_element_type=jnp.float32,
    )
    grad_post = (grad_gated * mixed_signal).astype(jnp.bfloat16)
    grad_mixed = grad_gated * post_wide
    grad_real, grad_imag = frequency_response(grad_mixed)
    grad_input = to_signal(
        filter_real * grad_real + filter_imag * grad_imag,
        filter_real * grad_imag - filter_imag * grad_real,
    )
    grad_pre = (grad_input * feat_wide * keep_mask).astype(jnp.bfloat16)
    grad_features = (grad_input * pre_wide * keep_mask).astype(jnp.bfloat16)
    return (output, grad_post, grad_pre, grad_features)


def solution(mesh):
    in_specs = (
        P("ctx", "tp"),
        P("ctx", "tp"),
        P("ctx", "tp"),
        P("ctx", "tp"),
        P("ctx"),
        P("tp", None),
        P("ctx", "tp"),
    )
    out_specs = (P("ctx", "tp"), P("ctx", "tp"), P("ctx", "tp"), P("ctx", "tp"))
    return jax.shard_map(
        on_device, mesh=mesh, in_specs=in_specs, out_specs=out_specs, check_vma=False
    )
```

profile of v0, /device:TPU:0, one launch (start us, length us, event | category | flops | bytes accessed | tf_op | source)
XLA Modules:
  0.0 328.7 jit_solution(12616573419877767283)
XLA Ops:
  7.2 10.2 %all_gather.3 = bf16[128,2048]{1,0:T(8,128)(2,1)S(1)} all-gather(bf16[128,1024]{1,0:T(8,128)(2,1)} %param.13), channel_id=1, replica_groups=mesh['ctx'=16,'tp'=2] {'tp'}, dimensions={1}, use_global_device_ids=true | all-gather | bytes 786432 | tf_op jit(solution)/shard_map/all_gather | solution.py:140
  17.4 3.8 %fusion.247 = f32[128,1024]{1,0:T(8,128)S(1)} fusion(bf16[128,2048]{1,0:T(8,128)(2,1)S(1)} %all_gather.3, bf16[1024,2048]{1,0:T(8,128)(2,1)} %param.12), kind=kOutput, calls=%fused_computation.280 | convolution fusion | flops 536870912 | bytes 5242880 | tf_op jit(solution)/shard_map/dot_general | solution.py:139
  26.0 6.1 %all-to-all-start.6 = ((bf16[16,2,4096]{2,1,0:T(2,128)(2,1)}), bf16[16,2,4096]{2,1,0:T(2,128)(2,1)S(1)}, u32[]{:S(2)}, u32[]{:S(2)}) async-start(bf16[16,2,4096]{2,1,0:T(2,128)(2,1)} %reshape.257), calls=%async_computation.6 | async-start | bytes 524288 | tf_op jit(solution)/shard_map/all_to_all | solution.py:31
  33.1 3.7 %reduce.1 = bf16[128,2048]{1,0:T(8,128)(2,1)S(1)} reduce(bf16[128,1,2048]{2,1,0:T(2,128)(2,1)S(1)} %bitcast.214, bf16[]{:T(256)} %broadcast.582), dimensions={1}, to_apply=%bitcast.201.reduce_sub_computation | reduce | bytes 1048578
  38.2 4.0 %all-to-all-done.6 = bf16[16,2,4096]{2,1,0:T(2,128)(2,1)S(1)} async-done(((bf16[16,2,4096]{2,1,0:T(2,128)(2,1)}), bf16[16,2,4096]{2,1,0:T(2,128)(2,1)S(1)}, u32[]{:S(2)}, u32[]{:S(2)}) %all-to-all-start.6) | async-done | bytes 262176 | tf_op jit(solution)/shard_map/all_to_all | solution.py:31
  42.1 3.6 %all-to-all-start = ((bf16[16,2,8192]{2,1,0:T(2,128)(2,1)}), bf16[16,2,8192]{2,1,0:T(2,128)(2,1)S(1)}, u32[]{:S(2)}, u32[]{:S(2)}) async-start(bf16[16,2,8192]{2,1,0:T(2,128)(2,1)} %reshape.255), calls=%async_computation | async-start | bytes 1048576 | tf_op jit(solution)/shard_map/all_to_all | solution.py:31
  49.0 11.1 %all-to-all-done = bf16[16,2,8192]{2,1,0:T(2,128)(2,1)S(1)} async-done(((bf16[16,2,8192]{2,1,0:T(2,128)(2,1)}), bf16[16,2,8192]{2,1,0:T(2,128)(2,1)S(1)}, u32[]{:S(2)}, u32[]{:S(2)}) %all-to-all-start) | async-done | bytes 524320 | tf_op jit(solution)/shard_map/all_to_all | solution.py:31
  60.1 4.0 %all-to-all-start.7 = ((bf16[8,32,1024]{2,0,1:T(8,128)(2,1)}), bf16[8,32,1024]{2,0,1:T(8,128)(2,1)S(1)}, u32[]{:S(2)}, u32[]{:S(2)}) async-start(bf16[8,32,1024]{2,0,1:T(8,128)(2,1)} %copy.110), calls=%async_computation.7 | async-start | bytes 1048576 | tf_op jit(solution)/shard_map/all_to_all | solution.py:38
  65.3 13.4 %all-to-all-done.7 = bf16[8,32,1024]{2,0,1:T(8,128)(2,1)S(1)} async-done(((bf16[8,32,1024]{2,0,1:T(8,128)(2,1)}), bf16[8,32,1024]{2,0,1:T(8,128)(2,1)S(1)}, u32[]{:S(2)}, u32[]{:S(2)}) %all-to-all-start.7) | async-done | bytes 524320 | tf_op jit(solution)/shard_map/all_to_all | solution.py:38
  78.6 15.6 %all-to-all-start.8 = ((bf16[8,32,1024]{2,0,1:T(8,128)(2,1)}), bf16[8,32,1024]{2,0,1:T(8,128)(2,1)S(1)}, u32[]{:S(2)}, u32[]{:S(2)}) async-start(bf16[8,32,1024]{2,0,1:T(8,128)(2,1)} %copy.112), calls=%async_computation.8 | async-start | bytes 1048576 | tf_op jit(solution)/shard_map/all_to_all | solution.py:41
  99.5 9.1 %all-to-all-done.8 = bf16[8,32,1024]{2,0,1:T(8,128)(2,1)S(1)} async-done(((bf16[8,32,1024]{2,0,1:T(8,128)(2,1)}), bf16[8,32,1024]{2,0,1:T(8,128)(2,1)S(1)}, u32[]{:S(2)}, u32[]{:S(2)}) %all-to-all-start.8) | async-done | bytes 524320 | tf_op jit(solution)/shard_map/all_to_all | solution.py:41
  108.7 4.1 %all-to-all-start.1 = ((bf16[8,32,2048]{2,0,1:T(8,128)(2,1)}), bf16[8,32,2048]{2,0,1:T(8,128)(2,1)S(1)}, u32[]{:S(2)}, u32[]{:S(2)}) async-start(bf16[8,32,2048]{2,0,1:T(8,128)(2,1)} %copy.92), calls=%async_computation.1 | async-start | bytes 2097152 | tf_op jit(solution)/shard_map/all_to_all | solution.py:38
  114.4 21.4 %all-to-all-done.1 = bf16[8,32,2048]{2,0,1:T(8,128)(2,1)S(1)} async-done(((bf16[8,32,2048]{2,0,1:T(8,128)(2,1)}), bf16[8,32,2048]{2,0,1:T(8,128)(2,1)S(1)}, u32[]{:S(2)}, u32[]{:S(2)}) %all-to-all-start.1) | async-done | bytes 1048608 | tf_op jit(solution)/shard_map/all_to_all | solution.py:38
  135.7 6.9 %all-to-all-start.2 = ((bf16[8,32,2048]{2,0,1:T(8,128)(2,1)}), bf16[8,32,2048]{2,0,1:T(8,128)(2,1)S(1)}, u32[]{:S(2)}, u32[]{:S(2)}) async-start(bf16[8,32,2048]{2,0,1:T(8,128)(2,1)} %copy.94), calls=%async_computation.2 | async-start | bytes 2097152 | tf_op jit(solution)/shard_map/all_to_all | solution.py:41
  147.2 2.6 fusion.9
  149.8 15.7 %all-to-all-done.2 = bf16[8,32,2048]{2,0,1:T(8,128)(2,1)S(1)} async-done(((bf16[8,32,2048]{2,0,1:T(8,128)(2,1)}), bf16[8,32,2048]{2,0,1:T(8,128)(2,1)S(1)}, u32[]{:S(2)}, u32[]{:S(2)}) %all-to-all-start.2) | async-done | bytes 1048608 | tf_op jit(solution)/shard_map/all_to_all | solution.py:41
  175.1 2.4 convolution_add_fusion.2
  185.3 2.5 fusion.31
  189.2 6.9 %all-to-all-start.9 = ((bf16[2,128,1024]{2,0,1:T(2,128)(2,1)}), bf16[2,128,1024]{2,0,1:T(2,128)(2,1)S(1)}, u32[]{:S(2)}, u32[]{:S(2)}) async-start(bf16[2,128,1024]{2,0,1:T(2,128)(2,1)} %copy.118), calls=%async_computation.9 | async-start | bytes 1048576 | tf_op jit(solution)/shard_map/all_to_all | solution.py:38
  197.2 13.3 %all-to-all-done.9 = bf16[2,128,1024]{2,0,1:T(2,128)(2,1)S(1)} async-done(((bf16[2,128,1024]{2,0,1:T(2,128)(2,1)}), bf16[2,128,1024]{2,0,1:T(2,128)(2,1)S(1)}, u32[]{:S(2)}, u32[]{:S(2)}) %all-to-all-start.9) | async-done | bytes 524320 | tf_op jit(solution)/shard_map/all_to_all | solution.py:38
  210.5 4.1 %all-to-all-start.10 = ((bf16[2,128,1024]{2,0,1:T(2,128)(2,1)}), bf16[2,128,1024]{2,0,1:T(2,128)(2,1)S(1)}, u32[]{:S(2)}, u32[]{:S(2)}) async-start(bf16[2,128,1024]{2,0,1:T(2,128)(2,1)} %copy.121), calls=%async_computation.10 | async-start | bytes 1048576 | tf_op jit(solution)/shard_map/all_to_all | solution.py:41
  215.7 13.3 %all-to-all-done.10 = bf16[2,128,1024]{2,0,1:T(2,128)(2,1)S(1)} async-done(((bf16[2,128,1024]{2,0,1:T(2,128)(2,1)}), bf16[2,128,1024]{2,0,1:T(2,128)(2,1)S(1)}, u32[]{:S(2)}, u32[]{:S(2)}) %all-to-all-start.10) | async-done | bytes 524320 | tf_op jit(solution)/shard_map/all_to_all | solution.py:41
  229.1 4.1 %all-to-all-start.3 = ((bf16[2,128,1024]{2,0,1:T(2,128)(2,1)}), bf16[2,128,1024]{2,0,1:T(2,128)(2,1)S(1)}, u32[]{:S(2)}, u32[]{:S(2)}) async-start(bf16[2,128,1024]{2,0,1:T(2,128)(2,1)} %copy.100), calls=%async_computation.3 | async-start | bytes 1048576 | tf_op jit(solution)/shard_map/all_to_all | solution.py:38
  234.3 13.3 %all-to-all-done.3 = bf16[2,128,1024]{2,0,1:T(2,128)(2,1)S(1)} async-done(((bf16[2,128,1024]{2,0,1:T(2,128)(2,1)}), bf16[2,128,1024]{2,0,1:T(2,128)(2,1)S(1)}, u32[]{:S(2)}, u32[]{:S(2)}) %all-to-all-start.3) | async-done | bytes 524320 | tf_op jit(solution)/shard_map/all_to_all | solution.py:38
  247.6 4.1 %all-to-all-start.4 = ((bf16[2,128,1024]{2,0,1:T(2,128)(2,1)}), bf16[2,128,1024]{2,0,1:T(2,128)(2,1)S(1)}, u32[]{:S(2)}, u32[]{:S(2)}) async-start(bf16[2,128,1024]{2,0,1:T(2,128)(2,1)} %copy.103), calls=%async_computation.4 | async-start | bytes 1048576 | tf_op jit(solution)/shard_map/all_to_all | solution.py:41
  254.8 11.4 %all-to-all-done.4 = bf16[2,128,1024]{2,0,1:T(2,128)(2,1)S(1)} async-done(((bf16[2,128,1024]{2,0,1:T(2,128)(2,1)}), bf16[2,128,1024]{2,0,1:T(2,128)(2,1)S(1)}, u32[]{:S(2)}, u32[]{:S(2)}) %all-to-all-start.4) | async-done | bytes 524320 | tf_op jit(solution)/shard_map/all_to_all | solution.py:41
  268.4 4.1 %all-to-all-start.5 = ((bf16[8,16,1024]{2,0,1:T(8,128)(2,1)}), bf16[8,16,1024]{2,0,1:T(8,128)(2,1)S(1)}, u32[]{:S(2)}, u32[]{:S(2)}) async-start(bf16[8,16,1024]{2,0,1:T(8,128)(2,1)} %copy.106), calls=%async_computation.5 | async-start | bytes 524288 | tf_op jit(solution)/shard_map/all_to_all | solution.py:31
  274.2 8.3 %all-to-all-done.5 = bf16[8,16,1024]{2,0,1:T(8,128)(2,1)S(1)} async-done(((bf16[8,16,1024]{2,0,1:T(8,128)(2,1)}), bf16[8,16,1024]{2,0,1:T(8,128)(2,1)S(1)}, u32[]{:S(2)}, u32[]{:S(2)}) %all-to-all-start.5) | async-done | bytes 262176 | tf_op jit(solution)/shard_map/all_to_all | solution.py:31
  282.5 3.5 %all-to-all-start.11 = ((bf16[8,16,1024]{2,0,1:T(8,128)(2,1)}), bf16[8,16,1024]{2,0,1:T(8,128)(2,1)S(1)}, u32[]{:S(2)}, u32[]{:S(2)}) async-start(bf16[8,16,1024]{2,0,1:T(8,128)(2,1)} %copy.124), calls=%async_computation.11 | async-start | bytes 524288 | tf_op jit(solution)/shard_map/all_to_all | solution.py:31
  286.2 3.8 %convolution_convert_fusion = bf16[128,2048]{1,0:T(8,128)(2,1)} fusion(bf16[1024,2048]{1,0:T(8,128)(2,1)} %param.12, bf16[128,1024]{1,0:T(8,128)(2,1)S(1)} %copy-done.5, bf16[8,16,1024]{2,0,1:T(8,128)(2,1)S(1)} %all-to-all-done.5), kind=kOutput, calls=%fused_computation.3 | convolution fusion | flops 537657344 | bytes 5242880 | tf_op jit(solution)/shard_map/dot_general | solution.py:133
  290.7 5.3 %all-to-all-done.11 = bf16[8,16,1024]{2,0,1:T(8,128)(2,1)S(1)} async-done(((bf16[8,16,1024]{2,0,1:T(8,128)(2,1)}), bf16[8,16,1024]{2,0,1:T(8,128)(2,1)S(1)}, u32[]{:S(2)}, u32[]{:S(2)}) %all-to-all-start.11) | async-done | bytes 262176 | tf_op jit(solution)/shard_map/all_to_all | solution.py:31
  297.0 23.0 %all-reduce.2.cloned.1.call-done = bf16[128,2048]{1,0:T(8,128)(2,1)} async-done(((bf16[128,2048]{1,0:T(8,128)(2,1)}), bf16[128,2048]{1,0:T(8,128)(2,1)}) %all-reduce.2.cloned.1.call-update) | async-done | bytes 524304 | tf_op jit(solution)/shard_map/psum | solution.py:134
  (91 shorter events, 55.2 us)
Async XLA Ops:
  17.4 4.6 %copy-start.5 = (bf16[128,1024]{1,0:T(8,128)(2,1)S(1)}, bf16[128,1024]{1,0:T(8,128)(2,1)}, u32[]{:S(2)}) copy-start(bf16[128,1024]{1,0:T(8,128)(2,1)} %param.7) | copy-start | bytes 786436
  21.1 0.8 copy-start.1
  21.9 10.1 %copy-start.11 = (s32[128]{0:T(128)S(1)}, s32[128]{0:T(128)}, u32[]{:S(2)}) copy-start(s32[128]{0:T(128)} %param.11) | copy-start | bytes 1540
  21.9 10.2 %copy-start.6 = (bf16[128,1024]{1,0:T(8,128)(2,1)S(1)}, bf16[128,1024]{1,0:T(8,128)(2,1)}, u32[]{:S(2)}) copy-start(bf16[128,1024]{1,0:T(8,128)(2,1)} %param.9) | copy-start | bytes 786436
  22.0 10.2 %copy-start.8 = (bf16[128,1024]{1,0:T(8,128)(2,1)S(1)}, bf16[128,1024]{1,0:T(8,128)(2,1)}, u32[]{:S(2)}) copy-start(bf16[128,1024]{1,0:T(8,128)(2,1)} %param.8) | copy-start | bytes 786436
  22.0 10.2 %copy-start.10 = (f32[128,1024]{1,0:T(8,128)S(1)}, f32[128,1024]{1,0:T(8,128)}, u32[]{:S(2)}) copy-start(f32[128,1024]{1,0:T(8,128)} %param.10) | copy-start | bytes 1572868
  26.0 16.1 %all-to-all-start.6 = ((bf16[16,2,4096]{2,1,0:T(2,128)(2,1)}), bf16[16,2,4096]{2,1,0:T(2,128)(2,1)S(1)}, u32[]{:S(2)}, u32[]{:S(2)}) async-start(bf16[16,2,4096]{2,1,0:T(2,128)(2,1)} %reshape.257), calls=%async_computation.6 | async-start | bytes 524288 | tf_op jit(solution)/shard_map/all_to_all | solution.py:31
  42.1 18.0 %all-to-all-start = ((bf16[16,2,8192]{2,1,0:T(2,128)(2,1)}), bf16[16,2,8192]{2,1,0:T(2,128)(2,1)S(1)}, u32[]{:S(2)}, u32[]{:S(2)}) async-start(bf16[16,2,8192]{2,1,0:T(2,128)(2,1)} %reshape.255), calls=%async_computation | async-start | bytes 1048576 | tf_op jit(solution)/shard_map/all_to_all | solution.py:31
  60.1 18.5 %all-to-all-start.7 = ((bf16[8,32,1024]{2,0,1:T(8,128)(2,1)}), bf16[8,32,1024]{2,0,1:T(8,128)(2,1)S(1)}, u32[]{:S(2)}, u32[]{:S(2)}) async-start(bf16[8,32,1024]{2,0,1:T(8,128)(2,1)} %copy.110), calls=%async_computation.7 | async-start | bytes 1048576 | tf_op jit(solution)/shard_map/all_to_all | solution.py:38
  78.6 30.0 %all-to-all-start.8 = ((bf16[8,32,1024]{2,0,1:T(8,128)(2,1)}), bf16[8,32,1024]{2,0,1:T(8,128)(2,1)S(1)}, u32[]{:S(2)}, u32[]{:S(2)}) async-start(bf16[8,32,1024]{2,0,1:T(8,128)(2,1)} %copy.112), calls=%async_computation.8 | async-start | bytes 1048576 | tf_op jit(solution)/shard_map/all_to_all | solution.py:41
  108.7 27.1 %all-to-all-start.1 = ((bf16[8,32,2048]{2,0,1:T(8,128)(2,1)}), bf16[8,32,2048]{2,0,1:T(8,128)(2,1)S(1)}, u32[]{:S(2)}, u32[]{:S(2)}) async-start(bf16[8,32,2048]{2,0,1:T(8,128)(2,1)} %copy.92), calls=%async_computation.1 | async-start | bytes 2097152 | tf_op jit(solution)/shard_map/all_to_all | solution.py:38
  135.7 29.8 %all-to-all-start.2 = ((bf16[8,32,2048]{2,0,1:T(8,128)(2,1)}), bf16[8,32,2048]{2,0,1:T(8,128)(2,1)S(1)}, u32[]{:S(2)}, u32[]{:S(2)}) async-start(bf16[8,32,2048]{2,0,1:T(8,128)(2,1)} %copy.94), calls=%async_computation.2 | async-start | bytes 2097152 | tf_op jit(solution)/shard_map/all_to_all | solution.py:41
  165.6 1.6 copy-start
  168.4 1.3 copy-start.3
  168.4 1.5 copy-start.4
  189.2 21.3 %all-to-all-start.9 = ((bf16[2,128,1024]{2,0,1:T(2,128)(2,1)}), bf16[2,128,1024]{2,0,1:T(2,128)(2,1)S(1)}, u32[]{:S(2)}, u32[]{:S(2)}) async-start(bf16[2,128,1024]{2,0,1:T(2,128)(2,1)} %copy.118), calls=%async_computation.9 | async-start | bytes 1048576 | tf_op jit(solution)/shard_map/all_to_all | solution.py:38
  210.5 18.6 %all-to-all-start.10 = ((bf16[2,128,1024]{2,0,1:T(2,128)(2,1)}), bf16[2,128,1024]{2,0,1:T(2,128)(2,1)S(1)}, u32[]{:S(2)}, u32[]{:S(2)}) async-start(bf16[2,128,1024]{2,0,1:T(2,128)(2,1)} %copy.121), calls=%async_computation.10 | async-start | bytes 1048576 | tf_op jit(solution)/shard_map/all_to_all | solution.py:41
  229.1 18.6 %all-to-all-start.3 = ((bf16[2,128,1024]{2,0,1:T(2,128)(2,1)}), bf16[2,128,1024]{2,0,1:T(2,128)(2,1)S(1)}, u32[]{:S(2)}, u32[]{:S(2)}) async-start(bf16[2,128,1024]{2,0,1:T(2,128)(2,1)} %copy.100), calls=%async_computation.3 | async-start | bytes 1048576 | tf_op jit(solution)/shard_map/all_to_all | solution.py:38
  247.6 18.6 %all-to-all-start.4 = ((bf16[2,128,1024]{2,0,1:T(2,128)(2,1)}), bf16[2,128,1024]{2,0,1:T(2,128)(2,1)S(1)}, u32[]{:S(2)}, u32[]{:S(2)}) async-start(bf16[2,128,1024]{2,0,1:T(2,128)(2,1)} %copy.103), calls=%async_computation.4 | async-start | bytes 1048576 | tf_op jit(solution)/shard_map/all_to_all | solution.py:41
  268.4 14.2 %all-to-all-start.5 = ((bf16[8,16,1024]{2,0,1:T(8,128)(2,1)}), bf16[8,16,1024]{2,0,1:T(8,128)(2,1)S(1)}, u32[]{:S(2)}, u32[]{:S(2)}) async-start(bf16[8,16,1024]{2,0,1:T(8,128)(2,1)} %copy.106), calls=%async_computation.5 | async-start | bytes 524288 | tf_op jit(solution)/shard_map/all_to_all | solution.py:31
  282.5 13.5 %all-to-all-start.11 = ((bf16[8,16,1024]{2,0,1:T(8,128)(2,1)}), bf16[8,16,1024]{2,0,1:T(8,128)(2,1)S(1)}, u32[]{:S(2)}, u32[]{:S(2)}) async-start(bf16[8,16,1024]{2,0,1:T(8,128)(2,1)} %copy.124), calls=%async_computation.11 | async-start | bytes 524288 | tf_op jit(solution)/shard_map/all_to_all | solution.py:31
  286.1 3.9 %copy-start.2 = (f32[128,1024]{1,0:T(8,128)S(1)}, f32[128,1024]{1,0:T(8,128)}, u32[]{:S(2)}) copy-start(f32[128,1024]{1,0:T(8,128)} %copy-done.1) | copy-start | bytes 1572868
  286.1 10.0 %copy-start.7 = (bf16[128,1024]{1,0:T(8,128)(2,1)S(1)}, bf16[128,1024]{1,0:T(8,128)(2,1)}, u32[]{:S(2)}) copy-start(bf16[128,1024]{1,0:T(8,128)(2,1)} %param.9) | copy-start | bytes 786436
  286.1 10.0 %copy-start.9 = (bf16[128,1024]{1,0:T(8,128)(2,1)S(1)}, bf16[128,1024]{1,0:T(8,128)(2,1)}, u32[]{:S(2)}) copy-start(bf16[128,1024]{1,0:T(8,128)(2,1)} %param.8) | copy-start | bytes 786436
  286.1 33.9 %all-reduce.2.cloned.1.call-start = ((), (), s32[]{:S(2)}) async-start(), calls=%async_computation.12 | async-start | bytes 1048576 | tf_op jit(solution)/shard_map/psum | solution.py:134
Sparse Core Ops, SparseCore 0:
  290.1 29.8 all-reduce.1
where the time goes:
time: 333 us; the launch traced here: 329 us
  waiting for transfers between devices  163 us (49%)
  starting transfers between devices  67.1 us (20%)
  matrix products  42.4 us (13%)
  local copies, waits for them, and re-layouts  21.8 us (7%)
  between operations  14.8 us (4%)
  blocking collectives  10.2 us (3%)
  other arithmetic  9.7 us (3%)
    all_to_all x4, waiting for transfers between devices, regroup_spectra(): lax.all_to_all(real_part.astype(jnp.bfloat16), 'ctx', split_axis=1, conca...  61.4 us
    all_to_all x4, waiting for transfers between devices, regroup_spectra(): lax.all_to_all(imag_part.astype(jnp.bfloat16), 'ctx', split_axis=1, conca...  49.6 us
    dot_general x24, matrix products, contract(): return jnp.einsum(einsum_form, matrix_tab, operand, precision=exact_mode)  34.8 us
    all_to_all x4, starting transfers between devices, regroup_spectra(): lax.all_to_all(imag_part.astype(jnp.bfloat16), 'ctx', split_axis=1, conca...  30.7 us
    all_to_all x4, waiting for transfers between devices, regroup_tokens(): lax.all_to_all(signal.astype(jnp.bfloat16), 'ctx', split_axis=1, concat_a...  28.7 us
    psum x1, waiting for transfers between devices, on_device(): lax.psum(incomplete_result.astype(jnp.bfloat16), 'tp').astype(jnp.float32)  23 us
    all_to_all x4, starting transfers between devices, regroup_spectra(): lax.all_to_all(real_part.astype(jnp.bfloat16), 'ctx', split_axis=1, conca...  19.1 us
    all_to_all x4, starting transfers between devices, regroup_tokens(): lax.all_to_all(signal.astype(jnp.bfloat16), 'ctx', split_axis=1, concat_a...  17.3 us
  transfers between devices with their start and end apart: 13, of which 13 were waited for; matrix products, arithmetic and copies ran while one was open for 11% of the time, Pallas kernels for 0%

commit v1 on v0

v1 whole, which is shorter than its diff:
```python
import functools
import math

import jax
import jax.numpy as jnp
import numpy as np
from jax import lax
from jax.experimental import pallas as pl
from jax.experimental.pallas import tpu as pltpu
from jax.sharding import PartitionSpec as P

BASES = 4
LANES = 128
F32 = jnp.float32
BF16 = jnp.bfloat16


def complex_dft(values, sign):
    length = len(values)
    if length == 1:
        return values
    half = length // 2
    even = [
        (values[b][0] + values[b + half][0], values[b][1] + values[b + half][1])
        for b in range(half)
    ]
    odd = [
        twist(
            (values[b][0] - values[b + half][0], values[b][1] - values[b + half][1]),
            sign * b,
            length,
        )
        for b in range(half)
    ]
    even = complex_dft(even, sign)
    odd = complex_dft(odd, sign)
    return [part for pair in zip(even, odd) for part in pair]


def twist(value, step, length):
    real, imag = value
    step = step % length
    if step == 0:
        return real, imag
    if 4 * step == length:
        return -imag, real
    if 2 * step == length:
        return -real, -imag
    if 4 * step == 3 * length:
        return imag, -real
    cos = math.cos(2.0 * math.pi * step / length)
    sin = math.sin(2.0 * math.pi * step / length)
    if 8 * step % length == 0:
        root = math.sqrt(0.5)
        signed_cos = 1.0 if cos > 0 else -1.0
        signed_sin = 1.0 if sin > 0 else -1.0
        a = real * root
        b = imag * root
        if signed_cos == signed_sin:
            return (a - b, a + b) if signed_cos > 0 else (b - a, -a - b)
        return (a + b, b - a) if signed_cos > 0 else (-a - b, a - b)
    return real * cos - imag * sin, real * sin + imag * cos


def real_dft(values, length):
    if length == 2:
        if len(values) == 1:
            return [(values[0], None), (values[0], None)]
        return [(values[0] + values[1], None), (values[0] - values[1], None)]
    half, quarter = length // 2, length // 4
    if len(values) == length:
        total = [values[b] + values[b + half] for b in range(half)]
        rest = [values[b] - values[b + half] for b in range(half)]
    else:
        total = values
        rest = values
    out = [None] * (half + 1)
    for index, value in enumerate(real_dft(total, half)):
        out[2 * index] = value
    turned = [
        twist((rest[b], -rest[b + quarter]), -b, length) for b in range(quarter)
    ]
    for index, (real, imag) in enumerate(complex_dft(turned, -1)):
        place = 4 * index + 1
        if place <= half:
            out[place] = (real, imag)
        else:
            out[length - place] = (real, -imag)
    return out


def real_dft_transposed(spectrum, length, padded):
    if length == 2:
        first, second = spectrum[0][0], spectrum[1][0]
        return [first + second] if padded else [first + second, first - second]
    half, quarter = length // 2, length // 4
    total = real_dft_transposed(
        [spectrum[2 * index] for index in range(quarter + 1)], half, False
    )
    odd = []
    for index in range(quarter):
        place = 4 * index + 1
        if place <= half:
            odd.append(spectrum[place])
        else:
            real, imag = spectrum[length - place]
            odd.append((real, -imag))
    rest = [None] * half
    for b, value in enumerate(complex_dft(odd, 1)):
        real, imag = twist(value, b, length)
        rest[b] = real
        rest[b + quarter] = -imag
    low = [total[b] + rest[b] for b in range(half)]
    if padded:
        return low
    return low + [total[b] - rest[b] for b in range(half)]


def pack_rows(block, pieces):
    if pieces == 1:
        return block
    rows = block.shape[0] // pieces
    return jnp.concatenate(
        [block[i * rows : (i + 1) * rows] for i in range(pieces)], axis=1
    )


def unpack_rows(block, pieces):
    if pieces == 1:
        return block
    width = block.shape[1] // pieces
    return jnp.concatenate(
        [block[:, i * width : (i + 1) * width] for i in range(pieces)], axis=0
    )


def keep_rows(token_ref, width):
    keep = (token_ref[...] < BASES).astype(F32)
    length = keep.shape[1]
    return jnp.broadcast_to(keep, (length, length)).T[:, :1] * jnp.ones((1, width), F32)


def pack_inputs(n, token_ref, pre_ref, feat_ref, filt_ref, out_ref):
    width = pre_ref.shape[1] // n
    pieces = max(1, LANES // (2 * width))
    keep = keep_rows(token_ref, pre_ref.shape[1])
    mixer = pre_ref[...].astype(F32) * feat_ref[...].astype(F32) * keep
    filt = filt_ref[...]
    for k in range(n):
        cols = slice(k * width, (k + 1) * width)
        pair = jnp.concatenate([mixer[:, cols], filt[:, cols]], axis=1)
        out_ref[k] = pack_rows(pair, pieces).astype(BF16)


def pack_grad(n, rank_ref, own_ref, other_ref, weight_ref, post_ref, gated_ref, out_ref):
    width = post_ref.shape[1] // n
    pieces = max(1, LANES // width)
    columns = own_ref.shape[1]
    first = rank_ref[0] == 0
    own, other = own_ref[...], other_ref[...]
    left = jnp.where(first, own, other)
    right = jnp.where(first, other, own)
    dims = (((1,), (1,)), ((), ()))
    grad_gated = lax.dot_general(
        left, weight_ref[:, :columns], dims, preferred_element_type=F32
    ) + lax.dot_general(right, weight_ref[:, columns:], dims, preferred_element_type=F32)
    gated_ref[...] = grad_gated
    mixed = grad_gated * post_ref[...].astype(F32)
    for k in range(n):
        out_ref[k] = pack_rows(mixed[:, k * width : (k + 1) * width], pieces).astype(BF16)


def row_chunk(rows):
    return min(rows, 16)


def forward_blocks(n, blocks_ref, store):
    rows = blocks_ref.shape[1]
    chunk = row_chunk(rows)

    def body(index, carry):
        at = pl.ds(pl.multiple_of(index * chunk, chunk), chunk)
        spectrum = real_dft([blocks_ref[b, at].astype(F32) for b in range(n)], 2 * n)
        for m, (real, imag) in enumerate(spectrum):
            store(m, 0, at, real)
            store(m, 1, at, jnp.zeros_like(real) if imag is None else imag)
        return carry

    lax.fori_loop(0, rows // chunk, body, 0)


def inverse_blocks(n, spec_ref, out_ref):
    rows = out_ref.shape[1]
    chunk = row_chunk(rows)

    def body(index, carry):
        at = pl.ds(pl.multiple_of(index * chunk, chunk), chunk)
        spectrum = [(spec_ref[m, 0, at], spec_ref[m, 1, at]) for m in range(n + 1)]
        for b, value in enumerate(real_dft_transposed(spectrum, 2 * n, True)):
            out_ref[b, at] = value.astype(BF16)
        return carry

    lax.fori_loop(0, rows // chunk, body, 0)


def inverse_scale(m, n, length):
    edge = jnp.logical_or(m == 0, m == n)
    return jnp.where(edge, 0.5 / (n * length), 1.0 / (n * length))


def mix_forward(n, pair_ref, table_ref, back_ref, out_ref, filt_ref, mid_ref, spec_ref):
    length = table_ref.shape[1] // 2
    width = filt_ref.shape[2]
    pieces = max(1, LANES // width)
    pair_pieces = max(1, LANES // (2 * width))

    if pair_pieces == 1:

        def store(m, part, at, value):
            mid_ref[m, pl.ds(pl.multiple_of(part * length + at.start, at.size), at.size)] = (
                value.astype(BF16)
            )
    else:

        def store(m, part, at, value):
            for i in range(pair_pieces):
                start = part * length + i * (length // pair_pieces) + at.start
                mid_ref[m, pl.ds(pl.multiple_of(start, at.size), at.size)] = value[
                    :, i * 2 * width : (i + 1) * 2 * width
                ].astype(BF16)

    forward_blocks(n, pair_ref, store)

    def body(m, carry):
        spec = jnp.dot(table_ref[m], mid_ref[m], preferred_element_type=F32)
        real, imag = spec[:length, :width], spec[length:, :width]
        filt = spec[:, width:]
        filt_ref[m] = filt.astype(filt_ref.dtype)
        filt_real, filt_imag = filt[:length], filt[length:]
        scale = inverse_scale(m, n, length)
        product = jnp.concatenate(
            [
                (real * filt_real - imag * filt_imag) * scale,
                (real * filt_imag + imag * filt_real) * scale,
            ],
            axis=0,
        ).astype(BF16)
        mid = jnp.dot(back_ref[m], product, preferred_element_type=F32)
        spec_ref[m, 0] = pack_rows(mid[:length], pieces)
        spec_ref[m, 1] = pack_rows(mid[length:], pieces)
        return carry

    lax.fori_loop(0, n + 1, body, 0)
    inverse_blocks(n, spec_ref, out_ref)


def mix_backward(n, grad_ref, filt_ref, table_ref, back_ref, out_ref, spec_ref):
    length = table_ref.shape[1] // 2
    width = filt_ref.shape[2]
    pieces = max(1, LANES // width)

    def store(m, part, at, value):
        spec_ref[m, part, at] = value

    forward_blocks(n, grad_ref, store)

    def body(m, carry):
        mid = jnp.concatenate(
            [unpack_rows(spec_ref[m, 0], pieces), unpack_rows(spec_ref[m, 1], pieces)], axis=0
        ).astype(BF16)
        spec = jnp.dot(table_ref[m], mid, preferred_element_type=F32)
        real, imag = spec[:length], spec[length:]
        filt = filt_ref[m].astype(F32)
        filt_real, filt_imag = filt[:length], filt[length:]
        scale = inverse_scale(m, n, length)
        product = jnp.concatenate(
            [
                (filt_real * real + filt_imag * imag) * scale,
                (filt_real * imag - filt_imag * real) * scale,
            ],
            axis=0,
        ).astype(BF16)
        back = jnp.dot(back_ref[m], product, preferred_element_type=F32)
        spec_ref[m, 0] = pack_rows(back[:length], pieces)
        spec_ref[m, 1] = pack_rows(back[length:], pieces)
        return carry

    lax.fori_loop(0, n + 1, body, 0)
    inverse_blocks(n, spec_ref, out_ref)


def unpack_channels(n, packed_ref, pieces):
    return jnp.concatenate(
        [unpack_rows(packed_ref[k].astype(F32), pieces) for k in range(n)], axis=1
    )


def project(
    n, rank_ref, mixed_ref, post_ref, grad_ref, weight_ref, away_ref, home_ref, post_grad_ref
):
    channels = post_ref.shape[1]
    pieces = max(1, LANES // (channels // n))
    columns = home_ref.shape[1]
    mixed = unpack_channels(n, mixed_ref, pieces)
    gated = (post_ref[...].astype(F32) * mixed).astype(BF16)
    left = jnp.dot(gated, weight_ref[:, :columns], preferred_element_type=F32)
    right = jnp.dot(gated, weight_ref[:, columns:], preferred_element_type=F32)
    first = rank_ref[0] == 0
    home_ref[...] = jnp.where(first, left, right)
    away_ref[...] = jnp.where(first, right, left).astype(BF16)
    post_grad_ref[...] = (grad_ref[...] * mixed).astype(BF16)


def add_halves(home_ref, other_ref, out_ref):
    out_ref[...] = (home_ref[...] + other_ref[...].astype(F32)).astype(BF16)


def input_grads(n, packed_ref, token_ref, pre_ref, feat_ref, pre_grad_ref, feat_grad_ref):
    channels = pre_ref.shape[1]
    pieces = max(1, LANES // (channels // n))
    grad = unpack_channels(n, packed_ref, pieces) * keep_rows(token_ref, channels)
    pre_grad_ref[...] = (grad * feat_ref[...].astype(F32)).astype(BF16)
    feat_grad_ref[...] = (grad * pre_ref[...].astype(F32)).astype(BF16)


def dft_tables(n, length):
    full = 2 * n * length
    m = np.arange(n + 1)[:, None, None]
    q = np.arange(length)[None, :, None]
    p = np.arange(length)[None, None, :]
    angle = (2 * n * q + m) * p % full * (2.0 * math.pi / full)
    cos, sin = np.cos(angle), np.sin(angle)
    table = np.concatenate(
        [np.concatenate([cos, sin], axis=2), np.concatenate([-sin, cos], axis=2)], axis=1
    )
    return table.astype(jnp.bfloat16)


def call(kernel, outs, args, flops=0, scratch=(), scalars=0, limit=56):
    def size(x):
        return math.prod(x.shape) * np.dtype(x.dtype).itemsize

    return pl.pallas_call(
        kernel,
        out_shape=outs,
        in_specs=[pl.BlockSpec(memory_space=pltpu.SMEM)] * scalars
        + [pl.BlockSpec(memory_space=pltpu.VMEM)] * (len(args) - scalars),
        out_specs=jax.tree.map(lambda _: pl.BlockSpec(memory_space=pltpu.VMEM), outs),
        scratch_shapes=list(scratch),
        compiler_params=pltpu.CompilerParams(vmem_limit_bytes=limit * 2**20),
        cost_estimate=pl.CostEstimate(
            flops=flops,
            bytes_accessed=sum(size(x) for x in [*args, *jax.tree.leaves(outs)]),
            transcendentals=0,
        ),
    )(*args)


def exchange(block):
    return lax.all_to_all(block, "ctx", split_axis=0, concat_axis=0, tiled=True)


def swap_tp(block):
    count = lax.axis_size("tp")
    assert count == 2
    return lax.ppermute(block, "tp", [(0, 1), (1, 0)])


def on_device(
    tables, post_gate, pre_gate, features, filters, token_ids, out_weight, out_grad
):
    n = lax.axis_size("ctx")
    length, channels = post_gate.shape
    columns = out_grad.shape[1]
    width = channels // n
    pieces = max(1, LANES // width)
    pair_pieces = max(1, LANES // (2 * width))
    shape = jax.ShapeDtypeStruct
    one = shape((n, length // pieces, pieces * width), BF16)
    pair = shape((n, length // pair_pieces, pair_pieces * 2 * width), BF16)
    table, back = tables
    tokens = token_ids.reshape(1, length)
    rank = lax.axis_index("tp").astype(jnp.int32).reshape(1)
    filt_type = F32 if n <= 32 else BF16
    inner_flops = 2 * (n + 1) * (2 * length) ** 2 * width

    other_grad = swap_tp(out_grad)
    pair_out = call(
        functools.partial(pack_inputs, n), pair, (tokens, pre_gate, features, filters)
    )
    pair_in = exchange(pair_out)
    grad_gated, grad_out = call(
        functools.partial(pack_grad, n),
        (shape((length, channels), F32), one),
        (rank, out_grad, other_grad, out_weight, post_gate),
        flops=4 * length * channels * columns,
        scalars=1,
    )
    grad_in = exchange(grad_out)
    spec_scratch = pltpu.VMEM((n + 1, 2, length // pieces, pieces * width), F32)
    mixed_out, filt_spec = call(
        functools.partial(mix_forward, n),
        (one, shape((n + 1, 2 * length, width), filt_type)),
        (pair_in, table, back),
        flops=3 * inner_flops,
        scratch=[pltpu.VMEM((n + 1, 2 * length, 2 * width), BF16), spec_scratch],
    )
    mixed_in = exchange(mixed_out)
    grad_back_out = call(
        functools.partial(mix_backward, n),
        one,
        (grad_in, filt_spec, table, back),
        flops=2 * inner_flops,
        scratch=[spec_scratch],
    )
    grad_back_in = exchange(grad_back_out)
    away, home, grad_post = call(
        functools.partial(project, n),
        (
            shape((length, columns), BF16),
            shape((length, columns), F32),
            shape((length, channels), BF16),
        ),
        (rank, mixed_in, post_gate, grad_gated, out_weight),
        flops=4 * length * channels * columns,
        scalars=1,
    )
    output = call(add_halves, shape((length, columns), BF16), (home, swap_tp(away)))
    grad_pre, grad_features = call(
        functools.partial(input_grads, n),
        (shape((length, channels), BF16), shape((length, channels), BF16)),
        (grad_back_in, tokens, pre_gate, features),
    )
    return (output, grad_post, grad_pre, grad_features)


def solution(mesh):
    in_specs = (
        P("ctx", "tp"),
        P("ctx", "tp"),
        P("ctx", "tp"),
        P("ctx", "tp"),
        P("ctx"),
        P("tp", None),
        P("ctx", "tp"),
    )
    out_specs = (P("ctx", "tp"), P("ctx", "tp"), P("ctx", "tp"), P("ctx", "tp"))

    def run(*args):
        n = mesh.shape["ctx"]
        table = dft_tables(n, args[0].shape[0] // n)
        tables = (jnp.asarray(table), jnp.asarray(np.swapaxes(table, 1, 2)))
        return jax.shard_map(
            functools.partial(on_device, tables),
            mesh=mesh,
            in_specs=in_specs,
            out_specs=out_specs,
            check_vma=False,
        )(*args)

    return run
```

time: 333 us -> 85.5 us (0.26); the launches traced: 329 us -> 84.9 us
  waiting for transfers between devices: 163 us -> 11.8 us
  matrix products: 42.4 us -> 0 us
  Pallas kernels: 0 us -> 42.4 us
  starting transfers between devices: 67.1 us -> 27.9 us
  local copies, waits for them, and re-layouts: 21.8 us -> 2.13 us
  between operations: 14.8 us -> 0.71 us
  blocking collectives: 10.2 us -> 0 us
  other arithmetic: 9.7 us -> 0 us
    all_to_all x12 -> x4, waiting for transfers between devices: 140 us -> 4.48 us  [exchange(): return lax.all_to_all(block, 'ctx', split_axis=0, concat_axis=0, tiled=True)]
    pallas_call x0 -> x7, Pallas kernels: none -> 42.4 us  [call(): pl.pallas_call(kernel, out_shape=outs, in_specs=[pl.BlockSpec(memory_spac...]
    dot_general x26 -> x0, matrix products: 42.4 us -> none  [the longest x24 34.8 us: contract(): return jnp.einsum(einsum_form, matrix_tab, operand, precision=exact_mode)]
    all_to_all x12 -> x4, starting transfers between devices: 67 us -> 24.8 us  [exchange(): return lax.all_to_all(block, 'ctx', split_axis=0, concat_axis=0, tiled=True)]
    psum x1 -> x0, waiting for transfers between devices: 23 us -> none  [on_device(): lax.psum(incomplete_result.astype(jnp.bfloat16), 'tp').astype(jnp.float32)]
    convert_element_type x11 -> x0, local copies, waits for them, and re-layouts: 12.1 us -> none  [the longest x4 5.09 us: regroup_spectra(): real_part.astype(jnp.bfloat16)]
    all_gather x1 -> x0, blocking collectives: 10.2 us -> none  [on_device(): lax.all_gather(out_grad, 'tp', axis=1, tiled=True)]
    ppermute x0 -> x2, waiting for transfers between devices: none -> 7.27 us  [swap_tp(): return lax.ppermute(block, 'tp', [(0, 1), (1, 0)])]
  transfers between devices with their start and end apart: 13 -> 6, of which waited for: 13 -> 4; matrix products, arithmetic and copies ran while one was open for 11% -> 0% of each run, Pallas kernels for 0% -> 45%
where the time goes in v1:
time: 85.5 us; the launch traced here: 84.9 us
  Pallas kernels  42.4 us (50%)
  starting transfers between devices  27.9 us (33%)
  waiting for transfers between devices  11.8 us (14%)
  local copies, waits for them, and re-layouts  2.13 us (2%)
    pallas_call x7, Pallas kernels, call(): pl.pallas_call(kernel, out_shape=outs, in_specs=[pl.BlockSpec(memory_spac...  42.4 us
    all_to_all x4, starting transfers between devices, exchange(): return lax.all_to_all(block, 'ctx', split_axis=0, concat_axis=0, tiled=True)  24.8 us
    ppermute x2, waiting for transfers between devices, swap_tp(): return lax.ppermute(block, 'tp', [(0, 1), (1, 0)])  7.27 us
    all_to_all x4, waiting for transfers between devices, exchange(): return lax.all_to_all(block, 'ctx', split_axis=0, concat_axis=0, tiled=True)  4.48 us
    ppermute x2, starting transfers between devices, swap_tp(): return lax.ppermute(block, 'tp', [(0, 1), (1, 0)])  3.11 us
    unnamed x14, local copies, waits for them, and re-layouts  2.13 us
  transfers between devices with their start and end apart: 6, of which 4 were waited for; matrix products, arithmetic and copies ran while one was open for 0% of the time, Pallas kernels for 45%

profile of v1, /device:TPU:0, one launch (start us, length us, event | category | flops | bytes accessed | tf_op | source)
XLA Modules:
  0.0 84.9 jit_solution(17073698577464506530)
XLA Ops:
  0.6 0.0 copy-start.4
  0.6 2.4 %shard_map.120 = bf16[16,128,128]{2,1,0:T(8,128)(2,1)} custom-call(s32[1,128]{1,0:T(1,128)} %bitcast.2, bf16[128,1024]{1,0:T(8,128)(2,1)} %pre_ref.3, bf16[128,1024]{1,0:T(8,128)(2,1)} %feat_ref.3, f32[128,1024]{1,0:T(8,128)} %filt_ref.1), custom_call_target="tpu_custom_call" | custom-call | bytes 1573376 | tf_op jit(solution)/shard_map/pallas_call | solution.py:343
  3.0 7.4 %all-to-all-start = ((bf16[16,128,128]{2,1,0:T(8,128)(2,1)}), bf16[16,128,128]{2,1,0:T(8,128)(2,1)S(1)}, u32[]{:S(2)}, u32[]{:S(2)}) async-start(bf16[16,128,128]{2,1,0:T(8,128)(2,1)} %shard_map.120), calls=%async_computation | async-start | bytes 1048576 | tf_op jit(solution)/shard_map/all_to_all | solution.py:360
  10.4 0.0 copy-done.4
  10.4 1.6 %collective-permute-start = (bf16[128,1024]{1,0:T(8,128)(2,1)S(1)}, bf16[128,1024]{1,0:T(8,128)(2,1)S(1)}, u32[]{:S(2)}, u32[]{:S(2)}) collective-permute-start(bf16[128,1024]{1,0:T(8,128)(2,1)S(1)} %copy-done.4), channel_id=1, source_target_pairs={{0,1},{1,0},{2,3},{3,2},{4,5},{5,4},{6,7},{7,6},{8,9},{9,8},{10,11... | collective-permute-start | bytes 786440 | tf_op jit(solution)/shard_map/ppermute | solution.py:366
  12.0 7.1 %collective-permute-done.other_ref = bf16[128,1024]{1,0:T(8,128)(2,1)S(1)} collective-permute-done((bf16[128,1024]{1,0:T(8,128)(2,1)S(1)}, bf16[128,1024]{1,0:T(8,128)(2,1)S(1)}, u32[]{:S(2)}, u32[]{:S(2)}) %collective-permute-start) | collective-permute-done | bytes 262176 | tf_op jit(solution)/shard_map/ppermute | solution.py:366
  19.1 0.0 copy-start.5
  19.1 0.7 copy-done.5
  19.8 4.7 %shard_map.122 = (f32[128,1024]{1,0:T(8,128)}, bf16[16,64,128]{2,1,0:T(8,128)(2,1)}) custom-call(s32[1]{0:T(128)} %bitcast.rank_ref, bf16[128,1024]{1,0:T(8,128)(2,1)} %own_ref.1, bf16[128,1024]{1,0:T(8,128)(2,1)} %copy-done.5, bf16[1024,2048]{1,0:T(8,128)(2,1)} %weight_ref.3, bf16[128,1024]{1,0:T(8,128)(2,1)} %post_ref.3), custom_call_target="tpu_custom_call" | custom-call | flops 536870912 | bytes 5767172 | tf_op jit(solution)/shard_map/pallas_call | solution.py:343
  24.5 0.3 all-to-all-done.pair_ref
  24.8 0.0 copy-start
  24.8 5.4 %all-to-all-start.2 = ((bf16[16,64,128]{2,1,0:T(8,128)(2,1)}), bf16[16,64,128]{2,1,0:T(8,128)(2,1)S(1)}, u32[]{:S(2)}, u32[]{:S(2)}) async-start(bf16[16,64,128]{2,1,0:T(8,128)(2,1)} %get-tuple-element.18), calls=%async_computation.2 | async-start | bytes 524288 | tf_op jit(solution)/shard_map/all_to_all | solution.py:360
  30.3 0.0 copy-done
  30.3 13.7 %shard_map.121 = (bf16[16,64,128]{2,1,0:T(8,128)(2,1)}, f32[17,256,64]{2,1,0:T(8,128)}) custom-call(bf16[16,128,128]{2,1,0:T(8,128)(2,1)} %copy-done, bf16[17,256,256]{2,1,0:T(8,128)(2,1)} %constant.8.clone.table_ref, bf16[17,256,256]{2,1,0:T(8,128)(2,1)} %constant.9.clone.back_ref), custom_call_target="tpu_custom_call" | custom-call | flops 427819008 | bytes 6356992 | tf_op jit(solution)/shard_map/pallas_call | solution.py:343
  43.9 0.0 all-to-all-done.2.grad_ref
  43.9 0.0 copy-start.1
  43.9 6.0 %all-to-all-start.1 = ((bf16[16,64,128]{2,1,0:T(8,128)(2,1)}), bf16[16,64,128]{2,1,0:T(8,128)(2,1)S(1)}, u32[]{:S(2)}, u32[]{:S(2)}) async-start(bf16[16,64,128]{2,1,0:T(8,128)(2,1)} %get-tuple-element.13), calls=%async_computation.1 | async-start | bytes 524288 | tf_op jit(solution)/shard_map/all_to_all | solution.py:360
  50.0 0.0 copy-done.1
  50.0 13.2 %shard_map.125 = bf16[16,64,128]{2,1,0:T(8,128)(2,1)} custom-call(bf16[16,64,128]{2,1,0:T(8,128)(2,1)} %copy-done.1, f32[17,256,64]{2,1,0:T(8,128)} %get-tuple-element.19.filt_ref, bf16[17,256,256]{2,1,0:T(8,128)(2,1)} %constant.8.clone.table_ref, bf16[17,256,256]{2,1,0:T(8,128)(2,1)} %constant.9.clone.back_ref), custom_call_target="tpu_custom_call" | custom-call | flops 285212672 | bytes 6094848 | tf_op jit(solution)/shard_map/pallas_call | solution.py:343
  63.1 0.0 all-to-all-done.1.mixed_ref
  63.1 0.0 copy-start.3
  63.1 6.0 %all-to-all-start.3 = ((bf16[16,64,128]{2,1,0:T(8,128)(2,1)}), bf16[16,64,128]{2,1,0:T(8,128)(2,1)S(1)}, u32[]{:S(2)}, u32[]{:S(2)}) async-start(bf16[16,64,128]{2,1,0:T(8,128)(2,1)} %shard_map.125), calls=%async_computation.3 | async-start | bytes 524288 | tf_op jit(solution)/shard_map/all_to_all | solution.py:360
  69.2 0.0 copy-done.3
  69.2 4.3 %shard_map.123 = (bf16[128,1024]{1,0:T(8,128)(2,1)}, f32[128,1024]{1,0:T(8,128)}, bf16[128,1024]{1,0:T(8,128)(2,1)}) custom-call(s32[1]{0:T(128)} %bitcast.rank_ref, bf16[16,64,128]{2,1,0:T(8,128)(2,1)} %copy-done.3, bf16[128,1024]{1,0:T(8,128)(2,1)} %post_ref.3, f32[128,1024]{1,0:T(8,128)} %get-tuple-element.14.grad_ref, bf16[1024,2048]{1,0:T(8,128)(2,1)} %weight_ref.3), custom_call_target="tpu_custom_call" | custom-call | flops 536870912 | bytes 6291460 | tf_op jit(solution)/shard_map/pallas_call | solution.py:343
  73.5 1.5 %collective-permute-start.1 = (bf16[128,1024]{1,0:T(8,128)(2,1)}, bf16[128,1024]{1,0:T(8,128)(2,1)S(1)}, u32[]{:S(2)}, u32[]{:S(2)}) collective-permute-start(bf16[128,1024]{1,0:T(8,128)(2,1)} %get-tuple-element.16), channel_id=1, source_target_pairs={{0,1},{1,0},{2,3},{3,2},{4,5},{5,4},{6,7},{7,6},{8,9},{9,8},{10,11... | collective-permute-start | bytes 786440 | tf_op jit(solution)/shard_map/ppermute | solution.py:366
  75.0 4.2 %all-to-all-done.3.packed_ref = bf16[16,64,128]{2,1,0:T(8,128)(2,1)S(1)} async-done(((bf16[16,64,128]{2,1,0:T(8,128)(2,1)}), bf16[16,64,128]{2,1,0:T(8,128)(2,1)S(1)}, u32[]{:S(2)}, u32[]{:S(2)}) %all-to-all-start.3) | async-done | bytes 262176 | tf_op jit(solution)/shard_map/all_to_all | solution.py:360
  79.2 0.0 copy-start.2
  79.2 0.7 copy-done.2
  79.9 2.3 %shard_map.126 = (bf16[128,1024]{1,0:T(8,128)(2,1)}, bf16[128,1024]{1,0:T(8,128)(2,1)}) custom-call(bf16[16,64,128]{2,1,0:T(8,128)(2,1)} %copy-done.2, s32[1,128]{1,0:T(1,128)} %bitcast.3, bf16[128,1024]{1,0:T(8,128)(2,1)} %pre_ref.3, bf16[128,1024]{1,0:T(8,128)(2,1)} %feat_ref.3), custom_call_target="tpu_custom_call" | custom-call | bytes 1311232 | tf_op jit(solution)/shard_map/pallas_call | solution.py:343
  82.2 0.1 collective-permute-done.1.other_ref
  82.4 0.7 copy-done.6
  83.1 1.9 %shard_map.124 = bf16[128,1024]{1,0:T(8,128)(2,1)} custom-call(f32[128,1024]{1,0:T(8,128)} %get-tuple-element.15.home_ref, bf16[128,1024]{1,0:T(8,128)(2,1)} %copy-done.6), custom_call_target="tpu_custom_call" | custom-call | bytes 1048576 | tf_op jit(solution)/shard_map/pallas_call | solution.py:343
  (1 shorter events, 0.0 us)
Async XLA Ops:
  0.6 9.7 %copy-start.4 = (bf16[128,1024]{1,0:T(8,128)(2,1)S(1)}, bf16[128,1024]{1,0:T(8,128)(2,1)}, u32[]{:S(2)}) copy-start(bf16[128,1024]{1,0:T(8,128)(2,1)} %own_ref.1) | copy-start | bytes 786436
  3.0 21.8 %all-to-all-start = ((bf16[16,128,128]{2,1,0:T(8,128)(2,1)}), bf16[16,128,128]{2,1,0:T(8,128)(2,1)S(1)}, u32[]{:S(2)}, u32[]{:S(2)}) async-start(bf16[16,128,128]{2,1,0:T(8,128)(2,1)} %shard_map.120), calls=%async_computation | async-start | bytes 1048576 | tf_op jit(solution)/shard_map/all_to_all | solution.py:360
  10.4 8.7 %collective-permute-start = (bf16[128,1024]{1,0:T(8,128)(2,1)S(1)}, bf16[128,1024]{1,0:T(8,128)(2,1)S(1)}, u32[]{:S(2)}, u32[]{:S(2)}) collective-permute-start(bf16[128,1024]{1,0:T(8,128)(2,1)S(1)} %copy-done.4), channel_id=1, source_target_pairs={{0,1},{1,0},{2,3},{3,2},{4,5},{5,4},{6,7},{7,6},{8,9},{9,8},{10,11... | collective-permute-start | bytes 786440 | tf_op jit(solution)/shard_map/ppermute | solution.py:366
  19.1 0.7 copy-start.5
  24.8 5.4 %copy-start = (bf16[16,128,128]{2,1,0:T(8,128)(2,1)}, bf16[16,128,128]{2,1,0:T(8,128)(2,1)S(1)}, u32[]{:S(2)}) copy-start(bf16[16,128,128]{2,1,0:T(8,128)(2,1)S(1)} %all-to-all-done.pair_ref) | copy-start | bytes 1572868
  24.8 19.1 %all-to-all-start.2 = ((bf16[16,64,128]{2,1,0:T(8,128)(2,1)}), bf16[16,64,128]{2,1,0:T(8,128)(2,1)S(1)}, u32[]{:S(2)}, u32[]{:S(2)}) async-start(bf16[16,64,128]{2,1,0:T(8,128)(2,1)} %get-tuple-element.18), calls=%async_computation.2 | async-start | bytes 524288 | tf_op jit(solution)/shard_map/all_to_all | solution.py:360
  43.9 6.0 %copy-start.1 = (bf16[16,64,128]{2,1,0:T(8,128)(2,1)}, bf16[16,64,128]{2,1,0:T(8,128)(2,1)S(1)}, u32[]{:S(2)}) copy-start(bf16[16,64,128]{2,1,0:T(8,128)(2,1)S(1)} %all-to-all-done.2.grad_ref) | copy-start | bytes 786436
  43.9 19.2 %all-to-all-start.1 = ((bf16[16,64,128]{2,1,0:T(8,128)(2,1)}), bf16[16,64,128]{2,1,0:T(8,128)(2,1)S(1)}, u32[]{:S(2)}, u32[]{:S(2)}) async-start(bf16[16,64,128]{2,1,0:T(8,128)(2,1)} %get-tuple-element.13), calls=%async_computation.1 | async-start | bytes 524288 | tf_op jit(solution)/shard_map/all_to_all | solution.py:360
  63.1 6.0 %copy-start.3 = (bf16[16,64,128]{2,1,0:T(8,128)(2,1)}, bf16[16,64,128]{2,1,0:T(8,128)(2,1)S(1)}, u32[]{:S(2)}) copy-start(bf16[16,64,128]{2,1,0:T(8,128)(2,1)S(1)} %all-to-all-done.1.mixed_ref) | copy-start | bytes 786436
  63.1 16.1 %all-to-all-start.3 = ((bf16[16,64,128]{2,1,0:T(8,128)(2,1)}), bf16[16,64,128]{2,1,0:T(8,128)(2,1)S(1)}, u32[]{:S(2)}, u32[]{:S(2)}) async-start(bf16[16,64,128]{2,1,0:T(8,128)(2,1)} %shard_map.125), calls=%async_computation.3 | async-start | bytes 524288 | tf_op jit(solution)/shard_map/all_to_all | solution.py:360
  73.5 8.9 %collective-permute-start.1 = (bf16[128,1024]{1,0:T(8,128)(2,1)}, bf16[128,1024]{1,0:T(8,128)(2,1)S(1)}, u32[]{:S(2)}, u32[]{:S(2)}) collective-permute-start(bf16[128,1024]{1,0:T(8,128)(2,1)} %get-tuple-element.16), channel_id=1, source_target_pairs={{0,1},{1,0},{2,3},{3,2},{4,5},{5,4},{6,7},{7,6},{8,9},{9,8},{10,11... | collective-permute-start | bytes 786440 | tf_op jit(solution)/shard_map/ppermute | solution.py:366
  79.2 0.7 copy-start.2
  82.4 0.7 copy-start.6

commit v2 on v1

--- a/solution.py
+++ b/solution.py
@@ -11,6 +11,7 @@
 
 BASES = 4
 LANES = 128
+VMEM_MOST = 60 * 2**20
 F32 = jnp.float32
 BF16 = jnp.bfloat16
 
@@ -140,20 +141,20 @@
     return jnp.broadcast_to(keep, (length, length)).T[:, :1] * jnp.ones((1, width), F32)
 
 
-def pack_inputs(n, token_ref, pre_ref, feat_ref, filt_ref, out_ref):
-    width = pre_ref.shape[1] // n
+def pack_inputs(dests, token_ref, pre_ref, feat_ref, filt_ref, out_ref):
+    width = pre_ref.shape[1] // dests
     pieces = max(1, LANES // (2 * width))
     keep = keep_rows(token_ref, pre_ref.shape[1])
     mixer = pre_ref[...].astype(F32) * feat_ref[...].astype(F32) * keep
     filt = filt_ref[...]
-    for k in range(n):
+    for k in range(dests):
         cols = slice(k * width, (k + 1) * width)
         pair = jnp.concatenate([mixer[:, cols], filt[:, cols]], axis=1)
         out_ref[k] = pack_rows(pair, pieces).astype(BF16)
 
 
-def pack_grad(n, rank_ref, own_ref, other_ref, weight_ref, post_ref, gated_ref, out_ref):
-    width = post_ref.shape[1] // n
+def pack_grad(dests, rank_ref, own_ref, other_ref, weight_ref, post_ref, gated_ref, out_ref):
+    width = post_ref.shape[1] // dests
     pieces = max(1, LANES // width)
     columns = own_ref.shape[1]
     first = rank_ref[0] == 0
@@ -166,8 +167,16 @@
     ) + lax.dot_general(right, weight_ref[:, columns:], dims, preferred_element_type=F32)
     gated_ref[...] = grad_gated
     mixed = grad_gated * post_ref[...].astype(F32)
-    for k in range(n):
+    for k in range(dests):
         out_ref[k] = pack_rows(mixed[:, k * width : (k + 1) * width], pieces).astype(BF16)
+
+
+def each(count, body):
+    if count <= 32:
+        for index in range(count):
+            body(index)
+    else:
+        lax.fori_loop(0, count, lambda index, carry: (body(index), carry)[1], 0)
 
 
 def row_chunk(rows):
@@ -183,19 +192,24 @@
         spectrum = real_dft([blocks_ref[b, at].astype(F32) for b in range(n)], 2 * n)
         for m, (real, imag) in enumerate(spectrum):
             store(m, 0, at, real)
-            store(m, 1, at, jnp.zeros_like(real) if imag is None else imag)
+            if imag is not None:
+                store(m, 1, at, imag)
+            elif n > 31:
+                store(m, 1, at, jnp.zeros_like(real))
         return carry
 
     lax.fori_loop(0, rows // chunk, body, 0)
 
 
-def inverse_blocks(n, spec_ref, out_ref):
-    rows = out_ref.shape[1]
+def inverse_blocks(n, spec_ref, out_ref, rows):
     chunk = row_chunk(rows)
 
     def body(index, carry):
         at = pl.ds(pl.multiple_of(index * chunk, chunk), chunk)
-        spectrum = [(spec_ref[m, 0, at], spec_ref[m, 1, at]) for m in range(n + 1)]
+        spectrum = [
+            (spec_ref[m, 0, at], spec_ref[m, 1, at] if 0 < m < n else None)
+            for m in range(n + 1)
+        ]
         for b, value in enumerate(real_dft_transposed(spectrum, 2 * n, True)):
             out_ref[b, at] = value.astype(BF16)
         return carry
@@ -203,122 +217,203 @@
     lax.fori_loop(0, rows // chunk, body, 0)
 
 
+def is_edge(m, n):
+    return isinstance(m, int) and m in (0, n)
+
+
 def inverse_scale(m, n, length):
+    if isinstance(m, int):
+        return (0.5 if m in (0, n) else 1.0) / (n * length)
     edge = jnp.logical_or(m == 0, m == n)
     return jnp.where(edge, 0.5 / (n * length), 1.0 / (n * length))
 
 
-def mix_forward(n, pair_ref, table_ref, back_ref, out_ref, filt_ref, mid_ref, spec_ref):
+def inner_dft(m, n, table_ref, mid):
     length = table_ref.shape[1] // 2
-    width = filt_ref.shape[2]
+    if is_edge(m, n):
+        return jnp.dot(table_ref[m, :, :length], mid[:length], preferred_element_type=F32)
+    return jnp.dot(table_ref[m], mid, preferred_element_type=F32)
+
+
+def inner_back(m, n, back_ref, real, imag, spec_ref, pieces):
+    length = real.shape[0]
+    scale = inverse_scale(m, n, length)
+    product = jnp.concatenate([real * scale, imag * scale], axis=0).astype(BF16)
+    if is_edge(m, n):
+        back = jnp.dot(back_ref[m, :length], product, preferred_element_type=F32)
+    else:
+        back = jnp.dot(back_ref[m], product, preferred_element_type=F32)
+        spec_ref[m, 1] = pack_rows(back[length:], pieces)
+    spec_ref[m, 0] = pack_rows(back[:length], pieces)
+
+
+def started(*copies):
+    made = [pltpu.make_async_copy(*copy) for copy in copies]
+    for copy in made:
+        copy.start()
+    return made
+
+
+def mix_forward(
+    n,
+    pair_ref,
+    grad_ref,
+    table_hbm,
+    back_hbm,
+    out_ref,
+    filt_hbm,
+    table_ref,
+    back_ref,
+    filt_ref,
+    mid_ref,
+    spec_ref,
+    sems,
+):
+    length = table_ref.shape[1] // 2
+    width = filt_ref.shape[2] // 2
     pieces = max(1, LANES // width)
     pair_pieces = max(1, LANES // (2 * width))
-
-    if pair_pieces == 1:
-
-        def store(m, part, at, value):
-            mid_ref[m, pl.ds(pl.multiple_of(part * length + at.start, at.size), at.size)] = (
-                value.astype(BF16)
-            )
-    else:
-
-        def store(m, part, at, value):
-            for i in range(pair_pieces):
-                start = part * length + i * (length // pair_pieces) + at.start
-                mid_ref[m, pl.ds(pl.multiple_of(start, at.size), at.size)] = value[
-                    :, i * 2 * width : (i + 1) * 2 * width
-                ].astype(BF16)
+    rows = length // pieces
+    table_copy, back_copy = started(
+        (table_hbm, table_ref, sems.at[0]), (back_hbm, back_ref, sems.at[1])
+    )
+
+    def store(m, part, at, value):
+        for i in range(pair_pieces):
+            start = part * length + i * (length // pair_pieces) + at.start
+            mid_ref[m, pl.ds(pl.multiple_of(start, at.size), at.size)] = value[
+                :, i * 2 * width : (i + 1) * 2 * width
+            ].astype(BF16)
 
     forward_blocks(n, pair_ref, store)
-
-    def body(m, carry):
-        spec = jnp.dot(table_ref[m], mid_ref[m], preferred_element_type=F32)
+    out_ref[:, rows:] = grad_ref[...]
+    table_copy.wait()
+    back_copy.wait()
+
+    def body(m):
+        spec = inner_dft(m, n, table_ref, mid_ref[m])
         real, imag = spec[:length, :width], spec[length:, :width]
-        filt = spec[:, width:]
-        filt_ref[m] = filt.astype(filt_ref.dtype)
-        filt_real, filt_imag = filt[:length], filt[length:]
-        scale = inverse_scale(m, n, length)
-        product = jnp.concatenate(
-            [
-                (real * filt_real - imag * filt_imag) * scale,
-                (real * filt_imag + imag * filt_real) * scale,
-            ],
-            axis=0,
-        ).astype(BF16)
-        mid = jnp.dot(back_ref[m], product, preferred_element_type=F32)
-        spec_ref[m, 0] = pack_rows(mid[:length], pieces)
-        spec_ref[m, 1] = pack_rows(mid[length:], pieces)
-        return carry
-
-    lax.fori_loop(0, n + 1, body, 0)
-    inverse_blocks(n, spec_ref, out_ref)
-
-
-def mix_backward(n, grad_ref, filt_ref, table_ref, back_ref, out_ref, spec_ref):
+        filt_real, filt_imag = spec[:length, width:], spec[length:, width:]
+        filt_ref[m] = jnp.concatenate([filt_real, filt_imag], axis=1).astype(BF16)
+        inner_back(
+            m,
+            n,
+            back_ref,
+            real * filt_real - imag * filt_imag,
+            real * filt_imag + imag * filt_real,
+            spec_ref,
+            pieces,
+        )
+
+    each(n + 1, body)
+    (filt_copy,) = started((filt_ref, filt_hbm, sems.at[2]))
+    inverse_blocks(n, spec_ref, out_ref, rows)
+    filt_copy.wait()
+
+
+def mix_backward(
+    n,
+    both_ref,
+    filt_hbm,
+    table_hbm,
+    back_hbm,
+    out_ref,
+    table_ref,
+    back_ref,
+    filt_ref,
+    spec_ref,
+    sems,
+):
     length = table_ref.shape[1] // 2
-    width = filt_ref.shape[2]
+    width = filt_ref.shape[2] // 2
     pieces = max(1, LANES // width)
+    rows = length // pieces
+    copies = started(
+        (table_hbm, table_ref, sems.at[0]),
+        (filt_hbm, filt_ref, sems.at[1]),
+        (back_hbm, back_ref, sems.at[2]),
+    )
 
     def store(m, part, at, value):
         spec_ref[m, part, at] = value
 
-    forward_blocks(n, grad_ref, store)
-
-    def body(m, carry):
-        mid = jnp.concatenate(
-            [unpack_rows(spec_ref[m, 0], pieces), unpack_rows(spec_ref[m, 1], pieces)], axis=0
-        ).astype(BF16)
-        spec = jnp.dot(table_ref[m], mid, preferred_element_type=F32)
+    forward_blocks(n, both_ref.at[:, rows:], store)
+    for copy in copies:
+        copy.wait()
+
+    def body(m):
+        mid = unpack_rows(spec_ref[m, 0], pieces)
+        if not is_edge(m, n):
+            mid = jnp.concatenate([mid, unpack_rows(spec_ref[m, 1], pieces)], axis=0)
+        spec = inner_dft(m, n, table_ref, mid.astype(BF16))
         real, imag = spec[:length], spec[length:]
         filt = filt_ref[m].astype(F32)
-        filt_real, filt_imag = filt[:length], filt[length:]
-        scale = inverse_scale(m, n, length)
-        product = jnp.concatenate(
-            [
-                (filt_real * real + filt_imag * imag) * scale,
-                (filt_real * imag - filt_imag * real) * scale,
-            ],
-            axis=0,
-        ).astype(BF16)
-        back = jnp.dot(back_ref[m], product, preferred_element_type=F32)
-        spec_ref[m, 0] = pack_rows(back[:length], pieces)
-        spec_ref[m, 1] = pack_rows(back[length:], pieces)
-        return carry
-
-    lax.fori_loop(0, n + 1, body, 0)
-    inverse_blocks(n, spec_ref, out_ref)
-
-
-def unpack_channels(n, packed_ref, pieces):
+        filt_real, filt_imag = filt[:, :width], filt[:, width:]
+        inner_back(
+            m,
+            n,
+            back_ref,
+            filt_real * real + filt_imag * imag,
+            filt_real * imag - filt_imag * real,
+            spec_ref,
+            pieces,
+        )
+
+    each(n + 1, body)
+    inverse_blocks(n, spec_ref, out_ref, rows)
+
+
+def unpack_channels(packed_ref, pieces):
     return jnp.concatenate(
-        [unpack_rows(packed_ref[k].astype(F32), pieces) for k in range(n)], axis=1
+        [unpack_rows(packed_ref[k].astype(F32), pieces) for k in range(packed_ref.shape[0])],
+        axis=1,
     )
 
 
 def project(
-    n, rank_ref, mixed_ref, post_ref, grad_ref, weight_ref, away_ref, home_ref, post_grad_ref
+    pieces, rank_ref, both_ref, post_ref, grad_ref, weight_hbm, away_ref, home_ref, post_grad_ref,
+    weight_ref, sems,
 ):
-    channels = post_ref.shape[1]
-    pieces = max(1, LANES // (channels // n))
-    columns = home_ref.shape[1]
-    mixed = unpack_channels(n, mixed_ref, pieces)
+    rows = both_ref.shape[1] // 2
+    channels, columns = post_ref.shape[1], home_ref.shape[1]
+    rank = rank_ref[0]
+    half = channels // 2
+    copies = started(
+        *(
+            (
+                weight_hbm.at[
+                    pl.ds(k * half, half),
+                    pl.ds(pl.multiple_of((1 - rank if side == 0 else rank) * columns, LANES), columns),
+                ],
+                weight_ref.at[side, pl.ds(k * half, half)],
+                sems.at[side, k],
+            )
+            for side in range(2)
+            for k in range(2)
+        )
+    )
+    mixed = unpack_channels(both_ref.at[:, :rows], pieces)
     gated = (post_ref[...].astype(F32) * mixed).astype(BF16)
-    left = jnp.dot(gated, weight_ref[:, :columns], preferred_element_type=F32)
-    right = jnp.dot(gated, weight_ref[:, columns:], preferred_element_type=F32)
-    first = rank_ref[0] == 0
-    home_ref[...] = jnp.where(first, left, right)
-    away_ref[...] = jnp.where(first, right, left).astype(BF16)
     post_grad_ref[...] = (grad_ref[...] * mixed).astype(BF16)
+
+    def part(side, k):
+        copies[2 * side + k].wait()
+        return jnp.dot(
+            gated[:, k * half : (k + 1) * half],
+            weight_ref[side, k * half : (k + 1) * half],
+            preferred_element_type=F32,
+        )
+
+    away_ref[...] = (part(0, 0) + part(0, 1)).astype(BF16)
+    home_ref[...] = part(1, 0) + part(1, 1)
 
 
 def add_halves(home_ref, other_ref, out_ref):
     out_ref[...] = (home_ref[...] + other_ref[...].astype(F32)).astype(BF16)
 
 
-def input_grads(n, packed_ref, token_ref, pre_ref, feat_ref, pre_grad_ref, feat_grad_ref):
-    channels = pre_ref.shape[1]
-    pieces = max(1, LANES // (channels // n))
-    grad = unpack_channels(n, packed_ref, pieces) * keep_rows(token_ref, channels)
+def input_grads(pieces, packed_ref, token_ref, pre_ref, feat_ref, pre_grad_ref, feat_grad_ref):
+    grad = unpack_channels(packed_ref, pieces) * keep_rows(token_ref, pre_ref.shape[1])
     pre_grad_ref[...] = (grad * feat_ref[...].astype(F32)).astype(BF16)
     feat_grad_ref[...] = (grad * pre_ref[...].astype(F32)).astype(BF16)
 
@@ -336,23 +431,51 @@
     return table.astype(jnp.bfloat16)
 
 
-def call(kernel, outs, args, flops=0, scratch=(), scalars=0, limit=56):
-    def size(x):
-        return math.prod(x.shape) * np.dtype(x.dtype).itemsize
-
+def padded_bytes(shape, dtype):
+    *rest, rows, lanes = (1, *shape)
+    item = np.dtype(dtype).itemsize
+    rows = -(-rows // 8) * 8
+    return math.prod(rest) * rows * -(-lanes // LANES) * LANES * item
+
+
+def call(kernel, outs, args, grid=None, blocks=None, out_blocks=None, flops=0, scratch=(), prefetch=0, limit=0):
+    leaves = jax.tree.leaves(outs)
+    tensors = args[prefetch:]
+
+    def spec(array, block):
+        if block == "hbm":
+            return pl.BlockSpec(memory_space=pltpu.HBM)
+        if block is None:
+            rank = len(array.shape)
+            if grid is None:
+                return pl.BlockSpec(memory_space=pltpu.VMEM)
+            return pl.BlockSpec(array.shape, lambda *_: (0,) * rank)
+        return pl.BlockSpec(*block)
+
+    blocks = blocks or [None] * len(tensors)
+    out_blocks = out_blocks or [None] * len(leaves)
+    in_specs = [spec(x, b) for x, b in zip(tensors, blocks)]
+    out_specs = [spec(x, b) for x, b in zip(leaves, out_blocks)]
+    held = sum(
+        padded_bytes(b[0] if b else x.shape, x.dtype) * (1 if grid is None else 2)
+        for x, b in [*zip(tensors, blocks), *zip(leaves, out_blocks)]
+        if b != "hbm"
+    ) + sum(padded_bytes(x.shape, x.dtype) for x in scratch if "sem" not in str(x.dtype))
+    moved = sum(math.prod(x.shape) * np.dtype(x.dtype).itemsize for x in [*tensors, *leaves])
     return pl.pallas_call(
         kernel,
         out_shape=outs,
-        in_specs=[pl.BlockSpec(memory_space=pltpu.SMEM)] * scalars
-        + [pl.BlockSpec(memory_space=pltpu.VMEM)] * (len(args) - scalars),
-        out_specs=jax.tree.map(lambda _: pl.BlockSpec(memory_space=pltpu.VMEM), outs),
-        scratch_shapes=list(scratch),
-        compiler_params=pltpu.CompilerParams(vmem_limit_bytes=limit * 2**20),
-        cost_estimate=pl.CostEstimate(
-            flops=flops,
-            bytes_accessed=sum(size(x) for x in [*args, *jax.tree.leaves(outs)]),
-            transcendentals=0,
+        grid_spec=pltpu.PrefetchScalarGridSpec(
+            num_scalar_prefetch=prefetch,
+            grid=grid or (),
+            in_specs=in_specs,
+            out_specs=out_specs if isinstance(outs, tuple) else out_specs[0],
+            scratch_shapes=list(scratch),
         ),
+        compiler_params=pltpu.CompilerParams(
+            vmem_limit_bytes=min(max(held + 6 * 2**20, limit), VMEM_MOST)
+        ),
+        cost_estimate=pl.CostEstimate(flops=flops, bytes_accessed=moved, transcendentals=0),
     )(*args)
 
 
@@ -381,55 +504,107 @@
     table, back = tables
     tokens = token_ids.reshape(1, length)
     rank = lax.axis_index("tp").astype(jnp.int32).reshape(1)
-    filt_type = F32 if n <= 32 else BF16
     inner_flops = 2 * (n + 1) * (2 * length) ** 2 * width
+    spec_scratch = pltpu.VMEM((n + 1, 2, length // pieces, pieces * width), F32)
+
+    def by_channels(steps):
+        cut, dests = channels // steps, n // steps
+        return (
+            ((length, cut), lambda i, *_: (0, i)),
+            ((dests, *one.shape[1:]), lambda i, *_: (i, 0, 0)),
+            ((dests, *pair.shape[1:]), lambda i, *_: (i, 0, 0)),
+        )
 
     other_grad = swap_tp(out_grad)
+    steps = 2
+    flat, packed, pair_block = by_channels(steps)
     pair_out = call(
-        functools.partial(pack_inputs, n), pair, (tokens, pre_gate, features, filters)
+        functools.partial(pack_inputs, n // steps),
+        pair,
+        (tokens, pre_gate, features, filters),
+        grid=(steps,),
+        blocks=[None, flat, flat, flat],
+        out_blocks=[pair_block],
+        limit=VMEM_MOST,
     )
     pair_in = exchange(pair_out)
+    steps = 4
+    flat, packed, _ = by_channels(steps)
     grad_gated, grad_out = call(
-        functools.partial(pack_grad, n),
+        functools.partial(pack_grad, n // steps),
         (shape((length, channels), F32), one),
         (rank, out_grad, other_grad, out_weight, post_gate),
+        grid=(steps,),
+        blocks=[
+            None,
+            None,
+            ((channels // steps, 2 * columns), lambda i, *_: (i, 0)),
+            flat,
+        ],
+        out_blocks=[flat, packed],
         flops=4 * length * channels * columns,
-        scalars=1,
-    )
-    grad_in = exchange(grad_out)
-    spec_scratch = pltpu.VMEM((n + 1, 2, length // pieces, pieces * width), F32)
-    mixed_out, filt_spec = call(
+        prefetch=1,
+        limit=57 * 2**20,
+    )
+    tables_scratch = [pltpu.VMEM(table.shape, BF16), pltpu.VMEM(back.shape, BF16)]
+    filt_shape = shape((n + 1, length, 2 * width), BF16)
+    both = shape((n, 2 * one.shape[1], one.shape[2]), BF16)
+    both_out, filt_spec = call(
         functools.partial(mix_forward, n),
-        (one, shape((n + 1, 2 * length, width), filt_type)),
-        (pair_in, table, back),
+        (both, filt_shape),
+        (pair_in, grad_out, table, back),
+        blocks=[None, None, "hbm", "hbm"],
+        out_blocks=[None, "hbm"],
         flops=3 * inner_flops,
-        scratch=[pltpu.VMEM((n + 1, 2 * length, 2 * width), BF16), spec_scratch],
-    )
-    mixed_in = exchange(mixed_out)
+        scratch=[
+            *tables_scratch,
+            pltpu.VMEM(filt_shape.shape, BF16),
+            pltpu.VMEM((n + 1, 2 * length, 2 * width), BF16),
+            spec_scratch,
+            pltpu.SemaphoreType.DMA((3,)),
+        ],
+    )
+    both_in = exchange(both_out)
     grad_back_out = call(
         functools.partial(mix_backward, n),
         one,
-        (grad_in, filt_spec, table, back),
+        (both_in, filt_spec, table, back),
+        blocks=[None, "hbm", "hbm", "hbm"],
         flops=2 * inner_flops,
-        scratch=[spec_scratch],
+        scratch=[
+            *tables_scratch,
+            pltpu.VMEM(filt_shape.shape, BF16),
+            spec_scratch,
+            pltpu.SemaphoreType.DMA((3,)),
+        ],
     )
     grad_back_in = exchange(grad_back_out)
     away, home, grad_post = call(
-        functools.partial(project, n),
+        functools.partial(project, pieces),
         (
             shape((length, columns), BF16),
             shape((length, columns), F32),
             shape((length, channels), BF16),
         ),
-        (rank, mixed_in, post_gate, grad_gated, out_weight),
+        (rank, both_in, post_gate, grad_gated, out_weight),
+        blocks=[None, None, None, "hbm"],
         flops=4 * length * channels * columns,
-        scalars=1,
+        scratch=[
+            pltpu.VMEM((2, channels, columns), BF16),
+            pltpu.SemaphoreType.DMA((2, 2)),
+        ],
+        prefetch=1,
     )
     output = call(add_halves, shape((length, columns), BF16), (home, swap_tp(away)))
+    steps = 2
+    flat, packed, _ = by_channels(steps)
     grad_pre, grad_features = call(
-        functools.partial(input_grads, n),
+        functools.partial(input_grads, pieces),
         (shape((length, channels), BF16), shape((length, channels), BF16)),
         (grad_back_in, tokens, pre_gate, features),
+        grid=(steps,),
+        blocks=[packed, None, flat, flat],
+        out_blocks=[flat, flat],
     )
     return (output, grad_post, grad_pre, grad_features)
 

time: 85.5 us -> 74.8 us (0.87)
  Pallas kernels: 42.4 us -> 19.2 us
  blocking collectives: 0 us -> 20 us
  starting transfers between devices: 27.9 us -> 14.6 us
  local copies, waits for them, and re-layouts: 2.13 us -> 5.49 us
  waiting for transfers between devices: 11.8 us -> 14.2 us
    pallas_call x7, Pallas kernels: 42.4 us -> 19.2 us  [call(): pl.pallas_call(kernel, out_shape=outs, grid_spec=pltpu.PrefetchScalarGrid...]
    all_to_all x0 -> x1, blocking collectives: none -> 20 us  [exchange(): return lax.all_to_all(block, 'ctx', split_axis=0, concat_axis=0, tiled=True)]
    all_to_all x4 -> x2, starting transfers between devices: 24.8 us -> 11.5 us  [exchange(): return lax.all_to_all(block, 'ctx', split_axis=0, concat_axis=0, tiled=True)]
    ppermute x2, waiting for transfers between devices: 7.27 us -> 14.2 us  [swap_tp(): return lax.ppermute(block, 'tp', [(0, 1), (1, 0)])]
    all_to_all x4 -> x2, waiting for transfers between devices: 4.48 us -> 0.01 us  [exchange(): return lax.all_to_all(block, 'ctx', split_axis=0, concat_axis=0, tiled=True)]
    unnamed x14 -> x24, local copies, waits for them, and re-layouts: 2.13 us -> 5.49 us
  transfers between devices with their start and end apart: 6 -> 4, of which waited for: 4 -> 2; matrix products, arithmetic and copies ran while one was open for 0% -> 0% of each run, Pallas kernels for 45% -> 11%
where the time goes in v2:
time: 74.8 us; the launch traced here: 74.3 us
  blocking collectives  20 us (27%)
  Pallas kernels  19.2 us (26%)
  starting transfers between devices  14.6 us (20%)
  waiting for transfers between devices  14.2 us (19%)
  local copies, waits for them, and re-layouts  5.49 us (7%)
    all_to_all x1, blocking collectives, exchange(): return lax.all_to_all(block, 'ctx', split_axis=0, concat_axis=0, tiled=True)  20 us
    pallas_call x7, Pallas kernels, call(): pl.pallas_call(kernel, out_shape=outs, grid_spec=pltpu.PrefetchScalarGrid...  19.2 us
    ppermute x2, waiting for transfers between devices, swap_tp(): return lax.ppermute(block, 'tp', [(0, 1), (1, 0)])  14.2 us
    all_to_all x2, starting transfers between devices, exchange(): return lax.all_to_all(block, 'ctx', split_axis=0, concat_axis=0, tiled=True)  11.5 us
    unnamed x24, local copies, waits for them, and re-layouts  5.49 us
    ppermute x2, starting transfers between devices, swap_tp(): return lax.ppermute(block, 'tp', [(0, 1), (1, 0)])  3.17 us
  transfers between devices with their start and end apart: 4, of which 2 were waited for; matrix products, arithmetic and copies ran while one was open for 0% of the time, Pallas kernels for 11%

profile of v2, /device:TPU:0, one launch (start us, length us, event | category | flops | bytes accessed | tf_op | source)
XLA Modules:
  0.0 74.3 jit_solution(3487385308990047544)
XLA Ops:
  0.6 0.0 copy-start.10
  0.6 2.4 %shard_map.120 = bf16[16,128,128]{2,1,0:T(8,128)(2,1)} custom-call(s32[1,128]{1,0:T(1,128)} %bitcast.2, bf16[128,1024]{1,0:T(8,128)(2,1)} %pre_ref.3, bf16[128,1024]{1,0:T(8,128)(2,1)} %feat_ref.3, f32[128,1024]{1,0:T(8,128)} %filt_ref.1), custom_call_target="tpu_custom_call" | custom-call | bytes 1573376 | tf_op jit(solution)/shard_map/pallas_call | solution.py:465
  3.0 7.4 %all-to-all-start = ((bf16[16,128,128]{2,1,0:T(8,128)(2,1)}), bf16[16,128,128]{2,1,0:T(8,128)(2,1)S(1)}, u32[]{:S(2)}, u32[]{:S(2)}) async-start(bf16[16,128,128]{2,1,0:T(8,128)(2,1)} %shard_map.120), calls=%async_computation | async-start | bytes 1048576 | tf_op jit(solution)/shard_map/all_to_all | solution.py:483
  10.4 0.0 copy-done.10
  10.4 1.6 %collective-permute-start = (bf16[128,1024]{1,0:T(8,128)(2,1)S(1)}, bf16[128,1024]{1,0:T(8,128)(2,1)S(1)}, u32[]{:S(2)}, u32[]{:S(2)}) collective-permute-start(bf16[128,1024]{1,0:T(8,128)(2,1)S(1)} %copy-done.10), channel_id=1, source_target_pairs={{0,1},{1,0},{2,3},{3,2},{4,5},{5,4},{6,7},{7,6},{8,9},{9,8},{10,11... | collective-permute-start | bytes 786440 | tf_op jit(solution)/shard_map/ppermute | solution.py:489
  12.0 7.1 %collective-permute-done.other_ref = bf16[128,1024]{1,0:T(8,128)(2,1)S(1)} collective-permute-done((bf16[128,1024]{1,0:T(8,128)(2,1)S(1)}, bf16[128,1024]{1,0:T(8,128)(2,1)S(1)}, u32[]{:S(2)}, u32[]{:S(2)}) %collective-permute-start) | collective-permute-done | bytes 262176 | tf_op jit(solution)/shard_map/ppermute | solution.py:489
  19.1 0.0 copy-start.11
  19.1 0.7 copy-done.11
  19.8 5.2 %shard_map.121 = (f32[128,1024]{1,0:T(8,128)}, bf16[16,64,128]{2,1,0:T(8,128)(2,1)}) custom-call(s32[1]{0:T(128)} %bitcast.rank_ref, bf16[128,1024]{1,0:T(8,128)(2,1)} %own_ref.1, bf16[128,1024]{1,0:T(8,128)(2,1)} %copy-done.11, bf16[1024,2048]{1,0:T(8,128)(2,1)} %weight_hbm.1, bf16[128,1024]{1,0:T(8,128)(2,1)} %post_ref.3), custom_call_target="tpu_custom_call" | custom-call | flops 536870912 | bytes 5767168 | tf_op jit(solution)/shard_map/pallas_call | solution.py:465
  25.0 0.0 all-to-all-done.pair_ref
  25.0 0.0 copy-done.1
  25.0 0.0 copy-start.2
  25.0 1.6 %copy-done.2 = bf16[17,256,256]{2,1,0:T(8,128)(2,1)S(1)} copy-done((bf16[17,256,256]{2,1,0:T(8,128)(2,1)S(1)}, bf16[17,256,256]{2,1,0:T(8,128)(2,1)}, u32[]{:S(2)}) %copy-start.2) | copy-done | bytes 2228248
  26.7 0.9 %copy-done.8 = bf16[16,64,128]{2,1,0:T(8,128)(2,1)S(1)} copy-done((bf16[16,64,128]{2,1,0:T(8,128)(2,1)S(1)}, bf16[16,64,128]{2,1,0:T(8,128)(2,1)}, u32[]{:S(2)}) %copy-start.8) | copy-done | bytes 262168
  27.6 3.2 %shard_map.122 = (bf16[16,128,128]{2,1,0:T(8,128)(2,1)S(1)}, bf16[17,128,128]{2,1,0:T(8,128)(2,1)S(1)}) custom-call(bf16[16,128,128]{2,1,0:T(8,128)(2,1)S(1)} %all-to-all-done.pair_ref, bf16[16,64,128]{2,1,0:T(8,128)(2,1)S(1)} %copy-done.8, bf16[17,256,256]{2,1,0:T(8,128)(2,1)S(1)} %copy-done.2, bf16[17,256,256]{2,1,0:T(8,128)(2,1)S(1)} %copy-done.1), custom_call_target="tpu_custom_call" | custom-call | flops 427819008 | bytes 6324224 | tf_op jit(solution)/shard_map/pallas_call | solution.py:465
  30.8 20.0 %all_to_all.15.both_ref = bf16[16,128,128]{2,1,0:T(8,128)(2,1)S(1)} all-to-all(bf16[16,128,128]{2,1,0:T(8,128)(2,1)S(1)} %get-tuple-element.14), channel_id=1, replica_groups=mesh['ctx'=16,'tp'=2] {'ctx'}, dimensions={0} | all-to-all | bytes 1048576 | tf_op jit(solution)/shard_map/all_to_all | solution.py:483
  50.8 0.0 copy-done.3
  50.8 4.1 %shard_map.125 = bf16[16,64,128]{2,1,0:T(8,128)(2,1)} custom-call(bf16[16,128,128]{2,1,0:T(8,128)(2,1)S(1)} %all_to_all.15.both_ref, bf16[17,128,128]{2,1,0:T(8,128)(2,1)S(1)} %get-tuple-element.19.filt_hbm, bf16[17,256,256]{2,1,0:T(8,128)(2,1)S(1)} %copy-done.3, bf16[17,256,256]{2,1,0:T(8,128)(2,1)S(1)} %copy-done.1), custom_call_target="tpu_custom_call" | custom-call | flops 285212672 | bytes 5799936 | tf_op jit(solution)/shard_map/pallas_call | solution.py:465
  54.9 4.1 %all-to-all-start.2 = ((bf16[16,64,128]{2,1,0:T(8,128)(2,1)}), bf16[16,64,128]{2,1,0:T(8,128)(2,1)S(1)}, u32[]{:S(2)}, u32[]{:S(2)}) async-start(bf16[16,64,128]{2,1,0:T(8,128)(2,1)} %shard_map.125), calls=%async_computation.2 | async-start | bytes 524288 | tf_op jit(solution)/shard_map/all_to_all | solution.py:483
  59.1 0.0 copy-done.4
  59.1 0.0 copy-done.7
  59.1 0.0 copy-start
  59.1 2.2 %copy-done = bf16[1024,2048]{1,0:T(8,128)(2,1)S(1)} copy-done((bf16[1024,2048]{1,0:T(8,128)(2,1)S(1)}, bf16[1024,2048]{1,0:T(8,128)(2,1)}, u32[]{:S(2)}) %copy-start) | copy-done | bytes 4194328
  61.3 2.1 %shard_map.123 = (bf16[128,1024]{1,0:T(8,128)(2,1)S(1)}, f32[128,1024]{1,0:T(8,128)S(1)}, bf16[128,1024]{1,0:T(8,128)(2,1)}) custom-call(s32[1]{0:T(128)} %bitcast.rank_ref, bf16[16,128,128]{2,1,0:T(8,128)(2,1)S(1)} %all_to_all.15.both_ref, bf16[128,1024]{1,0:T(8,128)(2,1)S(1)} %copy-done.4, f32[128,1024]{1,0:T(8,128)S(1)} %copy-done.7, ...), custom_call_target="tpu_custom_call" | custom-call | flops 536870912 | bytes 6553600 | tf_op jit(solution)/shard_map/pallas_call | solution.py:465
  63.4 1.6 %collective-permute-start.1 = (bf16[128,1024]{1,0:T(8,128)(2,1)S(1)}, bf16[128,1024]{1,0:T(8,128)(2,1)S(1)}, u32[]{:S(2)}, u32[]{:S(2)}) collective-permute-start(bf16[128,1024]{1,0:T(8,128)(2,1)S(1)} %get-tuple-element.17), channel_id=1, source_target_pairs={{0,1},{1,0},{2,3},{3,2},{4,5},{5,4},{6,7},{7,6},{8,9},{9,8},{10,11... | collective-permute-start | bytes 786440 | tf_op jit(solution)/shard_map/ppermute | solution.py:489
  65.0 7.1 %collective-permute-done.1.other_ref = bf16[128,1024]{1,0:T(8,128)(2,1)S(1)} collective-permute-done((bf16[128,1024]{1,0:T(8,128)(2,1)S(1)}, bf16[128,1024]{1,0:T(8,128)(2,1)S(1)}, u32[]{:S(2)}, u32[]{:S(2)}) %collective-permute-start.1) | collective-permute-done | bytes 262176 | tf_op jit(solution)/shard_map/ppermute | solution.py:489
  72.1 0.8 %shard_map.124 = bf16[128,1024]{1,0:T(8,128)(2,1)} custom-call(f32[128,1024]{1,0:T(8,128)S(1)} %get-tuple-element.16.home_ref, bf16[128,1024]{1,0:T(8,128)(2,1)S(1)} %collective-permute-done.1.other_ref), custom_call_target="tpu_custom_call" | custom-call | bytes 1048576 | tf_op jit(solution)/shard_map/pallas_call | solution.py:465
  72.8 0.0 all-to-all-done.2.packed_ref
  72.8 0.0 copy-done.5
  72.8 0.0 copy-done.6
  72.8 0.0 copy-done.9
  72.9 1.4 %shard_map.126 = (bf16[128,1024]{1,0:T(8,128)(2,1)}, bf16[128,1024]{1,0:T(8,128)(2,1)}) custom-call(bf16[16,64,128]{2,1,0:T(8,128)(2,1)S(1)} %all-to-all-done.2.packed_ref, s32[1,128]{1,0:T(1,128)S(1)} %bitcast.3, bf16[128,1024]{1,0:T(8,128)(2,1)S(1)} %copy-done.5, bf16[128,1024]{1,0:T(8,128)(2,1)S(1)} %copy-done.6), custom_call_target="tpu_custom_call" | custom-call | bytes 1311232 | tf_op jit(solution)/shard_map/pallas_call | solution.py:465
  (8 shorter events, 0.0 us)
Async XLA Ops:
  0.6 9.7 %copy-start.10 = (bf16[128,1024]{1,0:T(8,128)(2,1)S(1)}, bf16[128,1024]{1,0:T(8,128)(2,1)}, u32[]{:S(2)}) copy-start(bf16[128,1024]{1,0:T(8,128)(2,1)} %own_ref.1) | copy-start | bytes 786436
  3.0 22.0 %all-to-all-start = ((bf16[16,128,128]{2,1,0:T(8,128)(2,1)}), bf16[16,128,128]{2,1,0:T(8,128)(2,1)S(1)}, u32[]{:S(2)}, u32[]{:S(2)}) async-start(bf16[16,128,128]{2,1,0:T(8,128)(2,1)} %shard_map.120), calls=%async_computation | async-start | bytes 1048576 | tf_op jit(solution)/shard_map/all_to_all | solution.py:483
  10.4 8.7 %collective-permute-start = (bf16[128,1024]{1,0:T(8,128)(2,1)S(1)}, bf16[128,1024]{1,0:T(8,128)(2,1)S(1)}, u32[]{:S(2)}, u32[]{:S(2)}) collective-permute-start(bf16[128,1024]{1,0:T(8,128)(2,1)S(1)} %copy-done.10), channel_id=1, source_target_pairs={{0,1},{1,0},{2,3},{3,2},{4,5},{5,4},{6,7},{7,6},{8,9},{9,8},{10,11... | collective-permute-start | bytes 786440 | tf_op jit(solution)/shard_map/ppermute | solution.py:489
  19.1 0.7 copy-start.11
  19.8 5.2 %copy-start.1 = (bf16[17,256,256]{2,1,0:T(8,128)(2,1)S(1)}, bf16[17,256,256]{2,1,0:T(8,128)(2,1)}, u32[]{:S(2)}) copy-start(bf16[17,256,256]{2,1,0:T(8,128)(2,1)} %constant.9.clone.back_hbm) | copy-start | bytes 6684676
  25.0 1.6 %copy-start.2 = (bf16[17,256,256]{2,1,0:T(8,128)(2,1)S(1)}, bf16[17,256,256]{2,1,0:T(8,128)(2,1)}, u32[]{:S(2)}) copy-start(bf16[17,256,256]{2,1,0:T(8,128)(2,1)} %constant.8.clone.table_hbm) | copy-start | bytes 6684676
  26.7 0.9 %copy-start.8 = (bf16[16,64,128]{2,1,0:T(8,128)(2,1)S(1)}, bf16[16,64,128]{2,1,0:T(8,128)(2,1)}, u32[]{:S(2)}) copy-start(bf16[16,64,128]{2,1,0:T(8,128)(2,1)} %get-tuple-element.13.grad_ref) | copy-start | bytes 786436
  27.6 23.2 %copy-start.3 = (bf16[17,256,256]{2,1,0:T(8,128)(2,1)S(1)}, bf16[17,256,256]{2,1,0:T(8,128)(2,1)}, u32[]{:S(2)}) copy-start(bf16[17,256,256]{2,1,0:T(8,128)(2,1)} %constant.8.clone.table_hbm) | copy-start | bytes 6684676
  50.8 8.3 %copy-start.4 = (bf16[128,1024]{1,0:T(8,128)(2,1)S(1)}, bf16[128,1024]{1,0:T(8,128)(2,1)}, u32[]{:S(2)}) copy-start(bf16[128,1024]{1,0:T(8,128)(2,1)} %post_ref.3) | copy-start | bytes 786436
  50.8 8.3 %copy-start.7 = (f32[128,1024]{1,0:T(8,128)S(1)}, f32[128,1024]{1,0:T(8,128)}, u32[]{:S(2)}) copy-start(f32[128,1024]{1,0:T(8,128)} %get-tuple-element.15.grad_ref) | copy-start | bytes 1572868
  54.9 17.9 %all-to-all-start.2 = ((bf16[16,64,128]{2,1,0:T(8,128)(2,1)}), bf16[16,64,128]{2,1,0:T(8,128)(2,1)S(1)}, u32[]{:S(2)}, u32[]{:S(2)}) async-start(bf16[16,64,128]{2,1,0:T(8,128)(2,1)} %shard_map.125), calls=%async_computation.2 | async-start | bytes 524288 | tf_op jit(solution)/shard_map/all_to_all | solution.py:483
  59.1 2.2 %copy-start = (bf16[1024,2048]{1,0:T(8,128)(2,1)S(1)}, bf16[1024,2048]{1,0:T(8,128)(2,1)}, u32[]{:S(2)}) copy-start(bf16[1024,2048]{1,0:T(8,128)(2,1)} %weight_hbm.1) | copy-start | bytes 12582916
  61.3 11.6 %copy-start.5 = (bf16[128,1024]{1,0:T(8,128)(2,1)S(1)}, bf16[128,1024]{1,0:T(8,128)(2,1)}, u32[]{:S(2)}) copy-start(bf16[128,1024]{1,0:T(8,128)(2,1)} %pre_ref.3) | copy-start | bytes 786436
  61.3 11.6 %copy-start.6 = (bf16[128,1024]{1,0:T(8,128)(2,1)S(1)}, bf16[128,1024]{1,0:T(8,128)(2,1)}, u32[]{:S(2)}) copy-start(bf16[128,1024]{1,0:T(8,128)(2,1)} %feat_ref.3) | copy-start | bytes 786436
  61.3 11.6 %copy-start.9 = (s32[128]{0:T(128)S(1)}, s32[128]{0:T(128)}, u32[]{:S(2)}) copy-start(s32[128]{0:T(128)} %param.13) | copy-start | bytes 1540
  63.4 8.7 %collective-permute-start.1 = (bf16[128,1024]{1,0:T(8,128)(2,1)S(1)}, bf16[128,1024]{1,0:T(8,128)(2,1)S(1)}, u32[]{:S(2)}, u32[]{:S(2)}) collective-permute-start(bf16[128,1024]{1,0:T(8,128)(2,1)S(1)} %get-tuple-element.17), channel_id=1, source_target_pairs={{0,1},{1,0},{2,3},{3,2},{4,5},{5,4},{6,7},{7,6},{8,9},{9,8},{10,11... | collective-permute-start | bytes 786440 | tf_op jit(solution)/shard_map/ppermute | solution.py:489

commit v3 on v1

v3 whole, which is shorter than its diff:
```python
import functools
import math

import jax
import jax.numpy as jnp
import numpy as np
from jax import lax
from jax.experimental import pallas as pl
from jax.experimental.pallas import tpu as pltpu
from jax.sharding import PartitionSpec as P

BASES = 4
LANES = 128
MATRIX_ROWS = 512
VMEM_GRANT = 24 * 2**20
F32 = jnp.float32
BF16 = jnp.bfloat16


def complex_dft(values, sign):
    length = len(values)
    if length == 1:
        return values
    half = length // 2
    even = [
        (values[b][0] + values[b + half][0], values[b][1] + values[b + half][1])
        for b in range(half)
    ]
    odd = [
        twist(
            (values[b][0] - values[b + half][0], values[b][1] - values[b + half][1]),
            sign * b,
            length,
        )
        for b in range(half)
    ]
    even = complex_dft(even, sign)
    odd = complex_dft(odd, sign)
    return [part for pair in zip(even, odd) for part in pair]


def twist(value, step, length):
    real, imag = value
    step = step % length
    if step == 0:
        return real, imag
    if 4 * step == length:
        return -imag, real
    if 2 * step == length:
        return -real, -imag
    if 4 * step == 3 * length:
        return imag, -real
    cos = math.cos(2.0 * math.pi * step / length)
    sin = math.sin(2.0 * math.pi * step / length)
    if 8 * step % length == 0:
        root = math.sqrt(0.5)
        signed_cos = 1.0 if cos > 0 else -1.0
        signed_sin = 1.0 if sin > 0 else -1.0
        a = real * root
        b = imag * root
        if signed_cos == signed_sin:
            return (a - b, a + b) if signed_cos > 0 else (b - a, -a - b)
        return (a + b, b - a) if signed_cos > 0 else (-a - b, a - b)
    return real * cos - imag * sin, real * sin + imag * cos


def real_dft(values, length):
    if length == 2:
        if len(values) == 1:
            return [(values[0], None), (values[0], None)]
        return [(values[0] + values[1], None), (values[0] - values[1], None)]
    half, quarter = length // 2, length // 4
    if len(values) == length:
        total = [values[b] + values[b + half] for b in range(half)]
        rest = [values[b] - values[b + half] for b in range(half)]
    else:
        total = values
        rest = values
    out = [None] * (half + 1)
    for index, value in enumerate(real_dft(total, half)):
        out[2 * index] = value
    turned = [
        twist((rest[b], -rest[b + quarter]), -b, length) for b in range(quarter)
    ]
    for index, (real, imag) in enumerate(complex_dft(turned, -1)):
        place = 4 * index + 1
        if place <= half:
            out[place] = (real, imag)
        else:
            out[length - place] = (real, -imag)
    return out


def real_dft_transposed(spectrum, length, padded):
    if length == 2:
        first, second = spectrum[0][0], spectrum[1][0]
        return [first + second] if padded else [first + second, first - second]
    half, quarter = length // 2, length // 4
    total = real_dft_transposed(
        [spectrum[2 * index] for index in range(quarter + 1)], half, False
    )
    odd = []
    for index in range(quarter):
        place = 4 * index + 1
        if place <= half:
            odd.append(spectrum[place])
        else:
            real, imag = spectrum[length - place]
            odd.append((real, -imag))
    rest = [None] * half
    for b, value in enumerate(complex_dft(odd, 1)):
        real, imag = twist(value, b, length)
        rest[b] = real
        rest[b + quarter] = -imag
    low = [total[b] + rest[b] for b in range(half)]
    if padded:
        return low
    return low + [total[b] - rest[b] for b in range(half)]


def pack_inputs(
    parts,
    token_hbm,
    pre_hbm,
    feat_hbm,
    filt_hbm,
    out_hbm,
    token_ref,
    pre_ref,
    feat_ref,
    filt_ref,
    out_ref,
    in_sems,
    out_sems,
):
    n, rows, _ = out_ref.shape
    width, dests = rows // 2, n // parts
    cut = dests * width
    (token_copy,) = started((token_hbm, token_ref, in_sems.at[3, 0]))
    copies = [
        started(
            *(
                (source.at[:, pl.ds(k * cut, cut)], target.at[:, pl.ds(k * cut, cut)], in_sems.at[i, k])
                for i, (source, target) in enumerate(
                    ((pre_hbm, pre_ref), (feat_hbm, feat_ref), (filt_hbm, filt_ref))
                )
            )
        )
        for k in range(parts)
    ]
    token_copy.wait()
    keep = (token_ref[...] < BASES).astype(F32)
    row = lax.broadcasted_iota(jnp.int32, (cut, cut), 0)
    column = lax.broadcasted_iota(jnp.int32, (cut, cut), 1)
    identity = jnp.where(row == column, 1.0, 0.0).astype(BF16)
    sent = []
    for k in range(parts):
        for copy in copies[k]:
            copy.wait()
        at = slice(k * cut, (k + 1) * cut)
        mixer = (pre_ref[:, at].astype(F32) * feat_ref[:, at].astype(F32)).astype(BF16)
        mixer = (times_transposed(identity, mixer) * keep).astype(BF16)
        filt = times_transposed(identity, filt_ref[:, at].astype(BF16)).astype(BF16)
        for j in range(dests):
            mine = slice(j * width, (j + 1) * width)
            out_ref[k * dests + j] = jnp.concatenate([mixer[mine], filt[mine]], axis=0)
        here = pl.ds(k * dests, dests)
        sent += started((out_ref.at[here], out_hbm.at[here], out_sems.at[k]))
    for copy in sent:
        copy.wait()


def own_grad(rank_ref, own_ref, weight_ref, out_ref):
    out_ref[...] = times_transposed(weight_ref[...], own_ref[...])


def times_transposed(left, right):
    return lax.dot_general(left, right, (((1,), (1,)), ((), ())), preferred_element_type=F32)


def pack_grad(
    dests, rank_ref, other_ref, weight_ref, part_ref, post_ref, gated_ref, out_ref, away_ref
):
    width = out_ref.shape[1]
    weight = weight_ref[...]
    away_ref[...] = weight
    grad_gated = part_ref[...] + times_transposed(weight, other_ref[...])
    gated_ref[...] = grad_gated
    mixed = grad_gated * post_ref[...].T.astype(F32)
    for k in range(dests):
        out_ref[k] = mixed[k * width : (k + 1) * width].astype(BF16)


def started(*copies):
    made = [pltpu.make_async_copy(*copy) for copy in copies]
    for copy in made:
        copy.start()
    return made


def forward_blocks(n, load, twist_ref, mid_ref):
    rows, length = mid_ref.shape[1], mid_ref.shape[2] // 2
    chunk = rows // row_chunks(rows)

    def body(index, carry):
        at = pl.ds(pl.multiple_of(index * chunk, chunk), chunk)
        spectrum = real_dft([load(b, at).astype(F32) for b in range(n)], 2 * n)
        for m, (real, imag) in enumerate(spectrum):
            cos, sin = twist_ref[m : m + 1], twist_ref[n + 1 + m : n + 2 + m]
            if m == 0:
                imag = jnp.zeros_like(real)
            elif imag is None:
                real, imag = real * cos, -(real * sin)
            else:
                real, imag = real * cos + imag * sin, imag * cos - real * sin
            mid_ref[m, at, :length] = real.astype(mid_ref.dtype)
            mid_ref[m, at, length:] = imag.astype(mid_ref.dtype)
        return carry

    lax.fori_loop(0, rows // chunk, body, 0, unroll=min(2, rows // chunk))


def inverse_blocks(n, twist_ref, spec_ref, store, after=None):
    rows, length = spec_ref.shape[1], spec_ref.shape[2] // 2
    chunk = rows // row_chunks(rows)

    def body(index, carry):
        at = pl.ds(pl.multiple_of(index * chunk, chunk), chunk)
        spectrum = [(0.5 * spec_ref[0, at, :length], None)]
        for m in range(1, n + 1):
            cos, sin = twist_ref[m : m + 1], twist_ref[n + 1 + m : n + 2 + m]
            real, imag = spec_ref[m, at, :length], spec_ref[m, at, length:]
            if m == n:
                spectrum.append((0.5 * (real * cos - imag * sin), None))
            else:
                spectrum.append((real * cos - imag * sin, real * sin + imag * cos))
        for b, value in enumerate(real_dft_transposed(spectrum, 2 * n, True)):
            store(b, at, value.astype(BF16))
        if after is not None:
            after(index, at)
        return carry

    lax.fori_loop(0, rows // chunk, body, 0, unroll=min(2, rows // chunk))


def inner_product(values_ref, matrix, first, last):
    _, rows, wide = values_ref.shape
    values = values_ref[first:last].reshape((last - first) * rows, wide).astype(BF16)
    return jnp.dot(values, matrix, preferred_element_type=F32)


def frequency_groups(n, rows):
    step = max(1, MATRIX_ROWS // rows)
    return [(first, min(first + step, n + 1)) for first in range(0, n + 1, step)]


def inner_back(n, matrix, prod_ref, spec_ref):
    rows = prod_ref.shape[1]
    for first, last in frequency_groups(n, rows):
        back = inner_product(prod_ref, matrix, first, last)
        spec_ref[first:last] = back.reshape(last - first, rows, back.shape[1])


def mix_forward(
    n,
    pair_ref,
    grad_ref,
    twist_ref,
    dft_hbm,
    both_ref,
    filt_ref,
    dft_ref,
    mid_ref,
    prod_ref,
    spec_ref,
    sems,
):
    length = twist_ref.shape[1]
    width = grad_ref.shape[1]
    (dft_copy,) = started((dft_hbm, dft_ref, sems.at[0]))
    forward_blocks(n, lambda b, at: pair_ref[b, at], twist_ref, mid_ref)
    both_ref[:, :, length:] = grad_ref[...]
    dft_copy.wait()
    for first, last in frequency_groups(n, 2 * width):
        spec = inner_product(mid_ref, dft_ref[0], first, last)
        for m in range(first, last):
            at = (m - first) * 2 * width
            signal, filt = spec[at : at + width], spec[at + width : at + 2 * width]
            filt_ref[m] = filt.astype(filt_ref.dtype)
            real, imag = signal[:, :length], signal[:, length:]
            filt_real, filt_imag = filt[:, :length], filt[:, length:]
            prod_ref[m, :, :length] = (real * filt_real - imag * filt_imag).astype(prod_ref.dtype)
            prod_ref[m, :, length:] = (real * filt_imag + imag * filt_real).astype(prod_ref.dtype)
    inner_back(n, dft_ref[1], prod_ref, spec_ref)

    def store(b, at, value):
        both_ref[b, at, :length] = value

    inverse_blocks(n, twist_ref, spec_ref, store)


def mix_backward(
    n,
    both_ref,
    post_ref,
    twist_ref,
    dft_ref,
    filt_ref,
    weight_ref,
    out_hbm,
    gated_hbm,
    away_hbm,
    mid_ref,
    prod_ref,
    spec_ref,
    out_ref,
    gated_ref,
    away_ref,
    sems,
):
    length = twist_ref.shape[1]
    width = out_ref.shape[1]
    mixed = channel_rows(both_ref, length).T.astype(F32)
    gated = (post_ref[...].astype(F32) * mixed).astype(BF16)
    gated_ref[...] = gated
    away_ref[...] = jnp.dot(gated, weight_ref[...], preferred_element_type=F32).astype(BF16)
    copies = started((away_ref, away_hbm, sems.at[0]), (gated_ref, gated_hbm, sems.at[1]))
    forward_blocks(n, lambda b, at: both_ref[b, at, length:], twist_ref, mid_ref)
    for first, last in frequency_groups(n, width):
        spec = inner_product(mid_ref, dft_ref[0], first, last)
        for m in range(first, last):
            at = (m - first) * width
            signal, filt = spec[at : at + width], filt_ref[m].astype(F32)
            real, imag = signal[:, :length], signal[:, length:]
            filt_real, filt_imag = filt[:, :length], filt[:, length:]
            prod_ref[m, :, :length] = (filt_real * real + filt_imag * imag).astype(prod_ref.dtype)
            prod_ref[m, :, length:] = (filt_real * imag - filt_imag * real).astype(prod_ref.dtype)
    inner_back(n, dft_ref[1], prod_ref, spec_ref)

    def store(b, at, value):
        out_ref[b, at] = value

    def out_copy(index, at):
        return pltpu.make_async_copy(out_ref.at[:, at], out_hbm.at[:, at], sems.at[2 + index])

    chunks = row_chunks(width)
    if chunks == 1:
        inverse_blocks(n, twist_ref, spec_ref, store)
        copies += started((out_ref, out_hbm, sems.at[2]))
    else:
        inverse_blocks(
            n, twist_ref, spec_ref, store, lambda index, at: out_copy(index, at).start()
        )
        step = width // chunks
        copies += [out_copy(index, pl.ds(index * step, step)) for index in range(chunks)]
    for copy in copies:
        copy.wait()


def row_chunks(rows):
    return max(1, rows // 16)


def channel_rows(blocks_ref, length):
    return jnp.concatenate(
        [blocks_ref[k, :, :length] for k in range(blocks_ref.shape[0])], axis=0
    )


def weight_copies(parts, side, weight_hbm, weight_ref, sems):
    channels, columns = weight_ref.shape
    rows = channels // parts
    start = pl.multiple_of(side * columns, LANES)
    return started(
        *(
            (
                weight_hbm.at[pl.ds(k * rows, rows), pl.ds(start, columns)],
                weight_ref.at[pl.ds(k * rows, rows)],
                sems[k],
            )
            for k in range(parts)
        )
    )


def part_products(copies, gated, weight_ref):
    rows = weight_ref.shape[0] // len(copies)
    total = None
    for k, copy in enumerate(copies):
        copy.wait()
        at = slice(k * rows, (k + 1) * rows)
        product = jnp.dot(gated[:, at], weight_ref[at], preferred_element_type=F32)
        total = product if total is None else total + product
    return total


def project_home(
    parts,
    rank_ref,
    gated_ref,
    both_ref,
    grad_ref,
    weight_hbm,
    home_ref,
    post_grad_ref,
    weight_ref,
    sems,
):
    copies = weight_copies(
        parts, rank_ref[0], weight_hbm, weight_ref, [sems.at[k] for k in range(parts)]
    )
    mixed = channel_rows(both_ref, grad_ref.shape[1]).astype(F32)
    post_grad_ref[...] = (grad_ref[...] * mixed).astype(BF16).T
    home_ref[...] = part_products(copies, gated_ref[...], weight_ref)


def finish(
    token_ref,
    packed_ref,
    pre_ref,
    feat_ref,
    home_ref,
    other_ref,
    pre_grad_ref,
    feat_grad_ref,
    out_ref,
):
    keep = (token_ref[...] < BASES).astype(BF16)
    grad = (channel_rows(packed_ref, packed_ref.shape[2]) * keep).T.astype(F32)
    pre_grad_ref[...] = (grad * feat_ref[...].astype(F32)).astype(BF16)
    feat_grad_ref[...] = (grad * pre_ref[...].astype(F32)).astype(BF16)
    out_ref[...] = (home_ref[...] + other_ref[...].astype(F32)).astype(BF16)


def dft_tables(n, length):
    index = np.arange(length)
    angle = index[:, None] * index[None, :] % length * (2.0 * math.pi / length)
    cos, sin = np.cos(angle), np.sin(angle)
    matrix = np.block([[cos, -sin], [sin, cos]])
    dft = np.stack([matrix, matrix.T / (n * length)]).astype(jnp.bfloat16)
    angle = np.arange(n + 1)[:, None] * index[None, :] * (math.pi / (n * length))
    twist = np.concatenate([np.cos(angle), np.sin(angle)], axis=0).astype(np.float32)
    return twist, dft


def call(kernel, outs, args, grid=None, blocks=None, out_blocks=None, flops=0, scratch=(), prefetch=0, from_hbm=()):
    leaves = jax.tree.leaves(outs)
    args = [
        pltpu.with_memory_space_constraint(x, pltpu.HBM) if k in from_hbm else x
        for k, x in enumerate(args)
    ]
    tensors = args[prefetch:]

    def spec(array, block):
        if block == "hbm":
            return pl.BlockSpec(memory_space=pltpu.HBM)
        if block is None:
            rank = len(array.shape)
            if grid is None:
                return pl.BlockSpec(memory_space=pltpu.VMEM)
            return pl.BlockSpec(array.shape, lambda *_: (0,) * rank)
        return pl.BlockSpec(*block)

    blocks = blocks or [None] * len(tensors)
    out_blocks = out_blocks or [None] * len(leaves)
    in_specs = [spec(x, b) for x, b in zip(tensors, blocks)]
    out_specs = [spec(x, b) for x, b in zip(leaves, out_blocks)]
    moved = sum(math.prod(x.shape) * np.dtype(x.dtype).itemsize for x in [*tensors, *leaves])
    return pl.pallas_call(
        kernel,
        out_shape=outs,
        grid_spec=pltpu.PrefetchScalarGridSpec(
            num_scalar_prefetch=prefetch,
            grid=grid or (),
            in_specs=in_specs,
            out_specs=out_specs if isinstance(outs, tuple) else out_specs[0],
            scratch_shapes=list(scratch),
        ),
        compiler_params=pltpu.CompilerParams(vmem_limit_bytes=VMEM_GRANT),
        cost_estimate=pl.CostEstimate(flops=flops, bytes_accessed=moved, transcendentals=0),
    )(*args)


def exchange(block):
    return lax.all_to_all(block, "ctx", split_axis=0, concat_axis=0, tiled=True)


def swap_tp(block):
    count = lax.axis_size("tp")
    assert count == 2
    return lax.ppermute(block, "tp", [(0, 1), (1, 0)])


def on_device(
    tables, post_gate, pre_gate, features, filters, token_ids, out_weight, out_grad
):
    n = lax.axis_size("ctx")
    length, channels = post_gate.shape
    columns = out_grad.shape[1]
    width = channels // n
    shape = jax.ShapeDtypeStruct
    one = (n, width, length)
    pair = (n, 2 * width, length)
    both = (n, width, 2 * length)
    twist, dft = tables
    tokens = token_ids.reshape(1, length)
    rank = lax.axis_index("tp").astype(jnp.int32).reshape(1)
    inner_flops = 2 * (n + 1) * (2 * length) ** 2 * width
    spec_shape = (n + 1, width, 2 * length)
    narrow = BF16 if width >= 16 else F32
    spec_scratch = pltpu.VMEM(spec_shape, F32)
    narrow_scratch = pltpu.VMEM(spec_shape, narrow)

    def by_channels(steps):
        cut, dests = channels // steps, n // steps
        return (
            ((length, cut), lambda i, *_: (0, i)),
            ((cut, length), lambda i, *_: (i, 0)),
            ((dests, *one[1:]), lambda i, *_: (i, 0, 0)),
        )

    other_grad = swap_tp(out_grad)
    parts = 4
    pair_out = call(
        functools.partial(pack_inputs, parts),
        pltpu.HBM(pair, BF16),
        (tokens, pre_gate, features, filters),
        blocks=["hbm"] * 4,
        out_blocks=["hbm"],
        from_hbm=range(4),
        scratch=[
            pltpu.VMEM(tokens.shape, jnp.int32),
            pltpu.VMEM((length, channels), BF16),
            pltpu.VMEM((length, channels), BF16),
            pltpu.VMEM((length, channels), F32),
            pltpu.VMEM(pair, BF16),
            pltpu.SemaphoreType.DMA((4, parts)),
            pltpu.SemaphoreType.DMA((parts,)),
        ],
    )
    pair_in = exchange(pair_out)
    steps = 4
    flat, turned, packed = by_channels(steps)
    weight_block = (channels // steps, columns)
    grad_part = call(
        own_grad,
        pltpu.VMEM((channels, length), F32),
        (rank, out_grad, out_weight),
        grid=(steps,),
        blocks=[None, (weight_block, lambda i, rank: (i, rank[0]))],
        out_blocks=[turned],
        flops=2 * length * channels * columns,
        prefetch=1,
        from_hbm=(1, 2),
    )
    grad_gated, grad_out, away_weight = call(
        functools.partial(pack_grad, n // steps),
        (
            pltpu.HBM((channels, length), F32),
            pltpu.VMEM(one, BF16),
            pltpu.VMEM((channels, columns), BF16),
        ),
        (rank, other_grad, out_weight, grad_part, post_gate),
        grid=(steps,),
        blocks=[None, (weight_block, lambda i, rank: (i, 1 - rank[0])), turned, flat],
        out_blocks=[turned, packed, (weight_block, lambda i, *_: (i, 0))],
        flops=2 * length * channels * columns,
        prefetch=1,
        from_hbm=(2, 4),
    )
    both_out, filt_spec, kept_dft = call(
        functools.partial(mix_forward, n),
        (
            shape(both, BF16),
            pltpu.VMEM(spec_shape, narrow),
            pltpu.VMEM(dft.shape, BF16),
        ),
        (pair_in, grad_out, twist, dft),
        blocks=[None, None, None, "hbm"],
        from_hbm=(3,),
        flops=3 * inner_flops,
        scratch=[
            pltpu.VMEM((n + 1, 2 * width, 2 * length), BF16),
            narrow_scratch,
            spec_scratch,
            pltpu.SemaphoreType.DMA((1,)),
        ],
    )
    both_in = exchange(both_out)
    grad_back_out, gated, away = call(
        functools.partial(mix_backward, n),
        (
            pltpu.HBM(one, BF16),
            pltpu.HBM((length, channels), BF16),
            pltpu.HBM((length, columns), BF16),
        ),
        (both_in, post_gate, twist, kept_dft, filt_spec, away_weight),
        out_blocks=["hbm", "hbm", "hbm"],
        flops=2 * inner_flops + 2 * length * channels * columns,
        scratch=[
            narrow_scratch,
            narrow_scratch,
            spec_scratch,
            pltpu.VMEM(one, BF16),
            pltpu.VMEM((length, channels), BF16),
            pltpu.VMEM((length, columns), BF16),
            pltpu.SemaphoreType.DMA((2 + row_chunks(width),)),
        ],
    )
    grad_back_in = exchange(grad_back_out)
    other_part = swap_tp(away)
    parts = 2
    home, grad_post = call(
        functools.partial(project_home, parts),
        (shape((length, columns), F32), shape((length, channels), BF16)),
        (rank, gated, both_in, grad_gated, out_weight),
        grid=(1,),
        blocks=[None, (one, lambda *_: (0, 0, 0)), None, "hbm"],
        flops=2 * length * channels * columns,
        scratch=[pltpu.VMEM((channels, columns), BF16), pltpu.SemaphoreType.DMA((parts,))],
        prefetch=1,
    )
    steps = 2
    flat, _, packed = by_channels(steps)
    half = ((length, columns // steps), lambda i, *_: (0, i))
    grad_pre, grad_features, output = call(
        finish,
        (
            shape((length, channels), BF16),
            shape((length, channels), BF16),
            shape((length, columns), BF16),
        ),
        (tokens, grad_back_in, pre_gate, features, home, other_part),
        grid=(steps,),
        blocks=[None, packed, flat, flat, half, half],
        out_blocks=[flat, flat, half],
    )
    return (output, grad_post, grad_pre, grad_features)


def solution(mesh):
    in_specs = (
        P("ctx", "tp"),
        P("ctx", "tp"),
        P("ctx", "tp"),
        P("ctx", "tp"),
        P("ctx"),
        P("tp", None),
        P("ctx", "tp"),
    )
    out_specs = (P("ctx", "tp"), P("ctx", "tp"), P("ctx", "tp"), P("ctx", "tp"))

    def run(*args):
        n = mesh.shape["ctx"]
        tables = tuple(jnp.asarray(x) for x in dft_tables(n, args[0].shape[0] // n))
        return jax.shard_map(
            functools.partial(on_device, tables),
            mesh=mesh,
            in_specs=in_specs,
            out_specs=out_specs,
            check_vma=False,
        )(*args)

    return run
```

time: 85.5 us -> 64.1 us (0.75)
  Pallas kernels: 42.4 us -> 16.9 us
  blocking collectives: 0 us -> 18.4 us
  starting transfers between devices: 27.9 us -> 14.7 us
  waiting for transfers between devices: 11.8 us -> 8.63 us
  local copies, waits for them, and re-layouts: 2.13 us -> 4.2 us
    pallas_call x7, Pallas kernels: 42.4 us -> 16.9 us  [call(): pl.pallas_call(kernel, out_shape=outs, grid_spec=pltpu.PrefetchScalarGrid...]
    all_to_all x0 -> x1, blocking collectives: none -> 18.4 us  [exchange(): return lax.all_to_all(block, 'ctx', split_axis=0, concat_axis=0, tiled=True)]
    all_to_all x4 -> x2, starting transfers between devices: 24.8 us -> 11.5 us  [exchange(): return lax.all_to_all(block, 'ctx', split_axis=0, concat_axis=0, tiled=True)]
    unnamed x14 -> x16, local copies, waits for them, and re-layouts: 2.13 us -> 4.2 us
    all_to_all x4 -> x2, waiting for transfers between devices: 4.48 us -> 2.82 us  [exchange(): return lax.all_to_all(block, 'ctx', split_axis=0, concat_axis=0, tiled=True)]
    ppermute x2, waiting for transfers between devices: 7.27 us -> 5.81 us  [swap_tp(): return lax.ppermute(block, 'tp', [(0, 1), (1, 0)])]
  transfers between devices with their start and end apart: 6 -> 4, of which waited for: 4 -> 4; matrix products, arithmetic and copies ran while one was open for 0% -> 0% of each run, Pallas kernels for 45% -> 13%
where the time goes in v3:
time: 64.1 us; the launch traced here: 63.5 us
  blocking collectives  18.4 us (29%)
  Pallas kernels  16.9 us (26%)
  starting transfers between devices  14.7 us (23%)
  waiting for transfers between devices  8.63 us (13%)
  local copies, waits for them, and re-layouts  4.2 us (7%)
  between operations  0.71 us (1%)
    all_to_all x1, blocking collectives, exchange(): return lax.all_to_all(block, 'ctx', split_axis=0, concat_axis=0, tiled=True)  18.4 us
    pallas_call x7, Pallas kernels, call(): pl.pallas_call(kernel, out_shape=outs, grid_spec=pltpu.PrefetchScalarGrid...  16.9 us
    all_to_all x2, starting transfers between devices, exchange(): return lax.all_to_all(block, 'ctx', split_axis=0, concat_axis=0, tiled=True)  11.5 us
    ppermute x2, waiting for transfers between devices, swap_tp(): return lax.ppermute(block, 'tp', [(0, 1), (1, 0)])  5.81 us
    unnamed x16, local copies, waits for them, and re-layouts  4.2 us
    ppermute x2, starting transfers between devices, swap_tp(): return lax.ppermute(block, 'tp', [(0, 1), (1, 0)])  3.17 us
    all_to_all x2, waiting for transfers between devices, exchange(): return lax.all_to_all(block, 'ctx', split_axis=0, concat_axis=0, tiled=True)  2.82 us
  transfers between devices with their start and end apart: 4, of which 4 were waited for; matrix products, arithmetic and copies ran while one was open for 0% of the time, Pallas kernels for 13%

profile of v3, /device:TPU:0, one launch (start us, length us, event | category | flops | bytes accessed | tf_op | source)
XLA Modules:
  0.0 63.5 jit_solution(11063284629762443540)
XLA Ops:
  0.6 2.8 %shard_map.120 = bf16[16,128,128]{2,1,0:T(8,128)(2,1)} custom-call(s32[1,128]{1,0:T(1,128)} %bitcast.2, bf16[128,1024]{1,0:T(8,128)(2,1)} %pre_ref.1, bf16[128,1024]{1,0:T(8,128)(2,1)} %feat_ref.1, f32[128,1024]{1,0:T(8,128)} %filt_hbm.1), custom_call_target="tpu_custom_call" | custom-call | bytes 1573376 | tf_op jit(solution)/shard_map/pallas_call | solution.py:469
  3.4 7.4 %all-to-all-start = ((bf16[16,128,128]{2,1,0:T(8,128)(2,1)}), bf16[16,128,128]{2,1,0:T(8,128)(2,1)S(1)}, u32[]{:S(2)}, u32[]{:S(2)}) async-start(bf16[16,128,128]{2,1,0:T(8,128)(2,1)} %shard_map.120), calls=%async_computation | async-start | bytes 1048576 | tf_op jit(solution)/shard_map/all_to_all | solution.py:485
  10.8 1.6 %collective-permute-start = (bf16[128,1024]{1,0:T(8,128)(2,1)}, bf16[128,1024]{1,0:T(8,128)(2,1)S(1)}, u32[]{:S(2)}, u32[]{:S(2)}) collective-permute-start(bf16[128,1024]{1,0:T(8,128)(2,1)} %own_ref.1), channel_id=1, source_target_pairs={{0,1},{1,0},{2,3},{3,2},{4,5},{5,4},{6,7},{7,6},{8,9},{9,8},{10,11... | collective-permute-start | bytes 786440 | tf_op jit(solution)/shard_map/ppermute | solution.py:491
  12.4 0.0 copy-start.6
  12.4 3.1 %shard_map.121.part_ref = f32[1024,128]{1,0:T(8,128)S(1)} custom-call(s32[1]{0:T(128)} %bitcast.1.rank_ref, bf16[128,1024]{1,0:T(8,128)(2,1)} %own_ref.1, bf16[1024,2048]{1,0:T(8,128)(2,1)} %weight_hbm.1), custom_call_target="tpu_custom_call" | custom-call | flops 268435456 | bytes 4980736 | tf_op jit(solution)/shard_map/pallas_call | solution.py:469
  15.5 0.0 copy-start.3
  15.5 4.1 %collective-permute-done.other_ref = bf16[128,1024]{1,0:T(8,128)(2,1)S(1)} collective-permute-done((bf16[128,1024]{1,0:T(8,128)(2,1)}, bf16[128,1024]{1,0:T(8,128)(2,1)S(1)}, u32[]{:S(2)}, u32[]{:S(2)}) %collective-permute-start) | collective-permute-done | bytes 262176 | tf_op jit(solution)/shard_map/ppermute | solution.py:491
  19.6 4.0 %shard_map.122 = (f32[1024,128]{1,0:T(8,128)}, bf16[16,64,128]{2,1,0:T(8,128)(2,1)S(1)}, bf16[1024,1024]{1,0:T(8,128)(2,1)S(1)}) custom-call(s32[1]{0:T(128)} %bitcast.1.rank_ref, bf16[128,1024]{1,0:T(8,128)(2,1)S(1)} %collective-permute-done.other_ref, bf16[1024,2048]{1,0:T(8,128)(2,1)} %weight_hbm.1, f32[1024,128]{1,0:T(8,128)S(1)} %shard_map.121.part_ref, ...), custom_call_target="tpu_custom_call" | custom-call | flops 268435456 | bytes 8126464 | tf_op jit(solution)/shard_map/pallas_call | solution.py:469
  23.6 1.6 %all-to-all-done.pair_ref = bf16[16,128,128]{2,1,0:T(8,128)(2,1)S(1)} async-done(((bf16[16,128,128]{2,1,0:T(8,128)(2,1)}), bf16[16,128,128]{2,1,0:T(8,128)(2,1)S(1)}, u32[]{:S(2)}, u32[]{:S(2)}) %all-to-all-start) | async-done | bytes 524320 | tf_op jit(solution)/shard_map/all_to_all | solution.py:485
  25.2 0.0 copy-done.6
  25.2 2.0 %shard_map.123 = (bf16[16,64,256]{2,1,0:T(8,128)(2,1)S(1)}, bf16[17,64,256]{2,1,0:T(8,128)(2,1)S(1)}, bf16[2,256,256]{2,1,0:T(8,128)(2,1)S(1)}) custom-call(bf16[16,128,128]{2,1,0:T(8,128)(2,1)S(1)} %all-to-all-done.pair_ref, bf16[16,64,128]{2,1,0:T(8,128)(2,1)S(1)} %get-tuple-element.18.grad_ref, f32[34,128]{1,0:T(8,128)S(1)} %copy-done.6, ...), custom_call_target="tpu_custom_call" | custom-call | flops 427819008 | bytes 2409472 | tf_op jit(solution)/shard_map/pallas_call | solution.py:469
  27.3 18.4 %all_to_all.15.both_ref = bf16[16,64,256]{2,1,0:T(8,128)(2,1)S(1)} all-to-all(bf16[16,64,256]{2,1,0:T(8,128)(2,1)S(1)} %get-tuple-element.19), channel_id=1, replica_groups=mesh['ctx'=16,'tp'=2] {'ctx'}, dimensions={0} | all-to-all | bytes 1048576 | tf_op jit(solution)/shard_map/all_to_all | solution.py:485
  45.7 0.0 copy-done.3
  45.7 0.0 copy-start.1
  45.7 0.0 copy-start.2
  45.7 0.0 copy-start.7
  45.7 2.5 %shard_map.124 = (bf16[16,64,128]{2,1,0:T(8,128)(2,1)}, bf16[128,1024]{1,0:T(8,128)(2,1)}, bf16[128,1024]{1,0:T(8,128)(2,1)}) custom-call(bf16[16,64,256]{2,1,0:T(8,128)(2,1)S(1)} %all_to_all.15.both_ref, bf16[128,1024]{1,0:T(8,128)(2,1)S(1)} %copy-done.3, f32[34,128]{1,0:T(8,128)S(1)} %copy-done.6, bf16[2,256,256]{2,1,0:T(8,128)(2,1)S(1)} %get-tuple-element.20.dft_ref, ...), custom_call_target="tpu_custom_call" | custom-call | flops 553648128 | bytes 4506624 | tf_op jit(solution)/shard_map/pallas_call | solution.py:469
  48.2 4.1 %all-to-all-start.2 = ((bf16[16,64,128]{2,1,0:T(8,128)(2,1)}), bf16[16,64,128]{2,1,0:T(8,128)(2,1)S(1)}, u32[]{:S(2)}, u32[]{:S(2)}) async-start(bf16[16,64,128]{2,1,0:T(8,128)(2,1)} %get-tuple-element.23), calls=%async_computation.2 | async-start | bytes 524288 | tf_op jit(solution)/shard_map/all_to_all | solution.py:485
  52.3 1.6 %collective-permute-start.1 = (bf16[128,1024]{1,0:T(8,128)(2,1)}, bf16[128,1024]{1,0:T(8,128)(2,1)S(1)}, u32[]{:S(2)}, u32[]{:S(2)}) collective-permute-start(bf16[128,1024]{1,0:T(8,128)(2,1)} %get-tuple-element.27), channel_id=1, source_target_pairs={{0,1},{1,0},{2,3},{3,2},{4,5},{5,4},{6,7},{7,6},{8,9},{9,8},{10,11... | collective-permute-start | bytes 786440 | tf_op jit(solution)/shard_map/ppermute | solution.py:491
  53.9 0.0 copy-start
  53.9 2.2 %copy-done = bf16[1024,2048]{1,0:T(8,128)(2,1)S(1)} copy-done((bf16[1024,2048]{1,0:T(8,128)(2,1)S(1)}, bf16[1024,2048]{1,0:T(8,128)(2,1)}, u32[]{:S(2)}) %copy-start) | copy-done | bytes 4194328
  56.1 0.0 copy-start.4
  56.1 1.0 %copy-done.4 = f32[1024,128]{1,0:T(8,128)S(1)} copy-done((f32[1024,128]{1,0:T(8,128)S(1)}, f32[1024,128]{1,0:T(8,128)}, u32[]{:S(2)}) %copy-start.4) | copy-done | bytes 524312
  57.1 0.0 copy-start.5
  57.1 0.9 %copy-done.5 = bf16[128,1024]{1,0:T(8,128)(2,1)S(1)} copy-done((bf16[128,1024]{1,0:T(8,128)(2,1)S(1)}, bf16[128,1024]{1,0:T(8,128)(2,1)}, u32[]{:S(2)}) %copy-start.5) | copy-done | bytes 262168
  58.1 1.4 %shard_map.125 = (f32[128,1024]{1,0:T(8,128)S(1)}, bf16[128,1024]{1,0:T(8,128)(2,1)}) custom-call(s32[1]{0:T(128)} %bitcast.1.rank_ref, bf16[128,1024]{1,0:T(8,128)(2,1)S(1)} %copy-done.5, bf16[16,64,256]{2,1,0:T(8,128)(2,1)S(1)} %all_to_all.15.both_ref, f32[1024,128]{1,0:T(8,128)S(1)} %copy-done.4, bf16[1024,2048]{1,0:T(8,128)(2,1)S(1)} %copy-done), custom_call_target="tpu_custom_call" | custom-call | flops 268435456 | bytes 6291456 | tf_op jit(solution)/shard_map/pallas_call | solution.py:469
  59.4 1.7 %collective-permute-done.1.other_ref = bf16[128,1024]{1,0:T(8,128)(2,1)S(1)} collective-permute-done((bf16[128,1024]{1,0:T(8,128)(2,1)}, bf16[128,1024]{1,0:T(8,128)(2,1)S(1)}, u32[]{:S(2)}, u32[]{:S(2)}) %collective-permute-start.1) | collective-permute-done | bytes 262176 | tf_op jit(solution)/shard_map/ppermute | solution.py:491
  61.1 1.2 %all-to-all-done.2.packed_ref = bf16[16,64,128]{2,1,0:T(8,128)(2,1)S(1)} async-done(((bf16[16,64,128]{2,1,0:T(8,128)(2,1)}), bf16[16,64,128]{2,1,0:T(8,128)(2,1)S(1)}, u32[]{:S(2)}, u32[]{:S(2)}) %all-to-all-start.2) | async-done | bytes 262176 | tf_op jit(solution)/shard_map/all_to_all | solution.py:485
  62.3 0.0 copy-done.1
  62.3 0.0 copy-done.2
  62.3 0.0 copy-done.7
  62.4 1.2 %shard_map.126 = (bf16[128,1024]{1,0:T(8,128)(2,1)}, bf16[128,1024]{1,0:T(8,128)(2,1)}, bf16[128,1024]{1,0:T(8,128)(2,1)}) custom-call(s32[1,128]{1,0:T(1,128)S(1)} %bitcast.3, bf16[16,64,128]{2,1,0:T(8,128)(2,1)S(1)} %all-to-all-done.2.packed_ref, bf16[128,1024]{1,0:T(8,128)(2,1)S(1)} %copy-done.1, bf16[128,1024]{1,0:T(8,128)(2,1)S(1)} %copy-done.2, ...), custom_call_target="tpu_custom_call" | custom-call | bytes 2359808 | tf_op jit(solution)/shard_map/pallas_call | solution.py:469
Async XLA Ops:
  3.4 21.8 %all-to-all-start = ((bf16[16,128,128]{2,1,0:T(8,128)(2,1)}), bf16[16,128,128]{2,1,0:T(8,128)(2,1)S(1)}, u32[]{:S(2)}, u32[]{:S(2)}) async-start(bf16[16,128,128]{2,1,0:T(8,128)(2,1)} %shard_map.120), calls=%async_computation | async-start | bytes 1048576 | tf_op jit(solution)/shard_map/all_to_all | solution.py:485
  10.8 8.8 %collective-permute-start = (bf16[128,1024]{1,0:T(8,128)(2,1)}, bf16[128,1024]{1,0:T(8,128)(2,1)S(1)}, u32[]{:S(2)}, u32[]{:S(2)}) collective-permute-start(bf16[128,1024]{1,0:T(8,128)(2,1)} %own_ref.1), channel_id=1, source_target_pairs={{0,1},{1,0},{2,3},{3,2},{4,5},{5,4},{6,7},{7,6},{8,9},{9,8},{10,11... | collective-permute-start | bytes 786440 | tf_op jit(solution)/shard_map/ppermute | solution.py:491
  12.4 12.9 %copy-start.6 = (f32[34,128]{1,0:T(8,128)S(1)}, f32[34,128]{1,0:T(8,128)}, u32[]{:S(2)}) copy-start(f32[34,128]{1,0:T(8,128)} %constant.9.clone.twist_ref) | copy-start | bytes 52228
  15.5 30.2 %copy-start.3 = (bf16[128,1024]{1,0:T(8,128)(2,1)S(1)}, bf16[128,1024]{1,0:T(8,128)(2,1)}, u32[]{:S(2)}) copy-start(bf16[128,1024]{1,0:T(8,128)(2,1)} %post_ref.3) | copy-start | bytes 786436
  45.7 16.6 %copy-start.1 = (bf16[128,1024]{1,0:T(8,128)(2,1)S(1)}, bf16[128,1024]{1,0:T(8,128)(2,1)}, u32[]{:S(2)}) copy-start(bf16[128,1024]{1,0:T(8,128)(2,1)} %pre_ref.1) | copy-start | bytes 786436
  45.7 16.6 %copy-start.2 = (bf16[128,1024]{1,0:T(8,128)(2,1)S(1)}, bf16[128,1024]{1,0:T(8,128)(2,1)}, u32[]{:S(2)}) copy-start(bf16[128,1024]{1,0:T(8,128)(2,1)} %feat_ref.1) | copy-start | bytes 786436
  45.7 16.6 %copy-start.7 = (s32[128]{0:T(128)S(1)}, s32[128]{0:T(128)}, u32[]{:S(2)}) copy-start(s32[128]{0:T(128)} %param.13) | copy-start | bytes 1540
  48.2 14.2 %all-to-all-start.2 = ((bf16[16,64,128]{2,1,0:T(8,128)(2,1)}), bf16[16,64,128]{2,1,0:T(8,128)(2,1)S(1)}, u32[]{:S(2)}, u32[]{:S(2)}) async-start(bf16[16,64,128]{2,1,0:T(8,128)(2,1)} %get-tuple-element.23), calls=%async_computation.2 | async-start | bytes 524288 | tf_op jit(solution)/shard_map/all_to_all | solution.py:485
  52.3 8.8 %collective-permute-start.1 = (bf16[128,1024]{1,0:T(8,128)(2,1)}, bf16[128,1024]{1,0:T(8,128)(2,1)S(1)}, u32[]{:S(2)}, u32[]{:S(2)}) collective-permute-start(bf16[128,1024]{1,0:T(8,128)(2,1)} %get-tuple-element.27), channel_id=1, source_target_pairs={{0,1},{1,0},{2,3},{3,2},{4,5},{5,4},{6,7},{7,6},{8,9},{9,8},{10,11... | collective-permute-start | bytes 786440 | tf_op jit(solution)/shard_map/ppermute | solution.py:491
  53.9 2.2 %copy-start = (bf16[1024,2048]{1,0:T(8,128)(2,1)S(1)}, bf16[1024,2048]{1,0:T(8,128)(2,1)}, u32[]{:S(2)}) copy-start(bf16[1024,2048]{1,0:T(8,128)(2,1)} %weight_hbm.1) | copy-start | bytes 12582916
  56.1 1.0 %copy-start.4 = (f32[1024,128]{1,0:T(8,128)S(1)}, f32[1024,128]{1,0:T(8,128)}, u32[]{:S(2)}) copy-start(f32[1024,128]{1,0:T(8,128)} %get-tuple-element.25.grad_ref) | copy-start | bytes 1572868
  57.1 0.9 %copy-start.5 = (bf16[128,1024]{1,0:T(8,128)(2,1)S(1)}, bf16[128,1024]{1,0:T(8,128)(2,1)}, u32[]{:S(2)}) copy-start(bf16[128,1024]{1,0:T(8,128)(2,1)} %get-tuple-element.24.gated_ref) | copy-start | bytes 786436

commit v4 on v3

--- a/solution.py
+++ b/solution.py
@@ -11,7 +11,6 @@
 
 BASES = 4
 LANES = 128
-MATRIX_ROWS = 512
 VMEM_GRANT = 24 * 2**20
 F32 = jnp.float32
 BF16 = jnp.bfloat16
@@ -118,56 +117,14 @@
     return low + [total[b] - rest[b] for b in range(half)]
 
 
-def pack_inputs(
-    parts,
-    token_hbm,
-    pre_hbm,
-    feat_hbm,
-    filt_hbm,
-    out_hbm,
-    token_ref,
-    pre_ref,
-    feat_ref,
-    filt_ref,
-    out_ref,
-    in_sems,
-    out_sems,
-):
-    n, rows, _ = out_ref.shape
-    width, dests = rows // 2, n // parts
-    cut = dests * width
-    (token_copy,) = started((token_hbm, token_ref, in_sems.at[3, 0]))
-    copies = [
-        started(
-            *(
-                (source.at[:, pl.ds(k * cut, cut)], target.at[:, pl.ds(k * cut, cut)], in_sems.at[i, k])
-                for i, (source, target) in enumerate(
-                    ((pre_hbm, pre_ref), (feat_hbm, feat_ref), (filt_hbm, filt_ref))
-                )
-            )
-        )
-        for k in range(parts)
-    ]
-    token_copy.wait()
-    keep = (token_ref[...] < BASES).astype(F32)
-    row = lax.broadcasted_iota(jnp.int32, (cut, cut), 0)
-    column = lax.broadcasted_iota(jnp.int32, (cut, cut), 1)
-    identity = jnp.where(row == column, 1.0, 0.0).astype(BF16)
-    sent = []
-    for k in range(parts):
-        for copy in copies[k]:
-            copy.wait()
-        at = slice(k * cut, (k + 1) * cut)
-        mixer = (pre_ref[:, at].astype(F32) * feat_ref[:, at].astype(F32)).astype(BF16)
-        mixer = (times_transposed(identity, mixer) * keep).astype(BF16)
-        filt = times_transposed(identity, filt_ref[:, at].astype(BF16)).astype(BF16)
-        for j in range(dests):
-            mine = slice(j * width, (j + 1) * width)
-            out_ref[k * dests + j] = jnp.concatenate([mixer[mine], filt[mine]], axis=0)
-        here = pl.ds(k * dests, dests)
-        sent += started((out_ref.at[here], out_hbm.at[here], out_sems.at[k]))
-    for copy in sent:
-        copy.wait()
+def pack_inputs(dests, token_ref, pre_ref, feat_ref, filt_ref, out_ref):
+    width = out_ref.shape[1] // 2
+    keep = (token_ref[...] < BASES).astype(BF16)
+    mixer = (pre_ref[...].astype(F32) * feat_ref[...].astype(F32)).astype(BF16).T * keep
+    filt = filt_ref[...].astype(BF16).T
+    for k in range(dests):
+        at = slice(k * width, (k + 1) * width)
+        out_ref[k] = jnp.concatenate([mixer[at], filt[at]], axis=0)
 
 
 def own_grad(rank_ref, own_ref, weight_ref, out_ref):
@@ -198,67 +155,45 @@
     return made
 
 
-def forward_blocks(n, load, twist_ref, mid_ref):
-    rows, length = mid_ref.shape[1], mid_ref.shape[2] // 2
-    chunk = rows // row_chunks(rows)
-
-    def body(index, carry):
-        at = pl.ds(pl.multiple_of(index * chunk, chunk), chunk)
-        spectrum = real_dft([load(b, at).astype(F32) for b in range(n)], 2 * n)
-        for m, (real, imag) in enumerate(spectrum):
-            cos, sin = twist_ref[m : m + 1], twist_ref[n + 1 + m : n + 2 + m]
-            if m == 0:
-                imag = jnp.zeros_like(real)
-            elif imag is None:
-                real, imag = real * cos, -(real * sin)
-            else:
-                real, imag = real * cos + imag * sin, imag * cos - real * sin
-            mid_ref[m, at, :length] = real.astype(mid_ref.dtype)
-            mid_ref[m, at, length:] = imag.astype(mid_ref.dtype)
-        return carry
-
-    lax.fori_loop(0, rows // chunk, body, 0, unroll=min(2, rows // chunk))
-
-
-def inverse_blocks(n, twist_ref, spec_ref, store, after=None):
-    rows, length = spec_ref.shape[1], spec_ref.shape[2] // 2
-    chunk = rows // row_chunks(rows)
-
-    def body(index, carry):
-        at = pl.ds(pl.multiple_of(index * chunk, chunk), chunk)
-        spectrum = [(0.5 * spec_ref[0, at, :length], None)]
-        for m in range(1, n + 1):
-            cos, sin = twist_ref[m : m + 1], twist_ref[n + 1 + m : n + 2 + m]
-            real, imag = spec_ref[m, at, :length], spec_ref[m, at, length:]
-            if m == n:
-                spectrum.append((0.5 * (real * cos - imag * sin), None))
-            else:
-                spectrum.append((real * cos - imag * sin, real * sin + imag * cos))
-        for b, value in enumerate(real_dft_transposed(spectrum, 2 * n, True)):
-            store(b, at, value.astype(BF16))
-        if after is not None:
-            after(index, at)
-        return carry
-
-    lax.fori_loop(0, rows // chunk, body, 0, unroll=min(2, rows // chunk))
-
-
-def inner_product(values_ref, matrix, first, last):
-    _, rows, wide = values_ref.shape
-    values = values_ref[first:last].reshape((last - first) * rows, wide).astype(BF16)
+def forward_blocks(n, blocks, twist_ref, mid_ref, rows):
+    length = mid_ref.shape[2] // 2
+    for m, (real, imag) in enumerate(real_dft([x.astype(F32) for x in blocks], 2 * n)):
+        cos, sin = twist_ref[m : m + 1], twist_ref[n + 1 + m : n + 2 + m]
+        if m == 0:
+            imag = jnp.zeros_like(real)
+        elif imag is None:
+            real, imag = real * cos, -(real * sin)
+        else:
+            real, imag = real * cos + imag * sin, imag * cos - real * sin
+        mid_ref[m, rows, :length] = real.astype(mid_ref.dtype)
+        mid_ref[m, rows, length:] = imag.astype(mid_ref.dtype)
+
+
+def inverse_blocks(n, back, twist_ref):
+    length = back.shape[1] // 2
+    rows = back.shape[0] // (n + 1)
+    spectrum = []
+    for m in range(n + 1):
+        cos, sin = twist_ref[m : m + 1], twist_ref[n + 1 + m : n + 2 + m]
+        at = slice(m * rows, (m + 1) * rows)
+        real, imag = back[at, :length], back[at, length:]
+        if m == 0:
+            spectrum.append((0.5 * real, None))
+        elif m == n:
+            spectrum.append((0.5 * (real * cos - imag * sin), None))
+        else:
+            spectrum.append((real * cos - imag * sin, real * sin + imag * cos))
+    return [x.astype(BF16) for x in real_dft_transposed(spectrum, 2 * n, True)]
+
+
+def inner_product(values_ref, matrix):
+    count, rows, wide = values_ref.shape
+    values = values_ref[...].reshape(count * rows, wide).astype(BF16)
     return jnp.dot(values, matrix, preferred_element_type=F32)
 
 
-def frequency_groups(n, rows):
-    step = max(1, MATRIX_ROWS // rows)
-    return [(first, min(first + step, n + 1)) for first in range(0, n + 1, step)]
-
-
-def inner_back(n, matrix, prod_ref, spec_ref):
-    rows = prod_ref.shape[1]
-    for first, last in frequency_groups(n, rows):
-        back = inner_product(prod_ref, matrix, first, last)
-        spec_ref[first:last] = back.reshape(last - first, rows, back.shape[1])
+def row_chunks(rows):
+    return max(1, rows // 16)
 
 
 def mix_forward(
@@ -272,31 +207,40 @@
     dft_ref,
     mid_ref,
     prod_ref,
-    spec_ref,
     sems,
 ):
     length = twist_ref.shape[1]
     width = grad_ref.shape[1]
+    chunks = row_chunks(width)
+    step = width // chunks
     (dft_copy,) = started((dft_hbm, dft_ref, sems.at[0]))
-    forward_blocks(n, lambda b, at: pair_ref[b, at], twist_ref, mid_ref)
     both_ref[:, :, length:] = grad_ref[...]
-    dft_copy.wait()
-    for first, last in frequency_groups(n, 2 * width):
-        spec = inner_product(mid_ref, dft_ref[0], first, last)
-        for m in range(first, last):
-            at = (m - first) * 2 * width
-            signal, filt = spec[at : at + width], spec[at + width : at + 2 * width]
-            filt_ref[m] = filt.astype(filt_ref.dtype)
+    for c in range(chunks):
+        at = slice(c * step, (c + 1) * step)
+        for kind in range(2):
+            start = kind * width + c * step
+            blocks = [pair_ref[b, start : start + step] for b in range(n)]
+            forward_blocks(
+                n, blocks, twist_ref, mid_ref.at[c], slice(kind * step, (kind + 1) * step)
+            )
+        if c == 0:
+            dft_copy.wait()
+        spec = inner_product(mid_ref.at[c], dft_ref[0])
+        for m in range(n + 1):
+            first = 2 * m * step
+            signal, filt = spec[first : first + step], spec[first + step : first + 2 * step]
+            filt_ref[m, at] = filt.astype(filt_ref.dtype)
             real, imag = signal[:, :length], signal[:, length:]
             filt_real, filt_imag = filt[:, :length], filt[:, length:]
-            prod_ref[m, :, :length] = (real * filt_real - imag * filt_imag).astype(prod_ref.dtype)
-            prod_ref[m, :, length:] = (real * filt_imag + imag * filt_real).astype(prod_ref.dtype)
-    inner_back(n, dft_ref[1], prod_ref, spec_ref)
-
-    def store(b, at, value):
-        both_ref[b, at, :length] = value
-
-    inverse_blocks(n, twist_ref, spec_ref, store)
+            prod_ref[c, m, :, :length] = (real * filt_real - imag * filt_imag).astype(
+                prod_ref.dtype
+            )
+            prod_ref[c, m, :, length:] = (real * filt_imag + imag * filt_real).astype(
+                prod_ref.dtype
+            )
+        back = inner_product(prod_ref.at[c], dft_ref[1])
+        for b, value in enumerate(inverse_blocks(n, back, twist_ref)):
+            both_ref[b, at, :length] = value
 
 
 def mix_backward(
@@ -312,7 +256,6 @@
     away_hbm,
     mid_ref,
     prod_ref,
-    spec_ref,
     out_ref,
     gated_ref,
     away_ref,
@@ -325,40 +268,33 @@
     gated_ref[...] = gated
     away_ref[...] = jnp.dot(gated, weight_ref[...], preferred_element_type=F32).astype(BF16)
     copies = started((away_ref, away_hbm, sems.at[0]), (gated_ref, gated_hbm, sems.at[1]))
-    forward_blocks(n, lambda b, at: both_ref[b, at, length:], twist_ref, mid_ref)
-    for first, last in frequency_groups(n, width):
-        spec = inner_product(mid_ref, dft_ref[0], first, last)
-        for m in range(first, last):
-            at = (m - first) * width
-            signal, filt = spec[at : at + width], filt_ref[m].astype(F32)
+    chunks = row_chunks(width)
+    step = width // chunks
+    for c in range(chunks):
+        at = slice(c * step, (c + 1) * step)
+        blocks = [both_ref[b, at, length:] for b in range(n)]
+        forward_blocks(n, blocks, twist_ref, mid_ref.at[c], slice(0, step))
+        spec = inner_product(mid_ref.at[c], dft_ref[0])
+        for m in range(n + 1):
+            signal, filt = spec[m * step : (m + 1) * step], filt_ref[m, at].astype(F32)
             real, imag = signal[:, :length], signal[:, length:]
             filt_real, filt_imag = filt[:, :length], filt[:, length:]
-            prod_ref[m, :, :length] = (filt_real * real + filt_imag * imag).astype(prod_ref.dtype)
-            prod_ref[m, :, length:] = (filt_real * imag - filt_imag * real).astype(prod_ref.dtype)
-    inner_back(n, dft_ref[1], prod_ref, spec_ref)
-
-    def store(b, at, value):
-        out_ref[b, at] = value
-
-    def out_copy(index, at):
-        return pltpu.make_async_copy(out_ref.at[:, at], out_hbm.at[:, at], sems.at[2 + index])
-
-    chunks = row_chunks(width)
-    if chunks == 1:
-        inverse_blocks(n, twist_ref, spec_ref, store)
-        copies += started((out_ref, out_hbm, sems.at[2]))
-    else:
-        inverse_blocks(
-            n, twist_ref, spec_ref, store, lambda index, at: out_copy(index, at).start()
-        )
-        step = width // chunks
-        copies += [out_copy(index, pl.ds(index * step, step)) for index in range(chunks)]
+            prod_ref[c, m, :, :length] = (filt_real * real + filt_imag * imag).astype(
+                prod_ref.dtype
+            )
+            prod_ref[c, m, :, length:] = (filt_real * imag - filt_imag * real).astype(
+                prod_ref.dtype
+            )
+        back = inner_product(prod_ref.at[c], dft_ref[1])
+        for b, value in enumerate(inverse_blocks(n, back, twist_ref)):
+            out_ref[b, at] = value
+        if chunks == 1:
+            copies += started((out_ref, out_hbm, sems.at[2]))
+        else:
+            rows = pl.ds(c * step, step)
+            copies += started((out_ref.at[:, rows], out_hbm.at[:, rows], sems.at[2 + c]))
     for copy in copies:
         copy.wait()
-
-
-def row_chunks(rows):
-    return max(1, rows // 16)
 
 
 def channel_rows(blocks_ref, length):
@@ -508,8 +444,8 @@
     inner_flops = 2 * (n + 1) * (2 * length) ** 2 * width
     spec_shape = (n + 1, width, 2 * length)
     narrow = BF16 if width >= 16 else F32
-    spec_scratch = pltpu.VMEM(spec_shape, F32)
-    narrow_scratch = pltpu.VMEM(spec_shape, narrow)
+    chunks = row_chunks(width)
+    narrow_scratch = pltpu.VMEM((chunks, n + 1, width // chunks, 2 * length), narrow)
 
     def by_channels(steps):
         cut, dests = channels // steps, n // steps
@@ -520,23 +456,16 @@
         )
 
     other_grad = swap_tp(out_grad)
-    parts = 4
+    steps = 2
+    flat, _, _ = by_channels(steps)
     pair_out = call(
-        functools.partial(pack_inputs, parts),
+        functools.partial(pack_inputs, n // steps),
         pltpu.HBM(pair, BF16),
         (tokens, pre_gate, features, filters),
-        blocks=["hbm"] * 4,
-        out_blocks=["hbm"],
+        grid=(steps,),
+        blocks=[None, flat, flat, flat],
+        out_blocks=[((n // steps, *pair[1:]), lambda i, *_: (i, 0, 0))],
         from_hbm=range(4),
-        scratch=[
-            pltpu.VMEM(tokens.shape, jnp.int32),
-            pltpu.VMEM((length, channels), BF16),
-            pltpu.VMEM((length, channels), BF16),
-            pltpu.VMEM((length, channels), F32),
-            pltpu.VMEM(pair, BF16),
-            pltpu.SemaphoreType.DMA((4, parts)),
-            pltpu.SemaphoreType.DMA((parts,)),
-        ],
     )
     pair_in = exchange(pair_out)
     steps = 4
@@ -580,9 +509,8 @@
         from_hbm=(3,),
         flops=3 * inner_flops,
         scratch=[
-            pltpu.VMEM((n + 1, 2 * width, 2 * length), BF16),
+            pltpu.VMEM((chunks, n + 1, 2 * width // chunks, 2 * length), BF16),
             narrow_scratch,
-            spec_scratch,
             pltpu.SemaphoreType.DMA((1,)),
         ],
     )
@@ -600,11 +528,10 @@
         scratch=[
             narrow_scratch,
             narrow_scratch,
-            spec_scratch,
             pltpu.VMEM(one, BF16),
             pltpu.VMEM((length, channels), BF16),
             pltpu.VMEM((length, columns), BF16),
-            pltpu.SemaphoreType.DMA((2 + row_chunks(width),)),
+            pltpu.SemaphoreType.DMA((2 + chunks,)),
         ],
     )
     grad_back_in = exchange(grad_back_out)

time: 64.1 us -> 63.7 us (level)
  no operation moved by 1% of the time
where the time goes in v4:
time: 63.7 us; the launch traced here: 63.1 us
  blocking collectives  18.4 us (29%)
  Pallas kernels  16.5 us (26%)
  starting transfers between devices  14.6 us (23%)
  waiting for transfers between devices  8.64 us (14%)
  local copies, waits for them, and re-layouts  4.2 us (7%)
  between operations  0.71 us (1%)
    all_to_all x1, blocking collectives, exchange(): return lax.all_to_all(block, 'ctx', split_axis=0, concat_axis=0, tiled=True)  18.4 us
    pallas_call x7, Pallas kernels, call(): pl.pallas_call(kernel, out_shape=outs, grid_spec=pltpu.PrefetchScalarGrid...  16.5 us
    all_to_all x2, starting transfers between devices, exchange(): return lax.all_to_all(block, 'ctx', split_axis=0, concat_axis=0, tiled=True)  11.5 us
    ppermute x2, waiting for transfers between devices, swap_tp(): return lax.ppermute(block, 'tp', [(0, 1), (1, 0)])  5.81 us
    unnamed x16, local copies, waits for them, and re-layouts  4.2 us
    ppermute x2, starting transfers between devices, swap_tp(): return lax.ppermute(block, 'tp', [(0, 1), (1, 0)])  3.17 us
    all_to_all x2, waiting for transfers between devices, exchange(): return lax.all_to_all(block, 'ctx', split_axis=0, concat_axis=0, tiled=True)  2.82 us
  transfers between devices with their start and end apart: 4, of which 4 were waited for; matrix products, arithmetic and copies ran while one was open for 0% of the time, Pallas kernels for 13%

profile of v4, /device:TPU:0, one launch (start us, length us, event | category | flops | bytes accessed | tf_op | source)
XLA Modules:
  0.0 63.1 jit_solution(1651928933503394427)
XLA Ops:
  0.6 2.1 %shard_map.120 = bf16[16,128,128]{2,1,0:T(8,128)(2,1)} custom-call(s32[1,128]{1,0:T(1,128)} %bitcast.2, bf16[128,1024]{1,0:T(8,128)(2,1)} %pre_ref.3, bf16[128,1024]{1,0:T(8,128)(2,1)} %feat_ref.3, f32[128,1024]{1,0:T(8,128)} %filt_ref.1), custom_call_target="tpu_custom_call" | custom-call | bytes 1573376 | tf_op jit(solution)/shard_map/pallas_call | solution.py:405
  2.7 7.4 %all-to-all-start = ((bf16[16,128,128]{2,1,0:T(8,128)(2,1)}), bf16[16,128,128]{2,1,0:T(8,128)(2,1)S(1)}, u32[]{:S(2)}, u32[]{:S(2)}) async-start(bf16[16,128,128]{2,1,0:T(8,128)(2,1)} %shard_map.120), calls=%async_computation | async-start | bytes 1048576 | tf_op jit(solution)/shard_map/all_to_all | solution.py:421
  10.1 1.6 %collective-permute-start = (bf16[128,1024]{1,0:T(8,128)(2,1)}, bf16[128,1024]{1,0:T(8,128)(2,1)S(1)}, u32[]{:S(2)}, u32[]{:S(2)}) collective-permute-start(bf16[128,1024]{1,0:T(8,128)(2,1)} %own_ref.1), channel_id=1, source_target_pairs={{0,1},{1,0},{2,3},{3,2},{4,5},{5,4},{6,7},{7,6},{8,9},{9,8},{10,11... | collective-permute-start | bytes 786440 | tf_op jit(solution)/shard_map/ppermute | solution.py:427
  11.7 0.0 copy-start.6
  11.7 3.1 %shard_map.121.part_ref = f32[1024,128]{1,0:T(8,128)S(1)} custom-call(s32[1]{0:T(128)} %bitcast.1.rank_ref, bf16[128,1024]{1,0:T(8,128)(2,1)} %own_ref.1, bf16[1024,2048]{1,0:T(8,128)(2,1)} %weight_hbm.1), custom_call_target="tpu_custom_call" | custom-call | flops 268435456 | bytes 4980736 | tf_op jit(solution)/shard_map/pallas_call | solution.py:405
  14.8 0.0 copy-start.3
  14.8 4.1 %collective-permute-done.other_ref = bf16[128,1024]{1,0:T(8,128)(2,1)S(1)} collective-permute-done((bf16[128,1024]{1,0:T(8,128)(2,1)}, bf16[128,1024]{1,0:T(8,128)(2,1)S(1)}, u32[]{:S(2)}, u32[]{:S(2)}) %collective-permute-start) | collective-permute-done | bytes 262176 | tf_op jit(solution)/shard_map/ppermute | solution.py:427
  18.9 4.0 %shard_map.122 = (f32[1024,128]{1,0:T(8,128)}, bf16[16,64,128]{2,1,0:T(8,128)(2,1)S(1)}, bf16[1024,1024]{1,0:T(8,128)(2,1)S(1)}) custom-call(s32[1]{0:T(128)} %bitcast.1.rank_ref, bf16[128,1024]{1,0:T(8,128)(2,1)S(1)} %collective-permute-done.other_ref, bf16[1024,2048]{1,0:T(8,128)(2,1)} %weight_hbm.1, f32[1024,128]{1,0:T(8,128)S(1)} %shard_map.121.part_ref, ...), custom_call_target="tpu_custom_call" | custom-call | flops 268435456 | bytes 8126464 | tf_op jit(solution)/shard_map/pallas_call | solution.py:405
  23.0 1.6 %all-to-all-done.pair_ref = bf16[16,128,128]{2,1,0:T(8,128)(2,1)S(1)} async-done(((bf16[16,128,128]{2,1,0:T(8,128)(2,1)}), bf16[16,128,128]{2,1,0:T(8,128)(2,1)S(1)}, u32[]{:S(2)}, u32[]{:S(2)}) %all-to-all-start) | async-done | bytes 524320 | tf_op jit(solution)/shard_map/all_to_all | solution.py:421
  24.6 0.0 copy-done.6
  24.6 2.6 %shard_map.123 = (bf16[16,64,256]{2,1,0:T(8,128)(2,1)S(1)}, bf16[17,64,256]{2,1,0:T(8,128)(2,1)S(1)}, bf16[2,256,256]{2,1,0:T(8,128)(2,1)S(1)}) custom-call(bf16[16,128,128]{2,1,0:T(8,128)(2,1)S(1)} %all-to-all-done.pair_ref, bf16[16,64,128]{2,1,0:T(8,128)(2,1)S(1)} %get-tuple-element.18.grad_ref, f32[34,128]{1,0:T(8,128)S(1)} %copy-done.6, ...), custom_call_target="tpu_custom_call" | custom-call | flops 427819008 | bytes 2409472 | tf_op jit(solution)/shard_map/pallas_call | solution.py:405
  27.2 18.4 %all_to_all.15.both_ref = bf16[16,64,256]{2,1,0:T(8,128)(2,1)S(1)} all-to-all(bf16[16,64,256]{2,1,0:T(8,128)(2,1)S(1)} %get-tuple-element.19), channel_id=1, replica_groups=mesh['ctx'=16,'tp'=2] {'ctx'}, dimensions={0} | all-to-all | bytes 1048576 | tf_op jit(solution)/shard_map/all_to_all | solution.py:421
  45.6 0.0 copy-done.3
  45.6 0.0 copy-start.1
  45.6 0.0 copy-start.2
  45.6 0.0 copy-start.7
  45.6 2.1 %shard_map.124 = (bf16[16,64,128]{2,1,0:T(8,128)(2,1)}, bf16[128,1024]{1,0:T(8,128)(2,1)}, bf16[128,1024]{1,0:T(8,128)(2,1)}) custom-call(bf16[16,64,256]{2,1,0:T(8,128)(2,1)S(1)} %all_to_all.15.both_ref, bf16[128,1024]{1,0:T(8,128)(2,1)S(1)} %copy-done.3, f32[34,128]{1,0:T(8,128)S(1)} %copy-done.6, bf16[2,256,256]{2,1,0:T(8,128)(2,1)S(1)} %get-tuple-element.20.dft_ref, ...), custom_call_target="tpu_custom_call" | custom-call | flops 553648128 | bytes 4506624 | tf_op jit(solution)/shard_map/pallas_call | solution.py:405
  47.7 4.1 %all-to-all-start.2 = ((bf16[16,64,128]{2,1,0:T(8,128)(2,1)}), bf16[16,64,128]{2,1,0:T(8,128)(2,1)S(1)}, u32[]{:S(2)}, u32[]{:S(2)}) async-start(bf16[16,64,128]{2,1,0:T(8,128)(2,1)} %get-tuple-element.23), calls=%async_computation.2 | async-start | bytes 524288 | tf_op jit(solution)/shard_map/all_to_all | solution.py:421
  51.8 1.6 %collective-permute-start.1 = (bf16[128,1024]{1,0:T(8,128)(2,1)}, bf16[128,1024]{1,0:T(8,128)(2,1)S(1)}, u32[]{:S(2)}, u32[]{:S(2)}) collective-permute-start(bf16[128,1024]{1,0:T(8,128)(2,1)} %get-tuple-element.27), channel_id=1, source_target_pairs={{0,1},{1,0},{2,3},{3,2},{4,5},{5,4},{6,7},{7,6},{8,9},{9,8},{10,11... | collective-permute-start | bytes 786440 | tf_op jit(solution)/shard_map/ppermute | solution.py:427
  53.4 0.0 copy-start
  53.4 2.2 %copy-done = bf16[1024,2048]{1,0:T(8,128)(2,1)S(1)} copy-done((bf16[1024,2048]{1,0:T(8,128)(2,1)S(1)}, bf16[1024,2048]{1,0:T(8,128)(2,1)}, u32[]{:S(2)}) %copy-start) | copy-done | bytes 4194328
  55.6 0.0 copy-start.4
  55.6 1.0 %copy-done.4 = f32[1024,128]{1,0:T(8,128)S(1)} copy-done((f32[1024,128]{1,0:T(8,128)S(1)}, f32[1024,128]{1,0:T(8,128)}, u32[]{:S(2)}) %copy-start.4) | copy-done | bytes 524312
  56.7 0.0 copy-start.5
  56.7 0.9 %copy-done.5 = bf16[128,1024]{1,0:T(8,128)(2,1)S(1)} copy-done((bf16[128,1024]{1,0:T(8,128)(2,1)S(1)}, bf16[128,1024]{1,0:T(8,128)(2,1)}, u32[]{:S(2)}) %copy-start.5) | copy-done | bytes 262168
  57.6 1.4 %shard_map.125 = (f32[128,1024]{1,0:T(8,128)S(1)}, bf16[128,1024]{1,0:T(8,128)(2,1)}) custom-call(s32[1]{0:T(128)} %bitcast.1.rank_ref, bf16[128,1024]{1,0:T(8,128)(2,1)S(1)} %copy-done.5, bf16[16,64,256]{2,1,0:T(8,128)(2,1)S(1)} %all_to_all.15.both_ref, f32[1024,128]{1,0:T(8,128)S(1)} %copy-done.4, bf16[1024,2048]{1,0:T(8,128)(2,1)S(1)} %copy-done), custom_call_target="tpu_custom_call" | custom-call | flops 268435456 | bytes 6291456 | tf_op jit(solution)/shard_map/pallas_call | solution.py:405
  59.0 1.7 %collective-permute-done.1.other_ref = bf16[128,1024]{1,0:T(8,128)(2,1)S(1)} collective-permute-done((bf16[128,1024]{1,0:T(8,128)(2,1)}, bf16[128,1024]{1,0:T(8,128)(2,1)S(1)}, u32[]{:S(2)}, u32[]{:S(2)}) %collective-permute-start.1) | collective-permute-done | bytes 262176 | tf_op jit(solution)/shard_map/ppermute | solution.py:427
  60.7 1.2 %all-to-all-done.2.packed_ref = bf16[16,64,128]{2,1,0:T(8,128)(2,1)S(1)} async-done(((bf16[16,64,128]{2,1,0:T(8,128)(2,1)}), bf16[16,64,128]{2,1,0:T(8,128)(2,1)S(1)}, u32[]{:S(2)}, u32[]{:S(2)}) %all-to-all-start.2) | async-done | bytes 262176 | tf_op jit(solution)/shard_map/all_to_all | solution.py:421
  61.9 0.0 copy-done.1
  61.9 0.0 copy-done.2
  61.9 0.0 copy-done.7
  61.9 1.2 %shard_map.126 = (bf16[128,1024]{1,0:T(8,128)(2,1)}, bf16[128,1024]{1,0:T(8,128)(2,1)}, bf16[128,1024]{1,0:T(8,128)(2,1)}) custom-call(s32[1,128]{1,0:T(1,128)S(1)} %bitcast.3, bf16[16,64,128]{2,1,0:T(8,128)(2,1)S(1)} %all-to-all-done.2.packed_ref, bf16[128,1024]{1,0:T(8,128)(2,1)S(1)} %copy-done.1, bf16[128,1024]{1,0:T(8,128)(2,1)S(1)} %copy-done.2, ...), custom_call_target="tpu_custom_call" | custom-call | bytes 2359808 | tf_op jit(solution)/shard_map/pallas_call | solution.py:405
Async XLA Ops:
  2.7 21.8 %all-to-all-start = ((bf16[16,128,128]{2,1,0:T(8,128)(2,1)}), bf16[16,128,128]{2,1,0:T(8,128)(2,1)S(1)}, u32[]{:S(2)}, u32[]{:S(2)}) async-start(bf16[16,128,128]{2,1,0:T(8,128)(2,1)} %shard_map.120), calls=%async_computation | async-start | bytes 1048576 | tf_op jit(solution)/shard_map/all_to_all | solution.py:421
  10.1 8.8 %collective-permute-start = (bf16[128,1024]{1,0:T(8,128)(2,1)}, bf16[128,1024]{1,0:T(8,128)(2,1)S(1)}, u32[]{:S(2)}, u32[]{:S(2)}) collective-permute-start(bf16[128,1024]{1,0:T(8,128)(2,1)} %own_ref.1), channel_id=1, source_target_pairs={{0,1},{1,0},{2,3},{3,2},{4,5},{5,4},{6,7},{7,6},{8,9},{9,8},{10,11... | collective-permute-start | bytes 786440 | tf_op jit(solution)/shard_map/ppermute | solution.py:427
  11.7 12.9 %copy-start.6 = (f32[34,128]{1,0:T(8,128)S(1)}, f32[34,128]{1,0:T(8,128)}, u32[]{:S(2)}) copy-start(f32[34,128]{1,0:T(8,128)} %constant.9.clone.twist_ref) | copy-start | bytes 52228
  14.8 30.8 %copy-start.3 = (bf16[128,1024]{1,0:T(8,128)(2,1)S(1)}, bf16[128,1024]{1,0:T(8,128)(2,1)}, u32[]{:S(2)}) copy-start(bf16[128,1024]{1,0:T(8,128)(2,1)} %post_ref.3) | copy-start | bytes 786436
  45.6 16.3 %copy-start.1 = (bf16[128,1024]{1,0:T(8,128)(2,1)S(1)}, bf16[128,1024]{1,0:T(8,128)(2,1)}, u32[]{:S(2)}) copy-start(bf16[128,1024]{1,0:T(8,128)(2,1)} %pre_ref.3) | copy-start | bytes 786436
  45.6 16.3 %copy-start.2 = (bf16[128,1024]{1,0:T(8,128)(2,1)S(1)}, bf16[128,1024]{1,0:T(8,128)(2,1)}, u32[]{:S(2)}) copy-start(bf16[128,1024]{1,0:T(8,128)(2,1)} %feat_ref.3) | copy-start | bytes 786436
  45.6 16.3 %copy-start.7 = (s32[128]{0:T(128)S(1)}, s32[128]{0:T(128)}, u32[]{:S(2)}) copy-start(s32[128]{0:T(128)} %param.13) | copy-start | bytes 1540
  47.7 14.2 %all-to-all-start.2 = ((bf16[16,64,128]{2,1,0:T(8,128)(2,1)}), bf16[16,64,128]{2,1,0:T(8,128)(2,1)S(1)}, u32[]{:S(2)}, u32[]{:S(2)}) async-start(bf16[16,64,128]{2,1,0:T(8,128)(2,1)} %get-tuple-element.23), calls=%async_computation.2 | async-start | bytes 524288 | tf_op jit(solution)/shard_map/all_to_all | solution.py:421
  51.8 8.8 %collective-permute-start.1 = (bf16[128,1024]{1,0:T(8,128)(2,1)}, bf16[128,1024]{1,0:T(8,128)(2,1)S(1)}, u32[]{:S(2)}, u32[]{:S(2)}) collective-permute-start(bf16[128,1024]{1,0:T(8,128)(2,1)} %get-tuple-element.27), channel_id=1, source_target_pairs={{0,1},{1,0},{2,3},{3,2},{4,5},{5,4},{6,7},{7,6},{8,9},{9,8},{10,11... | collective-permute-start | bytes 786440 | tf_op jit(solution)/shard_map/ppermute | solution.py:427
  53.4 2.2 %copy-start = (bf16[1024,2048]{1,0:T(8,128)(2,1)S(1)}, bf16[1024,2048]{1,0:T(8,128)(2,1)}, u32[]{:S(2)}) copy-start(bf16[1024,2048]{1,0:T(8,128)(2,1)} %weight_hbm.1) | copy-start | bytes 12582916
  55.6 1.0 %copy-start.4 = (f32[1024,128]{1,0:T(8,128)S(1)}, f32[1024,128]{1,0:T(8,128)}, u32[]{:S(2)}) copy-start(f32[1024,128]{1,0:T(8,128)} %get-tuple-element.25.grad_ref) | copy-start | bytes 1572868
  56.7 0.9 %copy-start.5 = (bf16[128,1024]{1,0:T(8,128)(2,1)S(1)}, bf16[128,1024]{1,0:T(8,128)(2,1)}, u32[]{:S(2)}) copy-start(bf16[128,1024]{1,0:T(8,128)(2,1)} %get-tuple-element.24.gated_ref) | copy-start | bytes 786436

commit v5 on v4

--- a/solution.py
+++ b/solution.py
@@ -136,11 +136,22 @@
 
 
 def pack_grad(
-    dests, rank_ref, other_ref, weight_ref, part_ref, post_ref, gated_ref, out_ref, away_ref
+    dests,
+    rank_ref,
+    other_ref,
+    weight_ref,
+    part_ref,
+    post_ref,
+    dft_ref,
+    gated_ref,
+    out_ref,
+    away_ref,
+    kept_dft_ref,
 ):
     width = out_ref.shape[1]
     weight = weight_ref[...]
     away_ref[...] = weight
+    kept_dft_ref[...] = dft_ref[...]
     grad_gated = part_ref[...] + times_transposed(weight, other_ref[...])
     gated_ref[...] = grad_gated
     mixed = grad_gated * post_ref[...].T.astype(F32)
@@ -201,19 +212,16 @@
     pair_ref,
     grad_ref,
     twist_ref,
-    dft_hbm,
+    dft_ref,
     both_ref,
     filt_ref,
-    dft_ref,
     mid_ref,
     prod_ref,
-    sems,
 ):
     length = twist_ref.shape[1]
     width = grad_ref.shape[1]
     chunks = row_chunks(width)
     step = width // chunks
-    (dft_copy,) = started((dft_hbm, dft_ref, sems.at[0]))
     both_ref[:, :, length:] = grad_ref[...]
     for c in range(chunks):
         at = slice(c * step, (c + 1) * step)
@@ -223,8 +231,6 @@
             forward_blocks(
                 n, blocks, twist_ref, mid_ref.at[c], slice(kind * step, (kind + 1) * step)
             )
-        if c == 0:
-            dft_copy.wait()
         spec = inner_product(mid_ref.at[c], dft_ref[0])
         for m in range(n + 1):
             first = 2 * m * step
@@ -482,36 +488,33 @@
         prefetch=1,
         from_hbm=(1, 2),
     )
-    grad_gated, grad_out, away_weight = call(
+    grad_gated, grad_out, away_weight, kept_dft = call(
         functools.partial(pack_grad, n // steps),
         (
             pltpu.HBM((channels, length), F32),
             pltpu.VMEM(one, BF16),
             pltpu.VMEM((channels, columns), BF16),
+            pltpu.VMEM(dft.shape, BF16),
         ),
-        (rank, other_grad, out_weight, grad_part, post_gate),
+        (rank, other_grad, out_weight, grad_part, post_gate, dft),
         grid=(steps,),
-        blocks=[None, (weight_block, lambda i, rank: (i, 1 - rank[0])), turned, flat],
-        out_blocks=[turned, packed, (weight_block, lambda i, *_: (i, 0))],
+        blocks=[None, (weight_block, lambda i, rank: (i, 1 - rank[0])), turned, flat, None],
+        out_blocks=[turned, packed, (weight_block, lambda i, *_: (i, 0)), None],
         flops=2 * length * channels * columns,
         prefetch=1,
-        from_hbm=(2, 4),
-    )
-    both_out, filt_spec, kept_dft = call(
+        from_hbm=(2, 4, 5),
+    )
+    both_out, filt_spec = call(
         functools.partial(mix_forward, n),
         (
             shape(both, BF16),
             pltpu.VMEM(spec_shape, narrow),
-            pltpu.VMEM(dft.shape, BF16),
         ),
-        (pair_in, grad_out, twist, dft),
-        blocks=[None, None, None, "hbm"],
-        from_hbm=(3,),
+        (pair_in, grad_out, twist, kept_dft),
         flops=3 * inner_flops,
         scratch=[
             pltpu.VMEM((chunks, n + 1, 2 * width // chunks, 2 * length), BF16),
             narrow_scratch,
-            pltpu.SemaphoreType.DMA((1,)),
         ],
     )
     both_in = exchange(both_out)

time: 63.7 us -> 65.7 us (1.031)
  local copies, waits for them, and re-layouts: 4.2 us -> 6.81 us
  blocking collectives: 18.4 us -> 19.3 us
  Pallas kernels: 16.5 us -> 15.6 us
  waiting for transfers between devices: 8.64 us -> 7.91 us
    unnamed x16 -> x24, local copies, waits for them, and re-layouts: 4.2 us -> 6.81 us
    all_to_all x1, blocking collectives: 18.4 us -> 19.3 us  [exchange(): return lax.all_to_all(block, 'ctx', split_axis=0, concat_axis=0, tiled=True)]
    all_to_all x2, waiting for transfers between devices: 2.82 us -> 1.98 us  [exchange(): return lax.all_to_all(block, 'ctx', split_axis=0, concat_axis=0, tiled=True)]
    pallas_call x7, Pallas kernels: 16.5 us -> 15.6 us  [call(): pl.pallas_call(kernel, out_shape=outs, grid_spec=pltpu.PrefetchScalarGrid...]
where the time goes in v5:
time: 65.7 us; the launch traced here: 65 us
  blocking collectives  19.3 us (29%)
  Pallas kernels  15.6 us (24%)
  starting transfers between devices  14.6 us (22%)
  waiting for transfers between devices  7.91 us (12%)
  local copies, waits for them, and re-layouts  6.81 us (10%)
  between operations  0.71 us (1%)
    all_to_all x1, blocking collectives, exchange(): return lax.all_to_all(block, 'ctx', split_axis=0, concat_axis=0, tiled=True)  19.3 us
    pallas_call x7, Pallas kernels, call(): pl.pallas_call(kernel, out_shape=outs, grid_spec=pltpu.PrefetchScalarGrid...  15.6 us
    all_to_all x2, starting transfers between devices, exchange(): return lax.all_to_all(block, 'ctx', split_axis=0, concat_axis=0, tiled=True)  11.5 us
    unnamed x24, local copies, waits for them, and re-layouts  6.81 us
    ppermute x2, waiting for transfers between devices, swap_tp(): return lax.ppermute(block, 'tp', [(0, 1), (1, 0)])  5.93 us
    ppermute x2, starting transfers between devices, swap_tp(): return lax.ppermute(block, 'tp', [(0, 1), (1, 0)])  3.15 us
    all_to_all x2, waiting for transfers between devices, exchange(): return lax.all_to_all(block, 'ctx', split_axis=0, concat_axis=0, tiled=True)  1.98 us
  transfers between devices with their start and end apart: 4, of which 4 were waited for; matrix products, arithmetic and copies ran while one was open for 0% of the time, Pallas kernels for 13%

profile of v5, /device:TPU:0, one launch (start us, length us, event | category | flops | bytes accessed | tf_op | source)
XLA Modules:
  0.0 65.0 jit_solution(14151590415265780858)
XLA Ops:
  0.6 2.1 %shard_map.120 = bf16[16,128,128]{2,1,0:T(8,128)(2,1)} custom-call(s32[1,128]{1,0:T(1,128)} %bitcast.2, bf16[128,1024]{1,0:T(8,128)(2,1)} %pre_ref.3, bf16[128,1024]{1,0:T(8,128)(2,1)} %feat_ref.3, f32[128,1024]{1,0:T(8,128)} %filt_ref.1), custom_call_target="tpu_custom_call" | custom-call | bytes 1573376 | tf_op jit(solution)/shard_map/pallas_call | solution.py:411
  2.7 7.4 %all-to-all-start = ((bf16[16,128,128]{2,1,0:T(8,128)(2,1)}), bf16[16,128,128]{2,1,0:T(8,128)(2,1)S(1)}, u32[]{:S(2)}, u32[]{:S(2)}) async-start(bf16[16,128,128]{2,1,0:T(8,128)(2,1)} %shard_map.120), calls=%async_computation | async-start | bytes 1048576 | tf_op jit(solution)/shard_map/all_to_all | solution.py:427
  10.1 1.6 %collective-permute-start = (bf16[128,1024]{1,0:T(8,128)(2,1)}, bf16[128,1024]{1,0:T(8,128)(2,1)S(1)}, u32[]{:S(2)}, u32[]{:S(2)}) collective-permute-start(bf16[128,1024]{1,0:T(8,128)(2,1)} %own_ref.1), channel_id=1, source_target_pairs={{0,1},{1,0},{2,3},{3,2},{4,5},{5,4},{6,7},{7,6},{8,9},{9,8},{10,11... | collective-permute-start | bytes 786440 | tf_op jit(solution)/shard_map/ppermute | solution.py:433
  11.7 0.0 copy-start.8
  11.7 3.1 %shard_map.121.part_ref = f32[1024,128]{1,0:T(8,128)S(1)} custom-call(s32[1]{0:T(128)} %bitcast.1.rank_ref, bf16[128,1024]{1,0:T(8,128)(2,1)} %own_ref.1, bf16[1024,2048]{1,0:T(8,128)(2,1)} %weight_hbm.1), custom_call_target="tpu_custom_call" | custom-call | flops 268435456 | bytes 4980736 | tf_op jit(solution)/shard_map/pallas_call | solution.py:411
  14.8 0.0 copy-start.1
  14.8 4.1 %collective-permute-done.other_ref = bf16[128,1024]{1,0:T(8,128)(2,1)S(1)} collective-permute-done((bf16[128,1024]{1,0:T(8,128)(2,1)}, bf16[128,1024]{1,0:T(8,128)(2,1)S(1)}, u32[]{:S(2)}, u32[]{:S(2)}) %collective-permute-start) | collective-permute-done | bytes 262176 | tf_op jit(solution)/shard_map/ppermute | solution.py:433
  18.9 4.2 %shard_map.122 = (f32[1024,128]{1,0:T(8,128)}, bf16[16,64,128]{2,1,0:T(8,128)(2,1)S(1)}, bf16[1024,1024]{1,0:T(8,128)(2,1)S(1)}, bf16[2,256,256]{2,1,0:T(8,128)(2,1)S(1)}) custom-call(s32[1]{0:T(128)} %bitcast.1.rank_ref, bf16[128,1024]{1,0:T(8,128)(2,1)S(1)} %collective-permute-done.other_ref, bf16[1024,2048]{1,0:T(8,128)(2,1)} %weight_hbm.1, ...), custom_call_target="tpu_custom_call" | custom-call | flops 268435456 | bytes 8650752 | tf_op jit(solution)/shard_map/pallas_call | solution.py:411
  23.1 0.0 copy-start.10
  23.1 0.7 %copy-done.10 = bf16[16,64,128]{2,1,0:T(8,128)(2,1)} copy-done((bf16[16,64,128]{2,1,0:T(8,128)(2,1)}, bf16[16,64,128]{2,1,0:T(8,128)(2,1)S(1)}, u32[]{:S(2)}) %copy-start.10) | copy-done | bytes 262168
  23.8 0.0 copy-start.5
  23.8 0.8 %all-to-all-done.pair_ref = bf16[16,128,128]{2,1,0:T(8,128)(2,1)S(1)} async-done(((bf16[16,128,128]{2,1,0:T(8,128)(2,1)}), bf16[16,128,128]{2,1,0:T(8,128)(2,1)S(1)}, u32[]{:S(2)}, u32[]{:S(2)}) %all-to-all-start) | async-done | bytes 524320 | tf_op jit(solution)/shard_map/all_to_all | solution.py:427
  24.6 0.0 copy-done.8
  24.6 0.9 %copy-done.11 = bf16[16,64,128]{2,1,0:T(8,128)(2,1)S(1)} copy-done((bf16[16,64,128]{2,1,0:T(8,128)(2,1)S(1)}, bf16[16,64,128]{2,1,0:T(8,128)(2,1)}, u32[]{:S(2)}) %copy-start.11) | copy-done | bytes 262168
  25.5 1.8 %shard_map.123 = (bf16[16,64,256]{2,1,0:T(8,128)(2,1)S(1)}, bf16[17,64,256]{2,1,0:T(8,128)(2,1)S(1)}) custom-call(bf16[16,128,128]{2,1,0:T(8,128)(2,1)S(1)} %all-to-all-done.pair_ref, bf16[16,64,128]{2,1,0:T(8,128)(2,1)S(1)} %copy-done.11, f32[34,128]{1,0:T(8,128)S(1)} %copy-done.8, bf16[2,256,256]{2,1,0:T(8,128)(2,1)S(1)} %get-tuple-element.19.dft_ref), custom_call_target="tpu_custom_call" | custom-call | flops 427819008 | bytes 2147328 | tf_op jit(solution)/shard_map/pallas_call | solution.py:411
  27.3 19.3 %all_to_all.15.both_ref = bf16[16,64,256]{2,1,0:T(8,128)(2,1)S(1)} all-to-all(bf16[16,64,256]{2,1,0:T(8,128)(2,1)S(1)} %get-tuple-element.20), channel_id=1, replica_groups=mesh['ctx'=16,'tp'=2] {'ctx'}, dimensions={0} | all-to-all | bytes 1048576 | tf_op jit(solution)/shard_map/all_to_all | solution.py:427
  46.6 0.0 copy-done.5
  46.6 0.0 copy-done.1
  46.7 0.9 %copy-done.6 = bf16[2,256,256]{2,1,0:T(8,128)(2,1)S(1)} copy-done((bf16[2,256,256]{2,1,0:T(8,128)(2,1)S(1)}, bf16[2,256,256]{2,1,0:T(8,128)(2,1)}, u32[]{:S(2)}) %copy-start.6) | copy-done | bytes 262168
  47.6 2.1 %shard_map.124 = (bf16[16,64,128]{2,1,0:T(8,128)(2,1)}, bf16[128,1024]{1,0:T(8,128)(2,1)}, bf16[128,1024]{1,0:T(8,128)(2,1)}) custom-call(bf16[16,64,256]{2,1,0:T(8,128)(2,1)S(1)} %all_to_all.15.both_ref, bf16[128,1024]{1,0:T(8,128)(2,1)S(1)} %copy-done.1, f32[34,128]{1,0:T(8,128)S(1)} %copy-done.8, bf16[2,256,256]{2,1,0:T(8,128)(2,1)S(1)} %copy-done.6, ...), custom_call_target="tpu_custom_call" | custom-call | flops 553648128 | bytes 4506624 | tf_op jit(solution)/shard_map/pallas_call | solution.py:411
  49.7 4.1 %all-to-all-start.2 = ((bf16[16,64,128]{2,1,0:T(8,128)(2,1)}), bf16[16,64,128]{2,1,0:T(8,128)(2,1)S(1)}, u32[]{:S(2)}, u32[]{:S(2)}) async-start(bf16[16,64,128]{2,1,0:T(8,128)(2,1)} %get-tuple-element.23), calls=%async_computation.2 | async-start | bytes 524288 | tf_op jit(solution)/shard_map/all_to_all | solution.py:427
  53.8 1.6 %collective-permute-start.1 = (bf16[128,1024]{1,0:T(8,128)(2,1)}, bf16[128,1024]{1,0:T(8,128)(2,1)S(1)}, u32[]{:S(2)}, u32[]{:S(2)}) collective-permute-start(bf16[128,1024]{1,0:T(8,128)(2,1)} %get-tuple-element.27), channel_id=1, source_target_pairs={{0,1},{1,0},{2,3},{3,2},{4,5},{5,4},{6,7},{7,6},{8,9},{9,8},{10,11... | collective-permute-start | bytes 786440 | tf_op jit(solution)/shard_map/ppermute | solution.py:433
  55.4 2.2 %copy-done = bf16[1024,2048]{1,0:T(8,128)(2,1)S(1)} copy-done((bf16[1024,2048]{1,0:T(8,128)(2,1)S(1)}, bf16[1024,2048]{1,0:T(8,128)(2,1)}, u32[]{:S(2)}) %copy-start) | copy-done | bytes 4194328
  57.6 1.0 %copy-done.4 = f32[1024,128]{1,0:T(8,128)S(1)} copy-done((f32[1024,128]{1,0:T(8,128)S(1)}, f32[1024,128]{1,0:T(8,128)}, u32[]{:S(2)}) %copy-start.4) | copy-done | bytes 524312
  58.6 0.9 %copy-done.7 = bf16[128,1024]{1,0:T(8,128)(2,1)S(1)} copy-done((bf16[128,1024]{1,0:T(8,128)(2,1)S(1)}, bf16[128,1024]{1,0:T(8,128)(2,1)}, u32[]{:S(2)}) %copy-start.7) | copy-done | bytes 262168
  59.6 1.2 %shard_map.125 = (f32[128,1024]{1,0:T(8,128)S(1)}, bf16[128,1024]{1,0:T(8,128)(2,1)}) custom-call(s32[1]{0:T(128)} %bitcast.1.rank_ref, bf16[128,1024]{1,0:T(8,128)(2,1)S(1)} %copy-done.7, bf16[16,64,256]{2,1,0:T(8,128)(2,1)S(1)} %all_to_all.15.both_ref, f32[1024,128]{1,0:T(8,128)S(1)} %copy-done.4, bf16[1024,2048]{1,0:T(8,128)(2,1)S(1)} %copy-done), custom_call_target="tpu_custom_call" | custom-call | flops 268435456 | bytes 6291456 | tf_op jit(solution)/shard_map/pallas_call | solution.py:411
  60.8 1.8 %collective-permute-done.1.other_ref = bf16[128,1024]{1,0:T(8,128)(2,1)S(1)} collective-permute-done((bf16[128,1024]{1,0:T(8,128)(2,1)}, bf16[128,1024]{1,0:T(8,128)(2,1)S(1)}, u32[]{:S(2)}, u32[]{:S(2)}) %collective-permute-start.1) | collective-permute-done | bytes 262176 | tf_op jit(solution)/shard_map/ppermute | solution.py:433
  62.7 1.2 %all-to-all-done.2.packed_ref = bf16[16,64,128]{2,1,0:T(8,128)(2,1)S(1)} async-done(((bf16[16,64,128]{2,1,0:T(8,128)(2,1)}), bf16[16,64,128]{2,1,0:T(8,128)(2,1)S(1)}, u32[]{:S(2)}, u32[]{:S(2)}) %all-to-all-start.2) | async-done | bytes 262176 | tf_op jit(solution)/shard_map/all_to_all | solution.py:427
  63.9 0.0 copy-done.2
  63.9 0.0 copy-done.3
  63.9 0.0 copy-done.9
  63.9 1.2 %shard_map.126 = (bf16[128,1024]{1,0:T(8,128)(2,1)}, bf16[128,1024]{1,0:T(8,128)(2,1)}, bf16[128,1024]{1,0:T(8,128)(2,1)}) custom-call(s32[1,128]{1,0:T(1,128)S(1)} %bitcast.3, bf16[16,64,128]{2,1,0:T(8,128)(2,1)S(1)} %all-to-all-done.2.packed_ref, bf16[128,1024]{1,0:T(8,128)(2,1)S(1)} %copy-done.2, bf16[128,1024]{1,0:T(8,128)(2,1)S(1)} %copy-done.3, ...), custom_call_target="tpu_custom_call" | custom-call | bytes 2359808 | tf_op jit(solution)/shard_map/pallas_call | solution.py:411
  (8 shorter events, 0.0 us)
Async XLA Ops:
  2.7 21.8 %all-to-all-start = ((bf16[16,128,128]{2,1,0:T(8,128)(2,1)}), bf16[16,128,128]{2,1,0:T(8,128)(2,1)S(1)}, u32[]{:S(2)}, u32[]{:S(2)}) async-start(bf16[16,128,128]{2,1,0:T(8,128)(2,1)} %shard_map.120), calls=%async_computation | async-start | bytes 1048576 | tf_op jit(solution)/shard_map/all_to_all | solution.py:427
  10.1 8.8 %collective-permute-start = (bf16[128,1024]{1,0:T(8,128)(2,1)}, bf16[128,1024]{1,0:T(8,128)(2,1)S(1)}, u32[]{:S(2)}, u32[]{:S(2)}) collective-permute-start(bf16[128,1024]{1,0:T(8,128)(2,1)} %own_ref.1), channel_id=1, source_target_pairs={{0,1},{1,0},{2,3},{3,2},{4,5},{5,4},{6,7},{7,6},{8,9},{9,8},{10,11... | collective-permute-start | bytes 786440 | tf_op jit(solution)/shard_map/ppermute | solution.py:433
  11.7 12.9 %copy-start.8 = (f32[34,128]{1,0:T(8,128)S(1)}, f32[34,128]{1,0:T(8,128)}, u32[]{:S(2)}) copy-start(f32[34,128]{1,0:T(8,128)} %constant.9.clone.twist_ref) | copy-start | bytes 52228
  14.8 31.8 %copy-start.1 = (bf16[128,1024]{1,0:T(8,128)(2,1)S(1)}, bf16[128,1024]{1,0:T(8,128)(2,1)}, u32[]{:S(2)}) copy-start(bf16[128,1024]{1,0:T(8,128)(2,1)} %post_ref.3) | copy-start | bytes 786436
  23.1 0.7 %copy-start.10 = (bf16[16,64,128]{2,1,0:T(8,128)(2,1)}, bf16[16,64,128]{2,1,0:T(8,128)(2,1)S(1)}, u32[]{:S(2)}) copy-start(bf16[16,64,128]{2,1,0:T(8,128)(2,1)S(1)} %get-tuple-element.18.grad_ref) | copy-start | bytes 786436
  23.8 22.8 %copy-start.5 = (bf16[2,256,256]{2,1,0:T(8,128)(2,1)}, bf16[2,256,256]{2,1,0:T(8,128)(2,1)S(1)}, u32[]{:S(2)}) copy-start(bf16[2,256,256]{2,1,0:T(8,128)(2,1)S(1)} %get-tuple-element.19.dft_ref) | copy-start | bytes 786436
  24.6 1.0 %copy-start.11 = (bf16[16,64,128]{2,1,0:T(8,128)(2,1)S(1)}, bf16[16,64,128]{2,1,0:T(8,128)(2,1)}, u32[]{:S(2)}) copy-start(bf16[16,64,128]{2,1,0:T(8,128)(2,1)} %copy-done.10) | copy-start | bytes 786436
  46.6 1.0 %copy-start.6 = (bf16[2,256,256]{2,1,0:T(8,128)(2,1)S(1)}, bf16[2,256,256]{2,1,0:T(8,128)(2,1)}, u32[]{:S(2)}) copy-start(bf16[2,256,256]{2,1,0:T(8,128)(2,1)} %copy-done.5) | copy-start | bytes 786436
  47.6 16.3 %copy-start.2 = (bf16[128,1024]{1,0:T(8,128)(2,1)S(1)}, bf16[128,1024]{1,0:T(8,128)(2,1)}, u32[]{:S(2)}) copy-start(bf16[128,1024]{1,0:T(8,128)(2,1)} %pre_ref.3) | copy-start | bytes 786436
  47.6 16.3 %copy-start.3 = (bf16[128,1024]{1,0:T(8,128)(2,1)S(1)}, bf16[128,1024]{1,0:T(8,128)(2,1)}, u32[]{:S(2)}) copy-start(bf16[128,1024]{1,0:T(8,128)(2,1)} %feat_ref.3) | copy-start | bytes 786436
  47.6 16.3 %copy-start.9 = (s32[128]{0:T(128)S(1)}, s32[128]{0:T(128)}, u32[]{:S(2)}) copy-start(s32[128]{0:T(128)} %param.13) | copy-start | bytes 1540
  49.7 14.2 %all-to-all-start.2 = ((bf16[16,64,128]{2,1,0:T(8,128)(2,1)}), bf16[16,64,128]{2,1,0:T(8,128)(2,1)S(1)}, u32[]{:S(2)}, u32[]{:S(2)}) async-start(bf16[16,64,128]{2,1,0:T(8,128)(2,1)} %get-tuple-element.23), calls=%async_computation.2 | async-start | bytes 524288 | tf_op jit(solution)/shard_map/all_to_all | solution.py:427
  53.8 8.8 %collective-permute-start.1 = (bf16[128,1024]{1,0:T(8,128)(2,1)}, bf16[128,1024]{1,0:T(8,128)(2,1)S(1)}, u32[]{:S(2)}, u32[]{:S(2)}) collective-permute-start(bf16[128,1024]{1,0:T(8,128)(2,1)} %get-tuple-element.27), channel_id=1, source_target_pairs={{0,1},{1,0},{2,3},{3,2},{4,5},{5,4},{6,7},{7,6},{8,9},{9,8},{10,11... | collective-permute-start | bytes 786440 | tf_op jit(solution)/shard_map/ppermute | solution.py:433
  55.4 2.2 %copy-start = (bf16[1024,2048]{1,0:T(8,128)(2,1)S(1)}, bf16[1024,2048]{1,0:T(8,128)(2,1)}, u32[]{:S(2)}) copy-start(bf16[1024,2048]{1,0:T(8,128)(2,1)} %weight_hbm.1) | copy-start | bytes 12582916
  57.6 1.0 %copy-start.4 = (f32[1024,128]{1,0:T(8,128)S(1)}, f32[1024,128]{1,0:T(8,128)}, u32[]{:S(2)}) copy-start(f32[1024,128]{1,0:T(8,128)} %get-tuple-element.25.grad_ref) | copy-start | bytes 1572868
  58.6 0.9 %copy-start.7 = (bf16[128,1024]{1,0:T(8,128)(2,1)S(1)}, bf16[128,1024]{1,0:T(8,128)(2,1)}, u32[]{:S(2)}) copy-start(bf16[128,1024]{1,0:T(8,128)(2,1)} %get-tuple-element.24.gated_ref) | copy-start | bytes 786436

commit v6 on v4

--- a/solution.py
+++ b/solution.py
@@ -192,6 +192,19 @@
     return jnp.dot(values, matrix, preferred_element_type=F32)
 
 
+def dft_matrices(dft_ref, points):
+    length = dft_ref.shape[0]
+    cos, sin = dft_ref[:, :length], dft_ref[:, length:]
+    forward = jnp.concatenate(
+        [jnp.concatenate([cos, -sin], axis=1), jnp.concatenate([sin, cos], axis=1)], axis=0
+    )
+    cos, sin = cos * (1.0 / points), sin * (1.0 / points)
+    back = jnp.concatenate(
+        [jnp.concatenate([cos, sin], axis=1), jnp.concatenate([-sin, cos], axis=1)], axis=0
+    )
+    return forward, back
+
+
 def row_chunks(rows):
     return max(1, rows // 16)
 
@@ -201,19 +214,17 @@
     pair_ref,
     grad_ref,
     twist_ref,
-    dft_hbm,
+    dft_ref,
     both_ref,
     filt_ref,
-    dft_ref,
     mid_ref,
     prod_ref,
-    sems,
 ):
     length = twist_ref.shape[1]
     width = grad_ref.shape[1]
     chunks = row_chunks(width)
     step = width // chunks
-    (dft_copy,) = started((dft_hbm, dft_ref, sems.at[0]))
+    forward, back = dft_matrices(dft_ref, n * length)
     both_ref[:, :, length:] = grad_ref[...]
     for c in range(chunks):
         at = slice(c * step, (c + 1) * step)
@@ -223,9 +234,7 @@
             forward_blocks(
                 n, blocks, twist_ref, mid_ref.at[c], slice(kind * step, (kind + 1) * step)
             )
-        if c == 0:
-            dft_copy.wait()
-        spec = inner_product(mid_ref.at[c], dft_ref[0])
+        spec = inner_product(mid_ref.at[c], forward)
         for m in range(n + 1):
             first = 2 * m * step
             signal, filt = spec[first : first + step], spec[first + step : first + 2 * step]
@@ -238,8 +247,8 @@
             prod_ref[c, m, :, length:] = (real * filt_imag + imag * filt_real).astype(
                 prod_ref.dtype
             )
-        back = inner_product(prod_ref.at[c], dft_ref[1])
-        for b, value in enumerate(inverse_blocks(n, back, twist_ref)):
+        mid = inner_product(prod_ref.at[c], back)
+        for b, value in enumerate(inverse_blocks(n, mid, twist_ref)):
             both_ref[b, at, :length] = value
 
 
@@ -263,6 +272,7 @@
 ):
     length = twist_ref.shape[1]
     width = out_ref.shape[1]
+    forward, back = dft_matrices(dft_ref, n * length)
     mixed = channel_rows(both_ref, length).T.astype(F32)
     gated = (post_ref[...].astype(F32) * mixed).astype(BF16)
     gated_ref[...] = gated
@@ -274,7 +284,7 @@
         at = slice(c * step, (c + 1) * step)
         blocks = [both_ref[b, at, length:] for b in range(n)]
         forward_blocks(n, blocks, twist_ref, mid_ref.at[c], slice(0, step))
-        spec = inner_product(mid_ref.at[c], dft_ref[0])
+        spec = inner_product(mid_ref.at[c], forward)
         for m in range(n + 1):
             signal, filt = spec[m * step : (m + 1) * step], filt_ref[m, at].astype(F32)
             real, imag = signal[:, :length], signal[:, length:]
@@ -285,8 +295,8 @@
             prod_ref[c, m, :, length:] = (filt_real * imag - filt_imag * real).astype(
                 prod_ref.dtype
             )
-        back = inner_product(prod_ref.at[c], dft_ref[1])
-        for b, value in enumerate(inverse_blocks(n, back, twist_ref)):
+        mid = inner_product(prod_ref.at[c], back)
+        for b, value in enumerate(inverse_blocks(n, mid, twist_ref)):
             out_ref[b, at] = value
         if chunks == 1:
             copies += started((out_ref, out_hbm, sems.at[2]))
@@ -371,9 +381,7 @@
 def dft_tables(n, length):
     index = np.arange(length)
     angle = index[:, None] * index[None, :] % length * (2.0 * math.pi / length)
-    cos, sin = np.cos(angle), np.sin(angle)
-    matrix = np.block([[cos, -sin], [sin, cos]])
-    dft = np.stack([matrix, matrix.T / (n * length)]).astype(jnp.bfloat16)
+    dft = np.concatenate([np.cos(angle), np.sin(angle)], axis=1).astype(jnp.bfloat16)
     angle = np.arange(n + 1)[:, None] * index[None, :] * (math.pi / (n * length))
     twist = np.concatenate([np.cos(angle), np.sin(angle)], axis=0).astype(np.float32)
     return twist, dft
@@ -497,21 +505,17 @@
         prefetch=1,
         from_hbm=(2, 4),
     )
-    both_out, filt_spec, kept_dft = call(
+    both_out, filt_spec = call(
         functools.partial(mix_forward, n),
         (
             shape(both, BF16),
             pltpu.VMEM(spec_shape, narrow),
-            pltpu.VMEM(dft.shape, BF16),
         ),
         (pair_in, grad_out, twist, dft),
-        blocks=[None, None, None, "hbm"],
-        from_hbm=(3,),
         flops=3 * inner_flops,
         scratch=[
             pltpu.VMEM((chunks, n + 1, 2 * width // chunks, 2 * length), BF16),
             narrow_scratch,
-            pltpu.SemaphoreType.DMA((1,)),
         ],
     )
     both_in = exchange(both_out)
@@ -522,7 +526,7 @@
             pltpu.HBM((length, channels), BF16),
             pltpu.HBM((length, columns), BF16),
         ),
-        (both_in, post_gate, twist, kept_dft, filt_spec, away_weight),
+        (both_in, post_gate, twist, dft, filt_spec, away_weight),
         out_blocks=["hbm", "hbm", "hbm"],
         flops=2 * inner_flops + 2 * length * channels * columns,
         scratch=[

time: 63.7 us -> 62.9 us (0.987)
  Pallas kernels: 16.5 us -> 15.7 us
    pallas_call x7, Pallas kernels: 16.5 us -> 15.7 us  [call(): pl.pallas_call(kernel, out_shape=outs, grid_spec=pltpu.PrefetchScalarGrid...]
    unnamed x16 -> x18, local copies, waits for them, and re-layouts: 4.2 us -> 4.2 us
  transfers between devices with their start and end apart: 4 -> 4, of which waited for: 4 -> 4; matrix products, arithmetic and copies ran while one was open for 0% -> 0% of each run, Pallas kernels for 13% -> 14%
where the time goes in v6:
time: 62.9 us; the launch traced here: 62.2 us
  blocking collectives  18.4 us (29%)
  Pallas kernels  15.7 us (25%)
  starting transfers between devices  14.6 us (23%)
  waiting for transfers between devices  8.62 us (14%)
  local copies, waits for them, and re-layouts  4.2 us (7%)
  between operations  0.71 us (1%)
    all_to_all x1, blocking collectives, exchange(): return lax.all_to_all(block, 'ctx', split_axis=0, concat_axis=0, tiled=True)  18.4 us
    pallas_call x7, Pallas kernels, call(): pl.pallas_call(kernel, out_shape=outs, grid_spec=pltpu.PrefetchScalarGrid...  15.7 us
    all_to_all x2, starting transfers between devices, exchange(): return lax.all_to_all(block, 'ctx', split_axis=0, concat_axis=0, tiled=True)  11.5 us
    ppermute x2, waiting for transfers between devices, swap_tp(): return lax.ppermute(block, 'tp', [(0, 1), (1, 0)])  5.78 us
    unnamed x18, local copies, waits for them, and re-layouts  4.2 us
    ppermute x2, starting transfers between devices, swap_tp(): return lax.ppermute(block, 'tp', [(0, 1), (1, 0)])  3.16 us
    all_to_all x2, waiting for transfers between devices, exchange(): return lax.all_to_all(block, 'ctx', split_axis=0, concat_axis=0, tiled=True)  2.84 us
  transfers between devices with their start and end apart: 4, of which 4 were waited for; matrix products, arithmetic and copies ran while one was open for 0% of the time, Pallas kernels for 14%

profile of v6, /device:TPU:0, one launch (start us, length us, event | category | flops | bytes accessed | tf_op | source)
XLA Modules:
  0.0 62.2 jit_solution(10474184699097718282)
XLA Ops:
  0.6 2.1 %shard_map.120 = bf16[16,128,128]{2,1,0:T(8,128)(2,1)} custom-call(s32[1,128]{1,0:T(1,128)} %bitcast.2, bf16[128,1024]{1,0:T(8,128)(2,1)} %pre_ref.3, bf16[128,1024]{1,0:T(8,128)(2,1)} %feat_ref.3, f32[128,1024]{1,0:T(8,128)} %filt_ref.1), custom_call_target="tpu_custom_call" | custom-call | bytes 1573376 | tf_op jit(solution)/shard_map/pallas_call | solution.py:413
  2.7 7.4 %all-to-all-start = ((bf16[16,128,128]{2,1,0:T(8,128)(2,1)}), bf16[16,128,128]{2,1,0:T(8,128)(2,1)S(1)}, u32[]{:S(2)}, u32[]{:S(2)}) async-start(bf16[16,128,128]{2,1,0:T(8,128)(2,1)} %shard_map.120), calls=%async_computation | async-start | bytes 1048576 | tf_op jit(solution)/shard_map/all_to_all | solution.py:429
  10.1 1.6 %collective-permute-start = (bf16[128,1024]{1,0:T(8,128)(2,1)}, bf16[128,1024]{1,0:T(8,128)(2,1)S(1)}, u32[]{:S(2)}, u32[]{:S(2)}) collective-permute-start(bf16[128,1024]{1,0:T(8,128)(2,1)} %own_ref.1), channel_id=1, source_target_pairs={{0,1},{1,0},{2,3},{3,2},{4,5},{5,4},{6,7},{7,6},{8,9},{9,8},{10,11... | collective-permute-start | bytes 786440 | tf_op jit(solution)/shard_map/ppermute | solution.py:435
  11.7 0.0 copy-start.6
  11.7 0.0 copy-start.7
  11.7 3.2 %shard_map.121.part_ref = f32[1024,128]{1,0:T(8,128)S(1)} custom-call(s32[1]{0:T(128)} %bitcast.1.rank_ref, bf16[128,1024]{1,0:T(8,128)(2,1)} %own_ref.1, bf16[1024,2048]{1,0:T(8,128)(2,1)} %weight_hbm.1), custom_call_target="tpu_custom_call" | custom-call | flops 268435456 | bytes 4980736 | tf_op jit(solution)/shard_map/pallas_call | solution.py:413
  14.8 0.0 copy-start.3
  14.9 4.1 %collective-permute-done.other_ref = bf16[128,1024]{1,0:T(8,128)(2,1)S(1)} collective-permute-done((bf16[128,1024]{1,0:T(8,128)(2,1)}, bf16[128,1024]{1,0:T(8,128)(2,1)S(1)}, u32[]{:S(2)}, u32[]{:S(2)}) %collective-permute-start) | collective-permute-done | bytes 262176 | tf_op jit(solution)/shard_map/ppermute | solution.py:435
  18.9 4.0 %shard_map.122 = (f32[1024,128]{1,0:T(8,128)}, bf16[16,64,128]{2,1,0:T(8,128)(2,1)S(1)}, bf16[1024,1024]{1,0:T(8,128)(2,1)S(1)}) custom-call(s32[1]{0:T(128)} %bitcast.1.rank_ref, bf16[128,1024]{1,0:T(8,128)(2,1)S(1)} %collective-permute-done.other_ref, bf16[1024,2048]{1,0:T(8,128)(2,1)} %weight_hbm.1, f32[1024,128]{1,0:T(8,128)S(1)} %shard_map.121.part_ref, ...), custom_call_target="tpu_custom_call" | custom-call | flops 268435456 | bytes 8126464 | tf_op jit(solution)/shard_map/pallas_call | solution.py:413
  22.9 1.6 %all-to-all-done.pair_ref = bf16[16,128,128]{2,1,0:T(8,128)(2,1)S(1)} async-done(((bf16[16,128,128]{2,1,0:T(8,128)(2,1)}), bf16[16,128,128]{2,1,0:T(8,128)(2,1)S(1)}, u32[]{:S(2)}, u32[]{:S(2)}) %all-to-all-start) | async-done | bytes 524320 | tf_op jit(solution)/shard_map/all_to_all | solution.py:429
  24.6 0.0 copy-done.6
  24.6 0.0 copy-done.7
  24.6 1.8 %shard_map.123 = (bf16[16,64,256]{2,1,0:T(8,128)(2,1)S(1)}, bf16[17,64,256]{2,1,0:T(8,128)(2,1)S(1)}) custom-call(bf16[16,128,128]{2,1,0:T(8,128)(2,1)S(1)} %all-to-all-done.pair_ref, bf16[16,64,128]{2,1,0:T(8,128)(2,1)S(1)} %get-tuple-element.17.grad_ref, f32[34,128]{1,0:T(8,128)S(1)} %copy-done.7, bf16[128,256]{1,0:T(8,128)(2,1)S(1)} %copy-done.6), custom_call_target="tpu_custom_call" | custom-call | flops 427819008 | bytes 1950720 | tf_op jit(solution)/shard_map/pallas_call | solution.py:413
  26.4 18.4 %all_to_all.15.both_ref = bf16[16,64,256]{2,1,0:T(8,128)(2,1)S(1)} all-to-all(bf16[16,64,256]{2,1,0:T(8,128)(2,1)S(1)} %get-tuple-element.18), channel_id=1, replica_groups=mesh['ctx'=16,'tp'=2] {'ctx'}, dimensions={0} | all-to-all | bytes 1048576 | tf_op jit(solution)/shard_map/all_to_all | solution.py:429
  44.8 0.0 copy-done.3
  44.8 0.0 copy-start.1
  44.8 0.0 copy-start.2
  44.8 0.0 copy-start.8
  44.8 2.1 %shard_map.124 = (bf16[16,64,128]{2,1,0:T(8,128)(2,1)}, bf16[128,1024]{1,0:T(8,128)(2,1)}, bf16[128,1024]{1,0:T(8,128)(2,1)}) custom-call(bf16[16,64,256]{2,1,0:T(8,128)(2,1)S(1)} %all_to_all.15.both_ref, bf16[128,1024]{1,0:T(8,128)(2,1)S(1)} %copy-done.3, f32[34,128]{1,0:T(8,128)S(1)} %copy-done.7, bf16[128,256]{1,0:T(8,128)(2,1)S(1)} %copy-done.6, ...), custom_call_target="tpu_custom_call" | custom-call | flops 553648128 | bytes 4310016 | tf_op jit(solution)/shard_map/pallas_call | solution.py:413
  46.9 4.1 %all-to-all-start.2 = ((bf16[16,64,128]{2,1,0:T(8,128)(2,1)}), bf16[16,64,128]{2,1,0:T(8,128)(2,1)S(1)}, u32[]{:S(2)}, u32[]{:S(2)}) async-start(bf16[16,64,128]{2,1,0:T(8,128)(2,1)} %get-tuple-element.21), calls=%async_computation.2 | async-start | bytes 524288 | tf_op jit(solution)/shard_map/all_to_all | solution.py:429
  51.0 1.6 %collective-permute-start.1 = (bf16[128,1024]{1,0:T(8,128)(2,1)}, bf16[128,1024]{1,0:T(8,128)(2,1)S(1)}, u32[]{:S(2)}, u32[]{:S(2)}) collective-permute-start(bf16[128,1024]{1,0:T(8,128)(2,1)} %get-tuple-element.25), channel_id=1, source_target_pairs={{0,1},{1,0},{2,3},{3,2},{4,5},{5,4},{6,7},{7,6},{8,9},{9,8},{10,11... | collective-permute-start | bytes 786440 | tf_op jit(solution)/shard_map/ppermute | solution.py:435
  52.6 0.0 copy-start
  52.6 2.2 %copy-done = bf16[1024,2048]{1,0:T(8,128)(2,1)S(1)} copy-done((bf16[1024,2048]{1,0:T(8,128)(2,1)S(1)}, bf16[1024,2048]{1,0:T(8,128)(2,1)}, u32[]{:S(2)}) %copy-start) | copy-done | bytes 4194328
  54.8 1.0 %copy-done.4 = f32[1024,128]{1,0:T(8,128)S(1)} copy-done((f32[1024,128]{1,0:T(8,128)S(1)}, f32[1024,128]{1,0:T(8,128)}, u32[]{:S(2)}) %copy-start.4) | copy-done | bytes 524312
  55.8 0.9 %copy-done.5 = bf16[128,1024]{1,0:T(8,128)(2,1)S(1)} copy-done((bf16[128,1024]{1,0:T(8,128)(2,1)S(1)}, bf16[128,1024]{1,0:T(8,128)(2,1)}, u32[]{:S(2)}) %copy-start.5) | copy-done | bytes 262168
  56.8 1.4 %shard_map.125 = (f32[128,1024]{1,0:T(8,128)S(1)}, bf16[128,1024]{1,0:T(8,128)(2,1)}) custom-call(s32[1]{0:T(128)} %bitcast.1.rank_ref, bf16[128,1024]{1,0:T(8,128)(2,1)S(1)} %copy-done.5, bf16[16,64,256]{2,1,0:T(8,128)(2,1)S(1)} %all_to_all.15.both_ref, f32[1024,128]{1,0:T(8,128)S(1)} %copy-done.4, bf16[1024,2048]{1,0:T(8,128)(2,1)S(1)} %copy-done), custom_call_target="tpu_custom_call" | custom-call | flops 268435456 | bytes 6291456 | tf_op jit(solution)/shard_map/pallas_call | solution.py:413
  58.2 1.7 %collective-permute-done.1.other_ref = bf16[128,1024]{1,0:T(8,128)(2,1)S(1)} collective-permute-done((bf16[128,1024]{1,0:T(8,128)(2,1)}, bf16[128,1024]{1,0:T(8,128)(2,1)S(1)}, u32[]{:S(2)}, u32[]{:S(2)}) %collective-permute-start.1) | collective-permute-done | bytes 262176 | tf_op jit(solution)/shard_map/ppermute | solution.py:435
  59.9 1.2 %all-to-all-done.2.packed_ref = bf16[16,64,128]{2,1,0:T(8,128)(2,1)S(1)} async-done(((bf16[16,64,128]{2,1,0:T(8,128)(2,1)}), bf16[16,64,128]{2,1,0:T(8,128)(2,1)S(1)}, u32[]{:S(2)}, u32[]{:S(2)}) %all-to-all-start.2) | async-done | bytes 262176 | tf_op jit(solution)/shard_map/all_to_all | solution.py:429
  61.1 0.0 copy-done.1
  61.1 0.0 copy-done.2
  61.1 0.0 copy-done.8
  61.1 1.2 %shard_map.126 = (bf16[128,1024]{1,0:T(8,128)(2,1)}, bf16[128,1024]{1,0:T(8,128)(2,1)}, bf16[128,1024]{1,0:T(8,128)(2,1)}) custom-call(s32[1,128]{1,0:T(1,128)S(1)} %bitcast.3, bf16[16,64,128]{2,1,0:T(8,128)(2,1)S(1)} %all-to-all-done.2.packed_ref, bf16[128,1024]{1,0:T(8,128)(2,1)S(1)} %copy-done.1, bf16[128,1024]{1,0:T(8,128)(2,1)S(1)} %copy-done.2, ...), custom_call_target="tpu_custom_call" | custom-call | bytes 2359808 | tf_op jit(solution)/shard_map/pallas_call | solution.py:413
  (2 shorter events, 0.0 us)
Async XLA Ops:
  2.7 21.8 %all-to-all-start = ((bf16[16,128,128]{2,1,0:T(8,128)(2,1)}), bf16[16,128,128]{2,1,0:T(8,128)(2,1)S(1)}, u32[]{:S(2)}, u32[]{:S(2)}) async-start(bf16[16,128,128]{2,1,0:T(8,128)(2,1)} %shard_map.120), calls=%async_computation | async-start | bytes 1048576 | tf_op jit(solution)/shard_map/all_to_all | solution.py:429
  10.1 8.8 %collective-permute-start = (bf16[128,1024]{1,0:T(8,128)(2,1)}, bf16[128,1024]{1,0:T(8,128)(2,1)S(1)}, u32[]{:S(2)}, u32[]{:S(2)}) collective-permute-start(bf16[128,1024]{1,0:T(8,128)(2,1)} %own_ref.1), channel_id=1, source_target_pairs={{0,1},{1,0},{2,3},{3,2},{4,5},{5,4},{6,7},{7,6},{8,9},{9,8},{10,11... | collective-permute-start | bytes 786440 | tf_op jit(solution)/shard_map/ppermute | solution.py:435
  11.7 12.9 %copy-start.6 = (bf16[128,256]{1,0:T(8,128)(2,1)S(1)}, bf16[128,256]{1,0:T(8,128)(2,1)}, u32[]{:S(2)}) copy-start(bf16[128,256]{1,0:T(8,128)(2,1)} %constant.9.clone.dft_ref) | copy-start | bytes 196612
  11.7 12.9 %copy-start.7 = (f32[34,128]{1,0:T(8,128)S(1)}, f32[34,128]{1,0:T(8,128)}, u32[]{:S(2)}) copy-start(f32[34,128]{1,0:T(8,128)} %constant.8.clone.twist_ref) | copy-start | bytes 52228
  14.8 29.9 %copy-start.3 = (bf16[128,1024]{1,0:T(8,128)(2,1)S(1)}, bf16[128,1024]{1,0:T(8,128)(2,1)}, u32[]{:S(2)}) copy-start(bf16[128,1024]{1,0:T(8,128)(2,1)} %post_ref.3) | copy-start | bytes 786436
  44.8 16.3 %copy-start.1 = (bf16[128,1024]{1,0:T(8,128)(2,1)S(1)}, bf16[128,1024]{1,0:T(8,128)(2,1)}, u32[]{:S(2)}) copy-start(bf16[128,1024]{1,0:T(8,128)(2,1)} %pre_ref.3) | copy-start | bytes 786436
  44.8 16.3 %copy-start.2 = (bf16[128,1024]{1,0:T(8,128)(2,1)S(1)}, bf16[128,1024]{1,0:T(8,128)(2,1)}, u32[]{:S(2)}) copy-start(bf16[128,1024]{1,0:T(8,128)(2,1)} %feat_ref.3) | copy-start | bytes 786436
  44.8 16.3 %copy-start.8 = (s32[128]{0:T(128)S(1)}, s32[128]{0:T(128)}, u32[]{:S(2)}) copy-start(s32[128]{0:T(128)} %param.13) | copy-start | bytes 1540
  46.9 14.2 %all-to-all-start.2 = ((bf16[16,64,128]{2,1,0:T(8,128)(2,1)}), bf16[16,64,128]{2,1,0:T(8,128)(2,1)S(1)}, u32[]{:S(2)}, u32[]{:S(2)}) async-start(bf16[16,64,128]{2,1,0:T(8,128)(2,1)} %get-tuple-element.21), calls=%async_computation.2 | async-start | bytes 524288 | tf_op jit(solution)/shard_map/all_to_all | solution.py:429
  51.0 8.8 %collective-permute-start.1 = (bf16[128,1024]{1,0:T(8,128)(2,1)}, bf16[128,1024]{1,0:T(8,128)(2,1)S(1)}, u32[]{:S(2)}, u32[]{:S(2)}) collective-permute-start(bf16[128,1024]{1,0:T(8,128)(2,1)} %get-tuple-element.25), channel_id=1, source_target_pairs={{0,1},{1,0},{2,3},{3,2},{4,5},{5,4},{6,7},{7,6},{8,9},{9,8},{10,11... | collective-permute-start | bytes 786440 | tf_op jit(solution)/shard_map/ppermute | solution.py:435
  52.6 2.2 %copy-start = (bf16[1024,2048]{1,0:T(8,128)(2,1)S(1)}, bf16[1024,2048]{1,0:T(8,128)(2,1)}, u32[]{:S(2)}) copy-start(bf16[1024,2048]{1,0:T(8,128)(2,1)} %weight_hbm.1) | copy-start | bytes 12582916
  54.8 1.0 %copy-start.4 = (f32[1024,128]{1,0:T(8,128)S(1)}, f32[1024,128]{1,0:T(8,128)}, u32[]{:S(2)}) copy-start(f32[1024,128]{1,0:T(8,128)} %get-tuple-element.23.grad_ref) | copy-start | bytes 1572868
  55.8 0.9 %copy-start.5 = (bf16[128,1024]{1,0:T(8,128)(2,1)S(1)}, bf16[128,1024]{1,0:T(8,128)(2,1)}, u32[]{:S(2)}) copy-start(bf16[128,1024]{1,0:T(8,128)(2,1)} %get-tuple-element.22.gated_ref) | copy-start | bytes 786436

commit v7 on v6

--- a/solution.py
+++ b/solution.py
@@ -117,14 +117,50 @@
     return low + [total[b] - rest[b] for b in range(half)]
 
 
-def pack_inputs(dests, token_ref, pre_ref, feat_ref, filt_ref, out_ref):
-    width = out_ref.shape[1] // 2
-    keep = (token_ref[...] < BASES).astype(BF16)
-    mixer = (pre_ref[...].astype(F32) * feat_ref[...].astype(F32)).astype(BF16).T * keep
-    filt = filt_ref[...].astype(BF16).T
-    for k in range(dests):
-        at = slice(k * width, (k + 1) * width)
-        out_ref[k] = jnp.concatenate([mixer[at], filt[at]], axis=0)
+def pack_inputs(
+    parts,
+    token_hbm,
+    pre_hbm,
+    feat_hbm,
+    filt_hbm,
+    out_hbm,
+    token_ref,
+    pre_ref,
+    feat_ref,
+    filt_ref,
+    out_ref,
+    in_sems,
+    out_sems,
+):
+    n, rows, _ = out_ref.shape
+    width, dests = rows // 2, n // parts
+    cut = dests * width
+    pairs = ((pre_hbm, pre_ref), (feat_hbm, feat_ref), (filt_hbm, filt_ref))
+    copies = []
+    for k in range(parts):
+        at = pl.ds(k * cut, cut)
+        copies.append(
+            started(
+                *((a.at[:, at], b.at[:, at], in_sems.at[k, i]) for i, (a, b) in enumerate(pairs))
+            )
+        )
+        if k == 0:
+            copies[0] += started((token_hbm, token_ref, in_sems.at[k, 3]))
+    sent = []
+    for k in range(parts):
+        for copy in copies[k]:
+            copy.wait()
+        at = slice(k * cut, (k + 1) * cut)
+        keep = (token_ref[...] < BASES).astype(BF16)
+        mixer = (pre_ref[:, at].astype(F32) * feat_ref[:, at].astype(F32)).astype(BF16).T * keep
+        filt = filt_ref[:, at].astype(BF16).T
+        for j in range(dests):
+            mine = slice(j * width, (j + 1) * width)
+            out_ref[k * dests + j] = jnp.concatenate([mixer[mine], filt[mine]], axis=0)
+        here = pl.ds(k * dests, dests)
+        sent += started((out_ref.at[here], out_hbm.at[here], out_sems.at[k]))
+    for copy in sent:
+        copy.wait()
 
 
 def own_grad(rank_ref, own_ref, weight_ref, out_ref):
@@ -276,11 +312,17 @@
     mixed = channel_rows(both_ref, length).T.astype(F32)
     gated = (post_ref[...].astype(F32) * mixed).astype(BF16)
     gated_ref[...] = gated
-    away_ref[...] = jnp.dot(gated, weight_ref[...], preferred_element_type=F32).astype(BF16)
-    copies = started((away_ref, away_hbm, sems.at[0]), (gated_ref, gated_hbm, sems.at[1]))
+    copies = started((gated_ref, gated_hbm, sems.at[0]))
     chunks = row_chunks(width)
     step = width // chunks
+    cut = weight_ref.shape[1] // chunks
     for c in range(chunks):
+        share = slice(c * cut, (c + 1) * cut)
+        away_ref[:, share] = jnp.dot(
+            gated, weight_ref[:, share], preferred_element_type=F32
+        ).astype(BF16)
+        share = pl.ds(c * cut, cut)
+        copies += started((away_ref.at[:, share], away_hbm.at[:, share], sems.at[1 + c]))
         at = slice(c * step, (c + 1) * step)
         blocks = [both_ref[b, at, length:] for b in range(n)]
         forward_blocks(n, blocks, twist_ref, mid_ref.at[c], slice(0, step))
@@ -299,10 +341,12 @@
         for b, value in enumerate(inverse_blocks(n, mid, twist_ref)):
             out_ref[b, at] = value
         if chunks == 1:
-            copies += started((out_ref, out_hbm, sems.at[2]))
+            copies += started((out_ref, out_hbm, sems.at[1 + chunks]))
         else:
             rows = pl.ds(c * step, step)
-            copies += started((out_ref.at[:, rows], out_hbm.at[:, rows], sems.at[2 + c]))
+            copies += started(
+                (out_ref.at[:, rows], out_hbm.at[:, rows], sems.at[1 + chunks + c])
+            )
     for copy in copies:
         copy.wait()
 
@@ -464,16 +508,23 @@
         )
 
     other_grad = swap_tp(out_grad)
-    steps = 2
-    flat, _, _ = by_channels(steps)
+    parts = 2
     pair_out = call(
-        functools.partial(pack_inputs, n // steps),
+        functools.partial(pack_inputs, parts),
         pltpu.HBM(pair, BF16),
         (tokens, pre_gate, features, filters),
-        grid=(steps,),
-        blocks=[None, flat, flat, flat],
-        out_blocks=[((n // steps, *pair[1:]), lambda i, *_: (i, 0, 0))],
+        blocks=["hbm"] * 4,
+        out_blocks=["hbm"],
         from_hbm=range(4),
+        scratch=[
+            pltpu.VMEM(tokens.shape, jnp.int32),
+            pltpu.VMEM((length, channels), BF16),
+            pltpu.VMEM((length, channels), BF16),
+            pltpu.VMEM((length, channels), F32),
+            pltpu.VMEM(pair, BF16),
+            pltpu.SemaphoreType.DMA((parts, 4)),
+            pltpu.SemaphoreType.DMA((parts,)),
+        ],
     )
     pair_in = exchange(pair_out)
     steps = 4
@@ -535,7 +586,7 @@
             pltpu.VMEM(one, BF16),
             pltpu.VMEM((length, channels), BF16),
             pltpu.VMEM((length, columns), BF16),
-            pltpu.SemaphoreType.DMA((2 + chunks,)),
+            pltpu.SemaphoreType.DMA((1 + 2 * chunks,)),
         ],
     )
     grad_back_in = exchange(grad_back_out)

time: 62.9 us -> 62.9 us (level)
  no operation moved by 1% of the time
where the time goes in v7:
time: 62.9 us; the launch traced here: 62.3 us
  blocking collectives  18.4 us (29%)
  Pallas kernels  15.7 us (25%)
  starting transfers between devices  14.6 us (23%)
  waiting for transfers between devices  8.63 us (14%)
  local copies, waits for them, and re-layouts  4.2 us (7%)
  between operations  0.71 us (1%)
    all_to_all x1, blocking collectives, exchange(): return lax.all_to_all(block, 'ctx', split_axis=0, concat_axis=0, tiled=True)  18.4 us
    pallas_call x7, Pallas kernels, call(): pl.pallas_call(kernel, out_shape=outs, grid_spec=pltpu.PrefetchScalarGrid...  15.7 us
    all_to_all x2, starting transfers between devices, exchange(): return lax.all_to_all(block, 'ctx', split_axis=0, concat_axis=0, tiled=True)  11.5 us
    ppermute x2, waiting for transfers between devices, swap_tp(): return lax.ppermute(block, 'tp', [(0, 1), (1, 0)])  5.79 us
    unnamed x18, local copies, waits for them, and re-layouts  4.2 us
    ppermute x2, starting transfers between devices, swap_tp(): return lax.ppermute(block, 'tp', [(0, 1), (1, 0)])  3.16 us
    all_to_all x2, waiting for transfers between devices, exchange(): return lax.all_to_all(block, 'ctx', split_axis=0, concat_axis=0, tiled=True)  2.84 us
  transfers between devices with their start and end apart: 4, of which 4 were waited for; matrix products, arithmetic and copies ran while one was open for 0% of the time, Pallas kernels for 14%

profile of v7, /device:TPU:0, one launch (start us, length us, event | category | flops | bytes accessed | tf_op | source)
XLA Modules:
  0.0 62.3 jit_solution(5500899025252666132)
XLA Ops:
  0.6 2.2 %shard_map.120 = bf16[16,128,128]{2,1,0:T(8,128)(2,1)} custom-call(s32[1,128]{1,0:T(1,128)} %bitcast.2, bf16[128,1024]{1,0:T(8,128)(2,1)} %pre_ref.1, bf16[128,1024]{1,0:T(8,128)(2,1)} %feat_ref.1, f32[128,1024]{1,0:T(8,128)} %filt_hbm.1), custom_call_target="tpu_custom_call" | custom-call | bytes 1573376 | tf_op jit(solution)/shard_map/pallas_call | solution.py:457
  2.8 7.4 %all-to-all-start = ((bf16[16,128,128]{2,1,0:T(8,128)(2,1)}), bf16[16,128,128]{2,1,0:T(8,128)(2,1)S(1)}, u32[]{:S(2)}, u32[]{:S(2)}) async-start(bf16[16,128,128]{2,1,0:T(8,128)(2,1)} %shard_map.120), calls=%async_computation | async-start | bytes 1048576 | tf_op jit(solution)/shard_map/all_to_all | solution.py:473
  10.2 1.6 %collective-permute-start = (bf16[128,1024]{1,0:T(8,128)(2,1)}, bf16[128,1024]{1,0:T(8,128)(2,1)S(1)}, u32[]{:S(2)}, u32[]{:S(2)}) collective-permute-start(bf16[128,1024]{1,0:T(8,128)(2,1)} %own_ref.1), channel_id=1, source_target_pairs={{0,1},{1,0},{2,3},{3,2},{4,5},{5,4},{6,7},{7,6},{8,9},{9,8},{10,11... | collective-permute-start | bytes 786440 | tf_op jit(solution)/shard_map/ppermute | solution.py:479
  11.8 0.0 copy-start.6
  11.8 0.0 copy-start.7
  11.8 3.1 %shard_map.121.part_ref = f32[1024,128]{1,0:T(8,128)S(1)} custom-call(s32[1]{0:T(128)} %bitcast.1.rank_ref, bf16[128,1024]{1,0:T(8,128)(2,1)} %own_ref.1, bf16[1024,2048]{1,0:T(8,128)(2,1)} %weight_hbm.1), custom_call_target="tpu_custom_call" | custom-call | flops 268435456 | bytes 4980736 | tf_op jit(solution)/shard_map/pallas_call | solution.py:457
  14.9 0.0 copy-start.3
  14.9 4.1 %collective-permute-done.other_ref = bf16[128,1024]{1,0:T(8,128)(2,1)S(1)} collective-permute-done((bf16[128,1024]{1,0:T(8,128)(2,1)}, bf16[128,1024]{1,0:T(8,128)(2,1)S(1)}, u32[]{:S(2)}, u32[]{:S(2)}) %collective-permute-start) | collective-permute-done | bytes 262176 | tf_op jit(solution)/shard_map/ppermute | solution.py:479
  19.0 4.0 %shard_map.122 = (f32[1024,128]{1,0:T(8,128)}, bf16[16,64,128]{2,1,0:T(8,128)(2,1)S(1)}, bf16[1024,1024]{1,0:T(8,128)(2,1)S(1)}) custom-call(s32[1]{0:T(128)} %bitcast.1.rank_ref, bf16[128,1024]{1,0:T(8,128)(2,1)S(1)} %collective-permute-done.other_ref, bf16[1024,2048]{1,0:T(8,128)(2,1)} %weight_hbm.1, f32[1024,128]{1,0:T(8,128)S(1)} %shard_map.121.part_ref, ...), custom_call_target="tpu_custom_call" | custom-call | flops 268435456 | bytes 8126464 | tf_op jit(solution)/shard_map/pallas_call | solution.py:457
  23.0 1.6 %all-to-all-done.pair_ref = bf16[16,128,128]{2,1,0:T(8,128)(2,1)S(1)} async-done(((bf16[16,128,128]{2,1,0:T(8,128)(2,1)}), bf16[16,128,128]{2,1,0:T(8,128)(2,1)S(1)}, u32[]{:S(2)}, u32[]{:S(2)}) %all-to-all-start) | async-done | bytes 524320 | tf_op jit(solution)/shard_map/all_to_all | solution.py:473
  24.6 0.0 copy-done.6
  24.6 0.0 copy-done.7
  24.7 1.8 %shard_map.123 = (bf16[16,64,256]{2,1,0:T(8,128)(2,1)S(1)}, bf16[17,64,256]{2,1,0:T(8,128)(2,1)S(1)}) custom-call(bf16[16,128,128]{2,1,0:T(8,128)(2,1)S(1)} %all-to-all-done.pair_ref, bf16[16,64,128]{2,1,0:T(8,128)(2,1)S(1)} %get-tuple-element.17.grad_ref, f32[34,128]{1,0:T(8,128)S(1)} %copy-done.7, bf16[128,256]{1,0:T(8,128)(2,1)S(1)} %copy-done.6), custom_call_target="tpu_custom_call" | custom-call | flops 427819008 | bytes 1950720 | tf_op jit(solution)/shard_map/pallas_call | solution.py:457
  26.4 18.4 %all_to_all.15.both_ref = bf16[16,64,256]{2,1,0:T(8,128)(2,1)S(1)} all-to-all(bf16[16,64,256]{2,1,0:T(8,128)(2,1)S(1)} %get-tuple-element.18), channel_id=1, replica_groups=mesh['ctx'=16,'tp'=2] {'ctx'}, dimensions={0} | all-to-all | bytes 1048576 | tf_op jit(solution)/shard_map/all_to_all | solution.py:473
  44.9 0.0 copy-done.3
  44.9 0.0 copy-start.1
  44.9 0.0 copy-start.2
  44.9 0.0 copy-start.8
  44.9 2.1 %shard_map.124 = (bf16[16,64,128]{2,1,0:T(8,128)(2,1)}, bf16[128,1024]{1,0:T(8,128)(2,1)}, bf16[128,1024]{1,0:T(8,128)(2,1)}) custom-call(bf16[16,64,256]{2,1,0:T(8,128)(2,1)S(1)} %all_to_all.15.both_ref, bf16[128,1024]{1,0:T(8,128)(2,1)S(1)} %copy-done.3, f32[34,128]{1,0:T(8,128)S(1)} %copy-done.7, bf16[128,256]{1,0:T(8,128)(2,1)S(1)} %copy-done.6, ...), custom_call_target="tpu_custom_call" | custom-call | flops 553648128 | bytes 4310016 | tf_op jit(solution)/shard_map/pallas_call | solution.py:457
  47.0 4.1 %all-to-all-start.2 = ((bf16[16,64,128]{2,1,0:T(8,128)(2,1)}), bf16[16,64,128]{2,1,0:T(8,128)(2,1)S(1)}, u32[]{:S(2)}, u32[]{:S(2)}) async-start(bf16[16,64,128]{2,1,0:T(8,128)(2,1)} %get-tuple-element.21), calls=%async_computation.2 | async-start | bytes 524288 | tf_op jit(solution)/shard_map/all_to_all | solution.py:473
  51.1 1.6 %collective-permute-start.1 = (bf16[128,1024]{1,0:T(8,128)(2,1)}, bf16[128,1024]{1,0:T(8,128)(2,1)S(1)}, u32[]{:S(2)}, u32[]{:S(2)}) collective-permute-start(bf16[128,1024]{1,0:T(8,128)(2,1)} %get-tuple-element.25), channel_id=1, source_target_pairs={{0,1},{1,0},{2,3},{3,2},{4,5},{5,4},{6,7},{7,6},{8,9},{9,8},{10,11... | collective-permute-start | bytes 786440 | tf_op jit(solution)/shard_map/ppermute | solution.py:479
  52.7 0.0 copy-start
  52.7 2.2 %copy-done = bf16[1024,2048]{1,0:T(8,128)(2,1)S(1)} copy-done((bf16[1024,2048]{1,0:T(8,128)(2,1)S(1)}, bf16[1024,2048]{1,0:T(8,128)(2,1)}, u32[]{:S(2)}) %copy-start) | copy-done | bytes 4194328
  54.9 1.0 %copy-done.4 = f32[1024,128]{1,0:T(8,128)S(1)} copy-done((f32[1024,128]{1,0:T(8,128)S(1)}, f32[1024,128]{1,0:T(8,128)}, u32[]{:S(2)}) %copy-start.4) | copy-done | bytes 524312
  55.9 0.9 %copy-done.5 = bf16[128,1024]{1,0:T(8,128)(2,1)S(1)} copy-done((bf16[128,1024]{1,0:T(8,128)(2,1)S(1)}, bf16[128,1024]{1,0:T(8,128)(2,1)}, u32[]{:S(2)}) %copy-start.5) | copy-done | bytes 262168
  56.9 1.4 %shard_map.125 = (f32[128,1024]{1,0:T(8,128)S(1)}, bf16[128,1024]{1,0:T(8,128)(2,1)}) custom-call(s32[1]{0:T(128)} %bitcast.1.rank_ref, bf16[128,1024]{1,0:T(8,128)(2,1)S(1)} %copy-done.5, bf16[16,64,256]{2,1,0:T(8,128)(2,1)S(1)} %all_to_all.15.both_ref, f32[1024,128]{1,0:T(8,128)S(1)} %copy-done.4, bf16[1024,2048]{1,0:T(8,128)(2,1)S(1)} %copy-done), custom_call_target="tpu_custom_call" | custom-call | flops 268435456 | bytes 6291456 | tf_op jit(solution)/shard_map/pallas_call | solution.py:457
  58.2 1.7 %collective-permute-done.1.other_ref = bf16[128,1024]{1,0:T(8,128)(2,1)S(1)} collective-permute-done((bf16[128,1024]{1,0:T(8,128)(2,1)}, bf16[128,1024]{1,0:T(8,128)(2,1)S(1)}, u32[]{:S(2)}, u32[]{:S(2)}) %collective-permute-start.1) | collective-permute-done | bytes 262176 | tf_op jit(solution)/shard_map/ppermute | solution.py:479
  60.0 1.2 %all-to-all-done.2.packed_ref = bf16[16,64,128]{2,1,0:T(8,128)(2,1)S(1)} async-done(((bf16[16,64,128]{2,1,0:T(8,128)(2,1)}), bf16[16,64,128]{2,1,0:T(8,128)(2,1)S(1)}, u32[]{:S(2)}, u32[]{:S(2)}) %all-to-all-start.2) | async-done | bytes 262176 | tf_op jit(solution)/shard_map/all_to_all | solution.py:473
  61.2 0.0 copy-done.1
  61.2 0.0 copy-done.2
  61.2 0.0 copy-done.8
  61.2 1.2 %shard_map.126 = (bf16[128,1024]{1,0:T(8,128)(2,1)}, bf16[128,1024]{1,0:T(8,128)(2,1)}, bf16[128,1024]{1,0:T(8,128)(2,1)}) custom-call(s32[1,128]{1,0:T(1,128)S(1)} %bitcast.3, bf16[16,64,128]{2,1,0:T(8,128)(2,1)S(1)} %all-to-all-done.2.packed_ref, bf16[128,1024]{1,0:T(8,128)(2,1)S(1)} %copy-done.1, bf16[128,1024]{1,0:T(8,128)(2,1)S(1)} %copy-done.2, ...), custom_call_target="tpu_custom_call" | custom-call | bytes 2359808 | tf_op jit(solution)/shard_map/pallas_call | solution.py:457
  (2 shorter events, 0.0 us)
Async XLA Ops:
  2.8 21.8 %all-to-all-start = ((bf16[16,128,128]{2,1,0:T(8,128)(2,1)}), bf16[16,128,128]{2,1,0:T(8,128)(2,1)S(1)}, u32[]{:S(2)}, u32[]{:S(2)}) async-start(bf16[16,128,128]{2,1,0:T(8,128)(2,1)} %shard_map.120), calls=%async_computation | async-start | bytes 1048576 | tf_op jit(solution)/shard_map/all_to_all | solution.py:473
  10.2 8.8 %collective-permute-start = (bf16[128,1024]{1,0:T(8,128)(2,1)}, bf16[128,1024]{1,0:T(8,128)(2,1)S(1)}, u32[]{:S(2)}, u32[]{:S(2)}) collective-permute-start(bf16[128,1024]{1,0:T(8,128)(2,1)} %own_ref.1), channel_id=1, source_target_pairs={{0,1},{1,0},{2,3},{3,2},{4,5},{5,4},{6,7},{7,6},{8,9},{9,8},{10,11... | collective-permute-start | bytes 786440 | tf_op jit(solution)/shard_map/ppermute | solution.py:479
  11.8 12.9 %copy-start.6 = (bf16[128,256]{1,0:T(8,128)(2,1)S(1)}, bf16[128,256]{1,0:T(8,128)(2,1)}, u32[]{:S(2)}) copy-start(bf16[128,256]{1,0:T(8,128)(2,1)} %constant.9.clone.dft_ref) | copy-start | bytes 196612
  11.8 12.9 %copy-start.7 = (f32[34,128]{1,0:T(8,128)S(1)}, f32[34,128]{1,0:T(8,128)}, u32[]{:S(2)}) copy-start(f32[34,128]{1,0:T(8,128)} %constant.8.clone.twist_ref) | copy-start | bytes 52228
  14.9 29.9 %copy-start.3 = (bf16[128,1024]{1,0:T(8,128)(2,1)S(1)}, bf16[128,1024]{1,0:T(8,128)(2,1)}, u32[]{:S(2)}) copy-start(bf16[128,1024]{1,0:T(8,128)(2,1)} %post_ref.3) | copy-start | bytes 786436
  44.9 16.3 %copy-start.1 = (bf16[128,1024]{1,0:T(8,128)(2,1)S(1)}, bf16[128,1024]{1,0:T(8,128)(2,1)}, u32[]{:S(2)}) copy-start(bf16[128,1024]{1,0:T(8,128)(2,1)} %pre_ref.1) | copy-start | bytes 786436
  44.9 16.3 %copy-start.2 = (bf16[128,1024]{1,0:T(8,128)(2,1)S(1)}, bf16[128,1024]{1,0:T(8,128)(2,1)}, u32[]{:S(2)}) copy-start(bf16[128,1024]{1,0:T(8,128)(2,1)} %feat_ref.1) | copy-start | bytes 786436
  44.9 16.3 %copy-start.8 = (s32[128]{0:T(128)S(1)}, s32[128]{0:T(128)}, u32[]{:S(2)}) copy-start(s32[128]{0:T(128)} %param.13) | copy-start | bytes 1540
  47.0 14.2 %all-to-all-start.2 = ((bf16[16,64,128]{2,1,0:T(8,128)(2,1)}), bf16[16,64,128]{2,1,0:T(8,128)(2,1)S(1)}, u32[]{:S(2)}, u32[]{:S(2)}) async-start(bf16[16,64,128]{2,1,0:T(8,128)(2,1)} %get-tuple-element.21), calls=%async_computation.2 | async-start | bytes 524288 | tf_op jit(solution)/shard_map/all_to_all | solution.py:473
  51.1 8.8 %collective-permute-start.1 = (bf16[128,1024]{1,0:T(8,128)(2,1)}, bf16[128,1024]{1,0:T(8,128)(2,1)S(1)}, u32[]{:S(2)}, u32[]{:S(2)}) collective-permute-start(bf16[128,1024]{1,0:T(8,128)(2,1)} %get-tuple-element.25), channel_id=1, source_target_pairs={{0,1},{1,0},{2,3},{3,2},{4,5},{5,4},{6,7},{7,6},{8,9},{9,8},{10,11... | collective-permute-start | bytes 786440 | tf_op jit(solution)/shard_map/ppermute | solution.py:479
  52.7 2.2 %copy-start = (bf16[1024,2048]{1,0:T(8,128)(2,1)S(1)}, bf16[1024,2048]{1,0:T(8,128)(2,1)}, u32[]{:S(2)}) copy-start(bf16[1024,2048]{1,0:T(8,128)(2,1)} %weight_hbm.1) | copy-start | bytes 12582916
  54.9 1.0 %copy-start.4 = (f32[1024,128]{1,0:T(8,128)S(1)}, f32[1024,128]{1,0:T(8,128)}, u32[]{:S(2)}) copy-start(f32[1024,128]{1,0:T(8,128)} %get-tuple-element.23.grad_ref) | copy-start | bytes 1572868
  55.9 0.9 %copy-start.5 = (bf16[128,1024]{1,0:T(8,128)(2,1)S(1)}, bf16[128,1024]{1,0:T(8,128)(2,1)}, u32[]{:S(2)}) copy-start(bf16[128,1024]{1,0:T(8,128)(2,1)} %get-tuple-element.22.gated_ref) | copy-start | bytes 786436

commit v8 on v6

--- a/solution.py
+++ b/solution.py
@@ -226,14 +226,20 @@
     step = width // chunks
     forward, back = dft_matrices(dft_ref, n * length)
     both_ref[:, :, length:] = grad_ref[...]
-    for c in range(chunks):
-        at = slice(c * step, (c + 1) * step)
+
+    def transform(c):
         for kind in range(2):
             start = kind * width + c * step
             blocks = [pair_ref[b, start : start + step] for b in range(n)]
             forward_blocks(
                 n, blocks, twist_ref, mid_ref.at[c], slice(kind * step, (kind + 1) * step)
             )
+
+    transform(0)
+    for c in range(chunks):
+        at = slice(c * step, (c + 1) * step)
+        if c + 1 < chunks:
+            transform(c + 1)
         spec = inner_product(mid_ref.at[c], forward)
         for m in range(n + 1):
             first = 2 * m * step
@@ -280,10 +286,16 @@
     copies = started((away_ref, away_hbm, sems.at[0]), (gated_ref, gated_hbm, sems.at[1]))
     chunks = row_chunks(width)
     step = width // chunks
+
+    def transform(c):
+        blocks = [both_ref[b, c * step : (c + 1) * step, length:] for b in range(n)]
+        forward_blocks(n, blocks, twist_ref, mid_ref.at[c], slice(0, step))
+
+    transform(0)
     for c in range(chunks):
         at = slice(c * step, (c + 1) * step)
-        blocks = [both_ref[b, at, length:] for b in range(n)]
-        forward_blocks(n, blocks, twist_ref, mid_ref.at[c], slice(0, step))
+        if c + 1 < chunks:
+            transform(c + 1)
         spec = inner_product(mid_ref.at[c], forward)
         for m in range(n + 1):
             signal, filt = spec[m * step : (m + 1) * step], filt_ref[m, at].astype(F32)
@@ -361,21 +373,38 @@
 
 
 def finish(
+    parts,
     token_ref,
     packed_ref,
     pre_ref,
     feat_ref,
     home_ref,
     other_ref,
+    pre_grad_hbm,
+    feat_grad_hbm,
+    out_hbm,
     pre_grad_ref,
     feat_grad_ref,
     out_ref,
+    sems,
 ):
+    out_ref[...] = (home_ref[...] + other_ref[...].astype(F32)).astype(BF16)
+    copies = started((out_ref, out_hbm, sems.at[2, 0]))
     keep = (token_ref[...] < BASES).astype(BF16)
-    grad = (channel_rows(packed_ref, packed_ref.shape[2]) * keep).T.astype(F32)
-    pre_grad_ref[...] = (grad * feat_ref[...].astype(F32)).astype(BF16)
-    feat_grad_ref[...] = (grad * pre_ref[...].astype(F32)).astype(BF16)
-    out_ref[...] = (home_ref[...] + other_ref[...].astype(F32)).astype(BF16)
+    dests = packed_ref.shape[0] // parts
+    cut = pre_ref.shape[1] // parts
+    for k in range(parts):
+        at = pl.ds(k * cut, cut)
+        blocks = packed_ref.at[pl.ds(k * dests, dests)]
+        grad = (channel_rows(blocks, blocks.shape[2]) * keep).T.astype(F32)
+        pre_grad_ref[:, at] = (grad * feat_ref[:, at].astype(F32)).astype(BF16)
+        feat_grad_ref[:, at] = (grad * pre_ref[:, at].astype(F32)).astype(BF16)
+        copies += started(
+            (pre_grad_ref.at[:, at], pre_grad_hbm.at[:, at], sems.at[0, k]),
+            (feat_grad_ref.at[:, at], feat_grad_hbm.at[:, at], sems.at[1, k]),
+        )
+    for copy in copies:
+        copy.wait()
 
 
 def dft_tables(n, length):
@@ -551,20 +580,18 @@
         scratch=[pltpu.VMEM((channels, columns), BF16), pltpu.SemaphoreType.DMA((parts,))],
         prefetch=1,
     )
-    steps = 2
-    flat, _, packed = by_channels(steps)
-    half = ((length, columns // steps), lambda i, *_: (0, i))
+    flat = (length, channels)
     grad_pre, grad_features, output = call(
-        finish,
-        (
-            shape((length, channels), BF16),
-            shape((length, channels), BF16),
-            shape((length, columns), BF16),
-        ),
+        functools.partial(finish, parts),
+        (pltpu.HBM(flat, BF16), pltpu.HBM(flat, BF16), pltpu.HBM((length, columns), BF16)),
         (tokens, grad_back_in, pre_gate, features, home, other_part),
-        grid=(steps,),
-        blocks=[None, packed, flat, flat, half, half],
-        out_blocks=[flat, flat, half],
+        out_blocks=["hbm"] * 3,
+        scratch=[
+            pltpu.VMEM(flat, BF16),
+            pltpu.VMEM(flat, BF16),
+            pltpu.VMEM((length, columns), BF16),
+            pltpu.SemaphoreType.DMA((3, parts)),
+        ],
     )
     return (output, grad_post, grad_pre, grad_features)
 

time: 62.9 us -> 62.8 us (level)
  no operation moved by 1% of the time
where the time goes in v8:
time: 62.8 us; the launch traced here: 62.2 us
  blocking collectives  18.4 us (29%)
  Pallas kernels  15.6 us (25%)
  starting transfers between devices  14.6 us (23%)
  waiting for transfers between devices  8.62 us (14%)
  local copies, waits for them, and re-layouts  4.2 us (7%)
  between operations  0.71 us (1%)
    all_to_all x1, blocking collectives, exchange(): return lax.all_to_all(block, 'ctx', split_axis=0, concat_axis=0, tiled=True)  18.4 us
    pallas_call x7, Pallas kernels, call(): pl.pallas_call(kernel, out_shape=outs, grid_spec=pltpu.PrefetchScalarGrid...  15.6 us
    all_to_all x2, starting transfers between devices, exchange(): return lax.all_to_all(block, 'ctx', split_axis=0, concat_axis=0, tiled=True)  11.5 us
    ppermute x2, waiting for transfers between devices, swap_tp(): return lax.ppermute(block, 'tp', [(0, 1), (1, 0)])  5.78 us
    unnamed x18, local copies, waits for them, and re-layouts  4.2 us
    ppermute x2, starting transfers between devices, swap_tp(): return lax.ppermute(block, 'tp', [(0, 1), (1, 0)])  3.16 us
    all_to_all x2, waiting for transfers between devices, exchange(): return lax.all_to_all(block, 'ctx', split_axis=0, concat_axis=0, tiled=True)  2.84 us
  transfers between devices with their start and end apart: 4, of which 4 were waited for; matrix products, arithmetic and copies ran while one was open for 0% of the time, Pallas kernels for 14%

profile of v8, /device:TPU:0, one launch (start us, length us, event | category | flops | bytes accessed | tf_op | source)
XLA Modules:
  0.0 62.2 jit_solution(12134147493988900647)
XLA Ops:
  0.6 2.1 %shard_map.120 = bf16[16,128,128]{2,1,0:T(8,128)(2,1)} custom-call(s32[1,128]{1,0:T(1,128)} %bitcast.2, bf16[128,1024]{1,0:T(8,128)(2,1)} %pre_ref.3, bf16[128,1024]{1,0:T(8,128)(2,1)} %feat_ref.3, f32[128,1024]{1,0:T(8,128)} %filt_ref.1), custom_call_target="tpu_custom_call" | custom-call | bytes 1573376 | tf_op jit(solution)/shard_map/pallas_call | solution.py:442
  2.7 7.4 %all-to-all-start = ((bf16[16,128,128]{2,1,0:T(8,128)(2,1)}), bf16[16,128,128]{2,1,0:T(8,128)(2,1)S(1)}, u32[]{:S(2)}, u32[]{:S(2)}) async-start(bf16[16,128,128]{2,1,0:T(8,128)(2,1)} %shard_map.120), calls=%async_computation | async-start | bytes 1048576 | tf_op jit(solution)/shard_map/all_to_all | solution.py:458
  10.1 1.6 %collective-permute-start = (bf16[128,1024]{1,0:T(8,128)(2,1)}, bf16[128,1024]{1,0:T(8,128)(2,1)S(1)}, u32[]{:S(2)}, u32[]{:S(2)}) collective-permute-start(bf16[128,1024]{1,0:T(8,128)(2,1)} %own_ref.1), channel_id=1, source_target_pairs={{0,1},{1,0},{2,3},{3,2},{4,5},{5,4},{6,7},{7,6},{8,9},{9,8},{10,11... | collective-permute-start | bytes 786440 | tf_op jit(solution)/shard_map/ppermute | solution.py:464
  11.7 0.0 copy-start.6
  11.7 0.0 copy-start.7
  11.7 3.2 %shard_map.121.part_ref = f32[1024,128]{1,0:T(8,128)S(1)} custom-call(s32[1]{0:T(128)} %bitcast.1.rank_ref, bf16[128,1024]{1,0:T(8,128)(2,1)} %own_ref.1, bf16[1024,2048]{1,0:T(8,128)(2,1)} %weight_hbm.1), custom_call_target="tpu_custom_call" | custom-call | flops 268435456 | bytes 4980736 | tf_op jit(solution)/shard_map/pallas_call | solution.py:442
  14.8 0.0 copy-start.3
  14.9 4.1 %collective-permute-done.other_ref = bf16[128,1024]{1,0:T(8,128)(2,1)S(1)} collective-permute-done((bf16[128,1024]{1,0:T(8,128)(2,1)}, bf16[128,1024]{1,0:T(8,128)(2,1)S(1)}, u32[]{:S(2)}, u32[]{:S(2)}) %collective-permute-start) | collective-permute-done | bytes 262176 | tf_op jit(solution)/shard_map/ppermute | solution.py:464
  18.9 4.0 %shard_map.122 = (f32[1024,128]{1,0:T(8,128)}, bf16[16,64,128]{2,1,0:T(8,128)(2,1)S(1)}, bf16[1024,1024]{1,0:T(8,128)(2,1)S(1)}) custom-call(s32[1]{0:T(128)} %bitcast.1.rank_ref, bf16[128,1024]{1,0:T(8,128)(2,1)S(1)} %collective-permute-done.other_ref, bf16[1024,2048]{1,0:T(8,128)(2,1)} %weight_hbm.1, f32[1024,128]{1,0:T(8,128)S(1)} %shard_map.121.part_ref, ...), custom_call_target="tpu_custom_call" | custom-call | flops 268435456 | bytes 8126464 | tf_op jit(solution)/shard_map/pallas_call | solution.py:442
  22.9 1.6 %all-to-all-done.pair_ref = bf16[16,128,128]{2,1,0:T(8,128)(2,1)S(1)} async-done(((bf16[16,128,128]{2,1,0:T(8,128)(2,1)}), bf16[16,128,128]{2,1,0:T(8,128)(2,1)S(1)}, u32[]{:S(2)}, u32[]{:S(2)}) %all-to-all-start) | async-done | bytes 524320 | tf_op jit(solution)/shard_map/all_to_all | solution.py:458
  24.6 0.0 copy-done.6
  24.6 0.0 copy-done.7
  24.6 1.8 %shard_map.123 = (bf16[16,64,256]{2,1,0:T(8,128)(2,1)S(1)}, bf16[17,64,256]{2,1,0:T(8,128)(2,1)S(1)}) custom-call(bf16[16,128,128]{2,1,0:T(8,128)(2,1)S(1)} %all-to-all-done.pair_ref, bf16[16,64,128]{2,1,0:T(8,128)(2,1)S(1)} %get-tuple-element.17.grad_ref, f32[34,128]{1,0:T(8,128)S(1)} %copy-done.7, bf16[128,256]{1,0:T(8,128)(2,1)S(1)} %copy-done.6), custom_call_target="tpu_custom_call" | custom-call | flops 427819008 | bytes 1950720 | tf_op jit(solution)/shard_map/pallas_call | solution.py:442
  26.4 18.4 %all_to_all.15.both_ref = bf16[16,64,256]{2,1,0:T(8,128)(2,1)S(1)} all-to-all(bf16[16,64,256]{2,1,0:T(8,128)(2,1)S(1)} %get-tuple-element.18), channel_id=1, replica_groups=mesh['ctx'=16,'tp'=2] {'ctx'}, dimensions={0} | all-to-all | bytes 1048576 | tf_op jit(solution)/shard_map/all_to_all | solution.py:458
  44.8 0.0 copy-done.3
  44.8 0.0 copy-start.1
  44.8 0.0 copy-start.2
  44.8 0.0 copy-start.8
  44.8 2.1 %shard_map.124 = (bf16[16,64,128]{2,1,0:T(8,128)(2,1)}, bf16[128,1024]{1,0:T(8,128)(2,1)}, bf16[128,1024]{1,0:T(8,128)(2,1)}) custom-call(bf16[16,64,256]{2,1,0:T(8,128)(2,1)S(1)} %all_to_all.15.both_ref, bf16[128,1024]{1,0:T(8,128)(2,1)S(1)} %copy-done.3, f32[34,128]{1,0:T(8,128)S(1)} %copy-done.7, bf16[128,256]{1,0:T(8,128)(2,1)S(1)} %copy-done.6, ...), custom_call_target="tpu_custom_call" | custom-call | flops 553648128 | bytes 4310016 | tf_op jit(solution)/shard_map/pallas_call | solution.py:442
  46.9 4.1 %all-to-all-start.2 = ((bf16[16,64,128]{2,1,0:T(8,128)(2,1)}), bf16[16,64,128]{2,1,0:T(8,128)(2,1)S(1)}, u32[]{:S(2)}, u32[]{:S(2)}) async-start(bf16[16,64,128]{2,1,0:T(8,128)(2,1)} %get-tuple-element.21), calls=%async_computation.2 | async-start | bytes 524288 | tf_op jit(solution)/shard_map/all_to_all | solution.py:458
  51.0 1.6 %collective-permute-start.1 = (bf16[128,1024]{1,0:T(8,128)(2,1)}, bf16[128,1024]{1,0:T(8,128)(2,1)S(1)}, u32[]{:S(2)}, u32[]{:S(2)}) collective-permute-start(bf16[128,1024]{1,0:T(8,128)(2,1)} %get-tuple-element.25), channel_id=1, source_target_pairs={{0,1},{1,0},{2,3},{3,2},{4,5},{5,4},{6,7},{7,6},{8,9},{9,8},{10,11... | collective-permute-start | bytes 786440 | tf_op jit(solution)/shard_map/ppermute | solution.py:464
  52.6 0.0 copy-start
  52.6 2.2 %copy-done = bf16[1024,2048]{1,0:T(8,128)(2,1)S(1)} copy-done((bf16[1024,2048]{1,0:T(8,128)(2,1)S(1)}, bf16[1024,2048]{1,0:T(8,128)(2,1)}, u32[]{:S(2)}) %copy-start) | copy-done | bytes 4194328
  54.8 1.0 %copy-done.4 = f32[1024,128]{1,0:T(8,128)S(1)} copy-done((f32[1024,128]{1,0:T(8,128)S(1)}, f32[1024,128]{1,0:T(8,128)}, u32[]{:S(2)}) %copy-start.4) | copy-done | bytes 524312
  55.8 0.9 %copy-done.5 = bf16[128,1024]{1,0:T(8,128)(2,1)S(1)} copy-done((bf16[128,1024]{1,0:T(8,128)(2,1)S(1)}, bf16[128,1024]{1,0:T(8,128)(2,1)}, u32[]{:S(2)}) %copy-start.5) | copy-done | bytes 262168
  56.8 1.4 %shard_map.125 = (f32[128,1024]{1,0:T(8,128)S(1)}, bf16[128,1024]{1,0:T(8,128)(2,1)}) custom-call(s32[1]{0:T(128)} %bitcast.1.rank_ref, bf16[128,1024]{1,0:T(8,128)(2,1)S(1)} %copy-done.5, bf16[16,64,256]{2,1,0:T(8,128)(2,1)S(1)} %all_to_all.15.both_ref, f32[1024,128]{1,0:T(8,128)S(1)} %copy-done.4, bf16[1024,2048]{1,0:T(8,128)(2,1)S(1)} %copy-done), custom_call_target="tpu_custom_call" | custom-call | flops 268435456 | bytes 6291456 | tf_op jit(solution)/shard_map/pallas_call | solution.py:442
  58.2 1.7 %collective-permute-done.1.other_ref = bf16[128,1024]{1,0:T(8,128)(2,1)S(1)} collective-permute-done((bf16[128,1024]{1,0:T(8,128)(2,1)}, bf16[128,1024]{1,0:T(8,128)(2,1)S(1)}, u32[]{:S(2)}, u32[]{:S(2)}) %collective-permute-start.1) | collective-permute-done | bytes 262176 | tf_op jit(solution)/shard_map/ppermute | solution.py:464
  59.9 1.2 %all-to-all-done.2.packed_ref = bf16[16,64,128]{2,1,0:T(8,128)(2,1)S(1)} async-done(((bf16[16,64,128]{2,1,0:T(8,128)(2,1)}), bf16[16,64,128]{2,1,0:T(8,128)(2,1)S(1)}, u32[]{:S(2)}, u32[]{:S(2)}) %all-to-all-start.2) | async-done | bytes 262176 | tf_op jit(solution)/shard_map/all_to_all | solution.py:458
  61.1 0.0 copy-done.1
  61.1 0.0 copy-done.2
  61.1 0.0 copy-done.8
  61.1 1.1 %shard_map.126 = (bf16[128,1024]{1,0:T(8,128)(2,1)}, bf16[128,1024]{1,0:T(8,128)(2,1)}, bf16[128,1024]{1,0:T(8,128)(2,1)}) custom-call(s32[1,128]{1,0:T(1,128)S(1)} %bitcast.3, bf16[16,64,128]{2,1,0:T(8,128)(2,1)S(1)} %all-to-all-done.2.packed_ref, bf16[128,1024]{1,0:T(8,128)(2,1)S(1)} %copy-done.1, bf16[128,1024]{1,0:T(8,128)(2,1)S(1)} %copy-done.2, ...), custom_call_target="tpu_custom_call" | custom-call | bytes 2359808 | tf_op jit(solution)/shard_map/pallas_call | solution.py:442
  (2 shorter events, 0.0 us)
Async XLA Ops:
  2.7 21.8 %all-to-all-start = ((bf16[16,128,128]{2,1,0:T(8,128)(2,1)}), bf16[16,128,128]{2,1,0:T(8,128)(2,1)S(1)}, u32[]{:S(2)}, u32[]{:S(2)}) async-start(bf16[16,128,128]{2,1,0:T(8,128)(2,1)} %shard_map.120), calls=%async_computation | async-start | bytes 1048576 | tf_op jit(solution)/shard_map/all_to_all | solution.py:458
  10.1 8.8 %collective-permute-start = (bf16[128,1024]{1,0:T(8,128)(2,1)}, bf16[128,1024]{1,0:T(8,128)(2,1)S(1)}, u32[]{:S(2)}, u32[]{:S(2)}) collective-permute-start(bf16[128,1024]{1,0:T(8,128)(2,1)} %own_ref.1), channel_id=1, source_target_pairs={{0,1},{1,0},{2,3},{3,2},{4,5},{5,4},{6,7},{7,6},{8,9},{9,8},{10,11... | collective-permute-start | bytes 786440 | tf_op jit(solution)/shard_map/ppermute | solution.py:464
  11.7 12.9 %copy-start.6 = (bf16[128,256]{1,0:T(8,128)(2,1)S(1)}, bf16[128,256]{1,0:T(8,128)(2,1)}, u32[]{:S(2)}) copy-start(bf16[128,256]{1,0:T(8,128)(2,1)} %constant.9.clone.dft_ref) | copy-start | bytes 196612
  11.7 12.9 %copy-start.7 = (f32[34,128]{1,0:T(8,128)S(1)}, f32[34,128]{1,0:T(8,128)}, u32[]{:S(2)}) copy-start(f32[34,128]{1,0:T(8,128)} %constant.8.clone.twist_ref) | copy-start | bytes 52228
  14.8 29.9 %copy-start.3 = (bf16[128,1024]{1,0:T(8,128)(2,1)S(1)}, bf16[128,1024]{1,0:T(8,128)(2,1)}, u32[]{:S(2)}) copy-start(bf16[128,1024]{1,0:T(8,128)(2,1)} %post_ref.3) | copy-start | bytes 786436
  44.8 16.3 %copy-start.1 = (bf16[128,1024]{1,0:T(8,128)(2,1)S(1)}, bf16[128,1024]{1,0:T(8,128)(2,1)}, u32[]{:S(2)}) copy-start(bf16[128,1024]{1,0:T(8,128)(2,1)} %pre_ref.3) | copy-start | bytes 786436
  44.8 16.3 %copy-start.2 = (bf16[128,1024]{1,0:T(8,128)(2,1)S(1)}, bf16[128,1024]{1,0:T(8,128)(2,1)}, u32[]{:S(2)}) copy-start(bf16[128,1024]{1,0:T(8,128)(2,1)} %feat_ref.3) | copy-start | bytes 786436
  44.8 16.3 %copy-start.8 = (s32[128]{0:T(128)S(1)}, s32[128]{0:T(128)}, u32[]{:S(2)}) copy-start(s32[128]{0:T(128)} %param.13) | copy-start | bytes 1540
  46.9 14.2 %all-to-all-start.2 = ((bf16[16,64,128]{2,1,0:T(8,128)(2,1)}), bf16[16,64,128]{2,1,0:T(8,128)(2,1)S(1)}, u32[]{:S(2)}, u32[]{:S(2)}) async-start(bf16[16,64,128]{2,1,0:T(8,128)(2,1)} %get-tuple-element.21), calls=%async_computation.2 | async-start | bytes 524288 | tf_op jit(solution)/shard_map/all_to_all | solution.py:458
  51.0 8.8 %collective-permute-start.1 = (bf16[128,1024]{1,0:T(8,128)(2,1)}, bf16[128,1024]{1,0:T(8,128)(2,1)S(1)}, u32[]{:S(2)}, u32[]{:S(2)}) collective-permute-start(bf16[128,1024]{1,0:T(8,128)(2,1)} %get-tuple-element.25), channel_id=1, source_target_pairs={{0,1},{1,0},{2,3},{3,2},{4,5},{5,4},{6,7},{7,6},{8,9},{9,8},{10,11... | collective-permute-start | bytes 786440 | tf_op jit(solution)/shard_map/ppermute | solution.py:464
  52.6 2.2 %copy-start = (bf16[1024,2048]{1,0:T(8,128)(2,1)S(1)}, bf16[1024,2048]{1,0:T(8,128)(2,1)}, u32[]{:S(2)}) copy-start(bf16[1024,2048]{1,0:T(8,128)(2,1)} %weight_hbm.1) | copy-start | bytes 12582916
  54.8 1.0 %copy-start.4 = (f32[1024,128]{1,0:T(8,128)S(1)}, f32[1024,128]{1,0:T(8,128)}, u32[]{:S(2)}) copy-start(f32[1024,128]{1,0:T(8,128)} %get-tuple-element.23.grad_ref) | copy-start | bytes 1572868
  55.8 0.9 %copy-start.5 = (bf16[128,1024]{1,0:T(8,128)(2,1)S(1)}, bf16[128,1024]{1,0:T(8,128)(2,1)}, u32[]{:S(2)}) copy-start(bf16[128,1024]{1,0:T(8,128)(2,1)} %get-tuple-element.22.gated_ref) | copy-start | bytes 786436

commit v9 on v8

--- a/solution.py
+++ b/solution.py
@@ -148,6 +148,10 @@
         out_ref[k] = mixed[k * width : (k + 1) * width].astype(BF16)
 
 
+def group_order(n):
+    return list(range(n - 1, -1, -1))
+
+
 def started(*copies):
     made = [pltpu.make_async_copy(*copy) for copy in copies]
     for copy in made:
@@ -230,7 +234,7 @@
     def transform(c):
         for kind in range(2):
             start = kind * width + c * step
-            blocks = [pair_ref[b, start : start + step] for b in range(n)]
+            blocks = [pair_ref[b, start : start + step] for b in group_order(n)]
             forward_blocks(
                 n, blocks, twist_ref, mid_ref.at[c], slice(kind * step, (kind + 1) * step)
             )
@@ -254,7 +258,7 @@
                 prod_ref.dtype
             )
         mid = inner_product(prod_ref.at[c], back)
-        for b, value in enumerate(inverse_blocks(n, mid, twist_ref)):
+        for b, value in zip(group_order(n), inverse_blocks(n, mid, twist_ref)):
             both_ref[b, at, :length] = value
 
 
@@ -288,7 +292,7 @@
     step = width // chunks
 
     def transform(c):
-        blocks = [both_ref[b, c * step : (c + 1) * step, length:] for b in range(n)]
+        blocks = [both_ref[b, c * step : (c + 1) * step, length:] for b in group_order(n)]
         forward_blocks(n, blocks, twist_ref, mid_ref.at[c], slice(0, step))
 
     transform(0)
@@ -308,7 +312,7 @@
                 prod_ref.dtype
             )
         mid = inner_product(prod_ref.at[c], back)
-        for b, value in enumerate(inverse_blocks(n, mid, twist_ref)):
+        for b, value in zip(group_order(n), inverse_blocks(n, mid, twist_ref)):
             out_ref[b, at] = value
         if chunks == 1:
             copies += started((out_ref, out_hbm, sems.at[2]))
@@ -455,7 +459,14 @@
 
 
 def exchange(block):
-    return lax.all_to_all(block, "ctx", split_axis=0, concat_axis=0, tiled=True)
+    return lax.all_to_all(
+        block,
+        "ctx",
+        split_axis=0,
+        concat_axis=0,
+        tiled=True,
+        axis_index_groups=[group_order(block.shape[0])],
+    )
 
 
 def swap_tp(block):

time: 62.8 us -> 62.1 us (0.989)
  waiting for transfers between devices: 8.62 us -> 5.26 us
  starting transfers between devices: 14.6 us -> 17.7 us
    all_to_all x2, starting transfers between devices: 11.5 us -> 14.7 us  [exchange(): lax.all_to_all(block, 'ctx', split_axis=0, concat_axis=0, tiled=True, axi...]
    all_to_all x2, waiting for transfers between devices: 2.84 us -> 0.01 us  [exchange(): lax.all_to_all(block, 'ctx', split_axis=0, concat_axis=0, tiled=True, axi...]
  transfers between devices with their start and end apart: 4 -> 4, of which waited for: 4 -> 2; matrix products, arithmetic and copies ran while one was open for 0% -> 0% of each run, Pallas kernels for 14% -> 14%
where the time goes in v9:
time: 62.1 us; the launch traced here: 61.5 us
  blocking collectives  18 us (29%)
  starting transfers between devices  17.7 us (29%)
  Pallas kernels  15.6 us (25%)
  waiting for transfers between devices  5.26 us (8%)
  local copies, waits for them, and re-layouts  4.2 us (7%)
  between operations  0.71 us (1%)
    all_to_all x1, blocking collectives, exchange(): lax.all_to_all(block, 'ctx', split_axis=0, concat_axis=0, tiled=True, axi...  18 us
    pallas_call x7, Pallas kernels, call(): pl.pallas_call(kernel, out_shape=outs, grid_spec=pltpu.PrefetchScalarGrid...  15.6 us
    all_to_all x2, starting transfers between devices, exchange(): lax.all_to_all(block, 'ctx', split_axis=0, concat_axis=0, tiled=True, axi...  14.7 us
    ppermute x2, waiting for transfers between devices, swap_tp(): return lax.ppermute(block, 'tp', [(0, 1), (1, 0)])  5.25 us
    unnamed x18, local copies, waits for them, and re-layouts  4.2 us
    ppermute x2, starting transfers between devices, swap_tp(): return lax.ppermute(block, 'tp', [(0, 1), (1, 0)])  3.05 us
  transfers between devices with their start and end apart: 4, of which 2 were waited for; matrix products, arithmetic and copies ran while one was open for 0% of the time, Pallas kernels for 14%

profile of v9, /device:TPU:0, one launch (start us, length us, event | category | flops | bytes accessed | tf_op | source)
XLA Modules:
  0.0 61.5 jit_solution(7089355464134486350)
XLA Ops:
  0.6 2.1 %shard_map.120 = bf16[16,128,128]{2,1,0:T(8,128)(2,1)} custom-call(s32[1,128]{1,0:T(1,128)} %bitcast.2, bf16[128,1024]{1,0:T(8,128)(2,1)} %pre_ref.3, bf16[128,1024]{1,0:T(8,128)(2,1)} %feat_ref.3, f32[128,1024]{1,0:T(8,128)} %filt_ref.1), custom_call_target="tpu_custom_call" | custom-call | bytes 1573376 | tf_op jit(solution)/shard_map/pallas_call | solution.py:446
  2.7 8.9 %all-to-all-start = ((bf16[16,128,128]{2,1,0:T(8,128)(2,1)}), bf16[16,128,128]{2,1,0:T(8,128)(2,1)S(1)}, u32[]{:S(2)}, u32[]{:S(2)}) async-start(bf16[16,128,128]{2,1,0:T(8,128)(2,1)} %shard_map.120), calls=%async_computation | async-start | bytes 1048576 | tf_op jit(solution)/shard_map/all_to_all | solution.py:462
  11.6 1.5 %collective-permute-start = (bf16[128,1024]{1,0:T(8,128)(2,1)}, bf16[128,1024]{1,0:T(8,128)(2,1)S(1)}, u32[]{:S(2)}, u32[]{:S(2)}) collective-permute-start(bf16[128,1024]{1,0:T(8,128)(2,1)} %own_ref.1), channel_id=1, source_target_pairs={{0,1},{1,0},{2,3},{3,2},{4,5},{5,4},{6,7},{7,6},{8,9},{9,8},{10,11... | collective-permute-start | bytes 786440 | tf_op jit(solution)/shard_map/ppermute | solution.py:475
  13.1 0.0 copy-start.6
  13.1 0.0 copy-start.7
  13.2 3.1 %shard_map.121.part_ref = f32[1024,128]{1,0:T(8,128)S(1)} custom-call(s32[1]{0:T(128)} %bitcast.1.rank_ref, bf16[128,1024]{1,0:T(8,128)(2,1)} %own_ref.1, bf16[1024,2048]{1,0:T(8,128)(2,1)} %weight_hbm.1), custom_call_target="tpu_custom_call" | custom-call | flops 268435456 | bytes 4980736 | tf_op jit(solution)/shard_map/pallas_call | solution.py:446
  16.3 0.0 copy-start.3
  16.3 3.8 %collective-permute-done.other_ref = bf16[128,1024]{1,0:T(8,128)(2,1)S(1)} collective-permute-done((bf16[128,1024]{1,0:T(8,128)(2,1)}, bf16[128,1024]{1,0:T(8,128)(2,1)S(1)}, u32[]{:S(2)}, u32[]{:S(2)}) %collective-permute-start) | collective-permute-done | bytes 262176 | tf_op jit(solution)/shard_map/ppermute | solution.py:475
  20.1 4.0 %shard_map.122 = (f32[1024,128]{1,0:T(8,128)}, bf16[16,64,128]{2,1,0:T(8,128)(2,1)S(1)}, bf16[1024,1024]{1,0:T(8,128)(2,1)S(1)}) custom-call(s32[1]{0:T(128)} %bitcast.1.rank_ref, bf16[128,1024]{1,0:T(8,128)(2,1)S(1)} %collective-permute-done.other_ref, bf16[1024,2048]{1,0:T(8,128)(2,1)} %weight_hbm.1, f32[1024,128]{1,0:T(8,128)S(1)} %shard_map.121.part_ref, ...), custom_call_target="tpu_custom_call" | custom-call | flops 268435456 | bytes 8126464 | tf_op jit(solution)/shard_map/pallas_call | solution.py:446
  24.1 0.0 all-to-all-done.pair_ref
  24.1 0.0 copy-done.6
  24.1 0.0 copy-done.7
  24.2 1.8 %shard_map.123 = (bf16[16,64,256]{2,1,0:T(8,128)(2,1)S(1)}, bf16[17,64,256]{2,1,0:T(8,128)(2,1)S(1)}) custom-call(bf16[16,128,128]{2,1,0:T(8,128)(2,1)S(1)} %all-to-all-done.pair_ref, bf16[16,64,128]{2,1,0:T(8,128)(2,1)S(1)} %get-tuple-element.17.grad_ref, f32[34,128]{1,0:T(8,128)S(1)} %copy-done.7, bf16[128,256]{1,0:T(8,128)(2,1)S(1)} %copy-done.6), custom_call_target="tpu_custom_call" | custom-call | flops 427819008 | bytes 1950720 | tf_op jit(solution)/shard_map/pallas_call | solution.py:446
  26.0 18.0 %all_to_all.15.both_ref = bf16[16,64,256]{2,1,0:T(8,128)(2,1)S(1)} all-to-all(bf16[16,64,256]{2,1,0:T(8,128)(2,1)S(1)} %get-tuple-element.18), channel_id=1, replica_groups={{30,28,26,24,22,20,18,16,14,12,10,8,6,4,2,0},{31,29,27,25,23,21,19,17,1..., dimensions={0} | all-to-all | bytes 1048576 | tf_op jit(solution)/shard_map/all_to_all | solution.py:462
  43.9 0.0 copy-done.3
  43.9 0.0 copy-start.1
  43.9 0.0 copy-start.2
  43.9 0.0 copy-start.8
  44.0 2.1 %shard_map.124 = (bf16[16,64,128]{2,1,0:T(8,128)(2,1)}, bf16[128,1024]{1,0:T(8,128)(2,1)}, bf16[128,1024]{1,0:T(8,128)(2,1)}) custom-call(bf16[16,64,256]{2,1,0:T(8,128)(2,1)S(1)} %all_to_all.15.both_ref, bf16[128,1024]{1,0:T(8,128)(2,1)S(1)} %copy-done.3, f32[34,128]{1,0:T(8,128)S(1)} %copy-done.7, bf16[128,256]{1,0:T(8,128)(2,1)S(1)} %copy-done.6, ...), custom_call_target="tpu_custom_call" | custom-call | flops 553648128 | bytes 4310016 | tf_op jit(solution)/shard_map/pallas_call | solution.py:446
  46.1 5.8 %all-to-all-start.2 = ((bf16[16,64,128]{2,1,0:T(8,128)(2,1)}), bf16[16,64,128]{2,1,0:T(8,128)(2,1)S(1)}, u32[]{:S(2)}, u32[]{:S(2)}) async-start(bf16[16,64,128]{2,1,0:T(8,128)(2,1)} %get-tuple-element.21), calls=%async_computation.2 | async-start | bytes 524288 | tf_op jit(solution)/shard_map/all_to_all | solution.py:462
  51.9 1.5 %collective-permute-start.1 = (bf16[128,1024]{1,0:T(8,128)(2,1)}, bf16[128,1024]{1,0:T(8,128)(2,1)S(1)}, u32[]{:S(2)}, u32[]{:S(2)}) collective-permute-start(bf16[128,1024]{1,0:T(8,128)(2,1)} %get-tuple-element.25), channel_id=1, source_target_pairs={{0,1},{1,0},{2,3},{3,2},{4,5},{5,4},{6,7},{7,6},{8,9},{9,8},{10,11... | collective-permute-start | bytes 786440 | tf_op jit(solution)/shard_map/ppermute | solution.py:475
  53.4 0.0 copy-start
  53.4 2.2 %copy-done = bf16[1024,2048]{1,0:T(8,128)(2,1)S(1)} copy-done((bf16[1024,2048]{1,0:T(8,128)(2,1)S(1)}, bf16[1024,2048]{1,0:T(8,128)(2,1)}, u32[]{:S(2)}) %copy-start) | copy-done | bytes 4194328
  55.6 1.0 %copy-done.4 = f32[1024,128]{1,0:T(8,128)S(1)} copy-done((f32[1024,128]{1,0:T(8,128)S(1)}, f32[1024,128]{1,0:T(8,128)}, u32[]{:S(2)}) %copy-start.4) | copy-done | bytes 524312
  56.6 0.9 %copy-done.5 = bf16[128,1024]{1,0:T(8,128)(2,1)S(1)} copy-done((bf16[128,1024]{1,0:T(8,128)(2,1)S(1)}, bf16[128,1024]{1,0:T(8,128)(2,1)}, u32[]{:S(2)}) %copy-start.5) | copy-done | bytes 262168
  57.6 1.4 %shard_map.125 = (f32[128,1024]{1,0:T(8,128)S(1)}, bf16[128,1024]{1,0:T(8,128)(2,1)}) custom-call(s32[1]{0:T(128)} %bitcast.1.rank_ref, bf16[128,1024]{1,0:T(8,128)(2,1)S(1)} %copy-done.5, bf16[16,64,256]{2,1,0:T(8,128)(2,1)S(1)} %all_to_all.15.both_ref, f32[1024,128]{1,0:T(8,128)S(1)} %copy-done.4, bf16[1024,2048]{1,0:T(8,128)(2,1)S(1)} %copy-done), custom_call_target="tpu_custom_call" | custom-call | flops 268435456 | bytes 6291456 | tf_op jit(solution)/shard_map/pallas_call | solution.py:446
  58.9 1.4 %collective-permute-done.1.other_ref = bf16[128,1024]{1,0:T(8,128)(2,1)S(1)} collective-permute-done((bf16[128,1024]{1,0:T(8,128)(2,1)}, bf16[128,1024]{1,0:T(8,128)(2,1)S(1)}, u32[]{:S(2)}, u32[]{:S(2)}) %collective-permute-start.1) | collective-permute-done | bytes 262176 | tf_op jit(solution)/shard_map/ppermute | solution.py:475
  60.4 0.0 all-to-all-done.2.packed_ref
  60.4 0.0 copy-done.1
  60.4 0.0 copy-done.2
  60.4 0.0 copy-done.8
  60.4 1.1 %shard_map.126 = (bf16[128,1024]{1,0:T(8,128)(2,1)}, bf16[128,1024]{1,0:T(8,128)(2,1)}, bf16[128,1024]{1,0:T(8,128)(2,1)}) custom-call(s32[1,128]{1,0:T(1,128)S(1)} %bitcast.3, bf16[16,64,128]{2,1,0:T(8,128)(2,1)S(1)} %all-to-all-done.2.packed_ref, bf16[128,1024]{1,0:T(8,128)(2,1)S(1)} %copy-done.1, bf16[128,1024]{1,0:T(8,128)(2,1)S(1)} %copy-done.2, ...), custom_call_target="tpu_custom_call" | custom-call | bytes 2359808 | tf_op jit(solution)/shard_map/pallas_call | solution.py:446
  (2 shorter events, 0.0 us)
Async XLA Ops:
  2.7 21.4 %all-to-all-start = ((bf16[16,128,128]{2,1,0:T(8,128)(2,1)}), bf16[16,128,128]{2,1,0:T(8,128)(2,1)S(1)}, u32[]{:S(2)}, u32[]{:S(2)}) async-start(bf16[16,128,128]{2,1,0:T(8,128)(2,1)} %shard_map.120), calls=%async_computation | async-start | bytes 1048576 | tf_op jit(solution)/shard_map/all_to_all | solution.py:462
  11.6 8.5 %collective-permute-start = (bf16[128,1024]{1,0:T(8,128)(2,1)}, bf16[128,1024]{1,0:T(8,128)(2,1)S(1)}, u32[]{:S(2)}, u32[]{:S(2)}) collective-permute-start(bf16[128,1024]{1,0:T(8,128)(2,1)} %own_ref.1), channel_id=1, source_target_pairs={{0,1},{1,0},{2,3},{3,2},{4,5},{5,4},{6,7},{7,6},{8,9},{9,8},{10,11... | collective-permute-start | bytes 786440 | tf_op jit(solution)/shard_map/ppermute | solution.py:475
  13.1 11.0 %copy-start.6 = (bf16[128,256]{1,0:T(8,128)(2,1)S(1)}, bf16[128,256]{1,0:T(8,128)(2,1)}, u32[]{:S(2)}) copy-start(bf16[128,256]{1,0:T(8,128)(2,1)} %constant.9.clone.dft_ref) | copy-start | bytes 196612
  13.1 11.0 %copy-start.7 = (f32[34,128]{1,0:T(8,128)S(1)}, f32[34,128]{1,0:T(8,128)}, u32[]{:S(2)}) copy-start(f32[34,128]{1,0:T(8,128)} %constant.8.clone.twist_ref) | copy-start | bytes 52228
  16.3 27.6 %copy-start.3 = (bf16[128,1024]{1,0:T(8,128)(2,1)S(1)}, bf16[128,1024]{1,0:T(8,128)(2,1)}, u32[]{:S(2)}) copy-start(bf16[128,1024]{1,0:T(8,128)(2,1)} %post_ref.3) | copy-start | bytes 786436
  43.9 16.4 %copy-start.1 = (bf16[128,1024]{1,0:T(8,128)(2,1)S(1)}, bf16[128,1024]{1,0:T(8,128)(2,1)}, u32[]{:S(2)}) copy-start(bf16[128,1024]{1,0:T(8,128)(2,1)} %pre_ref.3) | copy-start | bytes 786436
  43.9 16.4 %copy-start.2 = (bf16[128,1024]{1,0:T(8,128)(2,1)S(1)}, bf16[128,1024]{1,0:T(8,128)(2,1)}, u32[]{:S(2)}) copy-start(bf16[128,1024]{1,0:T(8,128)(2,1)} %feat_ref.3) | copy-start | bytes 786436
  43.9 16.4 %copy-start.8 = (s32[128]{0:T(128)S(1)}, s32[128]{0:T(128)}, u32[]{:S(2)}) copy-start(s32[128]{0:T(128)} %param.13) | copy-start | bytes 1540
  46.1 14.3 %all-to-all-start.2 = ((bf16[16,64,128]{2,1,0:T(8,128)(2,1)}), bf16[16,64,128]{2,1,0:T(8,128)(2,1)S(1)}, u32[]{:S(2)}, u32[]{:S(2)}) async-start(bf16[16,64,128]{2,1,0:T(8,128)(2,1)} %get-tuple-element.21), calls=%async_computation.2 | async-start | bytes 524288 | tf_op jit(solution)/shard_map/all_to_all | solution.py:462
  51.9 8.5 %collective-permute-start.1 = (bf16[128,1024]{1,0:T(8,128)(2,1)}, bf16[128,1024]{1,0:T(8,128)(2,1)S(1)}, u32[]{:S(2)}, u32[]{:S(2)}) collective-permute-start(bf16[128,1024]{1,0:T(8,128)(2,1)} %get-tuple-element.25), channel_id=1, source_target_pairs={{0,1},{1,0},{2,3},{3,2},{4,5},{5,4},{6,7},{7,6},{8,9},{9,8},{10,11... | collective-permute-start | bytes 786440 | tf_op jit(solution)/shard_map/ppermute | solution.py:475
  53.4 2.2 %copy-start = (bf16[1024,2048]{1,0:T(8,128)(2,1)S(1)}, bf16[1024,2048]{1,0:T(8,128)(2,1)}, u32[]{:S(2)}) copy-start(bf16[1024,2048]{1,0:T(8,128)(2,1)} %weight_hbm.1) | copy-start | bytes 12582916
  55.6 1.0 %copy-start.4 = (f32[1024,128]{1,0:T(8,128)S(1)}, f32[1024,128]{1,0:T(8,128)}, u32[]{:S(2)}) copy-start(f32[1024,128]{1,0:T(8,128)} %get-tuple-element.23.grad_ref) | copy-start | bytes 1572868
  56.6 0.9 %copy-start.5 = (bf16[128,1024]{1,0:T(8,128)(2,1)S(1)}, bf16[128,1024]{1,0:T(8,128)(2,1)}, u32[]{:S(2)}) copy-start(bf16[128,1024]{1,0:T(8,128)(2,1)} %get-tuple-element.22.gated_ref) | copy-start | bytes 786436

commit v10 on v9

--- a/solution.py
+++ b/solution.py
@@ -149,7 +149,11 @@
 
 
 def group_order(n):
-    return list(range(n - 1, -1, -1))
+    return [*range(n // 2, n), *range(n // 2 - 1, -1, -1)]
+
+
+def group_places(n):
+    return [int(place) for place in np.argsort(group_order(n))]
 
 
 def started(*copies):
@@ -234,7 +238,7 @@
     def transform(c):
         for kind in range(2):
             start = kind * width + c * step
-            blocks = [pair_ref[b, start : start + step] for b in group_order(n)]
+            blocks = [pair_ref[b, start : start + step] for b in group_places(n)]
             forward_blocks(
                 n, blocks, twist_ref, mid_ref.at[c], slice(kind * step, (kind + 1) * step)
             )
@@ -258,7 +262,7 @@
                 prod_ref.dtype
             )
         mid = inner_product(prod_ref.at[c], back)
-        for b, value in zip(group_order(n), inverse_blocks(n, mid, twist_ref)):
+        for b, value in zip(group_places(n), inverse_blocks(n, mid, twist_ref)):
             both_ref[b, at, :length] = value
 
 
@@ -292,7 +296,7 @@
     step = width // chunks
 
     def transform(c):
-        blocks = [both_ref[b, c * step : (c + 1) * step, length:] for b in group_order(n)]
+        blocks = [both_ref[b, c * step : (c + 1) * step, length:] for b in group_places(n)]
         forward_blocks(n, blocks, twist_ref, mid_ref.at[c], slice(0, step))
 
     transform(0)
@@ -312,7 +316,7 @@
                 prod_ref.dtype
             )
         mid = inner_product(prod_ref.at[c], back)
-        for b, value in zip(group_order(n), inverse_blocks(n, mid, twist_ref)):
+        for b, value in zip(group_places(n), inverse_blocks(n, mid, twist_ref)):
             out_ref[b, at] = value
         if chunks == 1:
             copies += started((out_ref, out_hbm, sems.at[2]))
@@ -376,27 +380,22 @@
     home_ref[...] = part_products(copies, gated_ref[...], weight_ref)
 
 
-def finish(
+def input_grads(
     parts,
     token_ref,
     packed_ref,
     pre_ref,
     feat_ref,
-    home_ref,
-    other_ref,
     pre_grad_hbm,
     feat_grad_hbm,
-    out_hbm,
     pre_grad_ref,
     feat_grad_ref,
-    out_ref,
     sems,
 ):
-    out_ref[...] = (home_ref[...] + other_ref[...].astype(F32)).astype(BF16)
-    copies = started((out_ref, out_hbm, sems.at[2, 0]))
     keep = (token_ref[...] < BASES).astype(BF16)
     dests = packed_ref.shape[0] // parts
     cut = pre_ref.shape[1] // parts
+    copies = []
     for k in range(parts):
         at = pl.ds(k * cut, cut)
         blocks = packed_ref.at[pl.ds(k * dests, dests)]
@@ -409,6 +408,10 @@
         )
     for copy in copies:
         copy.wait()
+
+
+def add_halves(home_ref, other_ref, after_hbm, out_ref):
+    out_ref[...] = (home_ref[...] + other_ref[...].astype(F32)).astype(BF16)
 
 
 def dft_tables(n, length):
@@ -592,17 +595,23 @@
         prefetch=1,
     )
     flat = (length, channels)
-    grad_pre, grad_features, output = call(
-        functools.partial(finish, parts),
-        (pltpu.HBM(flat, BF16), pltpu.HBM(flat, BF16), pltpu.HBM((length, columns), BF16)),
-        (tokens, grad_back_in, pre_gate, features, home, other_part),
-        out_blocks=["hbm"] * 3,
+    grad_pre, grad_features = call(
+        functools.partial(input_grads, parts),
+        (pltpu.HBM(flat, BF16), pltpu.HBM(flat, BF16)),
+        (tokens, grad_back_in, pre_gate, features),
+        out_blocks=["hbm"] * 2,
         scratch=[
             pltpu.VMEM(flat, BF16),
             pltpu.VMEM(flat, BF16),
-            pltpu.VMEM((length, columns), BF16),
-            pltpu.SemaphoreType.DMA((3, parts)),
+            pltpu.SemaphoreType.DMA((2, parts)),
         ],
+    )
+    output = call(
+        add_halves,
+        pltpu.HBM((length, columns), BF16),
+        (home, other_part, grad_features),
+        blocks=[None, None, "hbm"],
+        from_hbm=(2,),
     )
     return (output, grad_post, grad_pre, grad_features)
 

time: 62.1 us -> 61.1 us (0.984)
  starting transfers between devices: 17.7 us -> 15.2 us
  waiting for transfers between devices: 5.26 us -> 6.33 us
    all_to_all x2, starting transfers between devices: 14.7 us -> 12.1 us  [exchange(): lax.all_to_all(block, 'ctx', split_axis=0, concat_axis=0, tiled=True, axi...]
    all_to_all x2, waiting for transfers between devices: 0.01 us -> 2.51 us  [exchange(): lax.all_to_all(block, 'ctx', split_axis=0, concat_axis=0, tiled=True, axi...]
    ppermute x2, waiting for transfers between devices: 5.25 us -> 3.81 us  [swap_tp(): return lax.ppermute(block, 'tp', [(0, 1), (1, 0)])]
    pallas_call x7 -> x8, Pallas kernels: 15.6 us -> 16.2 us  [call(): pl.pallas_call(kernel, out_shape=outs, grid_spec=pltpu.PrefetchScalarGrid...]
  transfers between devices with their start and end apart: 4 -> 4, of which waited for: 2 -> 3; matrix products, arithmetic and copies ran while one was open for 0% -> 0% of each run, Pallas kernels for 14% -> 16%
where the time goes in v10:
time: 61.1 us; the launch traced here: 60.5 us
  blocking collectives  17.9 us (29%)
  Pallas kernels  16.2 us (27%)
  starting transfers between devices  15.2 us (25%)
  waiting for transfers between devices  6.33 us (10%)
  local copies, waits for them, and re-layouts  4.2 us (7%)
  between operations  0.71 us (1%)
    all_to_all x1, blocking collectives, exchange(): lax.all_to_all(block, 'ctx', split_axis=0, concat_axis=0, tiled=True, axi...  17.9 us
    pallas_call x8, Pallas kernels, call(): pl.pallas_call(kernel, out_shape=outs, grid_spec=pltpu.PrefetchScalarGrid...  16.2 us
    all_to_all x2, starting transfers between devices, exchange(): lax.all_to_all(block, 'ctx', split_axis=0, concat_axis=0, tiled=True, axi...  12.1 us
    unnamed x18, local copies, waits for them, and re-layouts  4.2 us
    ppermute x2, waiting for transfers between devices, swap_tp(): return lax.ppermute(block, 'tp', [(0, 1), (1, 0)])  3.81 us
    ppermute x2, starting transfers between devices, swap_tp(): return lax.ppermute(block, 'tp', [(0, 1), (1, 0)])  3.03 us
    all_to_all x2, waiting for transfers between devices, exchange(): lax.all_to_all(block, 'ctx', split_axis=0, concat_axis=0, tiled=True, axi...  2.51 us
  transfers between devices with their start and end apart: 4, of which 3 were waited for; matrix products, arithmetic and copies ran while one was open for 0% of the time, Pallas kernels for 16%

profile of v10, /device:TPU:0, one launch (start us, length us, event | category | flops | bytes accessed | tf_op | source)
XLA Modules:
  0.0 60.5 jit_solution(16787957160371077712)
XLA Ops:
  0.6 2.1 %shard_map.120 = bf16[16,128,128]{2,1,0:T(8,128)(2,1)} custom-call(s32[1,128]{1,0:T(1,128)} %bitcast.2, bf16[128,1024]{1,0:T(8,128)(2,1)} %pre_ref.3, bf16[128,1024]{1,0:T(8,128)(2,1)} %feat_ref.3, f32[128,1024]{1,0:T(8,128)} %filt_ref.1), custom_call_target="tpu_custom_call" | custom-call | bytes 1573376 | tf_op jit(solution)/shard_map/pallas_call | solution.py:449
  2.7 7.9 %all-to-all-start = ((bf16[16,128,128]{2,1,0:T(8,128)(2,1)}), bf16[16,128,128]{2,1,0:T(8,128)(2,1)S(1)}, u32[]{:S(2)}, u32[]{:S(2)}) async-start(bf16[16,128,128]{2,1,0:T(8,128)(2,1)} %shard_map.120), calls=%async_computation | async-start | bytes 1048576 | tf_op jit(solution)/shard_map/all_to_all | solution.py:465
  10.6 1.5 %collective-permute-start = (bf16[128,1024]{1,0:T(8,128)(2,1)}, bf16[128,1024]{1,0:T(8,128)(2,1)S(1)}, u32[]{:S(2)}, u32[]{:S(2)}) collective-permute-start(bf16[128,1024]{1,0:T(8,128)(2,1)} %own_ref.1), channel_id=1, source_target_pairs={{0,1},{1,0},{2,3},{3,2},{4,5},{5,4},{6,7},{7,6},{8,9},{9,8},{10,11... | collective-permute-start | bytes 786440 | tf_op jit(solution)/shard_map/ppermute | solution.py:478
  12.1 0.0 copy-start.6
  12.1 0.0 copy-start.7
  12.1 3.1 %shard_map.121.part_ref = f32[1024,128]{1,0:T(8,128)S(1)} custom-call(s32[1]{0:T(128)} %bitcast.rank_ref, bf16[128,1024]{1,0:T(8,128)(2,1)} %own_ref.1, bf16[1024,2048]{1,0:T(8,128)(2,1)} %weight_hbm.1), custom_call_target="tpu_custom_call" | custom-call | flops 268435456 | bytes 4980736 | tf_op jit(solution)/shard_map/pallas_call | solution.py:449
  15.3 0.0 copy-start.3
  15.3 3.8 %collective-permute-done.other_ref = bf16[128,1024]{1,0:T(8,128)(2,1)S(1)} collective-permute-done((bf16[128,1024]{1,0:T(8,128)(2,1)}, bf16[128,1024]{1,0:T(8,128)(2,1)S(1)}, u32[]{:S(2)}, u32[]{:S(2)}) %collective-permute-start) | collective-permute-done | bytes 262176 | tf_op jit(solution)/shard_map/ppermute | solution.py:478
  19.1 4.0 %shard_map.122 = (f32[1024,128]{1,0:T(8,128)}, bf16[16,64,128]{2,1,0:T(8,128)(2,1)S(1)}, bf16[1024,1024]{1,0:T(8,128)(2,1)S(1)}) custom-call(s32[1]{0:T(128)} %bitcast.rank_ref, bf16[128,1024]{1,0:T(8,128)(2,1)S(1)} %collective-permute-done.other_ref, bf16[1024,2048]{1,0:T(8,128)(2,1)} %weight_hbm.1, f32[1024,128]{1,0:T(8,128)S(1)} %shard_map.121.part_ref, ...), custom_call_target="tpu_custom_call" | custom-call | flops 268435456 | bytes 8126464 | tf_op jit(solution)/shard_map/pallas_call | solution.py:449
  23.1 1.3 %all-to-all-done.pair_ref = bf16[16,128,128]{2,1,0:T(8,128)(2,1)S(1)} async-done(((bf16[16,128,128]{2,1,0:T(8,128)(2,1)}), bf16[16,128,128]{2,1,0:T(8,128)(2,1)S(1)}, u32[]{:S(2)}, u32[]{:S(2)}) %all-to-all-start) | async-done | bytes 524320 | tf_op jit(solution)/shard_map/all_to_all | solution.py:465
  24.5 0.0 copy-done.6
  24.5 0.0 copy-done.7
  24.5 1.8 %shard_map.123 = (bf16[16,64,256]{2,1,0:T(8,128)(2,1)S(1)}, bf16[17,64,256]{2,1,0:T(8,128)(2,1)S(1)}) custom-call(bf16[16,128,128]{2,1,0:T(8,128)(2,1)S(1)} %all-to-all-done.pair_ref, bf16[16,64,128]{2,1,0:T(8,128)(2,1)S(1)} %get-tuple-element.16.grad_ref, f32[34,128]{1,0:T(8,128)S(1)} %copy-done.7, bf16[128,256]{1,0:T(8,128)(2,1)S(1)} %copy-done.6), custom_call_target="tpu_custom_call" | custom-call | flops 427819008 | bytes 1950720 | tf_op jit(solution)/shard_map/pallas_call | solution.py:449
  26.3 17.9 %all_to_all.15.both_ref = bf16[16,64,256]{2,1,0:T(8,128)(2,1)S(1)} all-to-all(bf16[16,64,256]{2,1,0:T(8,128)(2,1)S(1)} %get-tuple-element.17), channel_id=1, replica_groups={{16,18,20,22,24,26,28,30,14,12,10,8,6,4,2,0},{17,19,21,23,25,27,29,31,1..., dimensions={0} | all-to-all | bytes 1048576 | tf_op jit(solution)/shard_map/all_to_all | solution.py:465
  44.2 0.0 copy-done.3
  44.2 0.0 copy-start.1
  44.2 0.0 copy-start.2
  44.2 0.0 copy-start.8
  44.2 2.1 %shard_map.124 = (bf16[16,64,128]{2,1,0:T(8,128)(2,1)}, bf16[128,1024]{1,0:T(8,128)(2,1)}, bf16[128,1024]{1,0:T(8,128)(2,1)}) custom-call(bf16[16,64,256]{2,1,0:T(8,128)(2,1)S(1)} %all_to_all.15.both_ref, bf16[128,1024]{1,0:T(8,128)(2,1)S(1)} %copy-done.3, f32[34,128]{1,0:T(8,128)S(1)} %copy-done.7, bf16[128,256]{1,0:T(8,128)(2,1)S(1)} %copy-done.6, ...), custom_call_target="tpu_custom_call" | custom-call | flops 553648128 | bytes 4310016 | tf_op jit(solution)/shard_map/pallas_call | solution.py:449
  46.3 4.3 %all-to-all-start.2 = ((bf16[16,64,128]{2,1,0:T(8,128)(2,1)}), bf16[16,64,128]{2,1,0:T(8,128)(2,1)S(1)}, u32[]{:S(2)}, u32[]{:S(2)}) async-start(bf16[16,64,128]{2,1,0:T(8,128)(2,1)} %get-tuple-element.24), calls=%async_computation.2 | async-start | bytes 524288 | tf_op jit(solution)/shard_map/all_to_all | solution.py:465
  50.6 1.5 %collective-permute-start.1 = (bf16[128,1024]{1,0:T(8,128)(2,1)}, bf16[128,1024]{1,0:T(8,128)(2,1)S(1)}, u32[]{:S(2)}, u32[]{:S(2)}) collective-permute-start(bf16[128,1024]{1,0:T(8,128)(2,1)} %get-tuple-element.23), channel_id=1, source_target_pairs={{0,1},{1,0},{2,3},{3,2},{4,5},{5,4},{6,7},{7,6},{8,9},{9,8},{10,11... | collective-permute-start | bytes 786440 | tf_op jit(solution)/shard_map/ppermute | solution.py:478
  52.1 2.2 %copy-done = bf16[1024,2048]{1,0:T(8,128)(2,1)S(1)} copy-done((bf16[1024,2048]{1,0:T(8,128)(2,1)S(1)}, bf16[1024,2048]{1,0:T(8,128)(2,1)}, u32[]{:S(2)}) %copy-start) | copy-done | bytes 4194328
  54.3 1.0 %copy-done.4 = f32[1024,128]{1,0:T(8,128)S(1)} copy-done((f32[1024,128]{1,0:T(8,128)S(1)}, f32[1024,128]{1,0:T(8,128)}, u32[]{:S(2)}) %copy-start.4) | copy-done | bytes 524312
  55.3 0.9 %copy-done.5 = bf16[128,1024]{1,0:T(8,128)(2,1)S(1)} copy-done((bf16[128,1024]{1,0:T(8,128)(2,1)S(1)}, bf16[128,1024]{1,0:T(8,128)(2,1)}, u32[]{:S(2)}) %copy-start.5) | copy-done | bytes 262168
  56.3 1.4 %shard_map.125 = (f32[128,1024]{1,0:T(8,128)S(1)}, bf16[128,1024]{1,0:T(8,128)(2,1)}) custom-call(s32[1]{0:T(128)} %bitcast.rank_ref, bf16[128,1024]{1,0:T(8,128)(2,1)S(1)} %copy-done.5, bf16[16,64,256]{2,1,0:T(8,128)(2,1)S(1)} %all_to_all.15.both_ref, f32[1024,128]{1,0:T(8,128)S(1)} %copy-done.4, bf16[1024,2048]{1,0:T(8,128)(2,1)S(1)} %copy-done), custom_call_target="tpu_custom_call" | custom-call | flops 268435456 | bytes 6291456 | tf_op jit(solution)/shard_map/pallas_call | solution.py:449
  57.6 1.2 %all-to-all-done.2.packed_ref = bf16[16,64,128]{2,1,0:T(8,128)(2,1)S(1)} async-done(((bf16[16,64,128]{2,1,0:T(8,128)(2,1)}), bf16[16,64,128]{2,1,0:T(8,128)(2,1)S(1)}, u32[]{:S(2)}, u32[]{:S(2)}) %all-to-all-start.2) | async-done | bytes 262176 | tf_op jit(solution)/shard_map/all_to_all | solution.py:465
  58.8 0.0 copy-done.1
  58.8 0.0 copy-done.2
  58.8 0.0 copy-done.8
  58.8 0.9 %shard_map.126 = (bf16[128,1024]{1,0:T(8,128)(2,1)}, bf16[128,1024]{1,0:T(8,128)(2,1)}) custom-call(s32[1,128]{1,0:T(1,128)S(1)} %bitcast.3, bf16[16,64,128]{2,1,0:T(8,128)(2,1)S(1)} %all-to-all-done.2.packed_ref, bf16[128,1024]{1,0:T(8,128)(2,1)S(1)} %copy-done.1, bf16[128,1024]{1,0:T(8,128)(2,1)S(1)} %copy-done.2), custom_call_target="tpu_custom_call" | custom-call | bytes 1311232 | tf_op jit(solution)/shard_map/pallas_call | solution.py:449
  59.8 0.0 collective-permute-done.1.other_ref
  59.8 0.7 %shard_map.127 = bf16[128,1024]{1,0:T(8,128)(2,1)} custom-call(f32[128,1024]{1,0:T(8,128)S(1)} %get-tuple-element.22.home_ref, bf16[128,1024]{1,0:T(8,128)(2,1)S(1)} %collective-permute-done.1.other_ref, bf16[128,1024]{1,0:T(8,128)(2,1)} %get-tuple-element.15.after_hbm), custom_call_target="tpu_custom_call" | custom-call | bytes 1310720 | tf_op jit(solution)/shard_map/pallas_call | solution.py:449
  (3 shorter events, 0.0 us)
Async XLA Ops:
  2.7 21.7 %all-to-all-start = ((bf16[16,128,128]{2,1,0:T(8,128)(2,1)}), bf16[16,128,128]{2,1,0:T(8,128)(2,1)S(1)}, u32[]{:S(2)}, u32[]{:S(2)}) async-start(bf16[16,128,128]{2,1,0:T(8,128)(2,1)} %shard_map.120), calls=%async_computation | async-start | bytes 1048576 | tf_op jit(solution)/shard_map/all_to_all | solution.py:465
  10.6 8.5 %collective-permute-start = (bf16[128,1024]{1,0:T(8,128)(2,1)}, bf16[128,1024]{1,0:T(8,128)(2,1)S(1)}, u32[]{:S(2)}, u32[]{:S(2)}) collective-permute-start(bf16[128,1024]{1,0:T(8,128)(2,1)} %own_ref.1), channel_id=1, source_target_pairs={{0,1},{1,0},{2,3},{3,2},{4,5},{5,4},{6,7},{7,6},{8,9},{9,8},{10,11... | collective-permute-start | bytes 786440 | tf_op jit(solution)/shard_map/ppermute | solution.py:478
  12.1 12.3 %copy-start.6 = (bf16[128,256]{1,0:T(8,128)(2,1)S(1)}, bf16[128,256]{1,0:T(8,128)(2,1)}, u32[]{:S(2)}) copy-start(bf16[128,256]{1,0:T(8,128)(2,1)} %constant.9.clone.dft_ref) | copy-start | bytes 196612
  12.1 12.3 %copy-start.7 = (f32[34,128]{1,0:T(8,128)S(1)}, f32[34,128]{1,0:T(8,128)}, u32[]{:S(2)}) copy-start(f32[34,128]{1,0:T(8,128)} %constant.8.clone.twist_ref) | copy-start | bytes 52228
  15.3 28.9 %copy-start.3 = (bf16[128,1024]{1,0:T(8,128)(2,1)S(1)}, bf16[128,1024]{1,0:T(8,128)(2,1)}, u32[]{:S(2)}) copy-start(bf16[128,1024]{1,0:T(8,128)(2,1)} %post_ref.3) | copy-start | bytes 786436
  44.2 14.6 %copy-start.1 = (bf16[128,1024]{1,0:T(8,128)(2,1)S(1)}, bf16[128,1024]{1,0:T(8,128)(2,1)}, u32[]{:S(2)}) copy-start(bf16[128,1024]{1,0:T(8,128)(2,1)} %pre_ref.3) | copy-start | bytes 786436
  44.2 14.6 %copy-start.2 = (bf16[128,1024]{1,0:T(8,128)(2,1)S(1)}, bf16[128,1024]{1,0:T(8,128)(2,1)}, u32[]{:S(2)}) copy-start(bf16[128,1024]{1,0:T(8,128)(2,1)} %feat_ref.3) | copy-start | bytes 786436
  44.2 14.6 %copy-start.8 = (s32[128]{0:T(128)S(1)}, s32[128]{0:T(128)}, u32[]{:S(2)}) copy-start(s32[128]{0:T(128)} %param.13) | copy-start | bytes 1540
  46.3 12.5 %all-to-all-start.2 = ((bf16[16,64,128]{2,1,0:T(8,128)(2,1)}), bf16[16,64,128]{2,1,0:T(8,128)(2,1)S(1)}, u32[]{:S(2)}, u32[]{:S(2)}) async-start(bf16[16,64,128]{2,1,0:T(8,128)(2,1)} %get-tuple-element.24), calls=%async_computation.2 | async-start | bytes 524288 | tf_op jit(solution)/shard_map/all_to_all | solution.py:465
  50.6 9.2 %collective-permute-start.1 = (bf16[128,1024]{1,0:T(8,128)(2,1)}, bf16[128,1024]{1,0:T(8,128)(2,1)S(1)}, u32[]{:S(2)}, u32[]{:S(2)}) collective-permute-start(bf16[128,1024]{1,0:T(8,128)(2,1)} %get-tuple-element.23), channel_id=1, source_target_pairs={{0,1},{1,0},{2,3},{3,2},{4,5},{5,4},{6,7},{7,6},{8,9},{9,8},{10,11... | collective-permute-start | bytes 786440 | tf_op jit(solution)/shard_map/ppermute | solution.py:478
  52.1 2.2 %copy-start = (bf16[1024,2048]{1,0:T(8,128)(2,1)S(1)}, bf16[1024,2048]{1,0:T(8,128)(2,1)}, u32[]{:S(2)}) copy-start(bf16[1024,2048]{1,0:T(8,128)(2,1)} %weight_hbm.1) | copy-start | bytes 12582916
  54.3 1.0 %copy-start.4 = (f32[1024,128]{1,0:T(8,128)S(1)}, f32[1024,128]{1,0:T(8,128)}, u32[]{:S(2)}) copy-start(f32[1024,128]{1,0:T(8,128)} %get-tuple-element.21.grad_ref) | copy-start | bytes 1572868
  55.3 0.9 %copy-start.5 = (bf16[128,1024]{1,0:T(8,128)(2,1)S(1)}, bf16[128,1024]{1,0:T(8,128)(2,1)}, u32[]{:S(2)}) copy-start(bf16[128,1024]{1,0:T(8,128)(2,1)} %get-tuple-element.20.gated_ref) | copy-start | bytes 786436

commit v11 on v9

--- a/solution.py
+++ b/solution.py
@@ -149,7 +149,12 @@
 
 
 def group_order(n):
-    return list(range(n - 1, -1, -1))
+    half = n // 2
+    return [rank for i in range(half) for rank in (half + i, half - 1 - i)]
+
+
+def group_places(n):
+    return [int(place) for place in np.argsort(group_order(n))]
 
 
 def started(*copies):
@@ -234,7 +239,7 @@
     def transform(c):
         for kind in range(2):
             start = kind * width + c * step
-            blocks = [pair_ref[b, start : start + step] for b in group_order(n)]
+            blocks = [pair_ref[b, start : start + step] for b in group_places(n)]
             forward_blocks(
                 n, blocks, twist_ref, mid_ref.at[c], slice(kind * step, (kind + 1) * step)
             )
@@ -258,7 +263,7 @@
                 prod_ref.dtype
             )
         mid = inner_product(prod_ref.at[c], back)
-        for b, value in zip(group_order(n), inverse_blocks(n, mid, twist_ref)):
+        for b, value in zip(group_places(n), inverse_blocks(n, mid, twist_ref)):
             both_ref[b, at, :length] = value
 
 
@@ -292,7 +297,7 @@
     step = width // chunks
 
     def transform(c):
-        blocks = [both_ref[b, c * step : (c + 1) * step, length:] for b in group_order(n)]
+        blocks = [both_ref[b, c * step : (c + 1) * step, length:] for b in group_places(n)]
         forward_blocks(n, blocks, twist_ref, mid_ref.at[c], slice(0, step))
 
     transform(0)
@@ -312,7 +317,7 @@
                 prod_ref.dtype
             )
         mid = inner_product(prod_ref.at[c], back)
-        for b, value in zip(group_order(n), inverse_blocks(n, mid, twist_ref)):
+        for b, value in zip(group_places(n), inverse_blocks(n, mid, twist_ref)):
             out_ref[b, at] = value
         if chunks == 1:
             copies += started((out_ref, out_hbm, sems.at[2]))

time: 62.1 us -> 60.7 us (0.977)
  starting transfers between devices: 17.7 us -> 16.4 us
    all_to_all x2, starting transfers between devices: 14.7 us -> 13.4 us  [exchange(): lax.all_to_all(block, 'ctx', split_axis=0, concat_axis=0, tiled=True, axi...]
  transfers between devices with their start and end apart: 4 -> 4, of which waited for: 2 -> 3; matrix products, arithmetic and copies ran while one was open for 0% -> 0% of each run, Pallas kernels for 14% -> 14%
where the time goes in v11:
time: 60.7 us; the launch traced here: 60.1 us
  blocking collectives  17.5 us (29%)
  starting transfers between devices  16.4 us (27%)
  Pallas kernels  15.6 us (26%)
  waiting for transfers between devices  5.67 us (9%)
  local copies, waits for them, and re-layouts  4.2 us (7%)
  between operations  0.7 us (1%)
    all_to_all x1, blocking collectives, exchange(): lax.all_to_all(block, 'ctx', split_axis=0, concat_axis=0, tiled=True, axi...  17.5 us
    pallas_call x7, Pallas kernels, call(): pl.pallas_call(kernel, out_shape=outs, grid_spec=pltpu.PrefetchScalarGrid...  15.6 us
    all_to_all x2, starting transfers between devices, exchange(): lax.all_to_all(block, 'ctx', split_axis=0, concat_axis=0, tiled=True, axi...  13.4 us
    ppermute x2, waiting for transfers between devices, swap_tp(): return lax.ppermute(block, 'tp', [(0, 1), (1, 0)])  5.25 us
    unnamed x18, local copies, waits for them, and re-layouts  4.2 us
    ppermute x2, starting transfers between devices, swap_tp(): return lax.ppermute(block, 'tp', [(0, 1), (1, 0)])  3.04 us
  transfers between devices with their start and end apart: 4, of which 3 were waited for; matrix products, arithmetic and copies ran while one was open for 0% of the time, Pallas kernels for 14%

profile of v11, /device:TPU:0, one launch (start us, length us, event | category | flops | bytes accessed | tf_op | source)
XLA Modules:
  0.0 60.1 jit_solution(1588880062400137680)
XLA Ops:
  0.6 2.1 %shard_map.120 = bf16[16,128,128]{2,1,0:T(8,128)(2,1)} custom-call(s32[1,128]{1,0:T(1,128)} %bitcast.2, bf16[128,1024]{1,0:T(8,128)(2,1)} %pre_ref.3, bf16[128,1024]{1,0:T(8,128)(2,1)} %feat_ref.3, f32[128,1024]{1,0:T(8,128)} %filt_ref.1), custom_call_target="tpu_custom_call" | custom-call | bytes 1573376 | tf_op jit(solution)/shard_map/pallas_call | solution.py:451
  2.7 7.9 %all-to-all-start = ((bf16[16,128,128]{2,1,0:T(8,128)(2,1)}), bf16[16,128,128]{2,1,0:T(8,128)(2,1)S(1)}, u32[]{:S(2)}, u32[]{:S(2)}) async-start(bf16[16,128,128]{2,1,0:T(8,128)(2,1)} %shard_map.120), calls=%async_computation | async-start | bytes 1048576 | tf_op jit(solution)/shard_map/all_to_all | solution.py:467
  10.6 1.5 %collective-permute-start = (bf16[128,1024]{1,0:T(8,128)(2,1)}, bf16[128,1024]{1,0:T(8,128)(2,1)S(1)}, u32[]{:S(2)}, u32[]{:S(2)}) collective-permute-start(bf16[128,1024]{1,0:T(8,128)(2,1)} %own_ref.1), channel_id=1, source_target_pairs={{0,1},{1,0},{2,3},{3,2},{4,5},{5,4},{6,7},{7,6},{8,9},{9,8},{10,11... | collective-permute-start | bytes 786440 | tf_op jit(solution)/shard_map/ppermute | solution.py:480
  12.1 0.0 copy-start.6
  12.1 0.0 copy-start.7
  12.1 3.1 %shard_map.121.part_ref = f32[1024,128]{1,0:T(8,128)S(1)} custom-call(s32[1]{0:T(128)} %bitcast.1.rank_ref, bf16[128,1024]{1,0:T(8,128)(2,1)} %own_ref.1, bf16[1024,2048]{1,0:T(8,128)(2,1)} %weight_hbm.1), custom_call_target="tpu_custom_call" | custom-call | flops 268435456 | bytes 4980736 | tf_op jit(solution)/shard_map/pallas_call | solution.py:451
  15.3 0.0 copy-start.3
  15.3 3.8 %collective-permute-done.other_ref = bf16[128,1024]{1,0:T(8,128)(2,1)S(1)} collective-permute-done((bf16[128,1024]{1,0:T(8,128)(2,1)}, bf16[128,1024]{1,0:T(8,128)(2,1)S(1)}, u32[]{:S(2)}, u32[]{:S(2)}) %collective-permute-start) | collective-permute-done | bytes 262176 | tf_op jit(solution)/shard_map/ppermute | solution.py:480
  19.1 4.0 %shard_map.122 = (f32[1024,128]{1,0:T(8,128)}, bf16[16,64,128]{2,1,0:T(8,128)(2,1)S(1)}, bf16[1024,1024]{1,0:T(8,128)(2,1)S(1)}) custom-call(s32[1]{0:T(128)} %bitcast.1.rank_ref, bf16[128,1024]{1,0:T(8,128)(2,1)S(1)} %collective-permute-done.other_ref, bf16[1024,2048]{1,0:T(8,128)(2,1)} %weight_hbm.1, f32[1024,128]{1,0:T(8,128)S(1)} %shard_map.121.part_ref, ...), custom_call_target="tpu_custom_call" | custom-call | flops 268435456 | bytes 8126464 | tf_op jit(solution)/shard_map/pallas_call | solution.py:451
  23.1 0.4 all-to-all-done.pair_ref
  23.5 0.0 copy-done.6
  23.5 0.0 copy-done.7
  23.5 1.8 %shard_map.123 = (bf16[16,64,256]{2,1,0:T(8,128)(2,1)S(1)}, bf16[17,64,256]{2,1,0:T(8,128)(2,1)S(1)}) custom-call(bf16[16,128,128]{2,1,0:T(8,128)(2,1)S(1)} %all-to-all-done.pair_ref, bf16[16,64,128]{2,1,0:T(8,128)(2,1)S(1)} %get-tuple-element.17.grad_ref, f32[34,128]{1,0:T(8,128)S(1)} %copy-done.7, bf16[128,256]{1,0:T(8,128)(2,1)S(1)} %copy-done.6), custom_call_target="tpu_custom_call" | custom-call | flops 427819008 | bytes 1950720 | tf_op jit(solution)/shard_map/pallas_call | solution.py:451
  25.3 17.5 %all_to_all.15.both_ref = bf16[16,64,256]{2,1,0:T(8,128)(2,1)S(1)} all-to-all(bf16[16,64,256]{2,1,0:T(8,128)(2,1)S(1)} %get-tuple-element.18), channel_id=1, replica_groups={{16,14,18,12,20,10,22,8,24,6,26,4,28,2,30,0},{17,15,19,13,21,11,23,9,25..., dimensions={0} | all-to-all | bytes 1048576 | tf_op jit(solution)/shard_map/all_to_all | solution.py:467
  42.8 0.0 copy-done.3
  42.8 0.0 copy-start.1
  42.8 0.0 copy-start.2
  42.8 2.1 %shard_map.124 = (bf16[16,64,128]{2,1,0:T(8,128)(2,1)}, bf16[128,1024]{1,0:T(8,128)(2,1)}, bf16[128,1024]{1,0:T(8,128)(2,1)}) custom-call(bf16[16,64,256]{2,1,0:T(8,128)(2,1)S(1)} %all_to_all.15.both_ref, bf16[128,1024]{1,0:T(8,128)(2,1)S(1)} %copy-done.3, f32[34,128]{1,0:T(8,128)S(1)} %copy-done.7, bf16[128,256]{1,0:T(8,128)(2,1)S(1)} %copy-done.6, ...), custom_call_target="tpu_custom_call" | custom-call | flops 553648128 | bytes 4310016 | tf_op jit(solution)/shard_map/pallas_call | solution.py:451
  45.0 5.5 %all-to-all-start.2 = ((bf16[16,64,128]{2,1,0:T(8,128)(2,1)}), bf16[16,64,128]{2,1,0:T(8,128)(2,1)S(1)}, u32[]{:S(2)}, u32[]{:S(2)}) async-start(bf16[16,64,128]{2,1,0:T(8,128)(2,1)} %get-tuple-element.21), calls=%async_computation.2 | async-start | bytes 524288 | tf_op jit(solution)/shard_map/all_to_all | solution.py:467
  50.5 1.5 %collective-permute-start.1 = (bf16[128,1024]{1,0:T(8,128)(2,1)}, bf16[128,1024]{1,0:T(8,128)(2,1)S(1)}, u32[]{:S(2)}, u32[]{:S(2)}) collective-permute-start(bf16[128,1024]{1,0:T(8,128)(2,1)} %get-tuple-element.25), channel_id=1, source_target_pairs={{0,1},{1,0},{2,3},{3,2},{4,5},{5,4},{6,7},{7,6},{8,9},{9,8},{10,11... | collective-permute-start | bytes 786440 | tf_op jit(solution)/shard_map/ppermute | solution.py:480
  52.0 0.0 copy-start
  52.0 2.2 %copy-done = bf16[1024,2048]{1,0:T(8,128)(2,1)S(1)} copy-done((bf16[1024,2048]{1,0:T(8,128)(2,1)S(1)}, bf16[1024,2048]{1,0:T(8,128)(2,1)}, u32[]{:S(2)}) %copy-start) | copy-done | bytes 4194328
  54.2 0.0 copy-start.4
  54.2 1.0 %copy-done.4 = f32[1024,128]{1,0:T(8,128)S(1)} copy-done((f32[1024,128]{1,0:T(8,128)S(1)}, f32[1024,128]{1,0:T(8,128)}, u32[]{:S(2)}) %copy-start.4) | copy-done | bytes 524312
  55.2 0.9 %copy-done.5 = bf16[128,1024]{1,0:T(8,128)(2,1)S(1)} copy-done((bf16[128,1024]{1,0:T(8,128)(2,1)S(1)}, bf16[128,1024]{1,0:T(8,128)(2,1)}, u32[]{:S(2)}) %copy-start.5) | copy-done | bytes 262168
  56.2 1.4 %shard_map.125 = (f32[128,1024]{1,0:T(8,128)S(1)}, bf16[128,1024]{1,0:T(8,128)(2,1)}) custom-call(s32[1]{0:T(128)} %bitcast.1.rank_ref, bf16[128,1024]{1,0:T(8,128)(2,1)S(1)} %copy-done.5, bf16[16,64,256]{2,1,0:T(8,128)(2,1)S(1)} %all_to_all.15.both_ref, f32[1024,128]{1,0:T(8,128)S(1)} %copy-done.4, bf16[1024,2048]{1,0:T(8,128)(2,1)S(1)} %copy-done), custom_call_target="tpu_custom_call" | custom-call | flops 268435456 | bytes 6291456 | tf_op jit(solution)/shard_map/pallas_call | solution.py:451
  57.5 1.4 %collective-permute-done.1.other_ref = bf16[128,1024]{1,0:T(8,128)(2,1)S(1)} collective-permute-done((bf16[128,1024]{1,0:T(8,128)(2,1)}, bf16[128,1024]{1,0:T(8,128)(2,1)S(1)}, u32[]{:S(2)}, u32[]{:S(2)}) %collective-permute-start.1) | collective-permute-done | bytes 262176 | tf_op jit(solution)/shard_map/ppermute | solution.py:480
  59.0 0.0 all-to-all-done.2.packed_ref
  59.0 0.0 copy-done.1
  59.0 0.0 copy-done.2
  59.0 0.0 copy-done.8
  59.0 1.1 %shard_map.126 = (bf16[128,1024]{1,0:T(8,128)(2,1)}, bf16[128,1024]{1,0:T(8,128)(2,1)}, bf16[128,1024]{1,0:T(8,128)(2,1)}) custom-call(s32[1,128]{1,0:T(1,128)S(1)} %bitcast.3, bf16[16,64,128]{2,1,0:T(8,128)(2,1)S(1)} %all-to-all-done.2.packed_ref, bf16[128,1024]{1,0:T(8,128)(2,1)S(1)} %copy-done.1, bf16[128,1024]{1,0:T(8,128)(2,1)S(1)} %copy-done.2, ...), custom_call_target="tpu_custom_call" | custom-call | bytes 2359808 | tf_op jit(solution)/shard_map/pallas_call | solution.py:451
  (2 shorter events, 0.0 us)
Async XLA Ops:
  2.7 20.8 %all-to-all-start = ((bf16[16,128,128]{2,1,0:T(8,128)(2,1)}), bf16[16,128,128]{2,1,0:T(8,128)(2,1)S(1)}, u32[]{:S(2)}, u32[]{:S(2)}) async-start(bf16[16,128,128]{2,1,0:T(8,128)(2,1)} %shard_map.120), calls=%async_computation | async-start | bytes 1048576 | tf_op jit(solution)/shard_map/all_to_all | solution.py:467
  10.6 8.5 %collective-permute-start = (bf16[128,1024]{1,0:T(8,128)(2,1)}, bf16[128,1024]{1,0:T(8,128)(2,1)S(1)}, u32[]{:S(2)}, u32[]{:S(2)}) collective-permute-start(bf16[128,1024]{1,0:T(8,128)(2,1)} %own_ref.1), channel_id=1, source_target_pairs={{0,1},{1,0},{2,3},{3,2},{4,5},{5,4},{6,7},{7,6},{8,9},{9,8},{10,11... | collective-permute-start | bytes 786440 | tf_op jit(solution)/shard_map/ppermute | solution.py:480
  12.1 11.4 %copy-start.6 = (bf16[128,256]{1,0:T(8,128)(2,1)S(1)}, bf16[128,256]{1,0:T(8,128)(2,1)}, u32[]{:S(2)}) copy-start(bf16[128,256]{1,0:T(8,128)(2,1)} %constant.9.clone.dft_ref) | copy-start | bytes 196612
  12.1 11.4 %copy-start.7 = (f32[34,128]{1,0:T(8,128)S(1)}, f32[34,128]{1,0:T(8,128)}, u32[]{:S(2)}) copy-start(f32[34,128]{1,0:T(8,128)} %constant.8.clone.twist_ref) | copy-start | bytes 52228
  15.3 27.5 %copy-start.3 = (bf16[128,1024]{1,0:T(8,128)(2,1)S(1)}, bf16[128,1024]{1,0:T(8,128)(2,1)}, u32[]{:S(2)}) copy-start(bf16[128,1024]{1,0:T(8,128)(2,1)} %post_ref.3) | copy-start | bytes 786436
  42.8 16.2 %copy-start.1 = (bf16[128,1024]{1,0:T(8,128)(2,1)S(1)}, bf16[128,1024]{1,0:T(8,128)(2,1)}, u32[]{:S(2)}) copy-start(bf16[128,1024]{1,0:T(8,128)(2,1)} %pre_ref.3) | copy-start | bytes 786436
  42.8 16.2 %copy-start.2 = (bf16[128,1024]{1,0:T(8,128)(2,1)S(1)}, bf16[128,1024]{1,0:T(8,128)(2,1)}, u32[]{:S(2)}) copy-start(bf16[128,1024]{1,0:T(8,128)(2,1)} %feat_ref.3) | copy-start | bytes 786436
  42.8 16.2 %copy-start.8 = (s32[128]{0:T(128)S(1)}, s32[128]{0:T(128)}, u32[]{:S(2)}) copy-start(s32[128]{0:T(128)} %param.13) | copy-start | bytes 1540
  45.0 14.0 %all-to-all-start.2 = ((bf16[16,64,128]{2,1,0:T(8,128)(2,1)}), bf16[16,64,128]{2,1,0:T(8,128)(2,1)S(1)}, u32[]{:S(2)}, u32[]{:S(2)}) async-start(bf16[16,64,128]{2,1,0:T(8,128)(2,1)} %get-tuple-element.21), calls=%async_computation.2 | async-start | bytes 524288 | tf_op jit(solution)/shard_map/all_to_all | solution.py:467
  50.5 8.5 %collective-permute-start.1 = (bf16[128,1024]{1,0:T(8,128)(2,1)}, bf16[128,1024]{1,0:T(8,128)(2,1)S(1)}, u32[]{:S(2)}, u32[]{:S(2)}) collective-permute-start(bf16[128,1024]{1,0:T(8,128)(2,1)} %get-tuple-element.25), channel_id=1, source_target_pairs={{0,1},{1,0},{2,3},{3,2},{4,5},{5,4},{6,7},{7,6},{8,9},{9,8},{10,11... | collective-permute-start | bytes 786440 | tf_op jit(solution)/shard_map/ppermute | solution.py:480
  52.0 2.2 %copy-start = (bf16[1024,2048]{1,0:T(8,128)(2,1)S(1)}, bf16[1024,2048]{1,0:T(8,128)(2,1)}, u32[]{:S(2)}) copy-start(bf16[1024,2048]{1,0:T(8,128)(2,1)} %weight_hbm.1) | copy-start | bytes 12582916
  54.2 1.0 %copy-start.4 = (f32[1024,128]{1,0:T(8,128)S(1)}, f32[1024,128]{1,0:T(8,128)}, u32[]{:S(2)}) copy-start(f32[1024,128]{1,0:T(8,128)} %get-tuple-element.23.grad_ref) | copy-start | bytes 1572868
  55.2 0.9 %copy-start.5 = (bf16[128,1024]{1,0:T(8,128)(2,1)S(1)}, bf16[128,1024]{1,0:T(8,128)(2,1)}, u32[]{:S(2)}) copy-start(bf16[128,1024]{1,0:T(8,128)(2,1)} %get-tuple-element.22.gated_ref) | copy-start | bytes 786436

commit v12 on v11

--- a/solution.py
+++ b/solution.py
@@ -149,8 +149,11 @@
 
 
 def group_order(n):
-    half = n // 2
-    return [rank for i in range(half) for rank in (half + i, half - 1 - i)]
+    first = n // 4
+    order = []
+    for i in range(first):
+        order += [first + 3 * i, first + 3 * i + 1, first + 3 * i + 2, first - 1 - i]
+    return order
 
 
 def group_places(n):

time: 60.7 us -> 61 us (level)
  transfers between devices with their start and end apart: 4 -> 4, of which waited for: 3 -> 4; matrix products, arithmetic and copies ran while one was open for 0% -> 0% of each run, Pallas kernels for 14% -> 14%
where the time goes in v12:
time: 61 us; the launch traced here: 60.4 us
  blocking collectives  17.9 us (29%)
  starting transfers between devices  15.9 us (26%)
  Pallas kernels  15.6 us (26%)
  waiting for transfers between devices  6 us (10%)
  local copies, waits for them, and re-layouts  4.2 us (7%)
  between operations  0.69 us (1%)
    all_to_all x1, blocking collectives, exchange(): lax.all_to_all(block, 'ctx', split_axis=0, concat_axis=0, tiled=True, axi...  17.9 us
    pallas_call x7, Pallas kernels, call(): pl.pallas_call(kernel, out_shape=outs, grid_spec=pltpu.PrefetchScalarGrid...  15.6 us
    all_to_all x2, starting transfers between devices, exchange(): lax.all_to_all(block, 'ctx', split_axis=0, concat_axis=0, tiled=True, axi...  12.9 us
    ppermute x2, waiting for transfers between devices, swap_tp(): return lax.ppermute(block, 'tp', [(0, 1), (1, 0)])  5.26 us
    unnamed x18, local copies, waits for them, and re-layouts  4.2 us
    ppermute x2, starting transfers between devices, swap_tp(): return lax.ppermute(block, 'tp', [(0, 1), (1, 0)])  3.04 us
  transfers between devices with their start and end apart: 4, of which 4 were waited for; matrix products, arithmetic and copies ran while one was open for 0% of the time, Pallas kernels for 14%

profile of v12, /device:TPU:0, one launch (start us, length us, event | category | flops | bytes accessed | tf_op | source)
XLA Modules:
  0.0 60.4 jit_solution(12020387539939454248)
XLA Ops:
  0.6 2.1 %shard_map.120 = bf16[16,128,128]{2,1,0:T(8,128)(2,1)} custom-call(s32[1,128]{1,0:T(1,128)} %bitcast.2, bf16[128,1024]{1,0:T(8,128)(2,1)} %pre_ref.3, bf16[128,1024]{1,0:T(8,128)(2,1)} %feat_ref.3, f32[128,1024]{1,0:T(8,128)} %filt_ref.1), custom_call_target="tpu_custom_call" | custom-call | bytes 1573376 | tf_op jit(solution)/shard_map/pallas_call | solution.py:454
  2.7 7.9 %all-to-all-start = ((bf16[16,128,128]{2,1,0:T(8,128)(2,1)}), bf16[16,128,128]{2,1,0:T(8,128)(2,1)S(1)}, u32[]{:S(2)}, u32[]{:S(2)}) async-start(bf16[16,128,128]{2,1,0:T(8,128)(2,1)} %shard_map.120), calls=%async_computation | async-start | bytes 1048576 | tf_op jit(solution)/shard_map/all_to_all | solution.py:470
  10.6 1.5 %collective-permute-start = (bf16[128,1024]{1,0:T(8,128)(2,1)}, bf16[128,1024]{1,0:T(8,128)(2,1)S(1)}, u32[]{:S(2)}, u32[]{:S(2)}) collective-permute-start(bf16[128,1024]{1,0:T(8,128)(2,1)} %own_ref.1), channel_id=1, source_target_pairs={{0,1},{1,0},{2,3},{3,2},{4,5},{5,4},{6,7},{7,6},{8,9},{9,8},{10,11... | collective-permute-start | bytes 786440 | tf_op jit(solution)/shard_map/ppermute | solution.py:483
  12.1 0.0 copy-start.6
  12.1 0.0 copy-start.7
  12.1 3.1 %shard_map.121.part_ref = f32[1024,128]{1,0:T(8,128)S(1)} custom-call(s32[1]{0:T(128)} %bitcast.1.rank_ref, bf16[128,1024]{1,0:T(8,128)(2,1)} %own_ref.1, bf16[1024,2048]{1,0:T(8,128)(2,1)} %weight_hbm.1), custom_call_target="tpu_custom_call" | custom-call | flops 268435456 | bytes 4980736 | tf_op jit(solution)/shard_map/pallas_call | solution.py:454
  15.3 0.0 copy-start.3
  15.3 3.8 %collective-permute-done.other_ref = bf16[128,1024]{1,0:T(8,128)(2,1)S(1)} collective-permute-done((bf16[128,1024]{1,0:T(8,128)(2,1)}, bf16[128,1024]{1,0:T(8,128)(2,1)S(1)}, u32[]{:S(2)}, u32[]{:S(2)}) %collective-permute-start) | collective-permute-done | bytes 262176 | tf_op jit(solution)/shard_map/ppermute | solution.py:483
  19.1 4.0 %shard_map.122 = (f32[1024,128]{1,0:T(8,128)}, bf16[16,64,128]{2,1,0:T(8,128)(2,1)S(1)}, bf16[1024,1024]{1,0:T(8,128)(2,1)S(1)}) custom-call(s32[1]{0:T(128)} %bitcast.1.rank_ref, bf16[128,1024]{1,0:T(8,128)(2,1)S(1)} %collective-permute-done.other_ref, bf16[1024,2048]{1,0:T(8,128)(2,1)} %weight_hbm.1, f32[1024,128]{1,0:T(8,128)S(1)} %shard_map.121.part_ref, ...), custom_call_target="tpu_custom_call" | custom-call | flops 268435456 | bytes 8126464 | tf_op jit(solution)/shard_map/pallas_call | solution.py:454
  23.1 0.6 %all-to-all-done.pair_ref = bf16[16,128,128]{2,1,0:T(8,128)(2,1)S(1)} async-done(((bf16[16,128,128]{2,1,0:T(8,128)(2,1)}), bf16[16,128,128]{2,1,0:T(8,128)(2,1)S(1)}, u32[]{:S(2)}, u32[]{:S(2)}) %all-to-all-start) | async-done | bytes 524320 | tf_op jit(solution)/shard_map/all_to_all | solution.py:470
  23.7 0.0 copy-done.6
  23.7 0.0 copy-done.7
  23.7 1.8 %shard_map.123 = (bf16[16,64,256]{2,1,0:T(8,128)(2,1)S(1)}, bf16[17,64,256]{2,1,0:T(8,128)(2,1)S(1)}) custom-call(bf16[16,128,128]{2,1,0:T(8,128)(2,1)S(1)} %all-to-all-done.pair_ref, bf16[16,64,128]{2,1,0:T(8,128)(2,1)S(1)} %get-tuple-element.17.grad_ref, f32[34,128]{1,0:T(8,128)S(1)} %copy-done.7, bf16[128,256]{1,0:T(8,128)(2,1)S(1)} %copy-done.6), custom_call_target="tpu_custom_call" | custom-call | flops 427819008 | bytes 1950720 | tf_op jit(solution)/shard_map/pallas_call | solution.py:454
  25.5 17.9 %all_to_all.15.both_ref = bf16[16,64,256]{2,1,0:T(8,128)(2,1)S(1)} all-to-all(bf16[16,64,256]{2,1,0:T(8,128)(2,1)S(1)} %get-tuple-element.18), channel_id=1, replica_groups={{8,10,12,6,14,16,18,4,20,22,24,2,26,28,30,0},{9,11,13,7,15,17,19,5,21,2..., dimensions={0} | all-to-all | bytes 1048576 | tf_op jit(solution)/shard_map/all_to_all | solution.py:470
  43.4 0.0 copy-done.3
  43.4 0.0 copy-start.1
  43.4 0.0 copy-start.2
  43.4 0.0 copy-start.8
  43.4 2.1 %shard_map.124 = (bf16[16,64,128]{2,1,0:T(8,128)(2,1)}, bf16[128,1024]{1,0:T(8,128)(2,1)}, bf16[128,1024]{1,0:T(8,128)(2,1)}) custom-call(bf16[16,64,256]{2,1,0:T(8,128)(2,1)S(1)} %all_to_all.15.both_ref, bf16[128,1024]{1,0:T(8,128)(2,1)S(1)} %copy-done.3, f32[34,128]{1,0:T(8,128)S(1)} %copy-done.7, bf16[128,256]{1,0:T(8,128)(2,1)S(1)} %copy-done.6, ...), custom_call_target="tpu_custom_call" | custom-call | flops 553648128 | bytes 4310016 | tf_op jit(solution)/shard_map/pallas_call | solution.py:454
  45.6 5.0 %all-to-all-start.2 = ((bf16[16,64,128]{2,1,0:T(8,128)(2,1)}), bf16[16,64,128]{2,1,0:T(8,128)(2,1)S(1)}, u32[]{:S(2)}, u32[]{:S(2)}) async-start(bf16[16,64,128]{2,1,0:T(8,128)(2,1)} %get-tuple-element.21), calls=%async_computation.2 | async-start | bytes 524288 | tf_op jit(solution)/shard_map/all_to_all | solution.py:470
  50.6 1.5 %collective-permute-start.1 = (bf16[128,1024]{1,0:T(8,128)(2,1)}, bf16[128,1024]{1,0:T(8,128)(2,1)S(1)}, u32[]{:S(2)}, u32[]{:S(2)}) collective-permute-start(bf16[128,1024]{1,0:T(8,128)(2,1)} %get-tuple-element.25), channel_id=1, source_target_pairs={{0,1},{1,0},{2,3},{3,2},{4,5},{5,4},{6,7},{7,6},{8,9},{9,8},{10,11... | collective-permute-start | bytes 786440 | tf_op jit(solution)/shard_map/ppermute | solution.py:483
  52.1 0.0 copy-start
  52.1 2.2 %copy-done = bf16[1024,2048]{1,0:T(8,128)(2,1)S(1)} copy-done((bf16[1024,2048]{1,0:T(8,128)(2,1)S(1)}, bf16[1024,2048]{1,0:T(8,128)(2,1)}, u32[]{:S(2)}) %copy-start) | copy-done | bytes 4194328
  54.3 1.0 %copy-done.4 = f32[1024,128]{1,0:T(8,128)S(1)} copy-done((f32[1024,128]{1,0:T(8,128)S(1)}, f32[1024,128]{1,0:T(8,128)}, u32[]{:S(2)}) %copy-start.4) | copy-done | bytes 524312
  55.3 0.9 %copy-done.5 = bf16[128,1024]{1,0:T(8,128)(2,1)S(1)} copy-done((bf16[128,1024]{1,0:T(8,128)(2,1)S(1)}, bf16[128,1024]{1,0:T(8,128)(2,1)}, u32[]{:S(2)}) %copy-start.5) | copy-done | bytes 262168
  56.3 1.4 %shard_map.125 = (f32[128,1024]{1,0:T(8,128)S(1)}, bf16[128,1024]{1,0:T(8,128)(2,1)}) custom-call(s32[1]{0:T(128)} %bitcast.1.rank_ref, bf16[128,1024]{1,0:T(8,128)(2,1)S(1)} %copy-done.5, bf16[16,64,256]{2,1,0:T(8,128)(2,1)S(1)} %all_to_all.15.both_ref, f32[1024,128]{1,0:T(8,128)S(1)} %copy-done.4, bf16[1024,2048]{1,0:T(8,128)(2,1)S(1)} %copy-done), custom_call_target="tpu_custom_call" | custom-call | flops 268435456 | bytes 6291456 | tf_op jit(solution)/shard_map/pallas_call | solution.py:454
  57.6 1.4 %collective-permute-done.1.other_ref = bf16[128,1024]{1,0:T(8,128)(2,1)S(1)} collective-permute-done((bf16[128,1024]{1,0:T(8,128)(2,1)}, bf16[128,1024]{1,0:T(8,128)(2,1)S(1)}, u32[]{:S(2)}, u32[]{:S(2)}) %collective-permute-start.1) | collective-permute-done | bytes 262176 | tf_op jit(solution)/shard_map/ppermute | solution.py:483
  59.1 0.1 all-to-all-done.2.packed_ref
  59.2 0.0 copy-done.1
  59.2 0.0 copy-done.2
  59.2 0.0 copy-done.8
  59.2 1.1 %shard_map.126 = (bf16[128,1024]{1,0:T(8,128)(2,1)}, bf16[128,1024]{1,0:T(8,128)(2,1)}, bf16[128,1024]{1,0:T(8,128)(2,1)}) custom-call(s32[1,128]{1,0:T(1,128)S(1)} %bitcast.3, bf16[16,64,128]{2,1,0:T(8,128)(2,1)S(1)} %all-to-all-done.2.packed_ref, bf16[128,1024]{1,0:T(8,128)(2,1)S(1)} %copy-done.1, bf16[128,1024]{1,0:T(8,128)(2,1)S(1)} %copy-done.2, ...), custom_call_target="tpu_custom_call" | custom-call | bytes 2359808 | tf_op jit(solution)/shard_map/pallas_call | solution.py:454
  (2 shorter events, 0.0 us)
Async XLA Ops:
  2.7 21.0 %all-to-all-start = ((bf16[16,128,128]{2,1,0:T(8,128)(2,1)}), bf16[16,128,128]{2,1,0:T(8,128)(2,1)S(1)}, u32[]{:S(2)}, u32[]{:S(2)}) async-start(bf16[16,128,128]{2,1,0:T(8,128)(2,1)} %shard_map.120), calls=%async_computation | async-start | bytes 1048576 | tf_op jit(solution)/shard_map/all_to_all | solution.py:470
  10.6 8.5 %collective-permute-start = (bf16[128,1024]{1,0:T(8,128)(2,1)}, bf16[128,1024]{1,0:T(8,128)(2,1)S(1)}, u32[]{:S(2)}, u32[]{:S(2)}) collective-permute-start(bf16[128,1024]{1,0:T(8,128)(2,1)} %own_ref.1), channel_id=1, source_target_pairs={{0,1},{1,0},{2,3},{3,2},{4,5},{5,4},{6,7},{7,6},{8,9},{9,8},{10,11... | collective-permute-start | bytes 786440 | tf_op jit(solution)/shard_map/ppermute | solution.py:483
  12.1 11.6 %copy-start.6 = (bf16[128,256]{1,0:T(8,128)(2,1)S(1)}, bf16[128,256]{1,0:T(8,128)(2,1)}, u32[]{:S(2)}) copy-start(bf16[128,256]{1,0:T(8,128)(2,1)} %constant.9.clone.dft_ref) | copy-start | bytes 196612
  12.1 11.6 %copy-start.7 = (f32[34,128]{1,0:T(8,128)S(1)}, f32[34,128]{1,0:T(8,128)}, u32[]{:S(2)}) copy-start(f32[34,128]{1,0:T(8,128)} %constant.8.clone.twist_ref) | copy-start | bytes 52228
  15.3 28.2 %copy-start.3 = (bf16[128,1024]{1,0:T(8,128)(2,1)S(1)}, bf16[128,1024]{1,0:T(8,128)(2,1)}, u32[]{:S(2)}) copy-start(bf16[128,1024]{1,0:T(8,128)(2,1)} %post_ref.3) | copy-start | bytes 786436
  43.4 15.8 %copy-start.1 = (bf16[128,1024]{1,0:T(8,128)(2,1)S(1)}, bf16[128,1024]{1,0:T(8,128)(2,1)}, u32[]{:S(2)}) copy-start(bf16[128,1024]{1,0:T(8,128)(2,1)} %pre_ref.3) | copy-start | bytes 786436
  43.4 15.8 %copy-start.2 = (bf16[128,1024]{1,0:T(8,128)(2,1)S(1)}, bf16[128,1024]{1,0:T(8,128)(2,1)}, u32[]{:S(2)}) copy-start(bf16[128,1024]{1,0:T(8,128)(2,1)} %feat_ref.3) | copy-start | bytes 786436
  43.4 15.8 %copy-start.8 = (s32[128]{0:T(128)S(1)}, s32[128]{0:T(128)}, u32[]{:S(2)}) copy-start(s32[128]{0:T(128)} %param.13) | copy-start | bytes 1540
  45.6 13.6 %all-to-all-start.2 = ((bf16[16,64,128]{2,1,0:T(8,128)(2,1)}), bf16[16,64,128]{2,1,0:T(8,128)(2,1)S(1)}, u32[]{:S(2)}, u32[]{:S(2)}) async-start(bf16[16,64,128]{2,1,0:T(8,128)(2,1)} %get-tuple-element.21), calls=%async_computation.2 | async-start | bytes 524288 | tf_op jit(solution)/shard_map/all_to_all | solution.py:470
  50.6 8.5 %collective-permute-start.1 = (bf16[128,1024]{1,0:T(8,128)(2,1)}, bf16[128,1024]{1,0:T(8,128)(2,1)S(1)}, u32[]{:S(2)}, u32[]{:S(2)}) collective-permute-start(bf16[128,1024]{1,0:T(8,128)(2,1)} %get-tuple-element.25), channel_id=1, source_target_pairs={{0,1},{1,0},{2,3},{3,2},{4,5},{5,4},{6,7},{7,6},{8,9},{9,8},{10,11... | collective-permute-start | bytes 786440 | tf_op jit(solution)/shard_map/ppermute | solution.py:483
  52.1 2.2 %copy-start = (bf16[1024,2048]{1,0:T(8,128)(2,1)S(1)}, bf16[1024,2048]{1,0:T(8,128)(2,1)}, u32[]{:S(2)}) copy-start(bf16[1024,2048]{1,0:T(8,128)(2,1)} %weight_hbm.1) | copy-start | bytes 12582916
  54.3 1.0 %copy-start.4 = (f32[1024,128]{1,0:T(8,128)S(1)}, f32[1024,128]{1,0:T(8,128)}, u32[]{:S(2)}) copy-start(f32[1024,128]{1,0:T(8,128)} %get-tuple-element.23.grad_ref) | copy-start | bytes 1572868
  55.3 0.9 %copy-start.5 = (bf16[128,1024]{1,0:T(8,128)(2,1)S(1)}, bf16[128,1024]{1,0:T(8,128)(2,1)}, u32[]{:S(2)}) copy-start(bf16[128,1024]{1,0:T(8,128)(2,1)} %get-tuple-element.22.gated_ref) | copy-start | bytes 786436

commit v13 on v10

--- a/solution.py
+++ b/solution.py
@@ -149,7 +149,8 @@
 
 
 def group_order(n):
-    return [*range(n // 2, n), *range(n // 2 - 1, -1, -1)]
+    half = n // 2
+    return [rank for i in range(half) for rank in (half + i, half - 1 - i)]
 
 
 def group_places(n):

time: 61.1 us -> 60.6 us (level)
  waiting for transfers between devices: 6.33 us -> 4.98 us
  starting transfers between devices: 15.2 us -> 16.4 us
    all_to_all x2, waiting for transfers between devices: 2.51 us -> 1.17 us  [exchange(): lax.all_to_all(block, 'ctx', split_axis=0, concat_axis=0, tiled=True, axi...]
    all_to_all x2, starting transfers between devices: 12.1 us -> 13.4 us  [exchange(): lax.all_to_all(block, 'ctx', split_axis=0, concat_axis=0, tiled=True, axi...]
where the time goes in v13:
time: 60.6 us; the launch traced here: 60 us
  blocking collectives  17.5 us (29%)
  starting transfers between devices  16.4 us (27%)
  Pallas kernels  16.2 us (27%)
  waiting for transfers between devices  4.98 us (8%)
  local copies, waits for them, and re-layouts  4.2 us (7%)
  between operations  0.71 us (1%)
    all_to_all x1, blocking collectives, exchange(): lax.all_to_all(block, 'ctx', split_axis=0, concat_axis=0, tiled=True, axi...  17.5 us
    pallas_call x8, Pallas kernels, call(): pl.pallas_call(kernel, out_shape=outs, grid_spec=pltpu.PrefetchScalarGrid...  16.2 us
    all_to_all x2, starting transfers between devices, exchange(): lax.all_to_all(block, 'ctx', split_axis=0, concat_axis=0, tiled=True, axi...  13.4 us
    unnamed x18, local copies, waits for them, and re-layouts  4.2 us
    ppermute x2, waiting for transfers between devices, swap_tp(): return lax.ppermute(block, 'tp', [(0, 1), (1, 0)])  3.81 us
    ppermute x2, starting transfers between devices, swap_tp(): return lax.ppermute(block, 'tp', [(0, 1), (1, 0)])  3.04 us
  transfers between devices with their start and end apart: 4, of which 3 were waited for; matrix products, arithmetic and copies ran while one was open for 0% of the time, Pallas kernels for 16%

profile of v13, /device:TPU:0, one launch (start us, length us, event | category | flops | bytes accessed | tf_op | source)
XLA Modules:
  0.0 60.0 jit_solution(12530766723469266661)
XLA Ops:
  0.6 2.1 %shard_map.120 = bf16[16,128,128]{2,1,0:T(8,128)(2,1)} custom-call(s32[1,128]{1,0:T(1,128)} %bitcast.2, bf16[128,1024]{1,0:T(8,128)(2,1)} %pre_ref.3, bf16[128,1024]{1,0:T(8,128)(2,1)} %feat_ref.3, f32[128,1024]{1,0:T(8,128)} %filt_ref.1), custom_call_target="tpu_custom_call" | custom-call | bytes 1573376 | tf_op jit(solution)/shard_map/pallas_call | solution.py:450
  2.7 7.9 %all-to-all-start = ((bf16[16,128,128]{2,1,0:T(8,128)(2,1)}), bf16[16,128,128]{2,1,0:T(8,128)(2,1)S(1)}, u32[]{:S(2)}, u32[]{:S(2)}) async-start(bf16[16,128,128]{2,1,0:T(8,128)(2,1)} %shard_map.120), calls=%async_computation | async-start | bytes 1048576 | tf_op jit(solution)/shard_map/all_to_all | solution.py:466
  10.6 1.5 %collective-permute-start = (bf16[128,1024]{1,0:T(8,128)(2,1)}, bf16[128,1024]{1,0:T(8,128)(2,1)S(1)}, u32[]{:S(2)}, u32[]{:S(2)}) collective-permute-start(bf16[128,1024]{1,0:T(8,128)(2,1)} %own_ref.1), channel_id=1, source_target_pairs={{0,1},{1,0},{2,3},{3,2},{4,5},{5,4},{6,7},{7,6},{8,9},{9,8},{10,11... | collective-permute-start | bytes 786440 | tf_op jit(solution)/shard_map/ppermute | solution.py:479
  12.1 0.0 copy-start.6
  12.1 0.0 copy-start.7
  12.1 3.2 %shard_map.121.part_ref = f32[1024,128]{1,0:T(8,128)S(1)} custom-call(s32[1]{0:T(128)} %bitcast.rank_ref, bf16[128,1024]{1,0:T(8,128)(2,1)} %own_ref.1, bf16[1024,2048]{1,0:T(8,128)(2,1)} %weight_hbm.1), custom_call_target="tpu_custom_call" | custom-call | flops 268435456 | bytes 4980736 | tf_op jit(solution)/shard_map/pallas_call | solution.py:450
  15.3 0.0 copy-start.3
  15.3 3.8 %collective-permute-done.other_ref = bf16[128,1024]{1,0:T(8,128)(2,1)S(1)} collective-permute-done((bf16[128,1024]{1,0:T(8,128)(2,1)}, bf16[128,1024]{1,0:T(8,128)(2,1)S(1)}, u32[]{:S(2)}, u32[]{:S(2)}) %collective-permute-start) | collective-permute-done | bytes 262176 | tf_op jit(solution)/shard_map/ppermute | solution.py:479
  19.1 4.0 %shard_map.122 = (f32[1024,128]{1,0:T(8,128)}, bf16[16,64,128]{2,1,0:T(8,128)(2,1)S(1)}, bf16[1024,1024]{1,0:T(8,128)(2,1)S(1)}) custom-call(s32[1]{0:T(128)} %bitcast.rank_ref, bf16[128,1024]{1,0:T(8,128)(2,1)S(1)} %collective-permute-done.other_ref, bf16[1024,2048]{1,0:T(8,128)(2,1)} %weight_hbm.1, f32[1024,128]{1,0:T(8,128)S(1)} %shard_map.121.part_ref, ...), custom_call_target="tpu_custom_call" | custom-call | flops 268435456 | bytes 8126464 | tf_op jit(solution)/shard_map/pallas_call | solution.py:450
  23.1 0.4 all-to-all-done.pair_ref
  23.5 0.0 copy-done.6
  23.5 0.0 copy-done.7
  23.5 1.8 %shard_map.123 = (bf16[16,64,256]{2,1,0:T(8,128)(2,1)S(1)}, bf16[17,64,256]{2,1,0:T(8,128)(2,1)S(1)}) custom-call(bf16[16,128,128]{2,1,0:T(8,128)(2,1)S(1)} %all-to-all-done.pair_ref, bf16[16,64,128]{2,1,0:T(8,128)(2,1)S(1)} %get-tuple-element.16.grad_ref, f32[34,128]{1,0:T(8,128)S(1)} %copy-done.7, bf16[128,256]{1,0:T(8,128)(2,1)S(1)} %copy-done.6), custom_call_target="tpu_custom_call" | custom-call | flops 427819008 | bytes 1950720 | tf_op jit(solution)/shard_map/pallas_call | solution.py:450
  25.3 17.5 %all_to_all.15.both_ref = bf16[16,64,256]{2,1,0:T(8,128)(2,1)S(1)} all-to-all(bf16[16,64,256]{2,1,0:T(8,128)(2,1)S(1)} %get-tuple-element.17), channel_id=1, replica_groups={{16,14,18,12,20,10,22,8,24,6,26,4,28,2,30,0},{17,15,19,13,21,11,23,9,25..., dimensions={0} | all-to-all | bytes 1048576 | tf_op jit(solution)/shard_map/all_to_all | solution.py:466
  42.8 0.0 copy-done.3
  42.8 0.0 copy-start.1
  42.8 0.0 copy-start.2
  42.8 0.0 copy-start.8
  42.8 2.1 %shard_map.124 = (bf16[16,64,128]{2,1,0:T(8,128)(2,1)}, bf16[128,1024]{1,0:T(8,128)(2,1)}, bf16[128,1024]{1,0:T(8,128)(2,1)}) custom-call(bf16[16,64,256]{2,1,0:T(8,128)(2,1)S(1)} %all_to_all.15.both_ref, bf16[128,1024]{1,0:T(8,128)(2,1)S(1)} %copy-done.3, f32[34,128]{1,0:T(8,128)S(1)} %copy-done.7, bf16[128,256]{1,0:T(8,128)(2,1)S(1)} %copy-done.6, ...), custom_call_target="tpu_custom_call" | custom-call | flops 553648128 | bytes 4310016 | tf_op jit(solution)/shard_map/pallas_call | solution.py:450
  44.9 5.5 %all-to-all-start.2 = ((bf16[16,64,128]{2,1,0:T(8,128)(2,1)}), bf16[16,64,128]{2,1,0:T(8,128)(2,1)S(1)}, u32[]{:S(2)}, u32[]{:S(2)}) async-start(bf16[16,64,128]{2,1,0:T(8,128)(2,1)} %get-tuple-element.24), calls=%async_computation.2 | async-start | bytes 524288 | tf_op jit(solution)/shard_map/all_to_all | solution.py:466
  50.5 1.5 %collective-permute-start.1 = (bf16[128,1024]{1,0:T(8,128)(2,1)}, bf16[128,1024]{1,0:T(8,128)(2,1)S(1)}, u32[]{:S(2)}, u32[]{:S(2)}) collective-permute-start(bf16[128,1024]{1,0:T(8,128)(2,1)} %get-tuple-element.23), channel_id=1, source_target_pairs={{0,1},{1,0},{2,3},{3,2},{4,5},{5,4},{6,7},{7,6},{8,9},{9,8},{10,11... | collective-permute-start | bytes 786440 | tf_op jit(solution)/shard_map/ppermute | solution.py:479
  52.0 2.2 %copy-done = bf16[1024,2048]{1,0:T(8,128)(2,1)S(1)} copy-done((bf16[1024,2048]{1,0:T(8,128)(2,1)S(1)}, bf16[1024,2048]{1,0:T(8,128)(2,1)}, u32[]{:S(2)}) %copy-start) | copy-done | bytes 4194328
  54.2 1.0 %copy-done.4 = f32[1024,128]{1,0:T(8,128)S(1)} copy-done((f32[1024,128]{1,0:T(8,128)S(1)}, f32[1024,128]{1,0:T(8,128)}, u32[]{:S(2)}) %copy-start.4) | copy-done | bytes 524312
  55.2 0.9 %copy-done.5 = bf16[128,1024]{1,0:T(8,128)(2,1)S(1)} copy-done((bf16[128,1024]{1,0:T(8,128)(2,1)S(1)}, bf16[128,1024]{1,0:T(8,128)(2,1)}, u32[]{:S(2)}) %copy-start.5) | copy-done | bytes 262168
  56.2 1.4 %shard_map.125 = (f32[128,1024]{1,0:T(8,128)S(1)}, bf16[128,1024]{1,0:T(8,128)(2,1)}) custom-call(s32[1]{0:T(128)} %bitcast.rank_ref, bf16[128,1024]{1,0:T(8,128)(2,1)S(1)} %copy-done.5, bf16[16,64,256]{2,1,0:T(8,128)(2,1)S(1)} %all_to_all.15.both_ref, f32[1024,128]{1,0:T(8,128)S(1)} %copy-done.4, bf16[1024,2048]{1,0:T(8,128)(2,1)S(1)} %copy-done), custom_call_target="tpu_custom_call" | custom-call | flops 268435456 | bytes 6291456 | tf_op jit(solution)/shard_map/pallas_call | solution.py:450
  57.5 0.8 %all-to-all-done.2.packed_ref = bf16[16,64,128]{2,1,0:T(8,128)(2,1)S(1)} async-done(((bf16[16,64,128]{2,1,0:T(8,128)(2,1)}), bf16[16,64,128]{2,1,0:T(8,128)(2,1)S(1)}, u32[]{:S(2)}, u32[]{:S(2)}) %all-to-all-start.2) | async-done | bytes 262176 | tf_op jit(solution)/shard_map/all_to_all | solution.py:466
  58.3 0.0 copy-done.1
  58.3 0.0 copy-done.2
  58.3 0.0 copy-done.8
  58.3 0.9 %shard_map.126 = (bf16[128,1024]{1,0:T(8,128)(2,1)}, bf16[128,1024]{1,0:T(8,128)(2,1)}) custom-call(s32[1,128]{1,0:T(1,128)S(1)} %bitcast.3, bf16[16,64,128]{2,1,0:T(8,128)(2,1)S(1)} %all-to-all-done.2.packed_ref, bf16[128,1024]{1,0:T(8,128)(2,1)S(1)} %copy-done.1, bf16[128,1024]{1,0:T(8,128)(2,1)S(1)} %copy-done.2), custom_call_target="tpu_custom_call" | custom-call | bytes 1311232 | tf_op jit(solution)/shard_map/pallas_call | solution.py:450
  59.3 0.0 collective-permute-done.1.other_ref
  59.3 0.7 %shard_map.127 = bf16[128,1024]{1,0:T(8,128)(2,1)} custom-call(f32[128,1024]{1,0:T(8,128)S(1)} %get-tuple-element.22.home_ref, bf16[128,1024]{1,0:T(8,128)(2,1)S(1)} %collective-permute-done.1.other_ref, bf16[128,1024]{1,0:T(8,128)(2,1)} %get-tuple-element.15.after_hbm), custom_call_target="tpu_custom_call" | custom-call | bytes 1310720 | tf_op jit(solution)/shard_map/pallas_call | solution.py:450
  (3 shorter events, 0.0 us)
Async XLA Ops:
  2.7 20.8 %all-to-all-start = ((bf16[16,128,128]{2,1,0:T(8,128)(2,1)}), bf16[16,128,128]{2,1,0:T(8,128)(2,1)S(1)}, u32[]{:S(2)}, u32[]{:S(2)}) async-start(bf16[16,128,128]{2,1,0:T(8,128)(2,1)} %shard_map.120), calls=%async_computation | async-start | bytes 1048576 | tf_op jit(solution)/shard_map/all_to_all | solution.py:466
  10.6 8.5 %collective-permute-start = (bf16[128,1024]{1,0:T(8,128)(2,1)}, bf16[128,1024]{1,0:T(8,128)(2,1)S(1)}, u32[]{:S(2)}, u32[]{:S(2)}) collective-permute-start(bf16[128,1024]{1,0:T(8,128)(2,1)} %own_ref.1), channel_id=1, source_target_pairs={{0,1},{1,0},{2,3},{3,2},{4,5},{5,4},{6,7},{7,6},{8,9},{9,8},{10,11... | collective-permute-start | bytes 786440 | tf_op jit(solution)/shard_map/ppermute | solution.py:479
  12.1 11.4 %copy-start.6 = (bf16[128,256]{1,0:T(8,128)(2,1)S(1)}, bf16[128,256]{1,0:T(8,128)(2,1)}, u32[]{:S(2)}) copy-start(bf16[128,256]{1,0:T(8,128)(2,1)} %constant.9.clone.dft_ref) | copy-start | bytes 196612
  12.1 11.4 %copy-start.7 = (f32[34,128]{1,0:T(8,128)S(1)}, f32[34,128]{1,0:T(8,128)}, u32[]{:S(2)}) copy-start(f32[34,128]{1,0:T(8,128)} %constant.8.clone.twist_ref) | copy-start | bytes 52228
  15.3 27.5 %copy-start.3 = (bf16[128,1024]{1,0:T(8,128)(2,1)S(1)}, bf16[128,1024]{1,0:T(8,128)(2,1)}, u32[]{:S(2)}) copy-start(bf16[128,1024]{1,0:T(8,128)(2,1)} %post_ref.3) | copy-start | bytes 786436
  42.8 15.5 %copy-start.1 = (bf16[128,1024]{1,0:T(8,128)(2,1)S(1)}, bf16[128,1024]{1,0:T(8,128)(2,1)}, u32[]{:S(2)}) copy-start(bf16[128,1024]{1,0:T(8,128)(2,1)} %pre_ref.3) | copy-start | bytes 786436
  42.8 15.5 %copy-start.2 = (bf16[128,1024]{1,0:T(8,128)(2,1)S(1)}, bf16[128,1024]{1,0:T(8,128)(2,1)}, u32[]{:S(2)}) copy-start(bf16[128,1024]{1,0:T(8,128)(2,1)} %feat_ref.3) | copy-start | bytes 786436
  42.8 15.5 %copy-start.8 = (s32[128]{0:T(128)S(1)}, s32[128]{0:T(128)}, u32[]{:S(2)}) copy-start(s32[128]{0:T(128)} %param.13) | copy-start | bytes 1540
  44.9 13.4 %all-to-all-start.2 = ((bf16[16,64,128]{2,1,0:T(8,128)(2,1)}), bf16[16,64,128]{2,1,0:T(8,128)(2,1)S(1)}, u32[]{:S(2)}, u32[]{:S(2)}) async-start(bf16[16,64,128]{2,1,0:T(8,128)(2,1)} %get-tuple-element.24), calls=%async_computation.2 | async-start | bytes 524288 | tf_op jit(solution)/shard_map/all_to_all | solution.py:466
  50.5 8.8 %collective-permute-start.1 = (bf16[128,1024]{1,0:T(8,128)(2,1)}, bf16[128,1024]{1,0:T(8,128)(2,1)S(1)}, u32[]{:S(2)}, u32[]{:S(2)}) collective-permute-start(bf16[128,1024]{1,0:T(8,128)(2,1)} %get-tuple-element.23), channel_id=1, source_target_pairs={{0,1},{1,0},{2,3},{3,2},{4,5},{5,4},{6,7},{7,6},{8,9},{9,8},{10,11... | collective-permute-start | bytes 786440 | tf_op jit(solution)/shard_map/ppermute | solution.py:479
  52.0 2.2 %copy-start = (bf16[1024,2048]{1,0:T(8,128)(2,1)S(1)}, bf16[1024,2048]{1,0:T(8,128)(2,1)}, u32[]{:S(2)}) copy-start(bf16[1024,2048]{1,0:T(8,128)(2,1)} %weight_hbm.1) | copy-start | bytes 12582916
  54.2 1.0 %copy-start.4 = (f32[1024,128]{1,0:T(8,128)S(1)}, f32[1024,128]{1,0:T(8,128)}, u32[]{:S(2)}) copy-start(f32[1024,128]{1,0:T(8,128)} %get-tuple-element.21.grad_ref) | copy-start | bytes 1572868
  55.2 0.9 %copy-start.5 = (bf16[128,1024]{1,0:T(8,128)(2,1)S(1)}, bf16[128,1024]{1,0:T(8,128)(2,1)}, u32[]{:S(2)}) copy-start(bf16[128,1024]{1,0:T(8,128)(2,1)} %get-tuple-element.20.gated_ref) | copy-start | bytes 786436

commit v14 on v10

--- a/solution.py
+++ b/solution.py
@@ -148,12 +148,18 @@
         out_ref[k] = mixed[k * width : (k + 1) * width].astype(BF16)
 
 
-def group_order(n):
-    return [*range(n // 2, n), *range(n // 2 - 1, -1, -1)]
-
-
-def group_places(n):
-    return [int(place) for place in np.argsort(group_order(n))]
+def group_order(n, turn):
+    first = (3 * n // 4, 3 * n // 4, 3 * n // 4)[turn]
+    return sorted(range(n), key=lambda rank: (abs(rank - first), rank))
+
+
+def block_places(n, turn):
+    return [int(place) for place in np.argsort(group_order(n, turn))]
+
+
+def channel_places(n, turn):
+    places = block_places(n, turn)
+    return [places[rank] for rank in group_order(n, 0)]
 
 
 def started(*copies):
@@ -233,12 +239,13 @@
     chunks = row_chunks(width)
     step = width // chunks
     forward, back = dft_matrices(dft_ref, n * length)
-    both_ref[:, :, length:] = grad_ref[...]
+    for group, place in enumerate(channel_places(n, 1)):
+        both_ref[place, :, length:] = grad_ref[group]
 
     def transform(c):
         for kind in range(2):
             start = kind * width + c * step
-            blocks = [pair_ref[b, start : start + step] for b in group_places(n)]
+            blocks = [pair_ref[b, start : start + step] for b in block_places(n, 0)]
             forward_blocks(
                 n, blocks, twist_ref, mid_ref.at[c], slice(kind * step, (kind + 1) * step)
             )
@@ -262,7 +269,7 @@
                 prod_ref.dtype
             )
         mid = inner_product(prod_ref.at[c], back)
-        for b, value in zip(group_places(n), inverse_blocks(n, mid, twist_ref)):
+        for b, value in zip(block_places(n, 1), inverse_blocks(n, mid, twist_ref)):
             both_ref[b, at, :length] = value
 
 
@@ -287,7 +294,7 @@
     length = twist_ref.shape[1]
     width = out_ref.shape[1]
     forward, back = dft_matrices(dft_ref, n * length)
-    mixed = channel_rows(both_ref, length).T.astype(F32)
+    mixed = channel_rows(both_ref, length, channel_places(n, 1)).T.astype(F32)
     gated = (post_ref[...].astype(F32) * mixed).astype(BF16)
     gated_ref[...] = gated
     away_ref[...] = jnp.dot(gated, weight_ref[...], preferred_element_type=F32).astype(BF16)
@@ -296,7 +303,7 @@
     step = width // chunks
 
     def transform(c):
-        blocks = [both_ref[b, c * step : (c + 1) * step, length:] for b in group_places(n)]
+        blocks = [both_ref[b, c * step : (c + 1) * step, length:] for b in block_places(n, 1)]
         forward_blocks(n, blocks, twist_ref, mid_ref.at[c], slice(0, step))
 
     transform(0)
@@ -316,7 +323,7 @@
                 prod_ref.dtype
             )
         mid = inner_product(prod_ref.at[c], back)
-        for b, value in zip(group_places(n), inverse_blocks(n, mid, twist_ref)):
+        for b, value in zip(block_places(n, 2), inverse_blocks(n, mid, twist_ref)):
             out_ref[b, at] = value
         if chunks == 1:
             copies += started((out_ref, out_hbm, sems.at[2]))
@@ -327,10 +334,8 @@
         copy.wait()
 
 
-def channel_rows(blocks_ref, length):
-    return jnp.concatenate(
-        [blocks_ref[k, :, :length] for k in range(blocks_ref.shape[0])], axis=0
-    )
+def channel_rows(blocks_ref, length, places):
+    return jnp.concatenate([blocks_ref[k, :, :length] for k in places], axis=0)
 
 
 def weight_copies(parts, side, weight_hbm, weight_ref, sems):
@@ -375,7 +380,8 @@
     copies = weight_copies(
         parts, rank_ref[0], weight_hbm, weight_ref, [sems.at[k] for k in range(parts)]
     )
-    mixed = channel_rows(both_ref, grad_ref.shape[1]).astype(F32)
+    places = channel_places(both_ref.shape[0], 1)
+    mixed = channel_rows(both_ref, grad_ref.shape[1], places).astype(F32)
     post_grad_ref[...] = (grad_ref[...] * mixed).astype(BF16).T
     home_ref[...] = part_products(copies, gated_ref[...], weight_ref)
 
@@ -393,13 +399,14 @@
     sems,
 ):
     keep = (token_ref[...] < BASES).astype(BF16)
-    dests = packed_ref.shape[0] // parts
+    places = channel_places(packed_ref.shape[0], 2)
+    dests = len(places) // parts
     cut = pre_ref.shape[1] // parts
     copies = []
     for k in range(parts):
         at = pl.ds(k * cut, cut)
-        blocks = packed_ref.at[pl.ds(k * dests, dests)]
-        grad = (channel_rows(blocks, blocks.shape[2]) * keep).T.astype(F32)
+        here = places[k * dests : (k + 1) * dests]
+        grad = (channel_rows(packed_ref, packed_ref.shape[2], here) * keep).T.astype(F32)
         pre_grad_ref[:, at] = (grad * feat_ref[:, at].astype(F32)).astype(BF16)
         feat_grad_ref[:, at] = (grad * pre_ref[:, at].astype(F32)).astype(BF16)
         copies += started(
@@ -461,14 +468,14 @@
     )(*args)
 
 
-def exchange(block):
+def exchange(block, turn):
     return lax.all_to_all(
         block,
         "ctx",
         split_axis=0,
         concat_axis=0,
         tiled=True,
-        axis_index_groups=[group_order(block.shape[0])],
+        axis_index_groups=[group_order(block.shape[0], turn)],
     )
 
 
@@ -518,7 +525,7 @@
         out_blocks=[((n // steps, *pair[1:]), lambda i, *_: (i, 0, 0))],
         from_hbm=range(4),
     )
-    pair_in = exchange(pair_out)
+    pair_in = exchange(pair_out, 0)
     steps = 4
     flat, turned, packed = by_channels(steps)
     weight_block = (channels // steps, columns)
@@ -561,7 +568,7 @@
             narrow_scratch,
         ],
     )
-    both_in = exchange(both_out)
+    both_in = exchange(both_out, 1)
     grad_back_out, gated, away = call(
         functools.partial(mix_backward, n),
         (
@@ -581,7 +588,7 @@
             pltpu.SemaphoreType.DMA((2 + chunks,)),
         ],
     )
-    grad_back_in = exchange(grad_back_out)
+    grad_back_in = exchange(grad_back_out, 2)
     other_part = swap_tp(away)
     parts = 2
     home, grad_post = call(

time: 61.1 us -> 61.9 us (1.013)
  starting transfers between devices: 15.2 us -> 18.8 us
  waiting for transfers between devices: 6.33 us -> 4.28 us
  blocking collectives: 17.9 us -> 17 us
    all_to_all x2, starting transfers between devices: 12.1 us -> 15.8 us  [exchange(): lax.all_to_all(block, 'ctx', split_axis=0, concat_axis=0, tiled=True, axi...]
    all_to_all x2, waiting for transfers between devices: 2.51 us -> 0.01 us  [exchange(): lax.all_to_all(block, 'ctx', split_axis=0, concat_axis=0, tiled=True, axi...]
    all_to_all x1, blocking collectives: 17.9 us -> 17 us  [exchange(): lax.all_to_all(block, 'ctx', split_axis=0, concat_axis=0, tiled=True, axi...]
  transfers between devices with their start and end apart: 4 -> 4, of which waited for: 3 -> 2; matrix products, arithmetic and copies ran while one was open for 0% -> 0% of each run, Pallas kernels for 16% -> 15%
where the time goes in v14:
time: 61.9 us; the launch traced here: 61.2 us
  starting transfers between devices  18.8 us (30%)
  blocking collectives  17 us (27%)
  Pallas kernels  16.2 us (26%)
  waiting for transfers between devices  4.28 us (7%)
  local copies, waits for them, and re-layouts  4.2 us (7%)
  between operations  0.74 us (1%)
    all_to_all x1, blocking collectives, exchange(): lax.all_to_all(block, 'ctx', split_axis=0, concat_axis=0, tiled=True, axi...  17 us
    pallas_call x8, Pallas kernels, call(): pl.pallas_call(kernel, out_shape=outs, grid_spec=pltpu.PrefetchScalarGrid...  16.2 us
    all_to_all x2, starting transfers between devices, exchange(): lax.all_to_all(block, 'ctx', split_axis=0, concat_axis=0, tiled=True, axi...  15.8 us
    ppermute x2, waiting for transfers between devices, swap_tp(): return lax.ppermute(block, 'tp', [(0, 1), (1, 0)])  4.28 us
    unnamed x18, local copies, waits for them, and re-layouts  4.2 us
    ppermute x2, starting transfers between devices, swap_tp(): return lax.ppermute(block, 'tp', [(0, 1), (1, 0)])  3.04 us
  transfers between devices with their start and end apart: 4, of which 2 were waited for; matrix products, arithmetic and copies ran while one was open for 0% of the time, Pallas kernels for 15%

profile of v14, /device:TPU:0, one launch (start us, length us, event | category | flops | bytes accessed | tf_op | source)
XLA Modules:
  0.0 61.2 jit_solution(5506274207579832100)
XLA Ops:
  0.6 2.1 %shard_map.120 = bf16[16,128,128]{2,1,0:T(8,128)(2,1)} custom-call(s32[1,128]{1,0:T(1,128)} %bitcast.2, bf16[128,1024]{1,0:T(8,128)(2,1)} %pre_ref.3, bf16[128,1024]{1,0:T(8,128)(2,1)} %feat_ref.3, f32[128,1024]{1,0:T(8,128)} %filt_ref.1), custom_call_target="tpu_custom_call" | custom-call | bytes 1573376 | tf_op jit(solution)/shard_map/pallas_call | solution.py:456
  2.7 8.5 %all-to-all-start = ((bf16[16,128,128]{2,1,0:T(8,128)(2,1)}), bf16[16,128,128]{2,1,0:T(8,128)(2,1)S(1)}, u32[]{:S(2)}, u32[]{:S(2)}) async-start(bf16[16,128,128]{2,1,0:T(8,128)(2,1)} %shard_map.120), calls=%async_computation | async-start | bytes 1048576 | tf_op jit(solution)/shard_map/all_to_all | solution.py:472
  11.3 1.5 %collective-permute-start = (bf16[128,1024]{1,0:T(8,128)(2,1)}, bf16[128,1024]{1,0:T(8,128)(2,1)S(1)}, u32[]{:S(2)}, u32[]{:S(2)}) collective-permute-start(bf16[128,1024]{1,0:T(8,128)(2,1)} %own_ref.1), channel_id=1, source_target_pairs={{0,1},{1,0},{2,3},{3,2},{4,5},{5,4},{6,7},{7,6},{8,9},{9,8},{10,11... | collective-permute-start | bytes 786440 | tf_op jit(solution)/shard_map/ppermute | solution.py:485
  12.8 0.0 copy-start.6
  12.8 0.0 copy-start.7
  12.8 3.1 %shard_map.121.part_ref = f32[1024,128]{1,0:T(8,128)S(1)} custom-call(s32[1]{0:T(128)} %bitcast.rank_ref, bf16[128,1024]{1,0:T(8,128)(2,1)} %own_ref.1, bf16[1024,2048]{1,0:T(8,128)(2,1)} %weight_hbm.1), custom_call_target="tpu_custom_call" | custom-call | flops 268435456 | bytes 4980736 | tf_op jit(solution)/shard_map/pallas_call | solution.py:456
  15.9 0.0 copy-start.3
  15.9 3.8 %collective-permute-done.other_ref = bf16[128,1024]{1,0:T(8,128)(2,1)S(1)} collective-permute-done((bf16[128,1024]{1,0:T(8,128)(2,1)}, bf16[128,1024]{1,0:T(8,128)(2,1)S(1)}, u32[]{:S(2)}, u32[]{:S(2)}) %collective-permute-start) | collective-permute-done | bytes 262176 | tf_op jit(solution)/shard_map/ppermute | solution.py:485
  19.8 4.0 %shard_map.122 = (f32[1024,128]{1,0:T(8,128)}, bf16[16,64,128]{2,1,0:T(8,128)(2,1)S(1)}, bf16[1024,1024]{1,0:T(8,128)(2,1)S(1)}) custom-call(s32[1]{0:T(128)} %bitcast.rank_ref, bf16[128,1024]{1,0:T(8,128)(2,1)S(1)} %collective-permute-done.other_ref, bf16[1024,2048]{1,0:T(8,128)(2,1)} %weight_hbm.1, f32[1024,128]{1,0:T(8,128)S(1)} %shard_map.121.part_ref, ...), custom_call_target="tpu_custom_call" | custom-call | flops 268435456 | bytes 8126464 | tf_op jit(solution)/shard_map/pallas_call | solution.py:456
  23.8 0.0 all-to-all-done.pair_ref
  23.8 0.0 copy-done.6
  23.8 0.0 copy-done.7
  23.8 1.8 %shard_map.123 = (bf16[16,64,256]{2,1,0:T(8,128)(2,1)S(1)}, bf16[17,64,256]{2,1,0:T(8,128)(2,1)S(1)}) custom-call(bf16[16,128,128]{2,1,0:T(8,128)(2,1)S(1)} %all-to-all-done.pair_ref, bf16[16,64,128]{2,1,0:T(8,128)(2,1)S(1)} %get-tuple-element.16.grad_ref, f32[34,128]{1,0:T(8,128)S(1)} %copy-done.7, bf16[128,256]{1,0:T(8,128)(2,1)S(1)} %copy-done.6), custom_call_target="tpu_custom_call" | custom-call | flops 427819008 | bytes 1950720 | tf_op jit(solution)/shard_map/pallas_call | solution.py:456
  25.6 17.0 %all_to_all.15.both_ref = bf16[16,64,256]{2,1,0:T(8,128)(2,1)S(1)} all-to-all(bf16[16,64,256]{2,1,0:T(8,128)(2,1)S(1)} %get-tuple-element.17), channel_id=1, replica_groups={{24,22,26,20,28,18,30,16,14,12,10,8,6,4,2,0},{25,23,27,21,29,19,31,17,1..., dimensions={0} | all-to-all | bytes 1048576 | tf_op jit(solution)/shard_map/all_to_all | solution.py:472
  42.6 0.0 copy-done.3
  42.6 0.0 copy-start.1
  42.6 0.0 copy-start.2
  42.6 0.0 copy-start.8
  42.6 2.1 %shard_map.124 = (bf16[16,64,128]{2,1,0:T(8,128)(2,1)}, bf16[128,1024]{1,0:T(8,128)(2,1)}, bf16[128,1024]{1,0:T(8,128)(2,1)}) custom-call(bf16[16,64,256]{2,1,0:T(8,128)(2,1)S(1)} %all_to_all.15.both_ref, bf16[128,1024]{1,0:T(8,128)(2,1)S(1)} %copy-done.3, f32[34,128]{1,0:T(8,128)S(1)} %copy-done.7, bf16[128,256]{1,0:T(8,128)(2,1)S(1)} %copy-done.6, ...), custom_call_target="tpu_custom_call" | custom-call | flops 553648128 | bytes 4310016 | tf_op jit(solution)/shard_map/pallas_call | solution.py:456
  44.7 7.3 %all-to-all-start.2 = ((bf16[16,64,128]{2,1,0:T(8,128)(2,1)}), bf16[16,64,128]{2,1,0:T(8,128)(2,1)S(1)}, u32[]{:S(2)}, u32[]{:S(2)}) async-start(bf16[16,64,128]{2,1,0:T(8,128)(2,1)} %get-tuple-element.24), calls=%async_computation.2 | async-start | bytes 524288 | tf_op jit(solution)/shard_map/all_to_all | solution.py:472
  52.0 1.5 %collective-permute-start.1 = (bf16[128,1024]{1,0:T(8,128)(2,1)}, bf16[128,1024]{1,0:T(8,128)(2,1)S(1)}, u32[]{:S(2)}, u32[]{:S(2)}) collective-permute-start(bf16[128,1024]{1,0:T(8,128)(2,1)} %get-tuple-element.23), channel_id=1, source_target_pairs={{0,1},{1,0},{2,3},{3,2},{4,5},{5,4},{6,7},{7,6},{8,9},{9,8},{10,11... | collective-permute-start | bytes 786440 | tf_op jit(solution)/shard_map/ppermute | solution.py:485
  53.5 2.2 %copy-done = bf16[1024,2048]{1,0:T(8,128)(2,1)S(1)} copy-done((bf16[1024,2048]{1,0:T(8,128)(2,1)S(1)}, bf16[1024,2048]{1,0:T(8,128)(2,1)}, u32[]{:S(2)}) %copy-start) | copy-done | bytes 4194328
  55.7 1.0 %copy-done.4 = f32[1024,128]{1,0:T(8,128)S(1)} copy-done((f32[1024,128]{1,0:T(8,128)S(1)}, f32[1024,128]{1,0:T(8,128)}, u32[]{:S(2)}) %copy-start.4) | copy-done | bytes 524312
  56.7 0.9 %copy-done.5 = bf16[128,1024]{1,0:T(8,128)(2,1)S(1)} copy-done((bf16[128,1024]{1,0:T(8,128)(2,1)S(1)}, bf16[128,1024]{1,0:T(8,128)(2,1)}, u32[]{:S(2)}) %copy-start.5) | copy-done | bytes 262168
  57.7 1.4 %shard_map.125 = (f32[128,1024]{1,0:T(8,128)S(1)}, bf16[128,1024]{1,0:T(8,128)(2,1)}) custom-call(s32[1]{0:T(128)} %bitcast.rank_ref, bf16[128,1024]{1,0:T(8,128)(2,1)S(1)} %copy-done.5, bf16[16,64,256]{2,1,0:T(8,128)(2,1)S(1)} %all_to_all.15.both_ref, f32[1024,128]{1,0:T(8,128)S(1)} %copy-done.4, bf16[1024,2048]{1,0:T(8,128)(2,1)S(1)} %copy-done), custom_call_target="tpu_custom_call" | custom-call | flops 268435456 | bytes 6291456 | tf_op jit(solution)/shard_map/pallas_call | solution.py:456
  59.0 0.0 all-to-all-done.2.packed_ref
  59.1 0.0 copy-done.1
  59.1 0.0 copy-done.2
  59.1 0.0 copy-done.8
  59.1 0.9 %shard_map.126 = (bf16[128,1024]{1,0:T(8,128)(2,1)}, bf16[128,1024]{1,0:T(8,128)(2,1)}) custom-call(s32[1,128]{1,0:T(1,128)S(1)} %bitcast.3, bf16[16,64,128]{2,1,0:T(8,128)(2,1)S(1)} %all-to-all-done.2.packed_ref, bf16[128,1024]{1,0:T(8,128)(2,1)S(1)} %copy-done.1, bf16[128,1024]{1,0:T(8,128)(2,1)S(1)} %copy-done.2), custom_call_target="tpu_custom_call" | custom-call | bytes 1311232 | tf_op jit(solution)/shard_map/pallas_call | solution.py:456
  60.0 0.5 collective-permute-done.1.other_ref
  60.5 0.7 %shard_map.127 = bf16[128,1024]{1,0:T(8,128)(2,1)} custom-call(f32[128,1024]{1,0:T(8,128)S(1)} %get-tuple-element.22.home_ref, bf16[128,1024]{1,0:T(8,128)(2,1)S(1)} %collective-permute-done.1.other_ref, bf16[128,1024]{1,0:T(8,128)(2,1)} %get-tuple-element.15.after_hbm), custom_call_target="tpu_custom_call" | custom-call | bytes 1310720 | tf_op jit(solution)/shard_map/pallas_call | solution.py:456
  (3 shorter events, 0.0 us)
Async XLA Ops:
  2.7 21.1 %all-to-all-start = ((bf16[16,128,128]{2,1,0:T(8,128)(2,1)}), bf16[16,128,128]{2,1,0:T(8,128)(2,1)S(1)}, u32[]{:S(2)}, u32[]{:S(2)}) async-start(bf16[16,128,128]{2,1,0:T(8,128)(2,1)} %shard_map.120), calls=%async_computation | async-start | bytes 1048576 | tf_op jit(solution)/shard_map/all_to_all | solution.py:472
  11.3 8.5 %collective-permute-start = (bf16[128,1024]{1,0:T(8,128)(2,1)}, bf16[128,1024]{1,0:T(8,128)(2,1)S(1)}, u32[]{:S(2)}, u32[]{:S(2)}) collective-permute-start(bf16[128,1024]{1,0:T(8,128)(2,1)} %own_ref.1), channel_id=1, source_target_pairs={{0,1},{1,0},{2,3},{3,2},{4,5},{5,4},{6,7},{7,6},{8,9},{9,8},{10,11... | collective-permute-start | bytes 786440 | tf_op jit(solution)/shard_map/ppermute | solution.py:485
  12.8 11.0 %copy-start.6 = (bf16[128,256]{1,0:T(8,128)(2,1)S(1)}, bf16[128,256]{1,0:T(8,128)(2,1)}, u32[]{:S(2)}) copy-start(bf16[128,256]{1,0:T(8,128)(2,1)} %constant.9.clone.dft_ref) | copy-start | bytes 196612
  12.8 11.0 %copy-start.7 = (f32[34,128]{1,0:T(8,128)S(1)}, f32[34,128]{1,0:T(8,128)}, u32[]{:S(2)}) copy-start(f32[34,128]{1,0:T(8,128)} %constant.8.clone.twist_ref) | copy-start | bytes 52228
  15.9 26.7 %copy-start.3 = (bf16[128,1024]{1,0:T(8,128)(2,1)S(1)}, bf16[128,1024]{1,0:T(8,128)(2,1)}, u32[]{:S(2)}) copy-start(bf16[128,1024]{1,0:T(8,128)(2,1)} %post_ref.3) | copy-start | bytes 786436
  42.6 16.5 %copy-start.1 = (bf16[128,1024]{1,0:T(8,128)(2,1)S(1)}, bf16[128,1024]{1,0:T(8,128)(2,1)}, u32[]{:S(2)}) copy-start(bf16[128,1024]{1,0:T(8,128)(2,1)} %pre_ref.3) | copy-start | bytes 786436
  42.6 16.5 %copy-start.2 = (bf16[128,1024]{1,0:T(8,128)(2,1)S(1)}, bf16[128,1024]{1,0:T(8,128)(2,1)}, u32[]{:S(2)}) copy-start(bf16[128,1024]{1,0:T(8,128)(2,1)} %feat_ref.3) | copy-start | bytes 786436
  42.6 16.5 %copy-start.8 = (s32[128]{0:T(128)S(1)}, s32[128]{0:T(128)}, u32[]{:S(2)}) copy-start(s32[128]{0:T(128)} %param.13) | copy-start | bytes 1540
  44.7 14.3 %all-to-all-start.2 = ((bf16[16,64,128]{2,1,0:T(8,128)(2,1)}), bf16[16,64,128]{2,1,0:T(8,128)(2,1)S(1)}, u32[]{:S(2)}, u32[]{:S(2)}) async-start(bf16[16,64,128]{2,1,0:T(8,128)(2,1)} %get-tuple-element.24), calls=%async_computation.2 | async-start | bytes 524288 | tf_op jit(solution)/shard_map/all_to_all | solution.py:472
  52.0 8.5 %collective-permute-start.1 = (bf16[128,1024]{1,0:T(8,128)(2,1)}, bf16[128,1024]{1,0:T(8,128)(2,1)S(1)}, u32[]{:S(2)}, u32[]{:S(2)}) collective-permute-start(bf16[128,1024]{1,0:T(8,128)(2,1)} %get-tuple-element.23), channel_id=1, source_target_pairs={{0,1},{1,0},{2,3},{3,2},{4,5},{5,4},{6,7},{7,6},{8,9},{9,8},{10,11... | collective-permute-start | bytes 786440 | tf_op jit(solution)/shard_map/ppermute | solution.py:485
  53.5 2.2 %copy-start = (bf16[1024,2048]{1,0:T(8,128)(2,1)S(1)}, bf16[1024,2048]{1,0:T(8,128)(2,1)}, u32[]{:S(2)}) copy-start(bf16[1024,2048]{1,0:T(8,128)(2,1)} %weight_hbm.1) | copy-start | bytes 12582916
  55.7 1.0 %copy-start.4 = (f32[1024,128]{1,0:T(8,128)S(1)}, f32[1024,128]{1,0:T(8,128)}, u32[]{:S(2)}) copy-start(f32[1024,128]{1,0:T(8,128)} %get-tuple-element.21.grad_ref) | copy-start | bytes 1572868
  56.7 0.9 %copy-start.5 = (bf16[128,1024]{1,0:T(8,128)(2,1)S(1)}, bf16[128,1024]{1,0:T(8,128)(2,1)}, u32[]{:S(2)}) copy-start(bf16[128,1024]{1,0:T(8,128)(2,1)} %get-tuple-element.20.gated_ref) | copy-start | bytes 786436

commit v15 on v13

--- a/solution.py
+++ b/solution.py
@@ -150,7 +150,8 @@
 
 def group_order(n):
     half = n // 2
-    return [rank for i in range(half) for rank in (half + i, half - 1 - i)]
+    order = [rank for i in range(half) for rank in (half + i, half - 1 - i)]
+    return [order[1], order[0], *order[2:]]
 
 
 def group_places(n):

time: 60.6 us -> 59.7 us (0.985)
  starting transfers between devices: 16.4 us -> 15 us
  waiting for transfers between devices: 4.98 us -> 5.75 us
    all_to_all x2, starting transfers between devices: 13.4 us -> 11.9 us  [exchange(): lax.all_to_all(block, 'ctx', split_axis=0, concat_axis=0, tiled=True, axi...]
    all_to_all x2, waiting for transfers between devices: 1.17 us -> 1.92 us  [exchange(): lax.all_to_all(block, 'ctx', split_axis=0, concat_axis=0, tiled=True, axi...]
where the time goes in v15:
time: 59.7 us; the launch traced here: 59.1 us
  blocking collectives  17.3 us (29%)
  Pallas kernels  16.2 us (27%)
  starting transfers between devices  15 us (25%)
  waiting for transfers between devices  5.75 us (10%)
  local copies, waits for them, and re-layouts  4.2 us (7%)
  between operations  0.71 us (1%)
    all_to_all x1, blocking collectives, exchange(): lax.all_to_all(block, 'ctx', split_axis=0, concat_axis=0, tiled=True, axi...  17.3 us
    pallas_call x8, Pallas kernels, call(): pl.pallas_call(kernel, out_shape=outs, grid_spec=pltpu.PrefetchScalarGrid...  16.2 us
    all_to_all x2, starting transfers between devices, exchange(): lax.all_to_all(block, 'ctx', split_axis=0, concat_axis=0, tiled=True, axi...  11.9 us
    unnamed x18, local copies, waits for them, and re-layouts  4.2 us
    ppermute x2, waiting for transfers between devices, swap_tp(): return lax.ppermute(block, 'tp', [(0, 1), (1, 0)])  3.83 us
    ppermute x2, starting transfers between devices, swap_tp(): return lax.ppermute(block, 'tp', [(0, 1), (1, 0)])  3.04 us
    all_to_all x2, waiting for transfers between devices, exchange(): lax.all_to_all(block, 'ctx', split_axis=0, concat_axis=0, tiled=True, axi...  1.92 us
  transfers between devices with their start and end apart: 4, of which 3 were waited for; matrix products, arithmetic and copies ran while one was open for 0% of the time, Pallas kernels for 16%

profile of v15, /device:TPU:0, one launch (start us, length us, event | category | flops | bytes accessed | tf_op | source)
XLA Modules:
  0.0 59.1 jit_solution(4323633609887377468)
XLA Ops:
  0.6 2.1 %shard_map.120 = bf16[16,128,128]{2,1,0:T(8,128)(2,1)} custom-call(s32[1,128]{1,0:T(1,128)} %bitcast.2, bf16[128,1024]{1,0:T(8,128)(2,1)} %pre_ref.3, bf16[128,1024]{1,0:T(8,128)(2,1)} %feat_ref.3, f32[128,1024]{1,0:T(8,128)} %filt_ref.1), custom_call_target="tpu_custom_call" | custom-call | bytes 1573376 | tf_op jit(solution)/shard_map/pallas_call | solution.py:451
  2.7 7.6 %all-to-all-start = ((bf16[16,128,128]{2,1,0:T(8,128)(2,1)}), bf16[16,128,128]{2,1,0:T(8,128)(2,1)S(1)}, u32[]{:S(2)}, u32[]{:S(2)}) async-start(bf16[16,128,128]{2,1,0:T(8,128)(2,1)} %shard_map.120), calls=%async_computation | async-start | bytes 1048576 | tf_op jit(solution)/shard_map/all_to_all | solution.py:467
  10.3 1.5 %collective-permute-start = (bf16[128,1024]{1,0:T(8,128)(2,1)}, bf16[128,1024]{1,0:T(8,128)(2,1)S(1)}, u32[]{:S(2)}, u32[]{:S(2)}) collective-permute-start(bf16[128,1024]{1,0:T(8,128)(2,1)} %own_ref.1), channel_id=1, source_target_pairs={{0,1},{1,0},{2,3},{3,2},{4,5},{5,4},{6,7},{7,6},{8,9},{9,8},{10,11... | collective-permute-start | bytes 786440 | tf_op jit(solution)/shard_map/ppermute | solution.py:480
  11.8 0.0 copy-start.6
  11.8 0.0 copy-start.7
  11.8 3.1 %shard_map.121.part_ref = f32[1024,128]{1,0:T(8,128)S(1)} custom-call(s32[1]{0:T(128)} %bitcast.rank_ref, bf16[128,1024]{1,0:T(8,128)(2,1)} %own_ref.1, bf16[1024,2048]{1,0:T(8,128)(2,1)} %weight_hbm.1), custom_call_target="tpu_custom_call" | custom-call | flops 268435456 | bytes 4980736 | tf_op jit(solution)/shard_map/pallas_call | solution.py:451
  15.0 0.0 copy-start.3
  15.0 3.8 %collective-permute-done.other_ref = bf16[128,1024]{1,0:T(8,128)(2,1)S(1)} collective-permute-done((bf16[128,1024]{1,0:T(8,128)(2,1)}, bf16[128,1024]{1,0:T(8,128)(2,1)S(1)}, u32[]{:S(2)}, u32[]{:S(2)}) %collective-permute-start) | collective-permute-done | bytes 262176 | tf_op jit(solution)/shard_map/ppermute | solution.py:480
  18.8 4.0 %shard_map.122 = (f32[1024,128]{1,0:T(8,128)}, bf16[16,64,128]{2,1,0:T(8,128)(2,1)S(1)}, bf16[1024,1024]{1,0:T(8,128)(2,1)S(1)}) custom-call(s32[1]{0:T(128)} %bitcast.rank_ref, bf16[128,1024]{1,0:T(8,128)(2,1)S(1)} %collective-permute-done.other_ref, bf16[1024,2048]{1,0:T(8,128)(2,1)} %weight_hbm.1, f32[1024,128]{1,0:T(8,128)S(1)} %shard_map.121.part_ref, ...), custom_call_target="tpu_custom_call" | custom-call | flops 268435456 | bytes 8126464 | tf_op jit(solution)/shard_map/pallas_call | solution.py:451
  22.9 1.0 %all-to-all-done.pair_ref = bf16[16,128,128]{2,1,0:T(8,128)(2,1)S(1)} async-done(((bf16[16,128,128]{2,1,0:T(8,128)(2,1)}), bf16[16,128,128]{2,1,0:T(8,128)(2,1)S(1)}, u32[]{:S(2)}, u32[]{:S(2)}) %all-to-all-start) | async-done | bytes 524320 | tf_op jit(solution)/shard_map/all_to_all | solution.py:467
  23.8 0.0 copy-done.6
  23.8 0.0 copy-done.7
  23.8 1.8 %shard_map.123 = (bf16[16,64,256]{2,1,0:T(8,128)(2,1)S(1)}, bf16[17,64,256]{2,1,0:T(8,128)(2,1)S(1)}) custom-call(bf16[16,128,128]{2,1,0:T(8,128)(2,1)S(1)} %all-to-all-done.pair_ref, bf16[16,64,128]{2,1,0:T(8,128)(2,1)S(1)} %get-tuple-element.16.grad_ref, f32[34,128]{1,0:T(8,128)S(1)} %copy-done.7, bf16[128,256]{1,0:T(8,128)(2,1)S(1)} %copy-done.6), custom_call_target="tpu_custom_call" | custom-call | flops 427819008 | bytes 1950720 | tf_op jit(solution)/shard_map/pallas_call | solution.py:451
  25.6 17.3 %all_to_all.15.both_ref = bf16[16,64,256]{2,1,0:T(8,128)(2,1)S(1)} all-to-all(bf16[16,64,256]{2,1,0:T(8,128)(2,1)S(1)} %get-tuple-element.17), channel_id=1, replica_groups={{14,16,18,12,20,10,22,8,24,6,26,4,28,2,30,0},{15,17,19,13,21,11,23,9,25..., dimensions={0} | all-to-all | bytes 1048576 | tf_op jit(solution)/shard_map/all_to_all | solution.py:467
  42.9 0.0 copy-done.3
  42.9 0.0 copy-start.1
  42.9 0.0 copy-start.2
  42.9 0.0 copy-start.8
  42.9 2.1 %shard_map.124 = (bf16[16,64,128]{2,1,0:T(8,128)(2,1)}, bf16[128,1024]{1,0:T(8,128)(2,1)}, bf16[128,1024]{1,0:T(8,128)(2,1)}) custom-call(bf16[16,64,256]{2,1,0:T(8,128)(2,1)S(1)} %all_to_all.15.both_ref, bf16[128,1024]{1,0:T(8,128)(2,1)S(1)} %copy-done.3, f32[34,128]{1,0:T(8,128)S(1)} %copy-done.7, bf16[128,256]{1,0:T(8,128)(2,1)S(1)} %copy-done.6, ...), custom_call_target="tpu_custom_call" | custom-call | flops 553648128 | bytes 4310016 | tf_op jit(solution)/shard_map/pallas_call | solution.py:451
  45.0 4.3 %all-to-all-start.2 = ((bf16[16,64,128]{2,1,0:T(8,128)(2,1)}), bf16[16,64,128]{2,1,0:T(8,128)(2,1)S(1)}, u32[]{:S(2)}, u32[]{:S(2)}) async-start(bf16[16,64,128]{2,1,0:T(8,128)(2,1)} %get-tuple-element.24), calls=%async_computation.2 | async-start | bytes 524288 | tf_op jit(solution)/shard_map/all_to_all | solution.py:467
  49.4 1.5 %collective-permute-start.1 = (bf16[128,1024]{1,0:T(8,128)(2,1)}, bf16[128,1024]{1,0:T(8,128)(2,1)S(1)}, u32[]{:S(2)}, u32[]{:S(2)}) collective-permute-start(bf16[128,1024]{1,0:T(8,128)(2,1)} %get-tuple-element.23), channel_id=1, source_target_pairs={{0,1},{1,0},{2,3},{3,2},{4,5},{5,4},{6,7},{7,6},{8,9},{9,8},{10,11... | collective-permute-start | bytes 786440 | tf_op jit(solution)/shard_map/ppermute | solution.py:480
  50.9 2.2 %copy-done = bf16[1024,2048]{1,0:T(8,128)(2,1)S(1)} copy-done((bf16[1024,2048]{1,0:T(8,128)(2,1)S(1)}, bf16[1024,2048]{1,0:T(8,128)(2,1)}, u32[]{:S(2)}) %copy-start) | copy-done | bytes 4194328
  53.1 1.0 %copy-done.4 = f32[1024,128]{1,0:T(8,128)S(1)} copy-done((f32[1024,128]{1,0:T(8,128)S(1)}, f32[1024,128]{1,0:T(8,128)}, u32[]{:S(2)}) %copy-start.4) | copy-done | bytes 524312
  54.1 0.9 %copy-done.5 = bf16[128,1024]{1,0:T(8,128)(2,1)S(1)} copy-done((bf16[128,1024]{1,0:T(8,128)(2,1)S(1)}, bf16[128,1024]{1,0:T(8,128)(2,1)}, u32[]{:S(2)}) %copy-start.5) | copy-done | bytes 262168
  55.1 1.4 %shard_map.125 = (f32[128,1024]{1,0:T(8,128)S(1)}, bf16[128,1024]{1,0:T(8,128)(2,1)}) custom-call(s32[1]{0:T(128)} %bitcast.rank_ref, bf16[128,1024]{1,0:T(8,128)(2,1)S(1)} %copy-done.5, bf16[16,64,256]{2,1,0:T(8,128)(2,1)S(1)} %all_to_all.15.both_ref, f32[1024,128]{1,0:T(8,128)S(1)} %copy-done.4, bf16[1024,2048]{1,0:T(8,128)(2,1)S(1)} %copy-done), custom_call_target="tpu_custom_call" | custom-call | flops 268435456 | bytes 6291456 | tf_op jit(solution)/shard_map/pallas_call | solution.py:451
  56.4 0.9 %all-to-all-done.2.packed_ref = bf16[16,64,128]{2,1,0:T(8,128)(2,1)S(1)} async-done(((bf16[16,64,128]{2,1,0:T(8,128)(2,1)}), bf16[16,64,128]{2,1,0:T(8,128)(2,1)S(1)}, u32[]{:S(2)}, u32[]{:S(2)}) %all-to-all-start.2) | async-done | bytes 262176 | tf_op jit(solution)/shard_map/all_to_all | solution.py:467
  57.4 0.0 copy-done.1
  57.4 0.0 copy-done.2
  57.4 0.0 copy-done.8
  57.4 0.9 %shard_map.126 = (bf16[128,1024]{1,0:T(8,128)(2,1)}, bf16[128,1024]{1,0:T(8,128)(2,1)}) custom-call(s32[1,128]{1,0:T(1,128)S(1)} %bitcast.3, bf16[16,64,128]{2,1,0:T(8,128)(2,1)S(1)} %all-to-all-done.2.packed_ref, bf16[128,1024]{1,0:T(8,128)(2,1)S(1)} %copy-done.1, bf16[128,1024]{1,0:T(8,128)(2,1)S(1)} %copy-done.2), custom_call_target="tpu_custom_call" | custom-call | bytes 1311232 | tf_op jit(solution)/shard_map/pallas_call | solution.py:451
  58.3 0.0 collective-permute-done.1.other_ref
  58.3 0.7 %shard_map.127 = bf16[128,1024]{1,0:T(8,128)(2,1)} custom-call(f32[128,1024]{1,0:T(8,128)S(1)} %get-tuple-element.22.home_ref, bf16[128,1024]{1,0:T(8,128)(2,1)S(1)} %collective-permute-done.1.other_ref, bf16[128,1024]{1,0:T(8,128)(2,1)} %get-tuple-element.15.after_hbm), custom_call_target="tpu_custom_call" | custom-call | bytes 1310720 | tf_op jit(solution)/shard_map/pallas_call | solution.py:451
  (3 shorter events, 0.0 us)
Async XLA Ops:
  2.7 21.1 %all-to-all-start = ((bf16[16,128,128]{2,1,0:T(8,128)(2,1)}), bf16[16,128,128]{2,1,0:T(8,128)(2,1)S(1)}, u32[]{:S(2)}, u32[]{:S(2)}) async-start(bf16[16,128,128]{2,1,0:T(8,128)(2,1)} %shard_map.120), calls=%async_computation | async-start | bytes 1048576 | tf_op jit(solution)/shard_map/all_to_all | solution.py:467
  10.3 8.5 %collective-permute-start = (bf16[128,1024]{1,0:T(8,128)(2,1)}, bf16[128,1024]{1,0:T(8,128)(2,1)S(1)}, u32[]{:S(2)}, u32[]{:S(2)}) collective-permute-start(bf16[128,1024]{1,0:T(8,128)(2,1)} %own_ref.1), channel_id=1, source_target_pairs={{0,1},{1,0},{2,3},{3,2},{4,5},{5,4},{6,7},{7,6},{8,9},{9,8},{10,11... | collective-permute-start | bytes 786440 | tf_op jit(solution)/shard_map/ppermute | solution.py:480
  11.8 12.0 %copy-start.6 = (bf16[128,256]{1,0:T(8,128)(2,1)S(1)}, bf16[128,256]{1,0:T(8,128)(2,1)}, u32[]{:S(2)}) copy-start(bf16[128,256]{1,0:T(8,128)(2,1)} %constant.9.clone.dft_ref) | copy-start | bytes 196612
  11.8 12.0 %copy-start.7 = (f32[34,128]{1,0:T(8,128)S(1)}, f32[34,128]{1,0:T(8,128)}, u32[]{:S(2)}) copy-start(f32[34,128]{1,0:T(8,128)} %constant.8.clone.twist_ref) | copy-start | bytes 52228
  15.0 27.9 %copy-start.3 = (bf16[128,1024]{1,0:T(8,128)(2,1)S(1)}, bf16[128,1024]{1,0:T(8,128)(2,1)}, u32[]{:S(2)}) copy-start(bf16[128,1024]{1,0:T(8,128)(2,1)} %post_ref.3) | copy-start | bytes 786436
  42.9 14.5 %copy-start.1 = (bf16[128,1024]{1,0:T(8,128)(2,1)S(1)}, bf16[128,1024]{1,0:T(8,128)(2,1)}, u32[]{:S(2)}) copy-start(bf16[128,1024]{1,0:T(8,128)(2,1)} %pre_ref.3) | copy-start | bytes 786436
  42.9 14.5 %copy-start.2 = (bf16[128,1024]{1,0:T(8,128)(2,1)S(1)}, bf16[128,1024]{1,0:T(8,128)(2,1)}, u32[]{:S(2)}) copy-start(bf16[128,1024]{1,0:T(8,128)(2,1)} %feat_ref.3) | copy-start | bytes 786436
  42.9 14.5 %copy-start.8 = (s32[128]{0:T(128)S(1)}, s32[128]{0:T(128)}, u32[]{:S(2)}) copy-start(s32[128]{0:T(128)} %param.13) | copy-start | bytes 1540
  45.0 12.3 %all-to-all-start.2 = ((bf16[16,64,128]{2,1,0:T(8,128)(2,1)}), bf16[16,64,128]{2,1,0:T(8,128)(2,1)S(1)}, u32[]{:S(2)}, u32[]{:S(2)}) async-start(bf16[16,64,128]{2,1,0:T(8,128)(2,1)} %get-tuple-element.24), calls=%async_computation.2 | async-start | bytes 524288 | tf_op jit(solution)/shard_map/all_to_all | solution.py:467
  49.4 9.0 %collective-permute-start.1 = (bf16[128,1024]{1,0:T(8,128)(2,1)}, bf16[128,1024]{1,0:T(8,128)(2,1)S(1)}, u32[]{:S(2)}, u32[]{:S(2)}) collective-permute-start(bf16[128,1024]{1,0:T(8,128)(2,1)} %get-tuple-element.23), channel_id=1, source_target_pairs={{0,1},{1,0},{2,3},{3,2},{4,5},{5,4},{6,7},{7,6},{8,9},{9,8},{10,11... | collective-permute-start | bytes 786440 | tf_op jit(solution)/shard_map/ppermute | solution.py:480
  50.9 2.2 %copy-start = (bf16[1024,2048]{1,0:T(8,128)(2,1)S(1)}, bf16[1024,2048]{1,0:T(8,128)(2,1)}, u32[]{:S(2)}) copy-start(bf16[1024,2048]{1,0:T(8,128)(2,1)} %weight_hbm.1) | copy-start | bytes 12582916
  53.1 1.0 %copy-start.4 = (f32[1024,128]{1,0:T(8,128)S(1)}, f32[1024,128]{1,0:T(8,128)}, u32[]{:S(2)}) copy-start(f32[1024,128]{1,0:T(8,128)} %get-tuple-element.21.grad_ref) | copy-start | bytes 1572868
  54.1 0.9 %copy-start.5 = (bf16[128,1024]{1,0:T(8,128)(2,1)S(1)}, bf16[128,1024]{1,0:T(8,128)(2,1)}, u32[]{:S(2)}) copy-start(bf16[128,1024]{1,0:T(8,128)(2,1)} %get-tuple-element.20.gated_ref) | copy-start | bytes 786436

commit v16 on v15

--- a/solution.py
+++ b/solution.py
@@ -151,7 +151,8 @@
 def group_order(n):
     half = n // 2
     order = [rank for i in range(half) for rank in (half + i, half - 1 - i)]
-    return [order[1], order[0], *order[2:]]
+    first = n // 4 - 1
+    return [first, *(rank for rank in order if rank != first)]
 
 
 def group_places(n):

time: 59.7 us -> 61.4 us (1.028)
  starting transfers between devices: 15 us -> 19.4 us
  waiting for transfers between devices: 5.75 us -> 4.31 us
  blocking collectives: 17.3 us -> 16 us
    all_to_all x2, starting transfers between devices: 11.9 us -> 16.4 us  [exchange(): lax.all_to_all(block, 'ctx', split_axis=0, concat_axis=0, tiled=True, axi...]
    all_to_all x2, waiting for transfers between devices: 1.92 us -> 0.33 us  [exchange(): lax.all_to_all(block, 'ctx', split_axis=0, concat_axis=0, tiled=True, axi...]
    all_to_all x1, blocking collectives: 17.3 us -> 16 us  [exchange(): lax.all_to_all(block, 'ctx', split_axis=0, concat_axis=0, tiled=True, axi...]
where the time goes in v16:
time: 61.4 us; the launch traced here: 60.8 us
  starting transfers between devices  19.4 us (32%)
  Pallas kernels  16.2 us (26%)
  blocking collectives  16 us (26%)
  waiting for transfers between devices  4.31 us (7%)
  local copies, waits for them, and re-layouts  4.2 us (7%)
  between operations  0.71 us (1%)
    all_to_all x2, starting transfers between devices, exchange(): lax.all_to_all(block, 'ctx', split_axis=0, concat_axis=0, tiled=True, axi...  16.4 us
    pallas_call x8, Pallas kernels, call(): pl.pallas_call(kernel, out_shape=outs, grid_spec=pltpu.PrefetchScalarGrid...  16.2 us
    all_to_all x1, blocking collectives, exchange(): lax.all_to_all(block, 'ctx', split_axis=0, concat_axis=0, tiled=True, axi...  16 us
    unnamed x18, local copies, waits for them, and re-layouts  4.2 us
    ppermute x2, waiting for transfers between devices, swap_tp(): return lax.ppermute(block, 'tp', [(0, 1), (1, 0)])  3.98 us
    ppermute x2, starting transfers between devices, swap_tp(): return lax.ppermute(block, 'tp', [(0, 1), (1, 0)])  3.04 us
  transfers between devices with their start and end apart: 4, of which 3 were waited for; matrix products, arithmetic and copies ran while one was open for 0% of the time, Pallas kernels for 16%

profile of v16, /device:TPU:0, one launch (start us, length us, event | category | flops | bytes accessed | tf_op | source)
XLA Modules:
  0.0 60.8 jit_solution(8142698556112901311)
XLA Ops:
  0.6 2.1 %shard_map.120 = bf16[16,128,128]{2,1,0:T(8,128)(2,1)} custom-call(s32[1,128]{1,0:T(1,128)} %bitcast.2, bf16[128,1024]{1,0:T(8,128)(2,1)} %pre_ref.3, bf16[128,1024]{1,0:T(8,128)(2,1)} %feat_ref.3, f32[128,1024]{1,0:T(8,128)} %filt_ref.1), custom_call_target="tpu_custom_call" | custom-call | bytes 1573376 | tf_op jit(solution)/shard_map/pallas_call | solution.py:452
  2.7 7.6 %all-to-all-start = ((bf16[16,128,128]{2,1,0:T(8,128)(2,1)}), bf16[16,128,128]{2,1,0:T(8,128)(2,1)S(1)}, u32[]{:S(2)}, u32[]{:S(2)}) async-start(bf16[16,128,128]{2,1,0:T(8,128)(2,1)} %shard_map.120), calls=%async_computation | async-start | bytes 1048576 | tf_op jit(solution)/shard_map/all_to_all | solution.py:468
  10.3 1.5 %collective-permute-start = (bf16[128,1024]{1,0:T(8,128)(2,1)}, bf16[128,1024]{1,0:T(8,128)(2,1)S(1)}, u32[]{:S(2)}, u32[]{:S(2)}) collective-permute-start(bf16[128,1024]{1,0:T(8,128)(2,1)} %own_ref.1), channel_id=1, source_target_pairs={{0,1},{1,0},{2,3},{3,2},{4,5},{5,4},{6,7},{7,6},{8,9},{9,8},{10,11... | collective-permute-start | bytes 786440 | tf_op jit(solution)/shard_map/ppermute | solution.py:481
  11.8 0.0 copy-start.6
  11.8 0.0 copy-start.7
  11.8 3.1 %shard_map.121.part_ref = f32[1024,128]{1,0:T(8,128)S(1)} custom-call(s32[1]{0:T(128)} %bitcast.rank_ref, bf16[128,1024]{1,0:T(8,128)(2,1)} %own_ref.1, bf16[1024,2048]{1,0:T(8,128)(2,1)} %weight_hbm.1), custom_call_target="tpu_custom_call" | custom-call | flops 268435456 | bytes 4980736 | tf_op jit(solution)/shard_map/pallas_call | solution.py:452
  15.0 0.0 copy-start.3
  15.0 3.8 %collective-permute-done.other_ref = bf16[128,1024]{1,0:T(8,128)(2,1)S(1)} collective-permute-done((bf16[128,1024]{1,0:T(8,128)(2,1)}, bf16[128,1024]{1,0:T(8,128)(2,1)S(1)}, u32[]{:S(2)}, u32[]{:S(2)}) %collective-permute-start) | collective-permute-done | bytes 262176 | tf_op jit(solution)/shard_map/ppermute | solution.py:481
  18.8 4.0 %shard_map.122 = (f32[1024,128]{1,0:T(8,128)}, bf16[16,64,128]{2,1,0:T(8,128)(2,1)S(1)}, bf16[1024,1024]{1,0:T(8,128)(2,1)S(1)}) custom-call(s32[1]{0:T(128)} %bitcast.rank_ref, bf16[128,1024]{1,0:T(8,128)(2,1)S(1)} %collective-permute-done.other_ref, bf16[1024,2048]{1,0:T(8,128)(2,1)} %weight_hbm.1, f32[1024,128]{1,0:T(8,128)S(1)} %shard_map.121.part_ref, ...), custom_call_target="tpu_custom_call" | custom-call | flops 268435456 | bytes 8126464 | tf_op jit(solution)/shard_map/pallas_call | solution.py:452
  22.9 0.0 all-to-all-done.pair_ref
  22.9 0.0 copy-done.6
  22.9 0.0 copy-done.7
  22.9 1.8 %shard_map.123 = (bf16[16,64,256]{2,1,0:T(8,128)(2,1)S(1)}, bf16[17,64,256]{2,1,0:T(8,128)(2,1)S(1)}) custom-call(bf16[16,128,128]{2,1,0:T(8,128)(2,1)S(1)} %all-to-all-done.pair_ref, bf16[16,64,128]{2,1,0:T(8,128)(2,1)S(1)} %get-tuple-element.16.grad_ref, f32[34,128]{1,0:T(8,128)S(1)} %copy-done.7, bf16[128,256]{1,0:T(8,128)(2,1)S(1)} %copy-done.6), custom_call_target="tpu_custom_call" | custom-call | flops 427819008 | bytes 1950720 | tf_op jit(solution)/shard_map/pallas_call | solution.py:452
  24.7 16.0 %all_to_all.15.both_ref = bf16[16,64,256]{2,1,0:T(8,128)(2,1)S(1)} all-to-all(bf16[16,64,256]{2,1,0:T(8,128)(2,1)S(1)} %get-tuple-element.17), channel_id=1, replica_groups={{6,16,14,18,12,20,10,22,8,24,26,4,28,2,30,0},{7,17,15,19,13,21,11,23,9,..., dimensions={0} | all-to-all | bytes 1048576 | tf_op jit(solution)/shard_map/all_to_all | solution.py:468
  40.6 0.0 copy-done.3
  40.6 0.0 copy-start.1
  40.6 0.0 copy-start.8
  40.6 2.1 %shard_map.124 = (bf16[16,64,128]{2,1,0:T(8,128)(2,1)}, bf16[128,1024]{1,0:T(8,128)(2,1)}, bf16[128,1024]{1,0:T(8,128)(2,1)}) custom-call(bf16[16,64,256]{2,1,0:T(8,128)(2,1)S(1)} %all_to_all.15.both_ref, bf16[128,1024]{1,0:T(8,128)(2,1)S(1)} %copy-done.3, f32[34,128]{1,0:T(8,128)S(1)} %copy-done.7, bf16[128,256]{1,0:T(8,128)(2,1)S(1)} %copy-done.6, ...), custom_call_target="tpu_custom_call" | custom-call | flops 553648128 | bytes 4310016 | tf_op jit(solution)/shard_map/pallas_call | solution.py:452
  42.7 8.8 %all-to-all-start.2 = ((bf16[16,64,128]{2,1,0:T(8,128)(2,1)}), bf16[16,64,128]{2,1,0:T(8,128)(2,1)S(1)}, u32[]{:S(2)}, u32[]{:S(2)}) async-start(bf16[16,64,128]{2,1,0:T(8,128)(2,1)} %get-tuple-element.24), calls=%async_computation.2 | async-start | bytes 524288 | tf_op jit(solution)/shard_map/all_to_all | solution.py:468
  51.5 1.5 %collective-permute-start.1 = (bf16[128,1024]{1,0:T(8,128)(2,1)}, bf16[128,1024]{1,0:T(8,128)(2,1)S(1)}, u32[]{:S(2)}, u32[]{:S(2)}) collective-permute-start(bf16[128,1024]{1,0:T(8,128)(2,1)} %get-tuple-element.23), channel_id=1, source_target_pairs={{0,1},{1,0},{2,3},{3,2},{4,5},{5,4},{6,7},{7,6},{8,9},{9,8},{10,11... | collective-permute-start | bytes 786440 | tf_op jit(solution)/shard_map/ppermute | solution.py:481
  53.1 0.0 copy-start
  53.1 2.2 %copy-done = bf16[1024,2048]{1,0:T(8,128)(2,1)S(1)} copy-done((bf16[1024,2048]{1,0:T(8,128)(2,1)S(1)}, bf16[1024,2048]{1,0:T(8,128)(2,1)}, u32[]{:S(2)}) %copy-start) | copy-done | bytes 4194328
  55.3 1.0 %copy-done.4 = f32[1024,128]{1,0:T(8,128)S(1)} copy-done((f32[1024,128]{1,0:T(8,128)S(1)}, f32[1024,128]{1,0:T(8,128)}, u32[]{:S(2)}) %copy-start.4) | copy-done | bytes 524312
  56.3 0.9 %copy-done.5 = bf16[128,1024]{1,0:T(8,128)(2,1)S(1)} copy-done((bf16[128,1024]{1,0:T(8,128)(2,1)S(1)}, bf16[128,1024]{1,0:T(8,128)(2,1)}, u32[]{:S(2)}) %copy-start.5) | copy-done | bytes 262168
  57.2 1.4 %shard_map.125 = (f32[128,1024]{1,0:T(8,128)S(1)}, bf16[128,1024]{1,0:T(8,128)(2,1)}) custom-call(s32[1]{0:T(128)} %bitcast.rank_ref, bf16[128,1024]{1,0:T(8,128)(2,1)S(1)} %copy-done.5, bf16[16,64,256]{2,1,0:T(8,128)(2,1)S(1)} %all_to_all.15.both_ref, f32[1024,128]{1,0:T(8,128)S(1)} %copy-done.4, bf16[1024,2048]{1,0:T(8,128)(2,1)S(1)} %copy-done), custom_call_target="tpu_custom_call" | custom-call | flops 268435456 | bytes 6291456 | tf_op jit(solution)/shard_map/pallas_call | solution.py:452
  58.6 0.3 all-to-all-done.2.packed_ref
  58.9 0.0 copy-done.1
  58.9 0.0 copy-done.2
  58.9 0.0 copy-done.8
  59.0 0.9 %shard_map.126 = (bf16[128,1024]{1,0:T(8,128)(2,1)}, bf16[128,1024]{1,0:T(8,128)(2,1)}) custom-call(s32[1,128]{1,0:T(1,128)S(1)} %bitcast.3, bf16[16,64,128]{2,1,0:T(8,128)(2,1)S(1)} %all-to-all-done.2.packed_ref, bf16[128,1024]{1,0:T(8,128)(2,1)S(1)} %copy-done.1, bf16[128,1024]{1,0:T(8,128)(2,1)S(1)} %copy-done.2), custom_call_target="tpu_custom_call" | custom-call | bytes 1311232 | tf_op jit(solution)/shard_map/pallas_call | solution.py:452
  59.9 0.2 collective-permute-done.1.other_ref
  60.1 0.7 %shard_map.127 = bf16[128,1024]{1,0:T(8,128)(2,1)} custom-call(f32[128,1024]{1,0:T(8,128)S(1)} %get-tuple-element.22.home_ref, bf16[128,1024]{1,0:T(8,128)(2,1)S(1)} %collective-permute-done.1.other_ref, bf16[128,1024]{1,0:T(8,128)(2,1)} %get-tuple-element.15.after_hbm), custom_call_target="tpu_custom_call" | custom-call | bytes 1310720 | tf_op jit(solution)/shard_map/pallas_call | solution.py:452
  (3 shorter events, 0.0 us)
Async XLA Ops:
  2.7 20.1 %all-to-all-start = ((bf16[16,128,128]{2,1,0:T(8,128)(2,1)}), bf16[16,128,128]{2,1,0:T(8,128)(2,1)S(1)}, u32[]{:S(2)}, u32[]{:S(2)}) async-start(bf16[16,128,128]{2,1,0:T(8,128)(2,1)} %shard_map.120), calls=%async_computation | async-start | bytes 1048576 | tf_op jit(solution)/shard_map/all_to_all | solution.py:468
  10.3 8.5 %collective-permute-start = (bf16[128,1024]{1,0:T(8,128)(2,1)}, bf16[128,1024]{1,0:T(8,128)(2,1)S(1)}, u32[]{:S(2)}, u32[]{:S(2)}) collective-permute-start(bf16[128,1024]{1,0:T(8,128)(2,1)} %own_ref.1), channel_id=1, source_target_pairs={{0,1},{1,0},{2,3},{3,2},{4,5},{5,4},{6,7},{7,6},{8,9},{9,8},{10,11... | collective-permute-start | bytes 786440 | tf_op jit(solution)/shard_map/ppermute | solution.py:481
  11.8 11.0 %copy-start.6 = (bf16[128,256]{1,0:T(8,128)(2,1)S(1)}, bf16[128,256]{1,0:T(8,128)(2,1)}, u32[]{:S(2)}) copy-start(bf16[128,256]{1,0:T(8,128)(2,1)} %constant.9.clone.dft_ref) | copy-start | bytes 196612
  11.8 11.0 %copy-start.7 = (f32[34,128]{1,0:T(8,128)S(1)}, f32[34,128]{1,0:T(8,128)}, u32[]{:S(2)}) copy-start(f32[34,128]{1,0:T(8,128)} %constant.8.clone.twist_ref) | copy-start | bytes 52228
  15.0 25.6 %copy-start.3 = (bf16[128,1024]{1,0:T(8,128)(2,1)S(1)}, bf16[128,1024]{1,0:T(8,128)(2,1)}, u32[]{:S(2)}) copy-start(bf16[128,1024]{1,0:T(8,128)(2,1)} %post_ref.3) | copy-start | bytes 786436
  40.6 18.3 %copy-start.1 = (bf16[128,1024]{1,0:T(8,128)(2,1)S(1)}, bf16[128,1024]{1,0:T(8,128)(2,1)}, u32[]{:S(2)}) copy-start(bf16[128,1024]{1,0:T(8,128)(2,1)} %pre_ref.3) | copy-start | bytes 786436
  40.6 18.3 %copy-start.2 = (bf16[128,1024]{1,0:T(8,128)(2,1)S(1)}, bf16[128,1024]{1,0:T(8,128)(2,1)}, u32[]{:S(2)}) copy-start(bf16[128,1024]{1,0:T(8,128)(2,1)} %feat_ref.3) | copy-start | bytes 786436
  40.6 18.3 %copy-start.8 = (s32[128]{0:T(128)S(1)}, s32[128]{0:T(128)}, u32[]{:S(2)}) copy-start(s32[128]{0:T(128)} %param.13) | copy-start | bytes 1540
  42.7 16.2 %all-to-all-start.2 = ((bf16[16,64,128]{2,1,0:T(8,128)(2,1)}), bf16[16,64,128]{2,1,0:T(8,128)(2,1)S(1)}, u32[]{:S(2)}, u32[]{:S(2)}) async-start(bf16[16,64,128]{2,1,0:T(8,128)(2,1)} %get-tuple-element.24), calls=%async_computation.2 | async-start | bytes 524288 | tf_op jit(solution)/shard_map/all_to_all | solution.py:468
  51.5 8.5 %collective-permute-start.1 = (bf16[128,1024]{1,0:T(8,128)(2,1)}, bf16[128,1024]{1,0:T(8,128)(2,1)S(1)}, u32[]{:S(2)}, u32[]{:S(2)}) collective-permute-start(bf16[128,1024]{1,0:T(8,128)(2,1)} %get-tuple-element.23), channel_id=1, source_target_pairs={{0,1},{1,0},{2,3},{3,2},{4,5},{5,4},{6,7},{7,6},{8,9},{9,8},{10,11... | collective-permute-start | bytes 786440 | tf_op jit(solution)/shard_map/ppermute | solution.py:481
  53.1 2.2 %copy-start = (bf16[1024,2048]{1,0:T(8,128)(2,1)S(1)}, bf16[1024,2048]{1,0:T(8,128)(2,1)}, u32[]{:S(2)}) copy-start(bf16[1024,2048]{1,0:T(8,128)(2,1)} %weight_hbm.1) | copy-start | bytes 12582916
  55.3 1.0 %copy-start.4 = (f32[1024,128]{1,0:T(8,128)S(1)}, f32[1024,128]{1,0:T(8,128)}, u32[]{:S(2)}) copy-start(f32[1024,128]{1,0:T(8,128)} %get-tuple-element.21.grad_ref) | copy-start | bytes 1572868
  56.3 0.9 %copy-start.5 = (bf16[128,1024]{1,0:T(8,128)(2,1)S(1)}, bf16[128,1024]{1,0:T(8,128)(2,1)}, u32[]{:S(2)}) copy-start(bf16[128,1024]{1,0:T(8,128)(2,1)} %get-tuple-element.20.gated_ref) | copy-start | bytes 786436
